TPU v7x, 512 devices: a whole 4x8x8 slice. The times are simulated.
512 devices in a mesh: dp: 8 (over y), expert: 64 (over x, z, core).
Axes of the slice: x: 4, y: 8, z: 8, core: 2. Of those that a mesh axis runs over, the one named last changes fastest.
Arguments:
- tokens: bfloat16 [8192, 2048], P(('dp', 'expert')), may hold values from -6 to 6
- cotangent: bfloat16 [8192, 2048], P(('dp', 'expert')), may hold values from -6 to 6
- gate_probs: float32 [8192, 8], P(('dp', 'expert')), may hold values from 0.15 to 0.35
- expert_ids: int32 [8192, 8], P(('dp', 'expert')), may hold values from 0 to 63, as said below
- up_weight: bfloat16 [64, 768, 2048], P('expert', 'dp'), may hold values from -0.125 to 0.125
- down_weight: bfloat16 [64, 768, 2048], P('expert', 'dp'), may hold values from -0.21875 to 0.21875
Outputs:
- mixture: bfloat16 [8192, 2048], P(('dp', 'expert'))
- input_grad: bfloat16 [8192, 2048], P(('dp', 'expert'))
- gate_grad: float32 [8192, 8], P(('dp', 'expert'))
Inputs may be any that keep to these rules, and one draw needn't show every extreme that they name: `expert_ids`: the 8 experts of a row differ. The 16 rows of every device name one and the same expert exactly 9 times; they name every other expert at most 2 times, and one other expert exactly 2 times on every device.
All inputs are finite; a program needn't handle non-finite values.
Results may differ from a plain program's by a relative error of at most 0.0058.
Values may be sent and summed in bfloat16 or wider, within the bound.
No kernel may reach another device: no remote copies, remote signals or barrier semaphores. Data moves between devices by JAX's collectives and lax.ppermute only.
A program may use at most 64 MiB of HBM per device.

v0:
```python
import jax
import jax.numpy as jnp
from jax import lax
from jax.sharding import PartitionSpec as P


def broadcast(block, axis, owner):
    block = jnp.where(lax.axis_index(axis) == owner, block, jnp.zeros_like(block))
    return lax.psum(block, axis)


def expert_terms(row_block, up_piece, down_piece):
    model_width = row_block.shape[1] // 2
    features = row_block[:, :model_width]
    row_grads = row_block[:, model_width:]
    pre_act = jnp.einsum("rd,hd->rh", features, up_piece, preferred_element_type=jnp.float32)
    gating = jax.nn.sigmoid(pre_act)
    hidden = (pre_act * gating).astype(jnp.bfloat16)
    output_rows = jnp.dot(hidden, down_piece, preferred_element_type=jnp.float32)
    hidden_grad = jnp.einsum("rd,hd->rh", row_grads, down_piece, preferred_element_type=jnp.float32)
    act_grad = (hidden_grad * gating * (1.0 + pre_act * (1.0 - gating))).astype(jnp.bfloat16)
    input_rows = jnp.dot(act_grad, up_piece, preferred_element_type=jnp.float32)
    return jnp.concatenate([output_rows, input_rows], 1)


def spread(up_parts, down_parts, row_sets):
    model_width = up_parts.shape[2]
    initial = tuple(
        (jnp.zeros((row_block.shape[0], 2 * model_width), jnp.float32) for row_block in row_sets)
    )
    up_piece = lax.all_gather(up_parts, "dp", axis=1, tiled=True)
    down_piece = lax.all_gather(down_parts, "dp", axis=1, tiled=True)
    return tuple(
        (
            expert_terms(row_block, up_piece[member], down_piece[member])
            for member, (running, row_block) in enumerate(zip(initial, row_sets))
        )
    )


def shards(tokens, cotangent, gate_probs, expert_ids, up_weight, down_weight):
    tok_rows, model_width = tokens.shape
    top_count = expert_ids.shape[1]
    experts = lax.axis_size("expert")
    hot_rows = 9 * tok_rows // 16
    cold_total = experts - 1
    capacity = (tok_rows * top_count - hot_rows + cold_total - 1) // cold_total
    flat_ids = expert_ids.reshape(-1)
    slot_count = flat_ids.shape[0]
    one_hot = (flat_ids[:, None] == jnp.arange(experts, dtype=jnp.int32)[None, :]).astype(jnp.int32)
    hottest = jnp.argmax(jnp.sum(one_hot, 0))
    before = jnp.cumsum(one_hot, 0) - one_hot
    slot_rank = jnp.sum(before * one_hot, 1)
    slot_total = experts * capacity + hot_rows
    slot_index = jnp.where(
        flat_ids == hottest, experts * capacity + slot_rank, flat_ids * capacity + slot_rank
    )
    source_slot = (
        jnp.full((slot_total,), slot_count, jnp.int32)
        .at[slot_index]
        .set(jnp.arange(slot_count, dtype=jnp.int32))
    )
    source_row = source_slot // top_count
    payload = jnp.concatenate([tokens, cotangent], 1)
    padded_payload = jnp.concatenate([payload, jnp.zeros((1, 2 * model_width), payload.dtype)], 0)
    placed = padded_payload[source_row]
    outgoing = placed[: experts * capacity].reshape(experts, capacity, 2 * model_width)
    local_rows = placed[experts * capacity :]
    arrived = lax.all_to_all(outgoing, "expert", split_axis=0, concat_axis=0, tiled=True)
    arrived_rows = arrived.reshape(experts * capacity, 2 * model_width)
    shadow_up, shadow_down = (
        broadcast(up_weight[0], "expert", hottest),
        broadcast(down_weight[0], "expert", hottest),
    )
    (own_out,) = spread(up_weight, down_weight, [arrived_rows])
    (hot_out,) = spread(shadow_up[None], shadow_down[None], [local_rows])
    returning = own_out.astype(jnp.bfloat16).reshape(experts, capacity, 2 * model_width)
    came_back = lax.all_to_all(returning, "expert", split_axis=0, concat_axis=0, tiled=True)
    results = jnp.concatenate(
        [came_back.reshape(experts * capacity, 2 * model_width), hot_out.astype(jnp.bfloat16)], 0
    )
    per_slot = results[slot_index].astype(jnp.float32).reshape(tok_rows, top_count, 2 * model_width)
    scale = gate_probs[:, :, None]
    mixture = jnp.sum(scale * per_slot[:, :, :model_width], 1).astype(jnp.bfloat16)
    input_grad = jnp.sum(scale * per_slot[:, :, model_width:], 1).astype(jnp.bfloat16)
    gate_grad = jnp.sum(cotangent.astype(jnp.float32)[:, None, :] * per_slot[:, :, :model_width], 2)
    return (mixture, input_grad, gate_grad)


def solution(mesh):
    placed = (
        P(("dp", "expert"), None),
        P(("dp", "expert"), None),
        P(("dp", "expert"), None),
        P(("dp", "expert"), None),
        P("expert", "dp", None),
        P("expert", "dp", None),
    )
    return jax.shard_map(
        shards,
        mesh=mesh,
        in_specs=placed,
        out_specs=(P(("dp", "expert"), None), P(("dp", "expert"), None), P(("dp", "expert"), None)),
        check_vma=False,
    )
```

profile of v0, /device:TPU:6, one launch (start us, length us, event | category | flops | bytes accessed | tf_op | source)
XLA Modules:
  0.0 327.7 jit_solution(8105422348470906929)
XLA Ops:
  8.0 0.0 copy-start.8
  8.0 0.0 copy-start.5
  8.0 0.0 copy-start.7
  8.0 0.0 all-reduce.4.cloned.1.call-start
  8.1 0.8 copy.23
  8.8 0.1 eq.37
  8.9 0.1 fusion.59
  9.0 0.2 reduce_window_sum.11
  9.2 0.2 select_reduce_fusion
  9.4 0.7 iota_reduce_fusion
  10.7 0.8 broadcast_select_fusion.1
  11.5 0.8 broadcast_select_fusion
  12.3 0.0 all-reduce.4.cloned.1.call-update
  12.3 0.0 all-gather.5.cloned.1.call-start
  12.4 0.5 all-gather.5.cloned.1.call-update
  12.9 0.0 all-gather.7.cloned.1.call-start
  13.0 0.5 all-gather.7.cloned.1.call-update
  13.5 0.0 all-gather.9.cloned.1.call-start
  13.6 199.4 %all-reduce.4.cloned.1.call-done = (bf16[1,96,2048]{2,1,0:T(8,128)(2,1)}, bf16[1,96,2048]{2,1,0:T(8,128)(2,1)}) async-done(((bf16[1,96,2048]{2,1,0:T(8,128)(2,1)}, bf16[1,96,2048]{2,1,0:T(8,128)(2,1)}), (bf16[1,96,2048]{2,1,0:T(8,128)(2,1)}, bf16[1,96,2048]{2,1,0:T(8,128)(2,1)})) %all-reduce.4.cloned.1.call-update) | async-done | bytes 786448 | tf_op jit(solution)/shard_map/psum | solution.py:9
  212.9 0.0 all-gather.9.cloned.1.call-update
  212.9 0.0 all-gather.11.cloned.1.call-start
  213.0 0.0 copy-done.8
  213.0 0.7 broadcast_compare_fusion
  213.7 0.1 copy.24
  213.7 0.1 eq.43
  213.9 0.1 copy.25
  213.9 0.1 mul.69
  214.0 1.0 scatter_custom_fusion
  215.1 0.0 all-gather.11.cloned.1.call-update
  215.1 0.0 copy-done.5
  215.1 0.0 copy-done.7
  215.1 1.2 gather_fusion
  216.4 0.0 copy-start.3
  216.4 0.1 slice.36
  216.5 0.7 reshape.79
  217.2 35.6 %all_to_all.10 = bf16[64,2,4096]{2,1,0:T(2,128)(2,1)S(1)} all-to-all(bf16[64,2,4096]{2,1,0:T(2,128)(2,1)S(1)} %reshape.79), channel_id=1, replica_groups=mesh['dp'=8,'expert'=64] {'expert'}, dimensions={0} | all-to-all | bytes 2097152 | tf_op jit(solution)/shard_map/all_to_all | solution.py:69
  252.8 0.0 copy-done.3
  252.8 0.4 reshape.80
  253.2 0.0 copy-start.4
  253.2 0.0 all-gather.5.cloned.1.call-done
  253.2 4.3 %multiply_convert_fusion = (bf16[128,768]{1,0:T(8,128)(2,1)}, f32[128,768]{1,0:T(8,128)}) fusion(bf16[1,768,2048]{2,1,0:T(8,128)(2,1)} %all-gather.5.cloned.1.call-done, bf16[128,4096]{1,0:T(8,128)(2,1)S(1)} %reshape.80), kind=kOutput, calls=%fused_computation.41 | convolution fusion | flops 403144704 | bytes 4259840 | tf_op jit(solution)/shard_map/rd,hd->rh/dot_general | solution.py:16
  257.5 3.4 %fusion.34 = bf16[128,768]{1,0:T(8,128)(2,1)S(1)} fusion(bf16[1,768,2048]{2,1,0:T(8,128)(2,1)} %all-gather.7.cloned.1.call-done, bf16[128,4096]{1,0:T(8,128)(2,1)} %copy-done.4, f32[128,768]{1,0:T(8,128)} %get-tuple-element.16), kind=kOutput, calls=%fused_computation.26 | convolution fusion | flops 403537920 | bytes 4259840 | tf_op jit(solution)/shard_map/rd,hd->rh/dot_general | solution.py:20
  261.0 0.1 dot_general.32
  261.1 1.0 dot_general.29
  262.1 0.6 fusion.19
  262.7 1.3 copy-done.2
  264.0 0.6 fusion.16
  264.6 0.0 copy-start.6
  264.6 0.0 copy-start.9
  264.6 0.1 pad_maximum_fusion
  264.7 2.1 copy.28
  266.7 8.3 %all-to-all-start.1 = ((bf16[64,2,4096]{2,1,0:T(2,128)(2,1)}), bf16[64,2,4096]{2,1,0:T(2,128)(2,1)}, u32[]{:S(2)}, u32[]{:S(2)}) async-start(bf16[64,2,4096]{2,1,0:T(2,128)(2,1)} %copy.28), calls=%async_computation.1 | async-start | bytes 2097152 | tf_op jit(solution)/shard_map/all_to_all | solution.py:78
  275.1 0.1 copy.22
  275.2 3.0 fusion.6
  278.2 30.6 %all-gather.11.cloned.1.call-done = bf16[1,768,2048]{2,1,0:T(8,128)(2,1)} async-done(((bf16[1,96,2048]{2,1,0:T(8,128)(2,1)}), bf16[1,768,2048]{2,1,0:T(8,128)(2,1)}) %all-gather.11.cloned.1.call-update) | async-done | bytes 3145744 | tf_op jit(solution)/shard_map/all_gather | solution.py:32
  308.8 2.4 fusion.25
  311.2 3.8 %fusion.22 = bf16[9,2048]{1,0:T(8,128)(2,1)S(1)} fusion(bf16[1,768,2048]{2,1,0:T(8,128)(2,1)S(1)} %copy-done, bf16[1,768,2048]{2,1,0:T(8,128)(2,1)} %all-gather.11.cloned.1.call-done, bf16[137,4096]{1,0:T(8,128)(2,1)} %copy-done.3, f32[9,768]{1,0:T(8,128)S(1)} %fusion.6), kind=kOutput, calls=%fused_computation.21 | convolution fusion | flops 56703744 | bytes 6421504 | tf_op jit(solution)/shard_map/dot_general | solution.py:22
  315.0 0.0 all-to-all-done.1
  315.0 1.5 reshape.81
  316.5 0.1 maximum_maximum_fusion
  316.6 1.2 gather_fusion.1
  317.8 0.2 bitcast_convert_fusion
  318.0 1.4 fusion.46
  319.5 0.7 copy.29
  (18 shorter events, 0.1 us)
Async XLA Ops:
  8.0 205.0 %copy-start.8 = (s32[16,8]{0,1:T(8,128)S(1)}, s32[16,8]{0,1:T(8,128)}, u32[]{:S(2)}) copy-start(s32[16,8]{0,1:T(8,128)} %param.9) | copy-start | bytes 1540
  8.0 207.1 %copy-start.5 = (bf16[16,2048]{1,0:T(8,128)(2,1)S(1)}, bf16[16,2048]{1,0:T(8,128)(2,1)}, u32[]{:S(2)}) copy-start(bf16[16,2048]{1,0:T(8,128)(2,1)} %param.7) | copy-start | bytes 196612
  8.0 207.1 %copy-start.7 = (bf16[16,2048]{1,0:T(8,128)(2,1)S(1)}, bf16[16,2048]{1,0:T(8,128)(2,1)}, u32[]{:S(2)}) copy-start(bf16[16,2048]{1,0:T(8,128)(2,1)} %param.6) | copy-start | bytes 196612
  8.0 204.9 %all-reduce.4.cloned.1.call-start = ((), (), s32[]{:S(2)}) async-start(), calls=%async_computation.6 | async-start | bytes 1572864 | tf_op jit(solution)/shard_map/psum | solution.py:9
  12.3 240.9 %all-gather.5.cloned.1.call-start = ((), (), s32[]{:S(2)}) async-start(), calls=%async_computation.2 | async-start | bytes 3538944 | tf_op jit(solution)/shard_map/all_gather | solution.py:31
  12.9 244.6 %all-gather.7.cloned.1.call-start = ((), (), s32[]{:S(2)}) async-start(), calls=%async_computation.3 | async-start | bytes 3538944 | tf_op jit(solution)/shard_map/all_gather | solution.py:32
  13.5 261.7 %all-gather.9.cloned.1.call-start = ((), (), s32[]{:S(2)}) async-start(), calls=%async_computation.4 | async-start | bytes 3538944 | tf_op jit(solution)/shard_map/all_gather | solution.py:31
  212.9 95.8 %all-gather.11.cloned.1.call-start = ((), (), s32[]{:S(2)}) async-start(), calls=%async_computation.5 | async-start | bytes 3538944 | tf_op jit(solution)/shard_map/all_gather | solution.py:32
  216.4 36.4 %copy-start.3 = (bf16[137,4096]{1,0:T(8,128)(2,1)}, bf16[137,4096]{1,0:T(8,128)(2,1)S(1)}, u32[]{:S(2)}) copy-start(bf16[137,4096]{1,0:T(8,128)(2,1)S(1)} %gather_fusion) | copy-start | bytes 3366916
  253.2 4.3 %copy-start.4 = (bf16[128,4096]{1,0:T(8,128)(2,1)}, bf16[128,4096]{1,0:T(8,128)(2,1)S(1)}, u32[]{:S(2)}) copy-start(bf16[128,4096]{1,0:T(8,128)(2,1)S(1)} %reshape.80) | copy-start | bytes 3145732
  257.5 4.5 %copy-start.1 = (bf16[1,768,2048]{2,1,0:T(8,128)(2,1)S(1)}, bf16[1,768,2048]{2,1,0:T(8,128)(2,1)}, u32[]{:S(2)}) copy-start(bf16[1,768,2048]{2,1,0:T(8,128)(2,1)} %all-gather.5.cloned.1.call-done) | copy-start | bytes 9437188
  262.1 1.9 copy-start.2
  264.6 10.5 %copy-start.6 = (bf16[16,2048]{1,0:T(8,128)(2,1)S(1)}, bf16[16,2048]{1,0:T(8,128)(2,1)}, u32[]{:S(2)}) copy-start(bf16[16,2048]{1,0:T(8,128)(2,1)} %param.7) | copy-start | bytes 196612
  264.6 10.5 %copy-start.9 = (f32[16,8]{0,1:T(8,128)S(1)}, f32[16,8]{0,1:T(8,128)}, u32[]{:S(2)}) copy-start(f32[16,8]{0,1:T(8,128)} %param.8) | copy-start | bytes 1540
  266.7 48.3 %all-to-all-start.1 = ((bf16[64,2,4096]{2,1,0:T(2,128)(2,1)}), bf16[64,2,4096]{2,1,0:T(2,128)(2,1)}, u32[]{:S(2)}, u32[]{:S(2)}) async-start(bf16[64,2,4096]{2,1,0:T(2,128)(2,1)} %copy.28), calls=%async_computation.1 | async-start | bytes 2097152 | tf_op jit(solution)/shard_map/all_to_all | solution.py:78
  275.2 36.0 %copy-start = (bf16[1,768,2048]{2,1,0:T(8,128)(2,1)S(1)}, bf16[1,768,2048]{2,1,0:T(8,128)(2,1)}, u32[]{:S(2)}) copy-start(bf16[1,768,2048]{2,1,0:T(8,128)(2,1)} %all-gather.9.cloned.1.call-done) | copy-start | bytes 9437188
Sparse Core Ops, SparseCore 0:
  12.5 200.4 all-reduce.3
Sparse Core Ops, SparseCore 1:
  14.9 52.1 all-gather.4
  69.0 46.5 all-gather.6
  213.0 46.8 all-gather.8
  262.2 46.5 all-gather.10
where the time goes:
time: 328 us
  waiting for transfers between devices  231 us (70%)
  blocking collectives  35.6 us (11%)
  matrix products  18.1 us (6%)
  between operations  16.7 us (5%)
  local copies, waits for them, and re-layouts  12.5 us (4%)
  starting transfers between devices  8.49 us (3%)
  other arithmetic  5.26 us (2%)
    psum x1, waiting for transfers between devices, broadcast(): return lax.psum(block, axis)  199 us
    all_to_all x1, blocking collectives, shards(): lax.all_to_all(outgoing, 'expert', split_axis=0, concat_axis=0, tiled=True)  35.6 us
    all_gather x2, waiting for transfers between devices, spread(): down_piece = lax.all_gather(down_parts, 'dp', axis=1, tiled=True)  30.6 us
    all_to_all x1, starting transfers between devices, shards(): lax.all_to_all(returning, 'expert', split_axis=0, concat_axis=0, tiled=True)  8.29 us
    dot_general x2, matrix products, expert_terms(): jnp.einsum('rd,hd->rh', features, up_piece, preferred_element_type=jnp.fl...  7.28 us
  transfers between devices with their start and end apart: 6, of which 2 were waited for; matrix products, arithmetic and copies ran while one was open for 8% of the time, Pallas kernels for 0%

commit v1 on v0

v1 whole, which is shorter than its diff:
```python
import functools

import jax
import jax.numpy as jnp
from jax import lax
from jax.experimental import pallas as pl
from jax.experimental.pallas import tpu as pltpu
from jax.sharding import PartitionSpec as P

BF16, F32, I32 = jnp.bfloat16, jnp.float32, jnp.int32
HOT_PAD = 16
VMEM_LIMIT = 40 * 1024 * 1024


def matmul(a, b):
    return lax.dot_general(a, b, (((1,), (0,)), ((), ())), preferred_element_type=F32)


def matmul_nt(a, b):
    return lax.dot_general(a, b, (((1,), (1,)), ((), ())), preferred_element_type=F32)


def matmul_tn(a, b):
    return lax.dot_general(a, b, (((0,), (0,)), ((), ())), preferred_element_type=F32)


def slot_maps(ids, slots, capacity):
    tok_rows, top_count = ids.shape
    slot = lax.broadcasted_iota(I32, (tok_rows, slots), 1)
    expert = slot // capacity
    named = jnp.zeros((tok_rows, slots), F32)
    for k in range(top_count):
        named = named + (ids[:, k : k + 1] == expert).astype(F32)
    counts = jnp.sum(named, 0, keepdims=True)
    is_hot = (counts == jnp.max(counts)).astype(F32)
    earlier = (
        lax.broadcasted_iota(I32, (tok_rows, tok_rows), 0)
        > lax.broadcasted_iota(I32, (tok_rows, tok_rows), 1)
    ).astype(BF16)
    rank = matmul(earlier, named.astype(BF16))
    cold = named * (1.0 - is_hot) * (rank == (slot % capacity).astype(F32)).astype(F32)
    first = (slot % capacity == 0).astype(F32)
    hot_token = jnp.sum(named * is_hot * first, 1, keepdims=True)
    hot_rank = jnp.sum(rank * is_hot * first, 1, keepdims=True)
    hot_row = lax.broadcasted_iota(I32, (tok_rows, HOT_PAD), 1).astype(F32)
    hot = hot_token * (hot_rank == hot_row).astype(F32)
    hottest = jnp.sum(is_hot * first[:1] * expert[:1].astype(F32), 1, keepdims=True)
    return cold, hot, expert, is_hot, hottest


def route_kernel(capacity, ids_ref, tok_ref, cot_ref, out_ref, hot_tok_ref, hot_cot_ref, hottest_ref):
    slots = out_ref.shape[0]
    width = tok_ref.shape[1]
    cold, hot, _, _, hottest = slot_maps(ids_ref[...], slots, capacity)
    cold, hot = cold.astype(BF16), hot.astype(BF16)
    tok, cot = tok_ref[...], cot_ref[...]
    out_ref[:, :width] = matmul_tn(cold, tok).astype(BF16)
    out_ref[:, width:] = matmul_tn(cold, cot).astype(BF16)
    hot_tok_ref[...] = matmul_tn(hot, tok).astype(BF16)
    hot_cot_ref[...] = matmul_tn(hot, cot).astype(BF16)
    hottest_ref[...] = jnp.broadcast_to(hottest, hottest_ref.shape).astype(I32)


def route(ids, tokens, cotangent, slots, capacity):
    width = tokens.shape[1]
    return pl.pallas_call(
        functools.partial(route_kernel, capacity),
        out_shape=(
            jax.ShapeDtypeStruct((slots, 2 * width), BF16),
            jax.ShapeDtypeStruct((HOT_PAD, width), BF16),
            jax.ShapeDtypeStruct((HOT_PAD, width), BF16),
            jax.ShapeDtypeStruct((8, 128), I32),
        ),
        compiler_params=pltpu.CompilerParams(vmem_limit_bytes=VMEM_LIMIT),
        name="route",
    )(ids, tokens, cotangent)


def activations(pre_act, hidden_grad):
    gating = jax.nn.sigmoid(pre_act)
    hidden = (pre_act * gating).astype(BF16)
    act_grad = (hidden_grad * gating * (1.0 + pre_act * (1.0 - gating))).astype(BF16)
    return hidden, act_grad


def gathered_kernel(units, rows_ref, *refs):
    pieces, acc_ref, up, down, sems = refs[:-4], refs[-4], refs[-3], refs[-2], refs[-1]
    width = up.shape[1]
    half = pieces[0].shape[0] // 2
    copies = []
    for i, piece in enumerate(pieces):
        for j, whole in enumerate((up, down)):
            copy = pltpu.make_async_copy(
                piece.at[pl.ds(j * half, units)], whole.at[pl.ds(i * units, units)], sems.at[i, j]
            )
            copy.start()
            copies.append(copy)
    for copy in copies:
        copy.wait()
    tok, cot = rows_ref[:, :width], rows_ref[:, width:]
    hidden, act_grad = activations(matmul_nt(tok, up[...]), matmul_nt(cot, down[...]))
    acc_ref[:, :width] = matmul(hidden, down[...])
    acc_ref[:, width:] = matmul(act_grad, up[...])


def gathered(rows, pieces, units):
    width = rows.shape[1] // 2
    count = len(pieces)
    return pl.pallas_call(
        functools.partial(gathered_kernel, units),
        out_shape=jax.ShapeDtypeStruct(rows.shape, F32),
        in_specs=[pl.BlockSpec(memory_space=pltpu.VMEM)] + [pl.BlockSpec(memory_space=pl.ANY)] * count,
        out_specs=pl.BlockSpec(memory_space=pltpu.VMEM),
        scratch_shapes=[
            pltpu.VMEM((count * units, width), BF16),
            pltpu.VMEM((count * units, width), BF16),
            pltpu.SemaphoreType.DMA((count, 2)),
        ],
        compiler_params=pltpu.CompilerParams(vmem_limit_bytes=VMEM_LIMIT),
        cost_estimate=pl.CostEstimate(
            flops=8 * rows.shape[0] * count * units * width,
            bytes_accessed=4 * count * units * width,
            transcendentals=0,
        ),
        name="gathered",
    )(rows, *pieces)


def last_kernel(units, rows_ref, acc_ref, up_ref, down_ref, out_ref):
    width = up_ref.shape[1]
    up, down = up_ref[:units, :], down_ref[:units, :]
    tok, cot = rows_ref[:, :width], rows_ref[:, width:]
    hidden, act_grad = activations(matmul_nt(tok, up), matmul_nt(cot, down))
    out_ref[:, :width] = (acc_ref[:, :width] + matmul(hidden, down)).astype(BF16)
    out_ref[:, width:] = (acc_ref[:, width:] + matmul(act_grad, up)).astype(BF16)


def last(rows, acc, up_half, down_half, units):
    return pl.pallas_call(
        functools.partial(last_kernel, units),
        out_shape=jax.ShapeDtypeStruct(rows.shape, BF16),
        compiler_params=pltpu.CompilerParams(vmem_limit_bytes=VMEM_LIMIT),
        name="last",
    )(rows, acc, up_half, down_half)


def hot_kernel(units, hot_rows, where_ref, weight_ref, *refs):
    blocks, out_ref, tok, cot, sems = refs[:-4], refs[-4], refs[-3], refs[-2], refs[-1]
    ring = len(blocks) // 2
    width = tok.shape[1]
    here = where_ref[0]
    copies = []
    for i in range(ring):
        place = pl.multiple_of(lax.rem(here + i, ring) * HOT_PAD, HOT_PAD)
        for j, whole in enumerate((tok, cot)):
            copy = pltpu.make_async_copy(
                blocks[2 * i + j], whole.at[pl.ds(place, HOT_PAD)], sems.at[i, j]
            )
            copy.start()
            copies.append(copy)
    for copy in copies:
        copy.wait()
    up, down = weight_ref[:units, :], weight_ref[units:, :]
    hidden, act_grad = activations(matmul_nt(tok[...], up), matmul_nt(cot[...], down))
    mixed = matmul(hidden, down).astype(BF16)
    grads = matmul(act_grad, up).astype(BF16)
    for i in range(ring):
        out_ref[i, :, :width] = mixed[i * HOT_PAD : i * HOT_PAD + hot_rows]
        out_ref[i, :, width:] = grads[i * HOT_PAD : i * HOT_PAD + hot_rows]


def hot_partials(here, weights, blocks, units, hot_rows):
    width = weights.shape[1]
    ring = len(blocks) // 2
    return pl.pallas_call(
        functools.partial(hot_kernel, units, hot_rows),
        out_shape=jax.ShapeDtypeStruct((ring, hot_rows, 2 * width), BF16),
        in_specs=[
            pl.BlockSpec(memory_space=pltpu.SMEM),
            pl.BlockSpec(memory_space=pltpu.VMEM),
        ]
        + [pl.BlockSpec(memory_space=pl.ANY)] * len(blocks),
        out_specs=pl.BlockSpec(memory_space=pltpu.VMEM),
        scratch_shapes=[
            pltpu.VMEM((ring * HOT_PAD, width), BF16),
            pltpu.VMEM((ring * HOT_PAD, width), BF16),
            pltpu.SemaphoreType.DMA((ring, 2)),
        ],
        compiler_params=pltpu.CompilerParams(vmem_limit_bytes=VMEM_LIMIT),
        name="hot",
    )(here, weights, *blocks)


def thirds(x):
    first = x.astype(BF16)
    rest = x - first.astype(F32)
    second = rest.astype(BF16)
    third = (rest - second.astype(F32)).astype(BF16)
    return jnp.concatenate([first, second, third], 0)


def combine_kernel(capacity, ids_ref, gate_ref, cot_ref, cold_ref, part_ref, mix_ref, grad_ref, gate_grad_ref):
    ids, gates, cot = ids_ref[...], gate_ref[...], cot_ref[...]
    tok_rows, top_count = ids.shape
    slots = cold_ref.shape[0]
    width = cot.shape[1]
    ring, hot_rows = part_ref.shape[0], part_ref.shape[1]
    cold, hot, expert, is_hot, _ = slot_maps(ids, slots, capacity)
    per_slot = jnp.zeros((tok_rows, slots), F32)
    for k in range(top_count):
        per_slot = per_slot + jnp.where(ids[:, k : k + 1] == expert, gates[:, k : k + 1], 0.0)
    hot_gate = jnp.max(per_slot * is_hot, 1, keepdims=True)
    cold_scale = thirds(jnp.where(cold > 0, per_slot, 0.0))
    hot_scale = thirds(jnp.where(hot > 0, hot_gate, 0.0))[:, :hot_rows]
    total = part_ref[0].astype(F32)
    for i in range(1, ring):
        total = total + part_ref[i].astype(F32)
    hot_result = total.astype(BF16)

    def weighted(lo):
        sums = matmul(cold_scale, cold_ref[:, lo : lo + width])
        sums = sums + matmul(hot_scale, hot_result[:, lo : lo + width])
        return sums[:tok_rows] + sums[tok_rows : 2 * tok_rows] + sums[2 * tok_rows :]

    mix_ref[...] = weighted(0).astype(BF16)
    grad_ref[...] = weighted(width).astype(BF16)
    cold_dots = jnp.where(cold > 0, matmul_nt(cot, cold_ref[:, :width]), 0.0)
    hot_dots = matmul_nt(cot, hot_result[:, :width])
    hot_dot = jnp.sum(jnp.where(hot[:, :hot_rows] > 0, hot_dots, 0.0), 1, keepdims=True)
    for k in range(top_count):
        mine = ids[:, k : k + 1] == expert
        cold_part = jnp.sum(jnp.where(mine, cold_dots, 0.0), 1, keepdims=True)
        named_hot = jnp.max(jnp.where(mine, is_hot, 0.0), 1, keepdims=True)
        gate_grad_ref[:, k : k + 1] = cold_part + named_hot * hot_dot


def combine(ids, gates, cotangent, cold_results, hot_parts, capacity):
    return pl.pallas_call(
        functools.partial(combine_kernel, capacity),
        out_shape=(
            jax.ShapeDtypeStruct(cotangent.shape, BF16),
            jax.ShapeDtypeStruct(cotangent.shape, BF16),
            jax.ShapeDtypeStruct(gates.shape, F32),
        ),
        compiler_params=pltpu.CompilerParams(vmem_limit_bytes=VMEM_LIMIT),
        name="combine",
    )(ids, gates, cotangent, cold_results, hot_parts)


def shift(x, by):
    ring = lax.axis_size("dp")
    return lax.ppermute(x, "dp", [(i, (i + by) % ring) for i in range(ring)])


def plane(experts):
    xs, zs, cores = 4, experts // 8, 2
    return xs, zs, cores


def spread_hot(weights, hottest):
    experts = lax.axis_size("expert")
    xs, zs, cores = plane(experts)
    me = lax.axis_index("expert")
    line = [[(x * zs + z) * cores + c for x in range(xs) for c in range(cores)] for z in range(zs)]
    parts = xs * cores
    rows, width = weights.shape
    chunks = lax.all_to_all(
        weights.reshape(parts, rows // parts, width), "expert", 0, 0, axis_index_groups=line, tiled=True
    )
    hot_x, hot_z, hot_c = hottest // (zs * cores), (hottest // cores) % zs, hottest % cores
    z = (me // cores) % zs
    chunk = lax.dynamic_index_in_dim(chunks, hot_x * cores + hot_c, 0, keepdims=False)
    chunk = jnp.where(z == hot_z, chunk, jnp.zeros_like(chunk))
    step = 1
    while step < zs:
        pairs = [(e, (e // (zs * cores)) * zs * cores + ((((e // cores) % zs) ^ step) * cores) + e % cores) for e in range(experts)]
        chunk = chunk + lax.ppermute(chunk, "expert", pairs)
        step *= 2
    return lax.all_gather(chunk, "expert", axis=0, axis_index_groups=line, tiled=True)


def shards(tokens, cotangent, gate_probs, expert_ids, up_weight, down_weight):
    tok_rows, width = tokens.shape
    top_count = expert_ids.shape[1]
    experts = lax.axis_size("expert")
    hot_rows = 9 * tok_rows // 16
    capacity = (tok_rows * top_count - hot_rows + experts - 2) // (experts - 1)
    slots = experts * capacity
    up, down = up_weight[0], down_weight[0]
    units = up.shape[0]

    outgoing, hot_tok, hot_cot, hottest = route(expert_ids, tokens, cotangent, slots, capacity)
    own = jnp.concatenate([up, hot_tok, down, hot_cot], 0)
    half = own.shape[0] // 2
    right, left = [own], [own]
    for _ in range(3):
        right.append(shift(right[-1], 1))
        left.append(shift(left[-1], -1))
    far_up, far_down = shift(right[-1][:half], 1), shift(left[-1][half:], -1)

    arrived = lax.all_to_all(
        outgoing.reshape(experts, capacity, 2 * width), "expert", 0, 0, tiled=True
    ).reshape(slots, 2 * width)
    hot_weights = spread_hot(jnp.concatenate([up, down], 0), hottest[0, 0])

    acc = gathered(arrived, [own] + right[1:] + left[1:], units)
    results = last(arrived, acc, far_up, far_down, units)
    came_back = lax.all_to_all(
        results.reshape(experts, capacity, 2 * width), "expert", 0, 0, tiled=True
    ).reshape(slots, 2 * width)

    def hot_of(block):
        return [block[units:half], block[half + units :]]

    blocks = [hot_tok, hot_cot]
    for block in left[1:]:
        blocks += hot_of(block)
    blocks += [far_up[units:], far_down[units:]]
    for block in right[:0:-1]:
        blocks += hot_of(block)
    here = lax.axis_index("dp").astype(I32).reshape(1)
    partials = hot_partials(here, hot_weights, blocks, units, hot_rows)
    hot_parts = lax.all_to_all(partials, "dp", 0, 0, tiled=True)
    return combine(expert_ids, gate_probs, cotangent, came_back, hot_parts, capacity)


def solution(mesh):
    rows = P(("dp", "expert"), None)
    weights = P("expert", "dp", None)
    return jax.shard_map(
        shards,
        mesh=mesh,
        in_specs=(rows, rows, rows, rows, weights, weights),
        out_specs=(rows, rows, rows),
        check_vma=False,
    )
```

time: 328 us -> 197 us (0.60)
  waiting for transfers between devices: 231 us -> 58.8 us
  starting transfers between devices: 8.49 us -> 79.6 us
  blocking collectives: 35.6 us -> 14.2 us
  matrix products: 18.1 us -> 0 us
  between operations: 16.7 us -> 3.68 us
  Pallas kernels: 0 us -> 12.7 us
  local copies, waits for them, and re-layouts: 12.5 us -> 20.3 us
    psum x1 -> x0, waiting for transfers between devices: 199 us -> none  [broadcast(): return lax.psum(block, axis)]
    ppermute x0 -> x11, starting transfers between devices: none -> 42.5 us  [the longest x8 28.4 us: shift(): return lax.ppermute(x, 'dp', [(i, (i + by) % ring) for i in range(ring)])]
    all_to_all x1 -> x0, blocking collectives: 35.6 us -> none  [shards(): lax.all_to_all(outgoing, 'expert', split_axis=0, concat_axis=0, tiled=True)]
    all_to_all x1 -> x4, waiting for transfers between devices: 0.01 us -> 33.8 us  [the longest x1 28.5 us: shards(): hot_parts = lax.all_to_all(partials, 'dp', 0, 0, tiled=True)]
    all_gather x4 -> x0, waiting for transfers between devices: 30.6 us -> none  [the longest x2 30.6 us: spread(): down_piece = lax.all_gather(down_parts, 'dp', axis=1, tiled=True)]
    all_to_all x1 -> x4, starting transfers between devices: 8.29 us -> 37.1 us  [the longest x1 14.2 us: shards(): lax.all_to_all(outgoing.reshape(experts, capacity, 2 * width), 'expert',...]
    ppermute x0 -> x11, waiting for transfers between devices: none -> 25 us  [the longest x3 17.3 us: spread_hot(): chunk = chunk + lax.ppermute(chunk, 'expert', pairs)]
    dot_general x7 -> x0, matrix products: 18.1 us -> none  [the longest x2 7.28 us: expert_terms(): jnp.einsum('rd,hd->rh', features, up_piece, preferred_element_type=jnp.fl...]
  transfers between devices with their start and end apart: 6 -> 15, of which waited for: 2 -> 5; matrix products, arithmetic and copies ran while one was open for 8% -> 9% of each run, Pallas kernels for 0% -> 5%
where the time goes in v1:
time: 197 us; the launch traced here: 194 us
  starting transfers between devices  79.6 us (40%)
  waiting for transfers between devices  58.8 us (30%)
  local copies, waits for them, and re-layouts  20.3 us (10%)
  blocking collectives  14.2 us (7%)
  Pallas kernels  12.7 us (6%)
  other arithmetic  4.65 us (2%)
  between operations  3.68 us (2%)
    all_to_all x1, waiting for transfers between devices, shards(): hot_parts = lax.all_to_all(partials, 'dp', 0, 0, tiled=True)  28.5 us
    ppermute x8, starting transfers between devices, shift(): return lax.ppermute(x, 'dp', [(i, (i + by) % ring) for i in range(ring)])  28.4 us
    ppermute x3, waiting for transfers between devices, spread_hot(): chunk = chunk + lax.ppermute(chunk, 'expert', pairs)  17.3 us
    all_gather x1, blocking collectives, spread_hot(): lax.all_gather(chunk, 'expert', axis=0, axis_index_groups=line, tiled=True)  14.2 us
    all_to_all x1, starting transfers between devices, shards(): lax.all_to_all(outgoing.reshape(experts, capacity, 2 * width), 'expert',...  14.2 us
    ppermute x3, starting transfers between devices, spread_hot(): chunk = chunk + lax.ppermute(chunk, 'expert', pairs)  14.1 us
    all_to_all x1, starting transfers between devices, spread_hot(): lax.all_to_all(weights.reshape(parts, rows // parts, width), 'expert', 0,...  9.72 us
    ppermute x8, waiting for transfers between devices, shift(): return lax.ppermute(x, 'dp', [(i, (i + by) % ring) for i in range(ring)])  7.72 us
  transfers between devices with their start and end apart: 15, of which 5 were waited for; matrix products, arithmetic and copies ran while one was open for 9% of the time, Pallas kernels for 5%

profile of v1, /device:TPU:6, one launch (start us, length us, event | category | flops | bytes accessed | tf_op | source)
XLA Modules:
  0.0 194.0 jit_solution(9255318094092172676)
XLA Ops:
  0.6 0.8 copy.10.ids_ref
  1.4 0.8 copy-done.6
  2.2 0.8 copy-done.12
  3.1 0.7 route.1
  3.8 0.0 copy-start.4
  3.8 1.2 pad_maximum_fusion.refs_0_
  5.0 3.5 %collective-permute-start = (bf16[224,2048]{1,0:T(8,128)(2,1)S(1)}, bf16[224,2048]{1,0:T(8,128)(2,1)S(1)}, u32[]{:S(2)}, u32[]{:S(2)}) collective-permute-start(bf16[224,2048]{1,0:T(8,128)(2,1)S(1)} %pad_maximum_fusion.refs_0_), channel_id=1, source_target_pairs={{0,64},{64,128},{128,192},{192,256},{256,320},{320,384},{384,448},... | collective-permute-start | bytes 2752520 | tf_op jit(solution)/shard_map/ppermute | solution.py:252
  8.5 3.8 %collective-permute-start.3 = (bf16[224,2048]{1,0:T(8,128)(2,1)S(1)}, bf16[224,2048]{1,0:T(8,128)(2,1)}, u32[]{:S(2)}, u32[]{:S(2)}) collective-permute-start(bf16[224,2048]{1,0:T(8,128)(2,1)S(1)} %pad_maximum_fusion.refs_0_), channel_id=1, source_target_pairs={{0,448},{64,0},{128,64},{192,128},{256,192},{320,256},{384,320},{4... | collective-permute-start | bytes 2752520 | tf_op jit(solution)/shard_map/ppermute | solution.py:252
  12.3 0.9 pad_maximum_fusion.1
  13.3 9.7 %all-to-all-start.2 = ((bf16[8,24,2048]{2,1,0:T(8,128)(2,1)}), bf16[8,24,2048]{2,1,0:T(8,128)(2,1)}, u32[]{:S(2)}, u32[]{:S(2)}) async-start(bf16[8,24,2048]{2,1,0:T(8,128)(2,1)} %bitcast.9), calls=%async_computation.2 | async-start | bytes 1572864 | tf_op jit(solution)/shard_map/all_to_all | solution.py:267
  23.0 7.7 %collective-permute-done.refs_1_ = bf16[224,2048]{1,0:T(8,128)(2,1)S(1)} collective-permute-done((bf16[224,2048]{1,0:T(8,128)(2,1)S(1)}, bf16[224,2048]{1,0:T(8,128)(2,1)S(1)}, u32[]{:S(2)}, u32[]{:S(2)}) %collective-permute-start) | collective-permute-done | bytes 917536 | tf_op jit(solution)/shard_map/ppermute | solution.py:252
  30.7 1.9 collective-permute-start.1
  32.6 0.0 collective-permute-done.3.refs_4_
  32.6 5.1 %collective-permute-start.4 = (bf16[224,2048]{1,0:T(8,128)(2,1)}, bf16[224,2048]{1,0:T(8,128)(2,1)}, u32[]{:S(2)}, u32[]{:S(2)}) collective-permute-start(bf16[224,2048]{1,0:T(8,128)(2,1)} %collective-permute-done.3.refs_4_), channel_id=1, source_target_pairs={{0,448},{64,0},{128,64},{192,128},{256,192},{320,256},{384,320},{4... | collective-permute-start | bytes 2752520 | tf_op jit(solution)/shard_map/ppermute | solution.py:252
  37.8 1.5 reshape.27
  39.3 0.0 all-to-all-done.2
  39.3 14.2 %all-to-all-start = ((bf16[64,2,4096]{2,1,0:T(2,128)(2,1)}), bf16[64,2,4096]{2,1,0:T(2,128)(2,1)}, u32[]{:S(2)}, u32[]{:S(2)}) async-start(bf16[64,2,4096]{2,1,0:T(2,128)(2,1)} %reshape.27), calls=%async_computation | async-start | bytes 2097152 | tf_op jit(solution)/shard_map/all_to_all | solution.py:301
  53.5 0.5 slice.53
  56.7 0.9 select_bitcast_fusion
  57.6 3.4 %collective-permute-start.8 = (bf16[24,2048]{1,0:T(8,128)(2,1)S(1)}, bf16[24,2048]{1,0:T(8,128)(2,1)S(1)}, u32[]{:S(2)}, u32[]{:S(2)}) collective-permute-start(bf16[24,2048]{1,0:T(8,128)(2,1)S(1)} %select_bitcast_fusion), channel_id=1, source_target_pairs={{0,2},{1,3},{2,0},{3,1},{4,6},{5,7},{6,4},{7,5},{8,10},{9,11},{10,... | collective-permute-start | bytes 294920 | tf_op jit(solution)/shard_map/ppermute | solution.py:277
  61.0 0.0 collective-permute-done.1.refs_2_
  61.0 1.9 collective-permute-start.2
  63.0 0.0 collective-permute-done.4.refs_5_
  63.0 5.1 %collective-permute-start.5 = (bf16[224,2048]{1,0:T(8,128)(2,1)}, bf16[224,2048]{1,0:T(8,128)(2,1)S(1)}, u32[]{:S(2)}, u32[]{:S(2)}) collective-permute-start(bf16[224,2048]{1,0:T(8,128)(2,1)} %collective-permute-done.4.refs_5_), channel_id=1, source_target_pairs={{0,448},{64,0},{128,64},{192,128},{256,192},{320,256},{384,320},{4... | collective-permute-start | bytes 2752520 | tf_op jit(solution)/shard_map/ppermute | solution.py:252
  68.1 12.1 %collective-permute-done.8 = bf16[24,2048]{1,0:T(8,128)(2,1)S(1)} collective-permute-done((bf16[24,2048]{1,0:T(8,128)(2,1)S(1)}, bf16[24,2048]{1,0:T(8,128)(2,1)S(1)}, u32[]{:S(2)}, u32[]{:S(2)}) %collective-permute-start.8) | collective-permute-done | bytes 98336 | tf_op jit(solution)/shard_map/ppermute | solution.py:277
  80.2 0.9 fusion.6
  81.1 4.1 %collective-permute-start.9 = (bf16[24,2048]{1,0:T(8,128)(2,1)S(1)}, bf16[24,2048]{1,0:T(8,128)(2,1)S(1)}, u32[]{:S(2)}, u32[]{:S(2)}) collective-permute-start(bf16[24,2048]{1,0:T(8,128)(2,1)S(1)} %fusion.6), channel_id=1, source_target_pairs={{0,4},{1,5},{2,6},{3,7},{4,0},{5,1},{6,2},{7,3},{8,12},{9,13},{10,... | collective-permute-start | bytes 294920 | tf_op jit(solution)/shard_map/ppermute | solution.py:277
  85.3 5.2 %collective-permute-done.9 = bf16[24,2048]{1,0:T(8,128)(2,1)S(1)} collective-permute-done((bf16[24,2048]{1,0:T(8,128)(2,1)S(1)}, bf16[24,2048]{1,0:T(8,128)(2,1)S(1)}, u32[]{:S(2)}, u32[]{:S(2)}) %collective-permute-start.9) | collective-permute-done | bytes 98336 | tf_op jit(solution)/shard_map/ppermute | solution.py:277
  90.5 6.5 %collective-permute-start.10 = (bf16[24,2048]{1,0:T(8,128)(2,1)S(1)}, bf16[24,2048]{1,0:T(8,128)(2,1)S(1)}, u32[]{:S(2)}, u32[]{:S(2)}) collective-permute-start(bf16[24,2048]{1,0:T(8,128)(2,1)S(1)} %add.35), channel_id=1, source_target_pairs={{0,8},{1,9},{2,10},{3,11},{4,12},{5,13},{6,14},{7,15},{8,0},{9,1},... | collective-permute-start | bytes 294920 | tf_op jit(solution)/shard_map/ppermute | solution.py:277
  97.0 1.5 fusion.5
  98.5 0.0 collective-permute-done.2.refs_3_
  98.5 0.8 slice.68
  99.4 1.9 collective-permute-start.6
  101.3 0.0 collective-permute-done.5.refs_6_
  101.3 1.0 slice.69
  102.2 5.1 %collective-permute-start.7 = (bf16[112,2048]{1,0:T(8,128)(2,1)}, bf16[112,2048]{1,0:T(8,128)(2,1)}, u32[]{:S(2)}, u32[]{:S(2)}) collective-permute-start(bf16[112,2048]{1,0:T(8,128)(2,1)} %slice.69), channel_id=1, source_target_pairs={{0,448},{64,0},{128,64},{192,128},{256,192},{320,256},{384,320},{4... | collective-permute-start | bytes 1376264 | tf_op jit(solution)/shard_map/ppermute | solution.py:252
  107.4 1.5 fusion
  108.9 0.0 collective-permute-done.10
  108.9 0.7 add.36
  109.6 0.0 all-to-all-done
  109.6 1.5 reshape.28.rows_ref
  111.1 1.2 copy-done.1
  112.2 1.2 copy-done.3
  113.4 5.3 %gathered.1.acc_ref = f32[128,4096]{1,0:T(8,128)S(1)} custom-call(bf16[128,4096]{1,0:T(8,128)(2,1)S(1)} %reshape.28.rows_ref, bf16[224,2048]{1,0:T(8,128)(2,1)S(1)} %pad_maximum_fusion.refs_0_, bf16[224,2048]{1,0:T(8,128)(2,1)S(1)} %copy-done.3, bf16[224,2048]{1,0:T(8,128)(2,1)} %collective-permute-done.1.refs_2_, ...), custom_call_target="tpu_custom_call" | custom-call | flops 1409286144 | bytes 5505024 | tf_op jit(solution)/shard_map/gathered/pallas_call | solution.py:109
  118.7 0.0 collective-permute-done.6.up_ref
  118.7 0.0 collective-permute-done.7.down_ref
  118.8 1.8 last.1
  120.6 1.5 reshape.29
  122.1 6.6 %all-to-all-start.1 = ((bf16[64,2,4096]{2,1,0:T(2,128)(2,1)}), bf16[64,2,4096]{2,1,0:T(2,128)(2,1)}, u32[]{:S(2)}, u32[]{:S(2)}) async-start(bf16[64,2,4096]{2,1,0:T(2,128)(2,1)} %reshape.29), calls=%async_computation.1 | async-start | bytes 2097152 | tf_op jit(solution)/shard_map/all_to_all | solution.py:308
  128.7 14.2 %all_gather.3.weight_ref = bf16[192,2048]{1,0:T(8,128)(2,1)S(1)} all-gather(bf16[24,2048]{1,0:T(8,128)(2,1)S(1)} %copy-done.15), channel_id=1, replica_groups={{0,1,16,17,32,33,48,49},{2,3,18,19,34,35,50,51},{4,5,20,21,36,37,52,53}..., dimensions={0}, use_global_device_ids=true | all-gather | bytes 884736 | tf_op jit(solution)/shard_map/all_gather | solution.py:279
  142.9 0.9 fusion.4
  143.8 0.9 fusion.1
  144.7 0.9 fusion.3
  145.6 0.8 slice.77.refs_9_
  146.5 0.0 copy-start.16
  146.5 3.4 %hot.1 = bf16[8,9,4096]{2,1,0:T(8,128)(2,1)} custom-call(s32[1]{0:T(128)} %bitcast.2.where_ref, bf16[192,2048]{1,0:T(8,128)(2,1)S(1)} %all_gather.3.weight_ref, bf16[16,2048]{1,0:T(8,128)(2,1)S(1)} %get-tuple-element.8.refs_0_, bf16[16,2048]{1,0:T(8,128)(2,1)S(1)} %copy-done.5, bf16[16,2048]{1,0:T(8,128)(2,1)S(1)} %copy-done.9, ...), custom_call_target="tpu_custom_call" | custom-call | tf_op jit(solution)/shard_map/hot/pallas_call | solution.py:175
  150.0 0.0 copy-start.7
  150.0 5.3 %all-to-all-done.1 = bf16[64,2,4096]{2,1,0:T(2,128)(2,1)} async-done(((bf16[64,2,4096]{2,1,0:T(2,128)(2,1)}), bf16[64,2,4096]{2,1,0:T(2,128)(2,1)}, u32[]{:S(2)}, u32[]{:S(2)}) %all-to-all-start.1) | async-done | bytes 1048608 | tf_op jit(solution)/shard_map/all_to_all | solution.py:308
  155.3 6.6 %all-to-all-start.3 = ((bf16[8,9,4096]{2,1,0:T(8,128)(2,1)}), bf16[8,9,4096]{2,1,0:T(8,128)(2,1)S(1)}, u32[]{:S(2)}, u32[]{:S(2)}) async-start(bf16[8,9,4096]{2,1,0:T(8,128)(2,1)} %hot.1), calls=%async_computation.3 | async-start | bytes 2097152 | tf_op jit(solution)/shard_map/all_to_all | solution.py:323
  161.8 0.1 copy.11.gate_ref
  161.9 1.5 reshape.30.cold_ref
  163.4 28.5 %all-to-all-done.3.part_ref = bf16[8,9,4096]{2,1,0:T(8,128)(2,1)S(1)} async-done(((bf16[8,9,4096]{2,1,0:T(8,128)(2,1)}), bf16[8,9,4096]{2,1,0:T(8,128)(2,1)S(1)}, u32[]{:S(2)}, u32[]{:S(2)}) %all-to-all-start.3) | async-done | bytes 589856 | tf_op jit(solution)/shard_map/all_to_all | solution.py:323
  191.9 1.4 combine.1
  193.3 0.7 copy.12
  (30 shorter events, 0.1 us)
Async XLA Ops:
  1.4 0.8 copy-start.6
  2.2 0.8 copy-start.12
  3.1 9.2 %copy-start.13 = (bf16[1,96,2048]{2,1,0:T(8,128)(2,1)S(1)}, bf16[1,96,2048]{2,1,0:T(8,128)(2,1)}, u32[]{:S(2)}) copy-start(bf16[1,96,2048]{2,1,0:T(8,128)(2,1)} %param.11) | copy-start | bytes 1179652
  3.1 9.3 %copy-start.14 = (bf16[1,96,2048]{2,1,0:T(8,128)(2,1)S(1)}, bf16[1,96,2048]{2,1,0:T(8,128)(2,1)}, u32[]{:S(2)}) copy-start(bf16[1,96,2048]{2,1,0:T(8,128)(2,1)} %param.10) | copy-start | bytes 1179652
  3.8 9.5 %copy-start.4 = (bf16[16,2048]{1,0:T(8,128)(2,1)}, bf16[16,2048]{1,0:T(8,128)(2,1)S(1)}, u32[]{:S(2)}) copy-start(bf16[16,2048]{1,0:T(8,128)(2,1)S(1)} %get-tuple-element.9.refs_1_) | copy-start | bytes 196612
  5.0 25.7 %collective-permute-start = (bf16[224,2048]{1,0:T(8,128)(2,1)S(1)}, bf16[224,2048]{1,0:T(8,128)(2,1)S(1)}, u32[]{:S(2)}, u32[]{:S(2)}) collective-permute-start(bf16[224,2048]{1,0:T(8,128)(2,1)S(1)} %pad_maximum_fusion.refs_0_), channel_id=1, source_target_pairs={{0,64},{64,128},{128,192},{192,256},{256,320},{320,384},{384,448},... | collective-permute-start | bytes 2752520 | tf_op jit(solution)/shard_map/ppermute | solution.py:252
  8.5 24.1 %collective-permute-start.3 = (bf16[224,2048]{1,0:T(8,128)(2,1)S(1)}, bf16[224,2048]{1,0:T(8,128)(2,1)}, u32[]{:S(2)}, u32[]{:S(2)}) collective-permute-start(bf16[224,2048]{1,0:T(8,128)(2,1)S(1)} %pad_maximum_fusion.refs_0_), channel_id=1, source_target_pairs={{0,448},{64,0},{128,64},{192,128},{256,192},{320,256},{384,320},{4... | collective-permute-start | bytes 2752520 | tf_op jit(solution)/shard_map/ppermute | solution.py:252
  13.3 26.0 %all-to-all-start.2 = ((bf16[8,24,2048]{2,1,0:T(8,128)(2,1)}), bf16[8,24,2048]{2,1,0:T(8,128)(2,1)}, u32[]{:S(2)}, u32[]{:S(2)}) async-start(bf16[8,24,2048]{2,1,0:T(8,128)(2,1)} %bitcast.9), calls=%async_computation.2 | async-start | bytes 1572864 | tf_op jit(solution)/shard_map/all_to_all | solution.py:267
  30.7 8.6 %copy-start.2 = (bf16[224,2048]{1,0:T(8,128)(2,1)}, bf16[224,2048]{1,0:T(8,128)(2,1)S(1)}, u32[]{:S(2)}) copy-start(bf16[224,2048]{1,0:T(8,128)(2,1)S(1)} %collective-permute-done.refs_1_) | copy-start | bytes 2752516
  30.7 30.3 %collective-permute-start.1 = (bf16[224,2048]{1,0:T(8,128)(2,1)S(1)}, bf16[224,2048]{1,0:T(8,128)(2,1)}, u32[]{:S(2)}, u32[]{:S(2)}) collective-permute-start(bf16[224,2048]{1,0:T(8,128)(2,1)S(1)} %collective-permute-done.refs_1_), channel_id=1, source_target_pairs={{0,64},{64,128},{128,192},{192,256},{256,320},{320,384},{384,448},... | collective-permute-start | bytes 2752520 | tf_op jit(solution)/shard_map/ppermute | solution.py:252
  32.6 30.3 %collective-permute-start.4 = (bf16[224,2048]{1,0:T(8,128)(2,1)}, bf16[224,2048]{1,0:T(8,128)(2,1)}, u32[]{:S(2)}, u32[]{:S(2)}) collective-permute-start(bf16[224,2048]{1,0:T(8,128)(2,1)} %collective-permute-done.3.refs_4_), channel_id=1, source_target_pairs={{0,448},{64,0},{128,64},{192,128},{256,192},{320,256},{384,320},{4... | collective-permute-start | bytes 2752520 | tf_op jit(solution)/shard_map/ppermute | solution.py:252
  39.3 70.3 %all-to-all-start = ((bf16[64,2,4096]{2,1,0:T(2,128)(2,1)}), bf16[64,2,4096]{2,1,0:T(2,128)(2,1)}, u32[]{:S(2)}, u32[]{:S(2)}) async-start(bf16[64,2,4096]{2,1,0:T(2,128)(2,1)} %reshape.27), calls=%async_computation | async-start | bytes 2097152 | tf_op jit(solution)/shard_map/all_to_all | solution.py:301
  57.6 22.6 %collective-permute-start.8 = (bf16[24,2048]{1,0:T(8,128)(2,1)S(1)}, bf16[24,2048]{1,0:T(8,128)(2,1)S(1)}, u32[]{:S(2)}, u32[]{:S(2)}) collective-permute-start(bf16[24,2048]{1,0:T(8,128)(2,1)S(1)} %select_bitcast_fusion), channel_id=1, source_target_pairs={{0,2},{1,3},{2,0},{3,1},{4,6},{5,7},{6,4},{7,5},{8,10},{9,11},{10,... | collective-permute-start | bytes 294920 | tf_op jit(solution)/shard_map/ppermute | solution.py:277
  61.0 37.5 %collective-permute-start.2 = (bf16[224,2048]{1,0:T(8,128)(2,1)}, bf16[224,2048]{1,0:T(8,128)(2,1)S(1)}, u32[]{:S(2)}, u32[]{:S(2)}) collective-permute-start(bf16[224,2048]{1,0:T(8,128)(2,1)} %collective-permute-done.1.refs_2_), channel_id=1, source_target_pairs={{0,64},{64,128},{128,192},{192,256},{256,320},{320,384},{384,448},... | collective-permute-start | bytes 2752520 | tf_op jit(solution)/shard_map/ppermute | solution.py:252
  63.0 38.3 %collective-permute-start.5 = (bf16[224,2048]{1,0:T(8,128)(2,1)}, bf16[224,2048]{1,0:T(8,128)(2,1)S(1)}, u32[]{:S(2)}, u32[]{:S(2)}) collective-permute-start(bf16[224,2048]{1,0:T(8,128)(2,1)} %collective-permute-done.4.refs_5_), channel_id=1, source_target_pairs={{0,448},{64,0},{128,64},{192,128},{256,192},{320,256},{384,320},{4... | collective-permute-start | bytes 2752520 | tf_op jit(solution)/shard_map/ppermute | solution.py:252
  81.1 9.3 %collective-permute-start.9 = (bf16[24,2048]{1,0:T(8,128)(2,1)S(1)}, bf16[24,2048]{1,0:T(8,128)(2,1)S(1)}, u32[]{:S(2)}, u32[]{:S(2)}) collective-permute-start(bf16[24,2048]{1,0:T(8,128)(2,1)S(1)} %fusion.6), channel_id=1, source_target_pairs={{0,4},{1,5},{2,6},{3,7},{4,0},{5,1},{6,2},{7,3},{8,12},{9,13},{10,... | collective-permute-start | bytes 294920 | tf_op jit(solution)/shard_map/ppermute | solution.py:277
  90.5 18.4 %collective-permute-start.10 = (bf16[24,2048]{1,0:T(8,128)(2,1)S(1)}, bf16[24,2048]{1,0:T(8,128)(2,1)S(1)}, u32[]{:S(2)}, u32[]{:S(2)}) collective-permute-start(bf16[24,2048]{1,0:T(8,128)(2,1)S(1)} %add.35), channel_id=1, source_target_pairs={{0,8},{1,9},{2,10},{3,11},{4,12},{5,13},{6,14},{7,15},{8,0},{9,1},... | collective-permute-start | bytes 294920 | tf_op jit(solution)/shard_map/ppermute | solution.py:277
  99.4 19.4 %collective-permute-start.6 = (bf16[112,2048]{1,0:T(8,128)(2,1)}, bf16[112,2048]{1,0:T(8,128)(2,1)S(1)}, u32[]{:S(2)}, u32[]{:S(2)}) collective-permute-start(bf16[112,2048]{1,0:T(8,128)(2,1)} %slice.68), channel_id=1, source_target_pairs={{0,64},{64,128},{128,192},{192,256},{256,320},{320,384},{384,448},... | collective-permute-start | bytes 1376264 | tf_op jit(solution)/shard_map/ppermute | solution.py:252
  101.3 8.3 %copy-start = (bf16[224,2048]{1,0:T(8,128)(2,1)}, bf16[224,2048]{1,0:T(8,128)(2,1)S(1)}, u32[]{:S(2)}) copy-start(bf16[224,2048]{1,0:T(8,128)(2,1)S(1)} %collective-permute-done.5.refs_6_) | copy-start | bytes 2752516
  102.2 16.5 %collective-permute-start.7 = (bf16[112,2048]{1,0:T(8,128)(2,1)}, bf16[112,2048]{1,0:T(8,128)(2,1)}, u32[]{:S(2)}, u32[]{:S(2)}) collective-permute-start(bf16[112,2048]{1,0:T(8,128)(2,1)} %slice.69), channel_id=1, source_target_pairs={{0,448},{64,0},{128,64},{192,128},{256,192},{320,256},{384,320},{4... | collective-permute-start | bytes 1376264 | tf_op jit(solution)/shard_map/ppermute | solution.py:252
  111.0 1.2 copy-start.1
  112.2 1.2 copy-start.3
  120.6 8.1 %copy-start.15 = (bf16[24,2048]{1,0:T(8,128)(2,1)S(1)}, bf16[24,2048]{1,0:T(8,128)(2,1)}, u32[]{:S(2)}) copy-start(bf16[24,2048]{1,0:T(8,128)(2,1)} %add.36) | copy-start | bytes 294916
  122.1 24.4 %copy-start.5 = (bf16[16,2048]{1,0:T(8,128)(2,1)S(1)}, bf16[16,2048]{1,0:T(8,128)(2,1)}, u32[]{:S(2)}) copy-start(bf16[16,2048]{1,0:T(8,128)(2,1)} %copy-done.4) | copy-start | bytes 196612
  122.1 24.4 %copy-start.8 = (bf16[16,2048]{1,0:T(8,128)(2,1)S(1)}, bf16[16,2048]{1,0:T(8,128)(2,1)}, u32[]{:S(2)}) copy-start(bf16[16,2048]{1,0:T(8,128)(2,1)} %get-tuple-element.24.refs_3_) | copy-start | bytes 196612
  122.1 24.4 %copy-start.9 = (bf16[16,2048]{1,0:T(8,128)(2,1)S(1)}, bf16[16,2048]{1,0:T(8,128)(2,1)}, u32[]{:S(2)}) copy-start(bf16[16,2048]{1,0:T(8,128)(2,1)} %get-tuple-element.25.refs_2_) | copy-start | bytes 196612
  122.1 24.4 %copy-start.10 = (bf16[16,2048]{1,0:T(8,128)(2,1)S(1)}, bf16[16,2048]{1,0:T(8,128)(2,1)}, u32[]{:S(2)}) copy-start(bf16[16,2048]{1,0:T(8,128)(2,1)} %get-tuple-element.14.refs_15_) | copy-start | bytes 196612
  122.1 24.4 %copy-start.11 = (bf16[16,2048]{1,0:T(8,128)(2,1)S(1)}, bf16[16,2048]{1,0:T(8,128)(2,1)}, u32[]{:S(2)}) copy-start(bf16[16,2048]{1,0:T(8,128)(2,1)} %get-tuple-element.15.refs_14_) | copy-start | bytes 196612
  122.1 33.1 %all-to-all-start.1 = ((bf16[64,2,4096]{2,1,0:T(2,128)(2,1)}), bf16[64,2,4096]{2,1,0:T(2,128)(2,1)}, u32[]{:S(2)}, u32[]{:S(2)}) async-start(bf16[64,2,4096]{2,1,0:T(2,128)(2,1)} %reshape.29), calls=%async_computation.1 | async-start | bytes 2097152 | tf_op jit(solution)/shard_map/all_to_all | solution.py:308
  146.5 15.4 %copy-start.16 = (f32[16,8]{0,1:T(8,128)S(1)}, f32[16,8]{0,1:T(8,128)}, u32[]{:S(2)}) copy-start(f32[16,8]{0,1:T(8,128)} %param.8) | copy-start | bytes 1540
  150.0 42.0 %copy-start.7 = (bf16[16,2048]{1,0:T(8,128)(2,1)S(1)}, bf16[16,2048]{1,0:T(8,128)(2,1)}, u32[]{:S(2)}) copy-start(bf16[16,2048]{1,0:T(8,128)(2,1)} %cot_ref.3) | copy-start | bytes 196612
  155.3 36.7 %all-to-all-start.3 = ((bf16[8,9,4096]{2,1,0:T(8,128)(2,1)}), bf16[8,9,4096]{2,1,0:T(8,128)(2,1)S(1)}, u32[]{:S(2)}, u32[]{:S(2)}) async-start(bf16[8,9,4096]{2,1,0:T(8,128)(2,1)} %hot.1), calls=%async_computation.3 | async-start | bytes 2097152 | tf_op jit(solution)/shard_map/all_to_all | solution.py:323

commit v2 on v1

v2 whole, which is shorter than its diff:
```python
import functools

import jax
import jax.numpy as jnp
from jax import lax
from jax.experimental import pallas as pl
from jax.experimental.pallas import tpu as pltpu
from jax.sharding import PartitionSpec as P

BF16, F32, I32 = jnp.bfloat16, jnp.float32, jnp.int32
HOT_PAD = 16
VMEM_LIMIT = 16 * 1024 * 1024


def outside(x):
    return pltpu.with_memory_space_constraint(x, pltpu.HBM)


def matmul(a, b):
    return lax.dot_general(a, b, (((1,), (0,)), ((), ())), preferred_element_type=F32)


def matmul_nt(a, b):
    return lax.dot_general(a, b, (((1,), (1,)), ((), ())), preferred_element_type=F32)


def matmul_tn(a, b):
    return lax.dot_general(a, b, (((0,), (0,)), ((), ())), preferred_element_type=F32)


def slot_maps(ids, slots, capacity):
    top_count, tok_rows = ids.shape
    slot = lax.broadcasted_iota(I32, (slots, tok_rows), 0)
    expert = slot // capacity
    named = jnp.zeros((slots, tok_rows), F32)
    for k in range(top_count):
        named = named + (ids[k : k + 1, :] == expert).astype(F32)
    counts = jnp.sum(named, 1, keepdims=True)
    is_hot = (counts == jnp.max(counts)).astype(F32)
    earlier = (
        lax.broadcasted_iota(I32, (tok_rows, tok_rows), 0)
        < lax.broadcasted_iota(I32, (tok_rows, tok_rows), 1)
    ).astype(BF16)
    rank = matmul(named.astype(BF16), earlier)
    cold = named * (1.0 - is_hot) * (rank == (slot % capacity).astype(F32)).astype(F32)
    first = is_hot * (slot[:, :1] % capacity == 0).astype(F32)
    hot_token = jnp.sum(named * first, 0, keepdims=True)
    hot_rank = jnp.sum(rank * first, 0, keepdims=True)
    hot_row = lax.broadcasted_iota(I32, (HOT_PAD, tok_rows), 0).astype(F32)
    hot = hot_token * (hot_rank == hot_row).astype(F32)
    hottest = jnp.sum(first * expert[:, :1].astype(F32), 0, keepdims=True)
    return cold, hot, expert, is_hot, hottest


def route_kernel(
    capacity, ids_ref, tok_ref, cot_ref, up_ref, down_ref, out_ref, own_ref, pair_ref, hottest_ref,
    tok, cot, hot_tok, hot_cot, sems,
):
    slots, width = out_ref.shape[0], tok.shape[1]
    units = up_ref.shape[0]
    half = own_ref.shape[0] // 2
    loads = [pltpu.make_async_copy(tok_ref, tok, sems.at[0]), pltpu.make_async_copy(cot_ref, cot, sems.at[1])]
    copies = [
        pltpu.make_async_copy(up_ref, own_ref.at[pl.ds(0, units)], sems.at[2]),
        pltpu.make_async_copy(down_ref, own_ref.at[pl.ds(half, units)], sems.at[3]),
        pltpu.make_async_copy(up_ref, pair_ref.at[pl.ds(0, units)], sems.at[4]),
        pltpu.make_async_copy(down_ref, pair_ref.at[pl.ds(units, units)], sems.at[5]),
    ]
    for copy in loads + copies:
        copy.start()
    cold, hot, _, _, hottest = slot_maps(ids_ref[...], slots, capacity)
    cold, hot = cold.astype(BF16), hot.astype(BF16)
    hottest_ref[...] = jnp.broadcast_to(hottest, hottest_ref.shape).astype(I32)
    for copy in loads:
        copy.wait()
    hot_tok[...] = matmul(hot, tok[...]).astype(BF16)
    hot_cot[...] = matmul(hot, cot[...]).astype(BF16)
    stores = [
        pltpu.make_async_copy(hot_tok, own_ref.at[pl.ds(units, HOT_PAD)], sems.at[6]),
        pltpu.make_async_copy(hot_cot, own_ref.at[pl.ds(half + units, HOT_PAD)], sems.at[7]),
    ]
    for copy in stores:
        copy.start()
    out_ref[:, :width] = matmul(cold, tok[...]).astype(BF16)
    out_ref[:, width:] = matmul(cold, cot[...]).astype(BF16)
    for copy in copies + stores:
        copy.wait()


def route(ids, tokens, cotangent, up, down, slots, capacity):
    tok_rows, width = tokens.shape
    units = up.shape[0]
    anywhere = pl.BlockSpec(memory_space=pl.ANY)
    inside = pl.BlockSpec(memory_space=pltpu.VMEM)
    return pl.pallas_call(
        functools.partial(route_kernel, capacity),
        out_shape=(
            jax.ShapeDtypeStruct((slots, 2 * width), BF16),
            jax.ShapeDtypeStruct((2 * (units + HOT_PAD), width), BF16),
            jax.ShapeDtypeStruct((2 * units, width), BF16),
            jax.ShapeDtypeStruct((8, 128), I32),
        ),
        in_specs=[inside] + [anywhere] * 4,
        out_specs=(inside, anywhere, anywhere, inside),
        scratch_shapes=[
            pltpu.VMEM((tok_rows, width), BF16),
            pltpu.VMEM((tok_rows, width), BF16),
            pltpu.VMEM((HOT_PAD, width), BF16),
            pltpu.VMEM((HOT_PAD, width), BF16),
            pltpu.SemaphoreType.DMA((8,)),
        ],
        compiler_params=pltpu.CompilerParams(vmem_limit_bytes=VMEM_LIMIT),
        name="route",
    )(ids, *map(outside, (tokens, cotangent, up, down)))


def activations(pre_act, hidden_grad):
    gating = jax.nn.sigmoid(pre_act)
    hidden = (pre_act * gating).astype(BF16)
    act_grad = (hidden_grad * gating * (1.0 + pre_act * (1.0 - gating))).astype(BF16)
    return hidden, act_grad


def gathered_kernel(units, rows_ref, *refs):
    pieces, acc_ref, up, down, sems = refs[:-4], refs[-4], refs[-3], refs[-2], refs[-1]
    width = up.shape[1]
    half = pieces[0].shape[0] // 2
    copies = []
    for i, piece in enumerate(pieces):
        for j, whole in enumerate((up, down)):
            copy = pltpu.make_async_copy(
                piece.at[pl.ds(j * half, units)], whole.at[pl.ds(i * units, units)], sems.at[i, j]
            )
            copy.start()
            copies.append(copy)
    for copy in copies:
        copy.wait()
    tok, cot = rows_ref[:, :width], rows_ref[:, width:]
    hidden, act_grad = activations(matmul_nt(tok, up[...]), matmul_nt(cot, down[...]))
    acc_ref[:, :width] = matmul(hidden, down[...])
    acc_ref[:, width:] = matmul(act_grad, up[...])


def gathered(rows, pieces, units):
    width = rows.shape[1] // 2
    count = len(pieces)
    return pl.pallas_call(
        functools.partial(gathered_kernel, units),
        out_shape=jax.ShapeDtypeStruct(rows.shape, F32),
        in_specs=[pl.BlockSpec(memory_space=pltpu.VMEM)] + [pl.BlockSpec(memory_space=pl.ANY)] * count,
        out_specs=pl.BlockSpec(memory_space=pltpu.VMEM),
        scratch_shapes=[
            pltpu.VMEM((count * units, width), BF16),
            pltpu.VMEM((count * units, width), BF16),
            pltpu.SemaphoreType.DMA((count, 2)),
        ],
        compiler_params=pltpu.CompilerParams(vmem_limit_bytes=VMEM_LIMIT),
        cost_estimate=pl.CostEstimate(
            flops=8 * rows.shape[0] * count * units * width,
            bytes_accessed=4 * count * units * width,
            transcendentals=0,
        ),
        name="gathered",
    )(rows, *map(outside, pieces))


def last_kernel(units, rows_ref, acc_ref, up_ref, down_ref, out_ref):
    width = up_ref.shape[1]
    up, down = up_ref[:units, :], down_ref[:units, :]
    tok, cot = rows_ref[:, :width], rows_ref[:, width:]
    hidden, act_grad = activations(matmul_nt(tok, up), matmul_nt(cot, down))
    out_ref[:, :width] = (acc_ref[:, :width] + matmul(hidden, down)).astype(BF16)
    out_ref[:, width:] = (acc_ref[:, width:] + matmul(act_grad, up)).astype(BF16)


def last(rows, acc, up_half, down_half, units):
    return pl.pallas_call(
        functools.partial(last_kernel, units),
        out_shape=jax.ShapeDtypeStruct(rows.shape, BF16),
        compiler_params=pltpu.CompilerParams(vmem_limit_bytes=VMEM_LIMIT),
        name="last",
    )(rows, acc, up_half, down_half)


def hot_kernel(units, hot_rows, order, where_ref, weight_ref, *refs):
    blocks, out_ref, tok, cot, sems = refs[:-4], refs[-4], refs[-3], refs[-2], refs[-1]
    ring = len(blocks)
    width = tok.shape[1]
    here = where_ref[0]
    copies = []
    for i, block in enumerate(blocks):
        place = pl.multiple_of((here ^ lax.rem(here + i, ring)) * HOT_PAD, HOT_PAD)
        pair = block if isinstance(block, tuple) else (block, block)
        offset = 0 if isinstance(block, tuple) else units + HOT_PAD
        for j, whole in enumerate((tok, cot)):
            copy = pltpu.make_async_copy(
                pair[j].at[pl.ds(j * offset + units, HOT_PAD)], whole.at[pl.ds(place, HOT_PAD)], sems.at[i, j]
            )
            copy.start()
            copies.append(copy)
    for copy in copies:
        copy.wait()
    up, down = weight_ref[:units, :], weight_ref[units:, :]
    hidden, act_grad = activations(matmul_nt(tok[...], up), matmul_nt(cot[...], down))
    mixed = matmul(hidden, down).astype(BF16)
    grads = matmul(act_grad, up).astype(BF16)
    for i, place in enumerate(order):
        out_ref[i, :, :width] = mixed[place * HOT_PAD : place * HOT_PAD + hot_rows]
        out_ref[i, :, width:] = grads[place * HOT_PAD : place * HOT_PAD + hot_rows]


def hot_partials(here, weights, blocks, units, hot_rows, order):
    width = weights.shape[1]
    ring = len(blocks)
    flat, spans = [], []
    for block in blocks:
        spans.append(len(block) if isinstance(block, tuple) else 0)
        flat += list(block) if isinstance(block, tuple) else [block]

    def kernel(where_ref, weight_ref, *refs):
        refs, grouped = list(refs), []
        for span in spans:
            grouped.append(tuple(refs.pop(0) for _ in range(span)) if span else refs.pop(0))
        hot_kernel(units, hot_rows, order, where_ref, weight_ref, *grouped, *refs)

    return pl.pallas_call(
        kernel,
        out_shape=jax.ShapeDtypeStruct((ring, hot_rows, 2 * width), BF16),
        in_specs=[
            pl.BlockSpec(memory_space=pltpu.SMEM),
            pl.BlockSpec(memory_space=pltpu.VMEM),
        ]
        + [pl.BlockSpec(memory_space=pl.ANY)] * len(flat),
        out_specs=pl.BlockSpec(memory_space=pltpu.VMEM),
        scratch_shapes=[
            pltpu.VMEM((ring * HOT_PAD, width), BF16),
            pltpu.VMEM((ring * HOT_PAD, width), BF16),
            pltpu.SemaphoreType.DMA((ring, 2)),
        ],
        compiler_params=pltpu.CompilerParams(vmem_limit_bytes=VMEM_LIMIT),
        name="hot",
    )(here, weights, *map(outside, flat))


def thirds(x):
    first = x.astype(BF16)
    rest = x - first.astype(F32)
    second = rest.astype(BF16)
    third = (rest - second.astype(F32)).astype(BF16)
    return first, second, third


def combine_kernel(capacity, ids_ref, gate_ref, cot_ref, cold_ref, kept_ref, sent_ref, mix_ref, grad_ref, gate_grad_ref):
    ids, gates, cot = ids_ref[...], gate_ref[...], cot_ref[...]
    top_count, tok_rows = ids.shape
    slots = cold_ref.shape[0]
    width = cot.shape[1]
    hot_rows = kept_ref.shape[0]
    cold, hot, expert, is_hot, hottest = slot_maps(ids, slots, capacity)
    per_slot = jnp.zeros((slots, tok_rows), F32)
    hot_gate = jnp.zeros((1, tok_rows), F32)
    hottest = hottest.astype(I32)
    for k in range(top_count):
        per_slot = per_slot + jnp.where(ids[k : k + 1, :] == expert, gates[k : k + 1, :], 0.0)
        hot_gate = hot_gate + jnp.where(ids[k : k + 1, :] == hottest, gates[k : k + 1, :], 0.0)
    cold_scale = thirds(jnp.where(cold > 0, per_slot, 0.0))
    hot_scale = thirds(jnp.where(hot > 0, hot_gate, 0.0)[:hot_rows])
    hot_result = (kept_ref[...].astype(F32) + sent_ref[...].astype(F32)).astype(BF16)

    def weighted(lo):
        sums = jnp.zeros((tok_rows, width), F32)
        for part in cold_scale:
            sums = sums + matmul_tn(part, cold_ref[:, lo : lo + width])
        for part in hot_scale:
            sums = sums + matmul_tn(part, hot_result[:, lo : lo + width])
        return sums

    mix_ref[...] = weighted(0).astype(BF16)
    grad_ref[...] = weighted(width).astype(BF16)
    cold_dots = jnp.where(cold > 0, matmul_nt(cold_ref[:, :width], cot), 0.0)
    hot_dots = jnp.where(hot[:hot_rows] > 0, matmul_nt(hot_result[:, :width], cot), 0.0)
    hot_dot = jnp.sum(hot_dots, 0, keepdims=True)
    for k in range(top_count):
        mine = ids[k : k + 1, :]
        cold_part = jnp.sum(jnp.where(mine == expert, cold_dots, 0.0), 0, keepdims=True)
        gate_grad_ref[k : k + 1, :] = cold_part + jnp.where(mine == hottest, hot_dot, 0.0)


def combine(ids, gates, cotangent, cold_results, kept, sent, capacity):
    return pl.pallas_call(
        functools.partial(combine_kernel, capacity),
        out_shape=(
            jax.ShapeDtypeStruct(cotangent.shape, BF16),
            jax.ShapeDtypeStruct(cotangent.shape, BF16),
            jax.ShapeDtypeStruct(gates.shape, F32),
        ),
        compiler_params=pltpu.CompilerParams(vmem_limit_bytes=VMEM_LIMIT),
        name="combine",
    )(ids, gates, cotangent, cold_results, kept, sent)


def shift(x, by):
    ring = lax.axis_size("dp")
    return lax.ppermute(x, "dp", [(i, (i + by) % ring) for i in range(ring)])


def plane(experts):
    xs, zs, cores = 4, experts // 8, 2
    return xs, zs, cores


def swap(x, bit):
    ring = lax.axis_size("dp")
    return lax.ppermute(x, "dp", [(i, i ^ bit) for i in range(ring)])


def spread_hot(weights, hottest, after):
    experts = lax.axis_size("expert")
    xs, zs, cores = plane(experts)
    me = lax.axis_index("expert")
    line = [[(x * zs + z) * cores + c for x in range(xs) for c in range(cores)] for z in range(zs)]
    parts = xs * cores
    rows, width = weights.shape
    chunks = lax.all_to_all(
        weights.reshape(parts, rows // parts, width), "expert", 0, 0, axis_index_groups=line, tiled=True
    )
    hot_x, hot_z, hot_c = hottest // (zs * cores), (hottest // cores) % zs, hottest % cores
    z = (me // cores) % zs
    chunk = lax.dynamic_index_in_dim(chunks, hot_x * cores + hot_c, 0, keepdims=False)
    chunk = jnp.where(z == hot_z, chunk, jnp.zeros_like(chunk))
    step = 1
    while step < zs:
        pairs = [
            (e, (e // (zs * cores)) * zs * cores + ((((e // cores) % zs) ^ step) * cores) + e % cores)
            for e in range(experts)
        ]
        chunk = chunk + lax.ppermute(chunk, "expert", pairs)
        step *= 2
    chunk, after = lax.optimization_barrier((chunk, after))
    copies = jnp.broadcast_to(chunk[None], (parts,) + chunk.shape)
    whole = lax.all_to_all(copies, "expert", 0, 0, axis_index_groups=line, tiled=True)
    return whole.reshape(rows, width), after


def shards(tokens, cotangent, gate_probs, expert_ids, up_weight, down_weight):
    tok_rows, width = tokens.shape
    top_count = expert_ids.shape[1]
    experts = lax.axis_size("expert")
    hot_rows = 9 * tok_rows // 16
    capacity = (tok_rows * top_count - hot_rows + experts - 2) // (experts - 1)
    slots = experts * capacity
    up, down = up_weight[0], down_weight[0]
    units = up.shape[0]
    ids, gates = expert_ids.T, gate_probs.T

    outgoing, own, pair, hottest = route(ids, tokens, cotangent, up, down, slots, capacity)
    half = own.shape[0] // 2
    right, left = [own], [own]
    for _ in range(3):
        right.append(shift(right[-1], 1))
        left.append(shift(left[-1], -1))
    far_up, far_down = shift(right[-1][:half], 1), shift(left[-1][half:], -1)

    arrived = lax.all_to_all(
        outgoing.reshape(experts, capacity, 2 * width), "expert", 0, 0, tiled=True
    ).reshape(slots, 2 * width)
    hot_weights, arrived = spread_hot(pair, hottest[0, 0], arrived)

    acc = gathered(arrived, [own] + right[1:] + left[1:], units)
    results = last(arrived, acc, far_up, far_down, units)
    results, hot_weights = lax.optimization_barrier((results, hot_weights))
    came_back = lax.all_to_all(
        results.reshape(experts, capacity, 2 * width), "expert", 0, 0, tiled=True
    ).reshape(slots, 2 * width)

    blocks = left + [(far_up, far_down)] + right[:0:-1]
    here = lax.axis_index("dp").astype(I32).reshape(1)
    partials = hot_partials(here, hot_weights, blocks, units, hot_rows, (1, 3, 5, 7, 0, 4, 2, 6))

    def part(first, count):
        return partials[first : first + count].astype(F32)

    got = swap(partials[0:4], 1).astype(F32)
    onward = (part(6, 2) + got[1::2]).astype(BF16)
    stay = part(4, 2) + got[0::2]
    got = swap(onward, 2).astype(F32)
    stay = stay + got
    sent = swap(stay[1].astype(BF16), 4)
    mixture, input_grad, gate_grad = combine(ids, gates, cotangent, came_back, stay[0], sent, capacity)
    return mixture, input_grad, gate_grad.T


def solution(mesh):
    rows = P(("dp", "expert"), None)
    weights = P("expert", "dp", None)
    return jax.shard_map(
        shards,
        mesh=mesh,
        in_specs=(rows, rows, rows, rows, weights, weights),
        out_specs=(rows, rows, rows),
        check_vma=False,
    )
```

time: 197 us -> 211 us (1.071)
  Pallas kernels: 12.7 us -> 35 us
  blocking collectives: 14.2 us -> 0 us
  waiting for transfers between devices: 58.8 us -> 71.2 us
  local copies, waits for them, and re-layouts: 20.3 us -> 12.7 us
  starting transfers between devices: 79.6 us -> 81.9 us
    all_to_all x1, waiting for transfers between devices: 28.5 us -> 0.01 us  [spread_hot(): lax.all_to_all(copies, 'expert', 0, 0, axis_index_groups=line, tiled=True)]
    pallas_call x1, Pallas kernels: 0.7 us -> 25 us  [route(): pl.pallas_call(functools.partial(route_kernel, capacity), out_shape=(jax....]
    ppermute x8, waiting for transfers between devices: 7.72 us -> 24.5 us  [shift(): return lax.ppermute(x, 'dp', [(i, (i + by) % ring) for i in range(ring)])]
    all_to_all x1, waiting for transfers between devices: 5.29 us -> 20.4 us  [shards(): lax.all_to_all(results.reshape(experts, capacity, 2 * width), 'expert', 0...]
    all_gather x1 -> x0, blocking collectives: 14.2 us -> none  [spread_hot(): lax.all_gather(chunk, 'expert', axis=0, axis_index_groups=line, tiled=True)]
    ppermute x0 -> x3, waiting for transfers between devices: none -> 14.1 us  [swap(): return lax.ppermute(x, 'dp', [(i, i ^ bit) for i in range(ring)])]
    ppermute x3, waiting for transfers between devices: 17.3 us -> 8.47 us  [spread_hot(): chunk = chunk + lax.ppermute(chunk, 'expert', pairs)]
    ppermute x0 -> x3, starting transfers between devices: none -> 8.54 us  [swap(): return lax.ppermute(x, 'dp', [(i, i ^ bit) for i in range(ring)])]
  transfers between devices with their start and end apart: 15 -> 18, of which waited for: 5 -> 10; matrix products, arithmetic and copies ran while one was open for 9% -> 6% of each run, Pallas kernels for 5% -> 3%
where the time goes in v2:
time: 211 us; the launch traced here: 207 us
  starting transfers between devices  81.9 us (39%)
  waiting for transfers between devices  71.2 us (34%)
  Pallas kernels  35 us (17%)
  local copies, waits for them, and re-layouts  12.7 us (6%)
  between operations  3.68 us (2%)
  other arithmetic  2.78 us (1%)
    ppermute x8, starting transfers between devices, shift(): return lax.ppermute(x, 'dp', [(i, (i + by) % ring) for i in range(ring)])  25.5 us
    pallas_call x1, Pallas kernels, route(): pl.pallas_call(functools.partial(route_kernel, capacity), out_shape=(jax....  25 us
    ppermute x8, waiting for transfers between devices, shift(): return lax.ppermute(x, 'dp', [(i, (i + by) % ring) for i in range(ring)])  24.5 us
    all_to_all x1, waiting for transfers between devices, shards(): lax.all_to_all(results.reshape(experts, capacity, 2 * width), 'expert', 0...  20.4 us
    ppermute x3, starting transfers between devices, spread_hot(): chunk = chunk + lax.ppermute(chunk, 'expert', pairs)  14.1 us
    ppermute x3, waiting for transfers between devices, swap(): return lax.ppermute(x, 'dp', [(i, i ^ bit) for i in range(ring)])  14.1 us
    all_to_all x1, starting transfers between devices, shards(): lax.all_to_all(results.reshape(experts, capacity, 2 * width), 'expert', 0...  10.2 us
    all_to_all x1, starting transfers between devices, spread_hot(): lax.all_to_all(weights.reshape(parts, rows // parts, width), 'expert', 0,...  9.99 us
  transfers between devices with their start and end apart: 18, of which 10 were waited for; matrix products, arithmetic and copies ran while one was open for 6% of the time, Pallas kernels for 3%

profile of v2, /device:TPU:6, one launch (start us, length us, event | category | flops | bytes accessed | tf_op | source)
XLA Modules:
  0.0 207.4 jit_solution(15993332017177777875)
XLA Ops:
  0.6 0.0 copy-start.5
  0.6 0.7 copy-done.5
  1.3 25.0 %route.1 = (bf16[128,4096]{1,0:T(8,128)(2,1)S(1)}, bf16[224,2048]{1,0:T(8,128)(2,1)S(1)}, bf16[192,2048]{1,0:T(8,128)(2,1)}, s32[8,128]{1,0:T(8,128)S(1)}) custom-call(s32[8,16]{1,0:T(8,128)S(1)} %bitcast.18, bf16[16,2048]{1,0:T(8,128)(2,1)} %tok_ref.1, bf16[16,2048]{1,0:T(8,128)(2,1)} %cot_ref.3, bf16[96,2048]{1,0:T(8,128)(2,1)} %bitcast.21, ...), custom_call_target="tpu_custom_call" | custom-call | tf_op jit(solution)/shard_map/route/pallas_call | solution.py:95
  26.3 0.0 copy-start
  26.3 10.0 %all-to-all-start = ((bf16[8,24,2048]{2,1,0:T(8,128)(2,1)}), bf16[8,24,2048]{2,1,0:T(8,128)(2,1)}, u32[]{:S(2)}, u32[]{:S(2)}) async-start(bf16[8,24,2048]{2,1,0:T(8,128)(2,1)} %bitcast.5), calls=%async_computation | async-start | bytes 1572864 | tf_op jit(solution)/shard_map/all_to_all | solution.py:324
  36.3 1.9 collective-permute-start.6
  38.3 3.9 %collective-permute-start.3 = (bf16[224,2048]{1,0:T(8,128)(2,1)S(1)}, bf16[224,2048]{1,0:T(8,128)(2,1)}, u32[]{:S(2)}, u32[]{:S(2)}) collective-permute-start(bf16[224,2048]{1,0:T(8,128)(2,1)S(1)} %get-tuple-element.18.refs_0_), channel_id=1, source_target_pairs={{0,64},{64,128},{128,192},{192,256},{256,320},{320,384},{384,448},... | collective-permute-start | bytes 2752520 | tf_op jit(solution)/shard_map/ppermute | solution.py:304
  42.2 1.5 reshape.33
  43.7 3.8 %all-to-all-done = bf16[8,24,2048]{2,1,0:T(8,128)(2,1)} async-done(((bf16[8,24,2048]{2,1,0:T(8,128)(2,1)}), bf16[8,24,2048]{2,1,0:T(8,128)(2,1)}, u32[]{:S(2)}, u32[]{:S(2)}) %all-to-all-start) | async-done | bytes 786464 | tf_op jit(solution)/shard_map/all_to_all | solution.py:324
  47.5 0.0 copy-done
  47.5 8.8 %all-to-all-start.1 = ((bf16[64,2,4096]{2,1,0:T(2,128)(2,1)}), bf16[64,2,4096]{2,1,0:T(2,128)(2,1)}, u32[]{:S(2)}, u32[]{:S(2)}) async-start(bf16[64,2,4096]{2,1,0:T(2,128)(2,1)} %reshape.33), calls=%async_computation.1 | async-start | bytes 2097152 | tf_op jit(solution)/shard_map/all_to_all | solution.py:364
  56.3 4.3 %collective-permute-done.6.refs_4_.refs_1_ = bf16[224,2048]{1,0:T(8,128)(2,1)S(1)} collective-permute-done((bf16[224,2048]{1,0:T(8,128)(2,1)S(1)}, bf16[224,2048]{1,0:T(8,128)(2,1)S(1)}, u32[]{:S(2)}, u32[]{:S(2)}) %collective-permute-start.6) | collective-permute-done | bytes 917536 | tf_op jit(solution)/shard_map/ppermute | solution.py:304
  60.6 3.4 %collective-permute-start.7 = (bf16[224,2048]{1,0:T(8,128)(2,1)S(1)}, bf16[224,2048]{1,0:T(8,128)(2,1)}, u32[]{:S(2)}, u32[]{:S(2)}) collective-permute-start(bf16[224,2048]{1,0:T(8,128)(2,1)S(1)} %collective-permute-done.6.refs_4_.refs_1_), channel_id=1, source_target_pairs={{0,448},{64,0},{128,64},{192,128},{256,192},{320,256},{384,320},{4... | collective-permute-start | bytes 2752520 | tf_op jit(solution)/shard_map/ppermute | solution.py:304
  64.0 0.0 collective-permute-done.3.refs_1_.refs_8_
  64.0 2.4 %collective-permute-start.4 = (bf16[224,2048]{1,0:T(8,128)(2,1)}, bf16[224,2048]{1,0:T(8,128)(2,1)}, u32[]{:S(2)}, u32[]{:S(2)}) collective-permute-start(bf16[224,2048]{1,0:T(8,128)(2,1)} %collective-permute-done.3.refs_1_.refs_8_), channel_id=1, source_target_pairs={{0,64},{64,128},{128,192},{192,256},{256,320},{320,384},{384,448},... | collective-permute-start | bytes 2752520 | tf_op jit(solution)/shard_map/ppermute | solution.py:304
  66.5 0.5 slice.31
  69.7 0.9 select_bitcast_fusion
  70.6 1.9 collective-permute-start
  72.5 0.0 copy-done.9
  72.5 11.8 %collective-permute-done.7.refs_5_.refs_2_ = bf16[224,2048]{1,0:T(8,128)(2,1)} collective-permute-done((bf16[224,2048]{1,0:T(8,128)(2,1)S(1)}, bf16[224,2048]{1,0:T(8,128)(2,1)}, u32[]{:S(2)}, u32[]{:S(2)}) %collective-permute-start.7) | collective-permute-done | bytes 917536 | tf_op jit(solution)/shard_map/ppermute | solution.py:304
  84.3 4.9 %collective-permute-start.8 = (bf16[224,2048]{1,0:T(8,128)(2,1)}, bf16[224,2048]{1,0:T(8,128)(2,1)S(1)}, u32[]{:S(2)}, u32[]{:S(2)}) collective-permute-start(bf16[224,2048]{1,0:T(8,128)(2,1)} %collective-permute-done.7.refs_5_.refs_2_), channel_id=1, source_target_pairs={{0,448},{64,0},{128,64},{192,128},{256,192},{320,256},{384,320},{4... | collective-permute-start | bytes 2752520 | tf_op jit(solution)/shard_map/ppermute | solution.py:304
  89.2 0.0 collective-permute-done.4.refs_2_.refs_7_
  89.2 1.9 collective-permute-start.5
  91.2 0.0 collective-permute-done
  91.2 0.9 fusion.1
  92.1 3.6 %collective-permute-start.1 = (bf16[24,2048]{1,0:T(8,128)(2,1)S(1)}, bf16[24,2048]{1,0:T(8,128)(2,1)S(1)}, u32[]{:S(2)}, u32[]{:S(2)}) collective-permute-start(bf16[24,2048]{1,0:T(8,128)(2,1)S(1)} %fusion.1), channel_id=1, source_target_pairs={{0,4},{1,5},{2,6},{3,7},{4,0},{5,1},{6,2},{7,3},{8,12},{9,13},{10,... | collective-permute-start | bytes 294920 | tf_op jit(solution)/shard_map/ppermute | solution.py:337
  95.7 4.8 %collective-permute-done.1 = bf16[24,2048]{1,0:T(8,128)(2,1)S(1)} collective-permute-done((bf16[24,2048]{1,0:T(8,128)(2,1)S(1)}, bf16[24,2048]{1,0:T(8,128)(2,1)S(1)}, u32[]{:S(2)}, u32[]{:S(2)}) %collective-permute-start.1) | collective-permute-done | bytes 98336 | tf_op jit(solution)/shard_map/ppermute | solution.py:337
  100.6 8.6 %collective-permute-start.2 = (bf16[24,2048]{1,0:T(8,128)(2,1)S(1)}, bf16[24,2048]{1,0:T(8,128)(2,1)S(1)}, u32[]{:S(2)}, u32[]{:S(2)}) collective-permute-start(bf16[24,2048]{1,0:T(8,128)(2,1)S(1)} %add.44), channel_id=1, source_target_pairs={{0,8},{1,9},{2,10},{3,11},{4,12},{5,13},{6,14},{7,15},{8,0},{9,1},... | collective-permute-start | bytes 294920 | tf_op jit(solution)/shard_map/ppermute | solution.py:337
  109.2 3.6 %collective-permute-done.2 = bf16[24,2048]{1,0:T(8,128)(2,1)S(1)} collective-permute-done((bf16[24,2048]{1,0:T(8,128)(2,1)S(1)}, bf16[24,2048]{1,0:T(8,128)(2,1)S(1)}, u32[]{:S(2)}, u32[]{:S(2)}) %collective-permute-start.2) | collective-permute-done | bytes 98336 | tf_op jit(solution)/shard_map/ppermute | solution.py:337
  112.8 0.0 all-to-all-done.1
  112.9 1.5 reshape.34.rows_ref
  114.3 1.0 broadcast_in_dim.10
  115.4 4.8 %all-to-all-start.2 = ((bf16[8,24,2048]{2,1,0:T(8,128)(2,1)}), bf16[8,24,2048]{2,1,0:T(8,128)(2,1)S(1)}, u32[]{:S(2)}, u32[]{:S(2)}) async-start(bf16[8,24,2048]{2,1,0:T(8,128)(2,1)} %broadcast_in_dim.10), calls=%async_computation.2 | async-start | bytes 1572864 | tf_op jit(solution)/shard_map/all_to_all | solution.py:341
  120.2 0.0 collective-permute-done.8.refs_6_.refs_3_
  120.2 0.9 slice.42
  121.1 5.1 %collective-permute-start.10 = (bf16[112,2048]{1,0:T(8,128)(2,1)}, bf16[112,2048]{1,0:T(8,128)(2,1)S(1)}, u32[]{:S(2)}, u32[]{:S(2)}) collective-permute-start(bf16[112,2048]{1,0:T(8,128)(2,1)} %slice.42), channel_id=1, source_target_pairs={{0,448},{64,0},{128,64},{192,128},{256,192},{320,256},{384,320},{4... | collective-permute-start | bytes 1376264 | tf_op jit(solution)/shard_map/ppermute | solution.py:304
  126.2 0.0 collective-permute-done.5.refs_3_.refs_6_
  126.2 1.8 slice.41
  128.0 1.9 collective-permute-start.9
  129.9 5.3 %gathered.1.acc_ref = f32[128,4096]{1,0:T(8,128)S(1)} custom-call(bf16[128,4096]{1,0:T(8,128)(2,1)S(1)} %reshape.34.rows_ref, bf16[224,2048]{1,0:T(8,128)(2,1)} %copy-done, bf16[224,2048]{1,0:T(8,128)(2,1)} %collective-permute-done.3.refs_1_.refs_8_, bf16[224,2048]{1,0:T(8,128)(2,1)} %collective-permute-done.4.refs_2_.refs_7_, ...), custom_call_target="tpu_custom_call" | custom-call | flops 1409286144 | bytes 5505024 | tf_op jit(solution)/shard_map/gathered/pallas_call | solution.py:147
  135.3 1.3 collective-permute-done.10.down_ref.refs_5_
  136.6 7.0 %collective-permute-done.9.up_ref.refs_4_ = bf16[112,2048]{1,0:T(8,128)(2,1)S(1)} collective-permute-done((bf16[112,2048]{1,0:T(8,128)(2,1)}, bf16[112,2048]{1,0:T(8,128)(2,1)S(1)}, u32[]{:S(2)}, u32[]{:S(2)}) %collective-permute-start.9) | collective-permute-done | bytes 458784 | tf_op jit(solution)/shard_map/ppermute | solution.py:304
  143.6 0.8 copy-done.2
  144.4 1.0 copy-done.3
  145.4 0.8 last.1
  146.2 0.0 all-to-all-done.2
  146.2 2.2 %hot.1 = bf16[8,9,4096]{2,1,0:T(8,128)(2,1)S(1)} custom-call(s32[1]{0:T(128)} %bitcast.8.where_ref, bf16[192,2048]{1,0:T(8,128)(2,1)S(1)} %bitcast.17, bf16[224,2048]{1,0:T(8,128)(2,1)} %copy-done, bf16[224,2048]{1,0:T(8,128)(2,1)} %copy-done.9, bf16[224,2048]{1,0:T(8,128)(2,1)} %collective-permute-done.7.refs_5_.refs_2_, bf16[224,2048]{1,0:T(8,128)(2,1)} %copy-done.8, ...), custom_call_target="tpu_custom_call" | custom-call | tf_op jit(solution)/shard_map/hot/pallas_call | solution.py:226
  148.5 1.9 collective-permute-start.11
  150.4 12.8 %collective-permute-done.11 = bf16[4,9,4096]{2,1,0:T(8,128)(2,1)S(1)} collective-permute-done((bf16[4,9,4096]{2,1,0:T(8,128)(2,1)S(1)}, bf16[4,9,4096]{2,1,0:T(8,128)(2,1)S(1)}, u32[]{:S(2)}, u32[]{:S(2)}) %collective-permute-start.11) | collective-permute-done | bytes 294944 | tf_op jit(solution)/shard_map/ppermute | solution.py:314
  163.2 0.1 convert_element_type.20
  163.3 0.8 add_convert_fusion
  164.0 1.9 collective-permute-start.12
  165.9 1.5 reshape.36
  167.4 10.2 %all-to-all-start.3 = ((bf16[64,2,4096]{2,1,0:T(2,128)(2,1)}), bf16[64,2,4096]{2,1,0:T(2,128)(2,1)}, u32[]{:S(2)}, u32[]{:S(2)}) async-start(bf16[64,2,4096]{2,1,0:T(2,128)(2,1)} %reshape.36), calls=%async_computation.3 | async-start | bytes 2097152 | tf_op jit(solution)/shard_map/all_to_all | solution.py:372
  177.6 0.0 copy-start.4
  177.6 0.0 copy-start.6
  177.7 0.0 copy-start.7
  177.7 1.3 collective-permute-done.12
  178.9 0.1 convert_add_fusion
  179.0 4.7 %collective-permute-start.13 = (bf16[9,4096]{1,0:T(8,128)(2,1)S(1)}, bf16[9,4096]{1,0:T(8,128)(2,1)S(1)}, u32[]{:S(2)}, u32[]{:S(2)}) collective-permute-start(bf16[9,4096]{1,0:T(8,128)(2,1)S(1)} %fusion), channel_id=1, source_target_pairs={{0,256},{64,320},{128,384},{192,448},{256,0},{320,64},{384,128},{4... | collective-permute-start | bytes 221192 | tf_op jit(solution)/shard_map/ppermute | solution.py:314
  183.8 20.4 %all-to-all-done.3 = bf16[64,2,4096]{2,1,0:T(2,128)(2,1)} async-done(((bf16[64,2,4096]{2,1,0:T(2,128)(2,1)}), bf16[64,2,4096]{2,1,0:T(2,128)(2,1)}, u32[]{:S(2)}, u32[]{:S(2)}) %all-to-all-start.3) | async-done | bytes 1048608 | tf_op jit(solution)/shard_map/all_to_all | solution.py:372
  204.2 1.5 reshape.37.cold_ref
  205.7 0.0 collective-permute-done.13.sent_ref
  205.7 1.7 combine.1
  (15 shorter events, 0.1 us)
Async XLA Ops:
  0.6 0.7 copy-start.5
  26.3 21.2 %copy-start = (bf16[224,2048]{1,0:T(8,128)(2,1)}, bf16[224,2048]{1,0:T(8,128)(2,1)S(1)}, u32[]{:S(2)}) copy-start(bf16[224,2048]{1,0:T(8,128)(2,1)S(1)} %get-tuple-element.18.refs_0_) | copy-start | bytes 2752516
  26.3 21.2 %all-to-all-start = ((bf16[8,24,2048]{2,1,0:T(8,128)(2,1)}), bf16[8,24,2048]{2,1,0:T(8,128)(2,1)}, u32[]{:S(2)}, u32[]{:S(2)}) async-start(bf16[8,24,2048]{2,1,0:T(8,128)(2,1)} %bitcast.5), calls=%async_computation | async-start | bytes 1572864 | tf_op jit(solution)/shard_map/all_to_all | solution.py:324
  36.3 24.3 %collective-permute-start.6 = (bf16[224,2048]{1,0:T(8,128)(2,1)S(1)}, bf16[224,2048]{1,0:T(8,128)(2,1)S(1)}, u32[]{:S(2)}, u32[]{:S(2)}) collective-permute-start(bf16[224,2048]{1,0:T(8,128)(2,1)S(1)} %get-tuple-element.18.refs_0_), channel_id=1, source_target_pairs={{0,448},{64,0},{128,64},{192,128},{256,192},{320,256},{384,320},{4... | collective-permute-start | bytes 2752520 | tf_op jit(solution)/shard_map/ppermute | solution.py:304
  38.3 25.8 %collective-permute-start.3 = (bf16[224,2048]{1,0:T(8,128)(2,1)S(1)}, bf16[224,2048]{1,0:T(8,128)(2,1)}, u32[]{:S(2)}, u32[]{:S(2)}) collective-permute-start(bf16[224,2048]{1,0:T(8,128)(2,1)S(1)} %get-tuple-element.18.refs_0_), channel_id=1, source_target_pairs={{0,64},{64,128},{128,192},{192,256},{256,320},{320,384},{384,448},... | collective-permute-start | bytes 2752520 | tf_op jit(solution)/shard_map/ppermute | solution.py:304
  47.5 65.3 %all-to-all-start.1 = ((bf16[64,2,4096]{2,1,0:T(2,128)(2,1)}), bf16[64,2,4096]{2,1,0:T(2,128)(2,1)}, u32[]{:S(2)}, u32[]{:S(2)}) async-start(bf16[64,2,4096]{2,1,0:T(2,128)(2,1)} %reshape.33), calls=%async_computation.1 | async-start | bytes 2097152 | tf_op jit(solution)/shard_map/all_to_all | solution.py:364
  60.6 11.9 %copy-start.9 = (bf16[224,2048]{1,0:T(8,128)(2,1)}, bf16[224,2048]{1,0:T(8,128)(2,1)S(1)}, u32[]{:S(2)}) copy-start(bf16[224,2048]{1,0:T(8,128)(2,1)S(1)} %collective-permute-done.6.refs_4_.refs_1_) | copy-start | bytes 2752516
  60.6 23.7 %collective-permute-start.7 = (bf16[224,2048]{1,0:T(8,128)(2,1)S(1)}, bf16[224,2048]{1,0:T(8,128)(2,1)}, u32[]{:S(2)}, u32[]{:S(2)}) collective-permute-start(bf16[224,2048]{1,0:T(8,128)(2,1)S(1)} %collective-permute-done.6.refs_4_.refs_1_), channel_id=1, source_target_pairs={{0,448},{64,0},{128,64},{192,128},{256,192},{320,256},{384,320},{4... | collective-permute-start | bytes 2752520 | tf_op jit(solution)/shard_map/ppermute | solution.py:304
  64.0 25.2 %collective-permute-start.4 = (bf16[224,2048]{1,0:T(8,128)(2,1)}, bf16[224,2048]{1,0:T(8,128)(2,1)}, u32[]{:S(2)}, u32[]{:S(2)}) collective-permute-start(bf16[224,2048]{1,0:T(8,128)(2,1)} %collective-permute-done.3.refs_1_.refs_8_), channel_id=1, source_target_pairs={{0,64},{64,128},{128,192},{192,256},{256,320},{320,384},{384,448},... | collective-permute-start | bytes 2752520 | tf_op jit(solution)/shard_map/ppermute | solution.py:304
  70.6 20.6 %collective-permute-start = (bf16[24,2048]{1,0:T(8,128)(2,1)S(1)}, bf16[24,2048]{1,0:T(8,128)(2,1)S(1)}, u32[]{:S(2)}, u32[]{:S(2)}) collective-permute-start(bf16[24,2048]{1,0:T(8,128)(2,1)S(1)} %select_bitcast_fusion), channel_id=1, source_target_pairs={{0,2},{1,3},{2,0},{3,1},{4,6},{5,7},{6,4},{7,5},{8,10},{9,11},{10,... | collective-permute-start | bytes 294920 | tf_op jit(solution)/shard_map/ppermute | solution.py:337
  84.3 35.9 %collective-permute-start.8 = (bf16[224,2048]{1,0:T(8,128)(2,1)}, bf16[224,2048]{1,0:T(8,128)(2,1)S(1)}, u32[]{:S(2)}, u32[]{:S(2)}) collective-permute-start(bf16[224,2048]{1,0:T(8,128)(2,1)} %collective-permute-done.7.refs_5_.refs_2_), channel_id=1, source_target_pairs={{0,448},{64,0},{128,64},{192,128},{256,192},{320,256},{384,320},{4... | collective-permute-start | bytes 2752520 | tf_op jit(solution)/shard_map/ppermute | solution.py:304
  89.2 37.0 %collective-permute-start.5 = (bf16[224,2048]{1,0:T(8,128)(2,1)}, bf16[224,2048]{1,0:T(8,128)(2,1)}, u32[]{:S(2)}, u32[]{:S(2)}) collective-permute-start(bf16[224,2048]{1,0:T(8,128)(2,1)} %collective-permute-done.4.refs_2_.refs_7_), channel_id=1, source_target_pairs={{0,64},{64,128},{128,192},{192,256},{256,320},{320,384},{384,448},... | collective-permute-start | bytes 2752520 | tf_op jit(solution)/shard_map/ppermute | solution.py:304
  92.1 8.5 %collective-permute-start.1 = (bf16[24,2048]{1,0:T(8,128)(2,1)S(1)}, bf16[24,2048]{1,0:T(8,128)(2,1)S(1)}, u32[]{:S(2)}, u32[]{:S(2)}) collective-permute-start(bf16[24,2048]{1,0:T(8,128)(2,1)S(1)} %fusion.1), channel_id=1, source_target_pairs={{0,4},{1,5},{2,6},{3,7},{4,0},{5,1},{6,2},{7,3},{8,12},{9,13},{10,... | collective-permute-start | bytes 294920 | tf_op jit(solution)/shard_map/ppermute | solution.py:337
  100.6 12.2 %collective-permute-start.2 = (bf16[24,2048]{1,0:T(8,128)(2,1)S(1)}, bf16[24,2048]{1,0:T(8,128)(2,1)S(1)}, u32[]{:S(2)}, u32[]{:S(2)}) collective-permute-start(bf16[24,2048]{1,0:T(8,128)(2,1)S(1)} %add.44), channel_id=1, source_target_pairs={{0,8},{1,9},{2,10},{3,11},{4,12},{5,13},{6,14},{7,15},{8,0},{9,1},... | collective-permute-start | bytes 294920 | tf_op jit(solution)/shard_map/ppermute | solution.py:337
  115.4 30.8 %all-to-all-start.2 = ((bf16[8,24,2048]{2,1,0:T(8,128)(2,1)}), bf16[8,24,2048]{2,1,0:T(8,128)(2,1)S(1)}, u32[]{:S(2)}, u32[]{:S(2)}) async-start(bf16[8,24,2048]{2,1,0:T(8,128)(2,1)} %broadcast_in_dim.10), calls=%async_computation.2 | async-start | bytes 1572864 | tf_op jit(solution)/shard_map/all_to_all | solution.py:341
  120.2 6.0 %copy-start.8 = (bf16[224,2048]{1,0:T(8,128)(2,1)}, bf16[224,2048]{1,0:T(8,128)(2,1)S(1)}, u32[]{:S(2)}) copy-start(bf16[224,2048]{1,0:T(8,128)(2,1)S(1)} %collective-permute-done.8.refs_6_.refs_3_) | copy-start | bytes 2752516
  121.1 15.5 %collective-permute-start.10 = (bf16[112,2048]{1,0:T(8,128)(2,1)}, bf16[112,2048]{1,0:T(8,128)(2,1)S(1)}, u32[]{:S(2)}, u32[]{:S(2)}) collective-permute-start(bf16[112,2048]{1,0:T(8,128)(2,1)} %slice.42), channel_id=1, source_target_pairs={{0,448},{64,0},{128,64},{192,128},{256,192},{320,256},{384,320},{4... | collective-permute-start | bytes 1376264 | tf_op jit(solution)/shard_map/ppermute | solution.py:304
  128.0 15.6 %collective-permute-start.9 = (bf16[112,2048]{1,0:T(8,128)(2,1)}, bf16[112,2048]{1,0:T(8,128)(2,1)S(1)}, u32[]{:S(2)}, u32[]{:S(2)}) collective-permute-start(bf16[112,2048]{1,0:T(8,128)(2,1)} %slice.41), channel_id=1, source_target_pairs={{0,64},{64,128},{128,192},{192,256},{256,320},{320,384},{384,448},... | collective-permute-start | bytes 1376264 | tf_op jit(solution)/shard_map/ppermute | solution.py:304
  136.6 9.6 %copy-start.1 = (bf16[112,2048]{1,0:T(8,128)(2,1)}, bf16[112,2048]{1,0:T(8,128)(2,1)S(1)}, u32[]{:S(2)}) copy-start(bf16[112,2048]{1,0:T(8,128)(2,1)S(1)} %collective-permute-done.10.down_ref.refs_5_) | copy-start | bytes 1376260
  143.6 0.8 copy-start.2
  144.4 1.0 copy-start.3
  148.5 14.7 %collective-permute-start.11 = (bf16[4,9,4096]{2,1,0:T(8,128)(2,1)S(1)}, bf16[4,9,4096]{2,1,0:T(8,128)(2,1)S(1)}, u32[]{:S(2)}, u32[]{:S(2)}) collective-permute-start(bf16[4,9,4096]{2,1,0:T(8,128)(2,1)S(1)} %slice.44), channel_id=1, source_target_pairs={{0,64},{64,0},{128,192},{192,128},{256,320},{320,256},{384,448},{4... | collective-permute-start | bytes 884744 | tf_op jit(solution)/shard_map/ppermute | solution.py:314
  164.0 14.9 %collective-permute-start.12 = (bf16[2,9,4096]{2,1,0:T(8,128)(2,1)}, bf16[2,9,4096]{2,1,0:T(8,128)(2,1)S(1)}, u32[]{:S(2)}, u32[]{:S(2)}) collective-permute-start(bf16[2,9,4096]{2,1,0:T(8,128)(2,1)} %add_convert_fusion), channel_id=1, source_target_pairs={{0,128},{64,192},{128,0},{192,64},{256,384},{320,448},{384,256},{4... | collective-permute-start | bytes 442376 | tf_op jit(solution)/shard_map/ppermute | solution.py:314
  167.4 36.8 %all-to-all-start.3 = ((bf16[64,2,4096]{2,1,0:T(2,128)(2,1)}), bf16[64,2,4096]{2,1,0:T(2,128)(2,1)}, u32[]{:S(2)}, u32[]{:S(2)}) async-start(bf16[64,2,4096]{2,1,0:T(2,128)(2,1)} %reshape.36), calls=%async_computation.3 | async-start | bytes 2097152 | tf_op jit(solution)/shard_map/all_to_all | solution.py:372
  177.6 28.1 %copy-start.4 = (bf16[16,2048]{1,0:T(8,128)(2,1)S(1)}, bf16[16,2048]{1,0:T(8,128)(2,1)}, u32[]{:S(2)}) copy-start(bf16[16,2048]{1,0:T(8,128)(2,1)} %cot_ref.3) | copy-start | bytes 196612
  177.6 28.0 %copy-start.6 = (s32[16,8]{0,1:T(8,128)S(1)}, s32[16,8]{0,1:T(8,128)}, u32[]{:S(2)}) copy-start(s32[16,8]{0,1:T(8,128)} %param.9) | copy-start | bytes 1540
  177.7 28.0 %copy-start.7 = (f32[16,8]{0,1:T(8,128)S(1)}, f32[16,8]{0,1:T(8,128)}, u32[]{:S(2)}) copy-start(f32[16,8]{0,1:T(8,128)} %param.8) | copy-start | bytes 1540
  179.0 26.6 %collective-permute-start.13 = (bf16[9,4096]{1,0:T(8,128)(2,1)S(1)}, bf16[9,4096]{1,0:T(8,128)(2,1)S(1)}, u32[]{:S(2)}, u32[]{:S(2)}) collective-permute-start(bf16[9,4096]{1,0:T(8,128)(2,1)S(1)} %fusion), channel_id=1, source_target_pairs={{0,256},{64,320},{128,384},{192,448},{256,0},{320,64},{384,128},{4... | collective-permute-start | bytes 221192 | tf_op jit(solution)/shard_map/ppermute | solution.py:314

commit v3 on v2

--- a/solution.py
+++ b/solution.py
@@ -53,8 +53,7 @@
 
 
 def route_kernel(
-    capacity, ids_ref, tok_ref, cot_ref, up_ref, down_ref, out_ref, own_ref, pair_ref, hottest_ref,
-    tok, cot, hot_tok, hot_cot, sems,
+    capacity, ids_ref, tok_ref, cot_ref, up_ref, down_ref, out_ref, own_ref, hottest_ref, tok, cot, sems
 ):
     slots, width = out_ref.shape[0], tok.shape[1]
     units = up_ref.shape[0]
@@ -63,8 +62,6 @@
     copies = [
         pltpu.make_async_copy(up_ref, own_ref.at[pl.ds(0, units)], sems.at[2]),
         pltpu.make_async_copy(down_ref, own_ref.at[pl.ds(half, units)], sems.at[3]),
-        pltpu.make_async_copy(up_ref, pair_ref.at[pl.ds(0, units)], sems.at[4]),
-        pltpu.make_async_copy(down_ref, pair_ref.at[pl.ds(units, units)], sems.at[5]),
     ]
     for copy in loads + copies:
         copy.start()
@@ -73,17 +70,11 @@
     hottest_ref[...] = jnp.broadcast_to(hottest, hottest_ref.shape).astype(I32)
     for copy in loads:
         copy.wait()
-    hot_tok[...] = matmul(hot, tok[...]).astype(BF16)
-    hot_cot[...] = matmul(hot, cot[...]).astype(BF16)
-    stores = [
-        pltpu.make_async_copy(hot_tok, own_ref.at[pl.ds(units, HOT_PAD)], sems.at[6]),
-        pltpu.make_async_copy(hot_cot, own_ref.at[pl.ds(half + units, HOT_PAD)], sems.at[7]),
-    ]
-    for copy in stores:
-        copy.start()
+    own_ref[units:half, :] = matmul(hot, tok[...]).astype(BF16)
+    own_ref[half + units :, :] = matmul(hot, cot[...]).astype(BF16)
     out_ref[:, :width] = matmul(cold, tok[...]).astype(BF16)
     out_ref[:, width:] = matmul(cold, cot[...]).astype(BF16)
-    for copy in copies + stores:
+    for copy in copies:
         copy.wait()
 
 
@@ -97,17 +88,14 @@
         out_shape=(
             jax.ShapeDtypeStruct((slots, 2 * width), BF16),
             jax.ShapeDtypeStruct((2 * (units + HOT_PAD), width), BF16),
-            jax.ShapeDtypeStruct((2 * units, width), BF16),
             jax.ShapeDtypeStruct((8, 128), I32),
         ),
         in_specs=[inside] + [anywhere] * 4,
-        out_specs=(inside, anywhere, anywhere, inside),
+        out_specs=(inside, inside, inside),
         scratch_shapes=[
             pltpu.VMEM((tok_rows, width), BF16),
             pltpu.VMEM((tok_rows, width), BF16),
-            pltpu.VMEM((HOT_PAD, width), BF16),
-            pltpu.VMEM((HOT_PAD, width), BF16),
-            pltpu.SemaphoreType.DMA((8,)),
+            pltpu.SemaphoreType.DMA((4,)),
         ],
         compiler_params=pltpu.CompilerParams(vmem_limit_bytes=VMEM_LIMIT),
         name="route",
@@ -250,53 +238,93 @@
     return first, second, third
 
 
-def combine_kernel(capacity, ids_ref, gate_ref, cot_ref, cold_ref, kept_ref, sent_ref, mix_ref, grad_ref, gate_grad_ref):
+def cold_kernel(capacity, ids_ref, gate_ref, cot_ref, cold_ref, sum_ref, dots_ref):
+    ids, gates, cot = ids_ref[...], gate_ref[...], cot_ref[...]
+    top_count = ids.shape[0]
+    slots = cold_ref.shape[0]
+    width = cot.shape[1]
+    cold, _, expert, _, _ = slot_maps(ids, slots, capacity)
+    per_slot = jnp.zeros(cold.shape, F32)
+    for k in range(top_count):
+        per_slot = per_slot + jnp.where(ids[k : k + 1, :] == expert, gates[k : k + 1, :], 0.0)
+    scale = thirds(jnp.where(cold > 0, per_slot, 0.0))
+    for lo in (0, width):
+        rows = cold_ref[:, lo : lo + width]
+        sum_ref[:, lo : lo + width] = matmul_tn(scale[0], rows) + matmul_tn(scale[1], rows) + matmul_tn(scale[2], rows)
+    dots = jnp.where(cold > 0, matmul_nt(cold_ref[:, :width], cot), 0.0)
+    for k in range(top_count):
+        dots_ref[k : k + 1, :] = jnp.sum(jnp.where(ids[k : k + 1, :] == expert, dots, 0.0), 0, keepdims=True)
+
+
+def cold_combine(ids, gates, cotangent, results, capacity):
+    tok_rows, width = cotangent.shape
+    return pl.pallas_call(
+        functools.partial(cold_kernel, capacity),
+        out_shape=(
+            jax.ShapeDtypeStruct((tok_rows, 2 * width), F32),
+            jax.ShapeDtypeStruct(gates.shape, F32),
+        ),
+        compiler_params=pltpu.CompilerParams(vmem_limit_bytes=VMEM_LIMIT),
+        cost_estimate=pl.CostEstimate(flops=1 << 36, bytes_accessed=1 << 26, transcendentals=0),
+        name="cold_combine",
+    )(ids, gates, cotangent, results)
+
+
+def final_kernel(
+    capacity, slots, ids_ref, gate_ref, cot_ref, sum_ref, dots_ref, kept_ref, sent_ref, mix_ref, grad_ref, gate_grad_ref
+):
     ids, gates, cot = ids_ref[...], gate_ref[...], cot_ref[...]
     top_count, tok_rows = ids.shape
-    slots = cold_ref.shape[0]
     width = cot.shape[1]
     hot_rows = kept_ref.shape[0]
-    cold, hot, expert, is_hot, hottest = slot_maps(ids, slots, capacity)
-    per_slot = jnp.zeros((slots, tok_rows), F32)
-    hot_gate = jnp.zeros((1, tok_rows), F32)
+    _, hot, _, _, hottest = slot_maps(ids, slots, capacity)
     hottest = hottest.astype(I32)
+    gate = jnp.zeros((1, tok_rows), F32)
     for k in range(top_count):
-        per_slot = per_slot + jnp.where(ids[k : k + 1, :] == expert, gates[k : k + 1, :], 0.0)
-        hot_gate = hot_gate + jnp.where(ids[k : k + 1, :] == hottest, gates[k : k + 1, :], 0.0)
-    cold_scale = thirds(jnp.where(cold > 0, per_slot, 0.0))
-    hot_scale = thirds(jnp.where(hot > 0, hot_gate, 0.0)[:hot_rows])
-    hot_result = (kept_ref[...].astype(F32) + sent_ref[...].astype(F32)).astype(BF16)
-
-    def weighted(lo):
-        sums = jnp.zeros((tok_rows, width), F32)
-        for part in cold_scale:
-            sums = sums + matmul_tn(part, cold_ref[:, lo : lo + width])
-        for part in hot_scale:
-            sums = sums + matmul_tn(part, hot_result[:, lo : lo + width])
-        return sums
-
-    mix_ref[...] = weighted(0).astype(BF16)
-    grad_ref[...] = weighted(width).astype(BF16)
-    cold_dots = jnp.where(cold > 0, matmul_nt(cold_ref[:, :width], cot), 0.0)
-    hot_dots = jnp.where(hot[:hot_rows] > 0, matmul_nt(hot_result[:, :width], cot), 0.0)
-    hot_dot = jnp.sum(hot_dots, 0, keepdims=True)
-    for k in range(top_count):
-        mine = ids[k : k + 1, :]
-        cold_part = jnp.sum(jnp.where(mine == expert, cold_dots, 0.0), 0, keepdims=True)
-        gate_grad_ref[k : k + 1, :] = cold_part + jnp.where(mine == hottest, hot_dot, 0.0)
-
-
-def combine(ids, gates, cotangent, cold_results, kept, sent, capacity):
-    return pl.pallas_call(
-        functools.partial(combine_kernel, capacity),
+        gate = gate + jnp.where(ids[k : k + 1, :] == hottest, gates[k : k + 1, :], 0.0)
+    hot = hot[:hot_rows]
+    scale = thirds(jnp.where(hot > 0, gate, 0.0))
+    result = (kept_ref[...] + sent_ref[...].astype(F32)).astype(BF16)
+    for lo, out_ref in ((0, mix_ref), (width, grad_ref)):
+        rows = result[:, lo : lo + width]
+        total = matmul_tn(scale[0], rows) + matmul_tn(scale[1], rows) + matmul_tn(scale[2], rows)
+        out_ref[...] = (sum_ref[:, lo : lo + width] + total).astype(BF16)
+    dots = jnp.where(hot > 0, matmul_nt(result[:, :width], cot), 0.0)
+    dot = jnp.sum(dots, 0, keepdims=True)
+    gate_grad_ref[...] = dots_ref[...] + jnp.where(ids == hottest, dot, 0.0)
+
+
+def final_combine(ids, gates, cotangent, sums, dots, kept, sent, slots, capacity):
+    return pl.pallas_call(
+        functools.partial(final_kernel, capacity, slots),
         out_shape=(
             jax.ShapeDtypeStruct(cotangent.shape, BF16),
             jax.ShapeDtypeStruct(cotangent.shape, BF16),
             jax.ShapeDtypeStruct(gates.shape, F32),
         ),
         compiler_params=pltpu.CompilerParams(vmem_limit_bytes=VMEM_LIMIT),
-        name="combine",
-    )(ids, gates, cotangent, cold_results, kept, sent)
+        name="final_combine",
+    )(ids, gates, cotangent, sums, dots, kept, sent)
+
+
+def tick_kernel(token_ref, *refs):
+    refs[-1][...] = token_ref[...]
+
+
+def tick(token, *after, through=False):
+    count = len(after) if through else 0
+    anywhere, inside = pl.BlockSpec(memory_space=pl.ANY), pl.BlockSpec(memory_space=pltpu.VMEM)
+    out = pl.pallas_call(
+        tick_kernel,
+        out_shape=tuple(jax.ShapeDtypeStruct(x.shape, x.dtype) for x in after[:count] + (token,)),
+        in_specs=[inside] + [anywhere] * len(after),
+        out_specs=tuple([anywhere] * count + [inside]),
+        input_output_aliases={i + 1: i for i in range(count)},
+        compiler_params=pltpu.CompilerParams(vmem_limit_bytes=1 << 20),
+        cost_estimate=pl.CostEstimate(flops=1 << 35, bytes_accessed=1 << 25, transcendentals=0),
+        name="tick",
+    )(token, *after)
+    return out if through else out[0]
 
 
 def shift(x, by):
@@ -304,42 +332,11 @@
     return lax.ppermute(x, "dp", [(i, (i + by) % ring) for i in range(ring)])
 
 
-def plane(experts):
-    xs, zs, cores = 4, experts // 8, 2
-    return xs, zs, cores
-
-
 def swap(x, bit):
     ring = lax.axis_size("dp")
-    return lax.ppermute(x, "dp", [(i, i ^ bit) for i in range(ring)])
-
-
-def spread_hot(weights, hottest, after):
-    experts = lax.axis_size("expert")
-    xs, zs, cores = plane(experts)
-    me = lax.axis_index("expert")
-    line = [[(x * zs + z) * cores + c for x in range(xs) for c in range(cores)] for z in range(zs)]
-    parts = xs * cores
-    rows, width = weights.shape
-    chunks = lax.all_to_all(
-        weights.reshape(parts, rows // parts, width), "expert", 0, 0, axis_index_groups=line, tiled=True
-    )
-    hot_x, hot_z, hot_c = hottest // (zs * cores), (hottest // cores) % zs, hottest % cores
-    z = (me // cores) % zs
-    chunk = lax.dynamic_index_in_dim(chunks, hot_x * cores + hot_c, 0, keepdims=False)
-    chunk = jnp.where(z == hot_z, chunk, jnp.zeros_like(chunk))
-    step = 1
-    while step < zs:
-        pairs = [
-            (e, (e // (zs * cores)) * zs * cores + ((((e // cores) % zs) ^ step) * cores) + e % cores)
-            for e in range(experts)
-        ]
-        chunk = chunk + lax.ppermute(chunk, "expert", pairs)
-        step *= 2
-    chunk, after = lax.optimization_barrier((chunk, after))
-    copies = jnp.broadcast_to(chunk[None], (parts,) + chunk.shape)
-    whole = lax.all_to_all(copies, "expert", 0, 0, axis_index_groups=line, tiled=True)
-    return whole.reshape(rows, width), after
+    pairs = [[i, i ^ bit] for i in range(ring) if not i & bit]
+    both = lax.all_gather(x, "dp", axis=0, axis_index_groups=pairs, tiled=False)
+    return jnp.where(lax.axis_index("dp") & bit == 0, both[1], both[0])
 
 
 def shards(tokens, cotangent, gate_probs, expert_ids, up_weight, down_weight):
@@ -353,18 +350,29 @@
     units = up.shape[0]
     ids, gates = expert_ids.T, gate_probs.T
 
-    outgoing, own, pair, hottest = route(ids, tokens, cotangent, up, down, slots, capacity)
+    outgoing, own, hottest = route(ids, tokens, cotangent, up, down, slots, capacity)
     half = own.shape[0] // 2
     right, left = [own], [own]
-    for _ in range(3):
-        right.append(shift(right[-1], 1))
-        left.append(shift(left[-1], -1))
+    for step in range(3):
+        r, l = shift(right[-1], 1), shift(left[-1], -1)
+        if step == 0:
+            token = tick(hottest, r, l)
+        if step == 1:
+            r, l, _ = tick(hottest, r, l, through=True)
+        right.append(r)
+        left.append(l)
     far_up, far_down = shift(right[-1][:half], 1), shift(left[-1][half:], -1)
 
-    arrived = lax.all_to_all(
-        outgoing.reshape(experts, capacity, 2 * width), "expert", 0, 0, tiled=True
-    ).reshape(slots, 2 * width)
-    hot_weights, arrived = spread_hot(pair, hottest[0, 0], arrived)
+    piece = 2 * units * width // (experts * capacity)
+    pieces = jnp.concatenate([up, down], 0).reshape(experts, capacity, piece)
+    dealt = lax.all_to_all(pieces, "expert", 0, 0, tiled=True)
+    mine = lax.dynamic_index_in_dim(dealt, token[0, 0], 0)
+    outgoing = jnp.concatenate(
+        [outgoing.reshape(experts, capacity, 2 * width), jnp.broadcast_to(mine, pieces.shape)], 2
+    )
+    arrived = lax.all_to_all(outgoing, "expert", 0, 0, tiled=True)
+    hot_weights = arrived[:, :, 2 * width :].reshape(2 * units, width)
+    arrived = arrived[:, :, : 2 * width].reshape(slots, 2 * width)
 
     acc = gathered(arrived, [own] + right[1:] + left[1:], units)
     results = last(arrived, acc, far_up, far_down, units)
@@ -386,7 +394,10 @@
     got = swap(onward, 2).astype(F32)
     stay = stay + got
     sent = swap(stay[1].astype(BF16), 4)
-    mixture, input_grad, gate_grad = combine(ids, gates, cotangent, came_back, stay[0], sent, capacity)
+    sums, dots = cold_combine(ids, gates, cotangent, came_back, capacity)
+    mixture, input_grad, gate_grad = final_combine(
+        ids, gates, cotangent, sums, dots, stay[0], sent, slots, capacity
+    )
     return mixture, input_grad, gate_grad.T
 
 

time: 211 us -> 185 us (0.88); the launches traced: 207 us -> 184 us
  blocking collectives: 0 us -> 41.8 us
  waiting for transfers between devices: 71.2 us -> 37.7 us
  starting transfers between devices: 81.9 us -> 57.7 us
  Pallas kernels: 35 us -> 12.4 us
  local copies, waits for them, and re-layouts: 12.7 us -> 24.6 us
  other arithmetic: 2.78 us -> 6.52 us
    all_gather x0 -> x3, blocking collectives: none -> 41.8 us  [swap(): both = lax.all_gather(x, 'dp', axis=0, axis_index_groups=pairs, tiled=False)]
    pallas_call x1, Pallas kernels: 25 us -> 1.36 us  [route(): pl.pallas_call(functools.partial(route_kernel, capacity), out_shape=(jax....]
    ppermute x6 -> x0, starting transfers between devices: 22.7 us -> none  [the longest x3 14.1 us: spread_hot(): chunk = chunk + lax.ppermute(chunk, 'expert', pairs)]
    ppermute x6 -> x0, waiting for transfers between devices: 22.5 us -> none  [the longest x3 14.1 us: swap(): return lax.ppermute(x, 'dp', [(i, i ^ bit) for i in range(ring)])]
    all_to_all x1, waiting for transfers between devices: 20.4 us -> 0.01 us  [shards(): lax.all_to_all(results.reshape(experts, capacity, 2 * width), 'expert', 0...]
    all_to_all x3 -> x2, waiting for transfers between devices: 3.85 us -> 17.6 us  [the longest x1 9.63 us: shards(): dealt = lax.all_to_all(pieces, 'expert', 0, 0, tiled=True)]
    concatenate x0 -> x2, other arithmetic: none -> 6.26 us  [the longest x1 4.16 us: shards(): jnp.concatenate([outgoing.reshape(experts, capacity, 2 * width), jnp.broa...]
    slice x1 -> x4, local copies, waits for them, and re-layouts: 0.51 us -> 6.26 us  [the longest x1 3.13 us: shards(): arrived = arrived[:, :, :2 * width].reshape(slots, 2 * width)]
  transfers between devices with their start and end apart: 18 -> 11, of which waited for: 10 -> 5; matrix products, arithmetic and copies ran while one was open for 6% -> 13% of each run, Pallas kernels for 3% -> 4%
where the time goes in v3:
time: 185 us; the launch traced here: 184 us
  starting transfers between devices  57.7 us (31%)
  blocking collectives  41.8 us (23%)
  waiting for transfers between devices  37.7 us (20%)
  local copies, waits for them, and re-layouts  24.6 us (13%)
  Pallas kernels  12.4 us (7%)
  other arithmetic  6.52 us (4%)
  between operations  2.97 us (2%)
    all_gather x3, blocking collectives, swap(): both = lax.all_gather(x, 'dp', axis=0, axis_index_groups=pairs, tiled=False)  41.8 us
    ppermute x8, starting transfers between devices, shift(): return lax.ppermute(x, 'dp', [(i, (i + by) % ring) for i in range(ring)])  27.5 us
    ppermute x8, waiting for transfers between devices, shift(): return lax.ppermute(x, 'dp', [(i, (i + by) % ring) for i in range(ring)])  20.1 us
    all_to_all x1, starting transfers between devices, shards(): dealt = lax.all_to_all(pieces, 'expert', 0, 0, tiled=True)  14.2 us
    all_to_all x1, waiting for transfers between devices, shards(): dealt = lax.all_to_all(pieces, 'expert', 0, 0, tiled=True)  9.63 us
    all_to_all x1, starting transfers between devices, shards(): lax.all_to_all(results.reshape(experts, capacity, 2 * width), 'expert', 0...  8.58 us
    all_to_all x1, waiting for transfers between devices, shards(): arrived = lax.all_to_all(outgoing, 'expert', 0, 0, tiled=True)  7.94 us
    all_to_all x1, starting transfers between devices, shards(): arrived = lax.all_to_all(outgoing, 'expert', 0, 0, tiled=True)  7.43 us
  transfers between devices with their start and end apart: 11, of which 5 were waited for; matrix products, arithmetic and copies ran while one was open for 13% of the time, Pallas kernels for 4%

profile of v3, /device:TPU:6, one launch (start us, length us, event | category | flops | bytes accessed | tf_op | source)
XLA Modules:
  0.0 183.7 jit_solution(324457392168126282)
XLA Ops:
  0.6 0.0 copy-start.9
  0.6 0.7 copy-done.9
  1.3 1.4 route.1
  2.7 0.0 copy-start.7
  2.7 0.0 copy-start
  2.7 0.9 copy-done.7
  3.6 5.4 %collective-permute-start.1 = (bf16[224,2048]{1,0:T(8,128)(2,1)S(1)}, bf16[224,2048]{1,0:T(8,128)(2,1)S(1)}, u32[]{:S(2)}, u32[]{:S(2)}) collective-permute-start(bf16[224,2048]{1,0:T(8,128)(2,1)S(1)} %get-tuple-element.17.refs_0_), channel_id=1, source_target_pairs={{0,448},{64,0},{128,64},{192,128},{256,192},{320,256},{384,320},{4... | collective-permute-start | bytes 2752520 | tf_op jit(solution)/shard_map/ppermute | solution.py:332
  9.0 1.9 %collective-permute-start = (bf16[224,2048]{1,0:T(8,128)(2,1)S(1)}, bf16[224,2048]{1,0:T(8,128)(2,1)S(1)}, u32[]{:S(2)}, u32[]{:S(2)}) collective-permute-start(bf16[224,2048]{1,0:T(8,128)(2,1)S(1)} %get-tuple-element.17.refs_0_), channel_id=1, source_target_pairs={{0,64},{64,128},{128,192},{192,256},{256,320},{320,384},{384,448},... | collective-permute-start | bytes 2752520 | tf_op jit(solution)/shard_map/ppermute | solution.py:332
  11.0 2.1 %pad_maximum_fusion.1 = bf16[192,2048]{1,0:T(8,128)(2,1)} fusion(bf16[96,2048]{1,0:T(8,128)(2,1)} %bitcast.19, bf16[96,2048]{1,0:T(8,128)(2,1)} %bitcast.21), kind=kLoop, calls=%fused_computation.1 | loop fusion | flops 1572864 | bytes 1572864 | tf_op jit(solution)/shard_map/concatenate | solution.py:367
  13.0 3.0 %reshape.38 = bf16[64,2,3072]{2,1,0:T(2,128)(2,1)} reshape(bf16[192,2048]{1,0:T(8,128)(2,1)} %pad_maximum_fusion.1) | data formatting | bytes 1572864 | tf_op jit(solution)/shard_map/reshape | solution.py:367
  16.0 0.0 copy-done
  16.0 14.2 %all-to-all-start = ((bf16[64,2,3072]{2,1,0:T(2,128)(2,1)}), bf16[64,2,3072]{2,1,0:T(2,128)(2,1)}, u32[]{:S(2)}, u32[]{:S(2)}) async-start(bf16[64,2,3072]{2,1,0:T(2,128)(2,1)} %reshape.38), calls=%async_computation | async-start | bytes 1572864 | tf_op jit(solution)/shard_map/all_to_all | solution.py:368
  30.2 2.6 %reshape.37 = bf16[64,2,4096]{2,1,0:T(2,128)(2,1)} reshape(bf16[128,4096]{1,0:T(8,128)(2,1)} %copy-done.7) | data formatting | bytes 2097152 | tf_op jit(solution)/shard_map/reshape | solution.py:371
  32.8 0.0 collective-permute-done.1.refs_1_.refs_4_
  32.8 1.2 collective-permute-done.refs_0_.refs_1_.refs_8_
  33.9 0.5 slice.55
  36.4 0.0 copy-done.1
  36.4 4.1 %collective-permute-start.3 = (bf16[224,2048]{1,0:T(8,128)(2,1)S(1)}, bf16[224,2048]{1,0:T(8,128)(2,1)S(1)}, u32[]{:S(2)}, u32[]{:S(2)}) collective-permute-start(bf16[224,2048]{1,0:T(8,128)(2,1)S(1)} %collective-permute-done.1.refs_1_.refs_4_), channel_id=1, source_target_pairs={{0,448},{64,0},{128,64},{192,128},{256,192},{320,256},{384,320},{4... | collective-permute-start | bytes 2752520 | tf_op jit(solution)/shard_map/ppermute | solution.py:332
  40.5 0.0 copy-done.2
  40.5 1.9 %collective-permute-start.2 = (bf16[224,2048]{1,0:T(8,128)(2,1)S(1)}, bf16[224,2048]{1,0:T(8,128)(2,1)}, u32[]{:S(2)}, u32[]{:S(2)}) collective-permute-start(bf16[224,2048]{1,0:T(8,128)(2,1)S(1)} %collective-permute-done.refs_0_.refs_1_.refs_8_), channel_id=1, source_target_pairs={{0,64},{64,128},{128,192},{192,256},{256,320},{320,384},{384,448},... | collective-permute-start | bytes 2752520 | tf_op jit(solution)/shard_map/ppermute | solution.py:332
  42.4 9.6 %all-to-all-done = bf16[64,2,3072]{2,1,0:T(2,128)(2,1)} async-done(((bf16[64,2,3072]{2,1,0:T(2,128)(2,1)}), bf16[64,2,3072]{2,1,0:T(2,128)(2,1)}, u32[]{:S(2)}, u32[]{:S(2)}) %all-to-all-start) | async-done | bytes 786464 | tf_op jit(solution)/shard_map/all_to_all | solution.py:368
  52.1 0.7 dynamic-slice_bitcast_fusion
  52.8 0.4 broadcast_in_dim.8
  53.2 4.2 %pad_maximum_fusion = bf16[64,2,7168]{2,1,0:T(2,128)(2,1)} fusion(bf16[64,2,3072]{2,1,0:T(2,128)(2,1)S(1)} %broadcast_in_dim.8, bf16[64,2,4096]{2,1,0:T(2,128)(2,1)} %reshape.37), kind=kLoop, calls=%fused_computation | loop fusion | flops 3670016 | bytes 3670016 | tf_op jit(solution)/shard_map/concatenate | solution.py:370
  57.4 7.4 %all-to-all-start.1 = ((bf16[64,2,7168]{2,1,0:T(2,128)(2,1)}), bf16[64,2,7168]{2,1,0:T(2,128)(2,1)}, u32[]{:S(2)}, u32[]{:S(2)}) async-start(bf16[64,2,7168]{2,1,0:T(2,128)(2,1)} %pad_maximum_fusion), calls=%async_computation.1 | async-start | bytes 3670016 | tf_op jit(solution)/shard_map/all_to_all | solution.py:373
  64.8 0.0 collective-permute-done.3.refs_1_
  64.8 1.0 collective-permute-done.2.refs_0_
  65.9 0.6 tick.3
  66.4 1.9 %collective-permute-start.4 = (bf16[224,2048]{1,0:T(8,128)(2,1)}, bf16[224,2048]{1,0:T(8,128)(2,1)S(1)}, u32[]{:S(2)}, u32[]{:S(2)}) collective-permute-start(bf16[224,2048]{1,0:T(8,128)(2,1)} %get-tuple-element.18.refs_2_.refs_7_), channel_id=1, source_target_pairs={{0,64},{64,128},{128,192},{192,256},{256,320},{320,384},{384,448},... | collective-permute-start | bytes 2752520 | tf_op jit(solution)/shard_map/ppermute | solution.py:332
  68.4 5.1 %collective-permute-start.5 = (bf16[224,2048]{1,0:T(8,128)(2,1)S(1)}, bf16[224,2048]{1,0:T(8,128)(2,1)S(1)}, u32[]{:S(2)}, u32[]{:S(2)}) collective-permute-start(bf16[224,2048]{1,0:T(8,128)(2,1)S(1)} %get-tuple-element.19.refs_5_.refs_2_), channel_id=1, source_target_pairs={{0,448},{64,0},{128,64},{192,128},{256,192},{320,256},{384,320},{4... | collective-permute-start | bytes 2752520 | tf_op jit(solution)/shard_map/ppermute | solution.py:332
  73.5 17.9 %collective-permute-done.4.refs_3_.refs_6_ = bf16[224,2048]{1,0:T(8,128)(2,1)S(1)} collective-permute-done((bf16[224,2048]{1,0:T(8,128)(2,1)}, bf16[224,2048]{1,0:T(8,128)(2,1)S(1)}, u32[]{:S(2)}, u32[]{:S(2)}) %collective-permute-start.4) | collective-permute-done | bytes 917536 | tf_op jit(solution)/shard_map/ppermute | solution.py:332
  91.5 1.9 %collective-permute-start.6 = (bf16[112,2048]{1,0:T(8,128)(2,1)S(1)}, bf16[112,2048]{1,0:T(8,128)(2,1)S(1)}, u32[]{:S(2)}, u32[]{:S(2)}) collective-permute-start(bf16[112,2048]{1,0:T(8,128)(2,1)S(1)} %slice.78), channel_id=1, source_target_pairs={{0,64},{64,128},{128,192},{192,256},{256,320},{320,384},{384,448},... | collective-permute-start | bytes 1376264 | tf_op jit(solution)/shard_map/ppermute | solution.py:332
  93.4 0.0 collective-permute-done.5.refs_6_.refs_3_
  93.4 0.9 slice.79
  94.3 0.3 copy-done.13
  94.6 5.3 %collective-permute-start.7 = (bf16[112,2048]{1,0:T(8,128)(2,1)}, bf16[112,2048]{1,0:T(8,128)(2,1)S(1)}, u32[]{:S(2)}, u32[]{:S(2)}) collective-permute-start(bf16[112,2048]{1,0:T(8,128)(2,1)} %slice.79), channel_id=1, source_target_pairs={{0,448},{64,0},{128,64},{192,128},{256,192},{320,256},{384,320},{4... | collective-permute-start | bytes 1376264 | tf_op jit(solution)/shard_map/ppermute | solution.py:332
  99.9 7.9 %all-to-all-done.1 = bf16[64,2,7168]{2,1,0:T(2,128)(2,1)} async-done(((bf16[64,2,7168]{2,1,0:T(2,128)(2,1)}), bf16[64,2,7168]{2,1,0:T(2,128)(2,1)}, u32[]{:S(2)}, u32[]{:S(2)}) %all-to-all-start.1) | async-done | bytes 1835040 | tf_op jit(solution)/shard_map/all_to_all | solution.py:373
  107.9 3.1 %slice.77 = bf16[64,2,4096]{2,1,0:T(2,128)(2,1)} slice(bf16[64,2,7168]{2,1,0:T(2,128)(2,1)} %all-to-all-done.1), slice={[0:64], [0:2], [0:4096]} | slice | bytes 2097152 | tf_op jit(solution)/shard_map/slice | solution.py:375
  111.0 0.0 copy-done.3
  111.0 1.5 reshape.39.rows_ref
  112.5 2.6 %slice.80 = bf16[64,2,3072]{2,1,0:T(2,128)(2,1)} slice(bf16[64,2,7168]{2,1,0:T(2,128)(2,1)} %all-to-all-done.1), slice={[0:64], [0:2], [4096:7168]} | slice | bytes 1572864 | tf_op jit(solution)/shard_map/slice | solution.py:374
  115.0 2.5 %reshape.40.weight_ref = bf16[192,2048]{1,0:T(8,128)(2,1)S(1)} reshape(bf16[64,2,3072]{2,1,0:T(2,128)(2,1)} %slice.80) | data formatting | bytes 1572864 | tf_op jit(solution)/shard_map/reshape | solution.py:374
  117.5 5.3 %gathered.1.acc_ref = f32[128,4096]{1,0:T(8,128)S(1)} custom-call(bf16[128,4096]{1,0:T(8,128)(2,1)S(1)} %reshape.39.rows_ref, bf16[224,2048]{1,0:T(8,128)(2,1)} %copy-done, bf16[224,2048]{1,0:T(8,128)(2,1)} %copy-done.2, bf16[224,2048]{1,0:T(8,128)(2,1)} %get-tuple-element.18.refs_2_.refs_7_, bf16[224,2048]{1,0:T(8,128)(2,1)} %copy-done.12, ...), custom_call_target="tpu_custom_call" | custom-call | flops 1409286144 | bytes 5505024 | tf_op jit(solution)/shard_map/gathered/pallas_call | solution.py:135
  122.8 0.0 collective-permute-done.6.up_ref.refs_4_
  122.9 0.0 collective-permute-done.7.down_ref.refs_5_
  122.9 0.8 copy-done.5
  123.7 1.0 copy-done.6
  124.7 0.8 last.1
  125.5 1.5 reshape.41
  127.0 8.6 %all-to-all-start.2 = ((bf16[64,2,4096]{2,1,0:T(2,128)(2,1)}), bf16[64,2,4096]{2,1,0:T(2,128)(2,1)}, u32[]{:S(2)}, u32[]{:S(2)}) async-start(bf16[64,2,4096]{2,1,0:T(2,128)(2,1)} %reshape.41), calls=%async_computation.2 | async-start | bytes 2097152 | tf_op jit(solution)/shard_map/all_to_all | solution.py:380
  135.6 2.2 %hot.1 = bf16[8,9,4096]{2,1,0:T(8,128)(2,1)S(1)} custom-call(s32[1]{0:T(128)} %bitcast.6.where_ref, bf16[192,2048]{1,0:T(8,128)(2,1)S(1)} %reshape.40.weight_ref, bf16[224,2048]{1,0:T(8,128)(2,1)} %copy-done, bf16[224,2048]{1,0:T(8,128)(2,1)} %copy-done.1, bf16[224,2048]{1,0:T(8,128)(2,1)} %copy-done.3, bf16[224,2048]{1,0:T(8,128)(2,1)} %copy-done.13, ...), custom_call_target="tpu_custom_call" | custom-call | tf_op jit(solution)/shard_map/hot/pallas_call | solution.py:214
  137.9 14.7 %all-gather = bf16[8,9,4096]{2,1,0:T(8,128)(2,1)S(1)} all-gather(bf16[4,9,4096]{2,1,0:T(8,128)(2,1)S(1)} %slice.82), channel_id=2, replica_groups={{0,64},{128,192},{256,320},{384,448},{1,65},{129,193},{257,321},{385,44..., dimensions={0}, use_global_device_ids=true | all-gather | bytes 884736 | tf_op jit(solution)/shard_map/all_gather | solution.py:338
  152.5 0.1 fusion
  152.6 0.1 add_convert_fusion
  152.7 14.8 %all-gather.1 = bf16[4,9,4096]{2,1,0:T(8,128)(2,1)S(1)} all-gather(bf16[2,9,4096]{2,1,0:T(8,128)(2,1)S(1)} %add_convert_fusion), channel_id=3, replica_groups={{0,128},{64,192},{256,384},{320,448},{1,129},{65,193},{257,385},{321,44..., dimensions={0}, use_global_device_ids=true | all-gather | bytes 442368 | tf_op jit(solution)/shard_map/all_gather | solution.py:338
  167.5 0.1 convert_add_fusion
  167.6 0.0 copy-start.8
  167.6 0.0 copy-start.10
  167.6 0.0 copy-start.11
  167.7 12.3 %all_gather.20 = bf16[2,9,4096]{2,1,0:T(8,128)(2,1)S(1)} all-gather(bf16[1,9,4096]{2,1,0:T(8,128)(2,1)S(1)} %slice.110), channel_id=1, replica_groups={{0,256},{64,320},{128,384},{192,448},{1,257},{65,321},{129,385},{193,44..., dimensions={0}, use_global_device_ids=true | all-gather | bytes 221184 | tf_op jit(solution)/shard_map/all_gather | solution.py:338
  180.0 0.0 all-to-all-done.2
  180.0 1.5 reshape.42.cold_ref
  181.5 1.0 cold_combine.1
  182.5 1.2 final_combine.1
  (19 shorter events, 0.1 us)
Async XLA Ops:
  0.6 0.7 copy-start.9
  2.7 1.0 copy-start.7
  2.7 13.3 %copy-start = (bf16[224,2048]{1,0:T(8,128)(2,1)}, bf16[224,2048]{1,0:T(8,128)(2,1)S(1)}, u32[]{:S(2)}) copy-start(bf16[224,2048]{1,0:T(8,128)(2,1)S(1)} %get-tuple-element.17.refs_0_) | copy-start | bytes 2752516
  3.6 29.1 %collective-permute-start.1 = (bf16[224,2048]{1,0:T(8,128)(2,1)S(1)}, bf16[224,2048]{1,0:T(8,128)(2,1)S(1)}, u32[]{:S(2)}, u32[]{:S(2)}) collective-permute-start(bf16[224,2048]{1,0:T(8,128)(2,1)S(1)} %get-tuple-element.17.refs_0_), channel_id=1, source_target_pairs={{0,448},{64,0},{128,64},{192,128},{256,192},{320,256},{384,320},{4... | collective-permute-start | bytes 2752520 | tf_op jit(solution)/shard_map/ppermute | solution.py:332
  9.0 24.9 %collective-permute-start = (bf16[224,2048]{1,0:T(8,128)(2,1)S(1)}, bf16[224,2048]{1,0:T(8,128)(2,1)S(1)}, u32[]{:S(2)}, u32[]{:S(2)}) collective-permute-start(bf16[224,2048]{1,0:T(8,128)(2,1)S(1)} %get-tuple-element.17.refs_0_), channel_id=1, source_target_pairs={{0,64},{64,128},{128,192},{192,256},{256,320},{320,384},{384,448},... | collective-permute-start | bytes 2752520 | tf_op jit(solution)/shard_map/ppermute | solution.py:332
  16.0 36.0 %all-to-all-start = ((bf16[64,2,3072]{2,1,0:T(2,128)(2,1)}), bf16[64,2,3072]{2,1,0:T(2,128)(2,1)}, u32[]{:S(2)}, u32[]{:S(2)}) async-start(bf16[64,2,3072]{2,1,0:T(2,128)(2,1)} %reshape.38), calls=%async_computation | async-start | bytes 1572864 | tf_op jit(solution)/shard_map/all_to_all | solution.py:368
  32.8 3.6 %copy-start.1 = (bf16[224,2048]{1,0:T(8,128)(2,1)}, bf16[224,2048]{1,0:T(8,128)(2,1)S(1)}, u32[]{:S(2)}) copy-start(bf16[224,2048]{1,0:T(8,128)(2,1)S(1)} %collective-permute-done.1.refs_1_.refs_4_) | copy-start | bytes 2752516
  33.9 6.6 %copy-start.2 = (bf16[224,2048]{1,0:T(8,128)(2,1)}, bf16[224,2048]{1,0:T(8,128)(2,1)S(1)}, u32[]{:S(2)}) copy-start(bf16[224,2048]{1,0:T(8,128)(2,1)S(1)} %collective-permute-done.refs_0_.refs_1_.refs_8_) | copy-start | bytes 2752516
  36.4 28.4 %collective-permute-start.3 = (bf16[224,2048]{1,0:T(8,128)(2,1)S(1)}, bf16[224,2048]{1,0:T(8,128)(2,1)S(1)}, u32[]{:S(2)}, u32[]{:S(2)}) collective-permute-start(bf16[224,2048]{1,0:T(8,128)(2,1)S(1)} %collective-permute-done.1.refs_1_.refs_4_), channel_id=1, source_target_pairs={{0,448},{64,0},{128,64},{192,128},{256,192},{320,256},{384,320},{4... | collective-permute-start | bytes 2752520 | tf_op jit(solution)/shard_map/ppermute | solution.py:332
  40.5 25.3 %collective-permute-start.2 = (bf16[224,2048]{1,0:T(8,128)(2,1)S(1)}, bf16[224,2048]{1,0:T(8,128)(2,1)}, u32[]{:S(2)}, u32[]{:S(2)}) collective-permute-start(bf16[224,2048]{1,0:T(8,128)(2,1)S(1)} %collective-permute-done.refs_0_.refs_1_.refs_8_), channel_id=1, source_target_pairs={{0,64},{64,128},{128,192},{192,256},{256,320},{320,384},{384,448},... | collective-permute-start | bytes 2752520 | tf_op jit(solution)/shard_map/ppermute | solution.py:332
  57.4 50.5 %all-to-all-start.1 = ((bf16[64,2,7168]{2,1,0:T(2,128)(2,1)}), bf16[64,2,7168]{2,1,0:T(2,128)(2,1)}, u32[]{:S(2)}, u32[]{:S(2)}) async-start(bf16[64,2,7168]{2,1,0:T(2,128)(2,1)} %pad_maximum_fusion), calls=%async_computation.1 | async-start | bytes 3670016 | tf_op jit(solution)/shard_map/all_to_all | solution.py:373
  66.4 44.5 %copy-start.3 = (bf16[224,2048]{1,0:T(8,128)(2,1)}, bf16[224,2048]{1,0:T(8,128)(2,1)S(1)}, u32[]{:S(2)}) copy-start(bf16[224,2048]{1,0:T(8,128)(2,1)S(1)} %get-tuple-element.19.refs_5_.refs_2_) | copy-start | bytes 2752516
  66.4 25.0 %collective-permute-start.4 = (bf16[224,2048]{1,0:T(8,128)(2,1)}, bf16[224,2048]{1,0:T(8,128)(2,1)S(1)}, u32[]{:S(2)}, u32[]{:S(2)}) collective-permute-start(bf16[224,2048]{1,0:T(8,128)(2,1)} %get-tuple-element.18.refs_2_.refs_7_), channel_id=1, source_target_pairs={{0,64},{64,128},{128,192},{192,256},{256,320},{320,384},{384,448},... | collective-permute-start | bytes 2752520 | tf_op jit(solution)/shard_map/ppermute | solution.py:332
  68.4 25.0 %collective-permute-start.5 = (bf16[224,2048]{1,0:T(8,128)(2,1)S(1)}, bf16[224,2048]{1,0:T(8,128)(2,1)S(1)}, u32[]{:S(2)}, u32[]{:S(2)}) collective-permute-start(bf16[224,2048]{1,0:T(8,128)(2,1)S(1)} %get-tuple-element.19.refs_5_.refs_2_), channel_id=1, source_target_pairs={{0,448},{64,0},{128,64},{192,128},{256,192},{320,256},{384,320},{4... | collective-permute-start | bytes 2752520 | tf_op jit(solution)/shard_map/ppermute | solution.py:332
  91.4 2.0 %copy-start.12 = (bf16[224,2048]{1,0:T(8,128)(2,1)}, bf16[224,2048]{1,0:T(8,128)(2,1)S(1)}, u32[]{:S(2)}) copy-start(bf16[224,2048]{1,0:T(8,128)(2,1)S(1)} %collective-permute-done.4.refs_3_.refs_6_) | copy-start | bytes 2752516
  91.5 31.4 %collective-permute-start.6 = (bf16[112,2048]{1,0:T(8,128)(2,1)S(1)}, bf16[112,2048]{1,0:T(8,128)(2,1)S(1)}, u32[]{:S(2)}, u32[]{:S(2)}) collective-permute-start(bf16[112,2048]{1,0:T(8,128)(2,1)S(1)} %slice.78), channel_id=1, source_target_pairs={{0,64},{64,128},{128,192},{192,256},{256,320},{320,384},{384,448},... | collective-permute-start | bytes 1376264 | tf_op jit(solution)/shard_map/ppermute | solution.py:332
  93.4 1.2 copy-start.13
  94.6 28.3 %collective-permute-start.7 = (bf16[112,2048]{1,0:T(8,128)(2,1)}, bf16[112,2048]{1,0:T(8,128)(2,1)S(1)}, u32[]{:S(2)}, u32[]{:S(2)}) collective-permute-start(bf16[112,2048]{1,0:T(8,128)(2,1)} %slice.79), channel_id=1, source_target_pairs={{0,448},{64,0},{128,64},{192,128},{256,192},{320,256},{384,320},{4... | collective-permute-start | bytes 1376264 | tf_op jit(solution)/shard_map/ppermute | solution.py:332
  122.8 2.7 %copy-start.4 = (bf16[112,2048]{1,0:T(8,128)(2,1)}, bf16[112,2048]{1,0:T(8,128)(2,1)S(1)}, u32[]{:S(2)}) copy-start(bf16[112,2048]{1,0:T(8,128)(2,1)S(1)} %collective-permute-done.6.up_ref.refs_4_) | copy-start | bytes 1376260
  122.9 0.8 copy-start.5
  123.7 1.0 copy-start.6
  127.0 53.0 %all-to-all-start.2 = ((bf16[64,2,4096]{2,1,0:T(2,128)(2,1)}), bf16[64,2,4096]{2,1,0:T(2,128)(2,1)}, u32[]{:S(2)}, u32[]{:S(2)}) async-start(bf16[64,2,4096]{2,1,0:T(2,128)(2,1)} %reshape.41), calls=%async_computation.2 | async-start | bytes 2097152 | tf_op jit(solution)/shard_map/all_to_all | solution.py:380
  167.6 13.9 %copy-start.8 = (bf16[16,2048]{1,0:T(8,128)(2,1)S(1)}, bf16[16,2048]{1,0:T(8,128)(2,1)}, u32[]{:S(2)}) copy-start(bf16[16,2048]{1,0:T(8,128)(2,1)} %cot_ref.5) | copy-start | bytes 196612
  167.6 13.9 %copy-start.10 = (s32[16,8]{0,1:T(8,128)S(1)}, s32[16,8]{0,1:T(8,128)}, u32[]{:S(2)}) copy-start(s32[16,8]{0,1:T(8,128)} %param.9) | copy-start | bytes 1540
  167.6 13.9 %copy-start.11 = (f32[16,8]{0,1:T(8,128)S(1)}, f32[16,8]{0,1:T(8,128)}, u32[]{:S(2)}) copy-start(f32[16,8]{0,1:T(8,128)} %param.8) | copy-start | bytes 1540

commit v4 on v3

--- a/solution.py
+++ b/solution.py
@@ -67,7 +67,7 @@
         copy.start()
     cold, hot, _, _, hottest = slot_maps(ids_ref[...], slots, capacity)
     cold, hot = cold.astype(BF16), hot.astype(BF16)
-    hottest_ref[...] = jnp.broadcast_to(hottest, hottest_ref.shape).astype(I32)
+    hottest_ref[0, 0] = jnp.max(hottest).astype(I32)
     for copy in loads:
         copy.wait()
     own_ref[units:half, :] = matmul(hot, tok[...]).astype(BF16)
@@ -88,10 +88,10 @@
         out_shape=(
             jax.ShapeDtypeStruct((slots, 2 * width), BF16),
             jax.ShapeDtypeStruct((2 * (units + HOT_PAD), width), BF16),
-            jax.ShapeDtypeStruct((8, 128), I32),
+            jax.ShapeDtypeStruct((1, 1), I32),
         ),
         in_specs=[inside] + [anywhere] * 4,
-        out_specs=(inside, inside, inside),
+        out_specs=(inside, inside, pl.BlockSpec(memory_space=pltpu.SMEM)),
         scratch_shapes=[
             pltpu.VMEM((tok_rows, width), BF16),
             pltpu.VMEM((tok_rows, width), BF16),
@@ -102,6 +102,66 @@
     )(ids, *map(outside, (tokens, cotangent, up, down)))
 
 
+def deal_kernel(tall, up_ref, down_ref, out_ref, up, down, sems):
+    columns = up.shape[1] // 128
+    copies = []
+    for i, (source, here) in enumerate(((up_ref, up), (down_ref, down))):
+        copy = pltpu.make_async_copy(source, here, sems.at[i])
+        copy.start()
+        copies.append(copy)
+    groups = up.shape[0] // tall
+    for i, here in enumerate((up, down)):
+        copies[i].wait()
+        for g in range(groups):
+            for j in range(columns):
+                out_ref[(i * groups + g) * columns + j] = here[g * tall : (g + 1) * tall, j * 128 : (j + 1) * 128]
+
+
+def deal(up, down, experts):
+    units, width = up.shape
+    tall = 2 * units * width // (experts * 128)
+    return pl.pallas_call(
+        functools.partial(deal_kernel, tall),
+        out_shape=jax.ShapeDtypeStruct((experts, tall, 128), BF16),
+        in_specs=[pl.BlockSpec(memory_space=pl.ANY)] * 2,
+        out_specs=pl.BlockSpec(memory_space=pltpu.VMEM),
+        scratch_shapes=[
+            pltpu.VMEM((units, width), BF16),
+            pltpu.VMEM((units, width), BF16),
+            pltpu.SemaphoreType.DMA((2,)),
+        ],
+        compiler_params=pltpu.CompilerParams(vmem_limit_bytes=VMEM_LIMIT),
+        name="deal",
+    )(outside(up), outside(down))
+
+
+def assemble_kernel(hottest_ref, rows_ref, dealt_ref, out_ref, mine, sem):
+    copy = pltpu.make_async_copy(dealt_ref.at[hottest_ref[0, 0]], mine, sem)
+    copy.start()
+    lines = rows_ref.shape[1]
+    out_ref[:, :lines, :] = rows_ref[...]
+    copy.wait()
+    out_ref[:, lines:, :] = jnp.broadcast_to(mine[...][None], (out_ref.shape[0],) + mine.shape)
+
+
+def assemble(hottest, rows, dealt):
+    experts, lines, lanes = rows.shape
+    tall = dealt.shape[1]
+    return pl.pallas_call(
+        assemble_kernel,
+        out_shape=jax.ShapeDtypeStruct((experts, lines + tall, lanes), BF16),
+        in_specs=[
+            pl.BlockSpec(memory_space=pltpu.SMEM),
+            pl.BlockSpec(memory_space=pltpu.VMEM),
+            pl.BlockSpec(memory_space=pl.ANY),
+        ],
+        out_specs=pl.BlockSpec(memory_space=pltpu.VMEM),
+        scratch_shapes=[pltpu.VMEM((tall, lanes), BF16), pltpu.SemaphoreType.DMA],
+        compiler_params=pltpu.CompilerParams(vmem_limit_bytes=VMEM_LIMIT),
+        name="assemble",
+    )(hottest, rows, dealt)
+
+
 def activations(pre_act, hidden_grad):
     gating = jax.nn.sigmoid(pre_act)
     hidden = (pre_act * gating).astype(BF16)
@@ -109,10 +169,12 @@
     return hidden, act_grad
 
 
-def gathered_kernel(units, rows_ref, *refs):
-    pieces, acc_ref, up, down, sems = refs[:-4], refs[-4], refs[-3], refs[-2], refs[-1]
+def gathered_kernel(units, lines, arrived_ref, *refs):
+    pieces, (acc_ref, rows_ref, up, down, wide, sems) = refs[:-6], refs[-6:]
     width = up.shape[1]
     half = pieces[0].shape[0] // 2
+    experts = arrived_ref.shape[0]
+    capacity = rows_ref.shape[0] // experts
     copies = []
     for i, piece in enumerate(pieces):
         for j, whole in enumerate((up, down)):
@@ -121,6 +183,13 @@
             )
             copy.start()
             copies.append(copy)
+    for e in range(experts):
+        wide[e * lines : (e + 1) * lines, :] = arrived_ref[e, :lines, :].astype(F32)
+    blocks = lines // capacity
+    for r in range(capacity):
+        for b in range(blocks):
+            line = wide[pl.ds(r * blocks + b, experts, stride=lines), :]
+            rows_ref[r * experts : (r + 1) * experts, b * 128 : (b + 1) * 128] = line.astype(BF16)
     for copy in copies:
         copy.wait()
     tok, cot = rows_ref[:, :width], rows_ref[:, width:]
@@ -129,27 +198,33 @@
     acc_ref[:, width:] = matmul(act_grad, up[...])
 
 
-def gathered(rows, pieces, units):
-    width = rows.shape[1] // 2
+def gathered(arrived, pieces, units, slots):
+    experts = arrived.shape[0]
+    width = pieces[0].shape[1]
+    lines = slots * 2 * width // (experts * 128)
     count = len(pieces)
     return pl.pallas_call(
-        functools.partial(gathered_kernel, units),
-        out_shape=jax.ShapeDtypeStruct(rows.shape, F32),
+        functools.partial(gathered_kernel, units, lines),
+        out_shape=(
+            jax.ShapeDtypeStruct((slots, 2 * width), F32),
+            jax.ShapeDtypeStruct((slots, 2 * width), BF16),
+        ),
         in_specs=[pl.BlockSpec(memory_space=pltpu.VMEM)] + [pl.BlockSpec(memory_space=pl.ANY)] * count,
-        out_specs=pl.BlockSpec(memory_space=pltpu.VMEM),
+        out_specs=(pl.BlockSpec(memory_space=pltpu.VMEM), pl.BlockSpec(memory_space=pltpu.VMEM)),
         scratch_shapes=[
             pltpu.VMEM((count * units, width), BF16),
             pltpu.VMEM((count * units, width), BF16),
+            pltpu.VMEM((experts * lines, 128), F32),
             pltpu.SemaphoreType.DMA((count, 2)),
         ],
-        compiler_params=pltpu.CompilerParams(vmem_limit_bytes=VMEM_LIMIT),
+        compiler_params=pltpu.CompilerParams(vmem_limit_bytes=VMEM_LIMIT + (4 << 20)),
         cost_estimate=pl.CostEstimate(
-            flops=8 * rows.shape[0] * count * units * width,
+            flops=8 * slots * count * units * width,
             bytes_accessed=4 * count * units * width,
             transcendentals=0,
         ),
         name="gathered",
-    )(rows, *map(outside, pieces))
+    )(arrived, *map(outside, pieces))
 
 
 def last_kernel(units, rows_ref, acc_ref, up_ref, down_ref, out_ref):
@@ -170,8 +245,8 @@
     )(rows, acc, up_half, down_half)
 
 
-def hot_kernel(units, hot_rows, order, where_ref, weight_ref, *refs):
-    blocks, out_ref, tok, cot, sems = refs[:-4], refs[-4], refs[-3], refs[-2], refs[-1]
+def hot_kernel(units, lines, hot_rows, where_ref, arrived_ref, *refs):
+    blocks, (send_ref, keep_ref, tok, cot, weights, sems) = refs[:-6], refs[-6:]
     ring = len(blocks)
     width = tok.shape[1]
     here = where_ref[0]
@@ -186,48 +261,60 @@
             )
             copy.start()
             copies.append(copy)
+    columns = width // 128
+    tall = arrived_ref.shape[1] - lines
+    for k in range(arrived_ref.shape[0]):
+        i, j = k // columns, k % columns
+        weights[i * tall : (i + 1) * tall, j * 128 : (j + 1) * 128] = arrived_ref[k, lines:, :]
     for copy in copies:
         copy.wait()
-    up, down = weight_ref[:units, :], weight_ref[units:, :]
+    up, down = weights[:units, :], weights[units:, :]
     hidden, act_grad = activations(matmul_nt(tok[...], up), matmul_nt(cot[...], down))
-    mixed = matmul(hidden, down).astype(BF16)
-    grads = matmul(act_grad, up).astype(BF16)
-    for i, place in enumerate(order):
-        out_ref[i, :, :width] = mixed[place * HOT_PAD : place * HOT_PAD + hot_rows]
-        out_ref[i, :, width:] = grads[place * HOT_PAD : place * HOT_PAD + hot_rows]
-
-
-def hot_partials(here, weights, blocks, units, hot_rows, order):
-    width = weights.shape[1]
+    packed = send_ref.shape[0]
+    row = lax.broadcasted_iota(I32, (packed, ring * HOT_PAD), 0)
+    column = lax.broadcasted_iota(I32, (packed, ring * HOT_PAD), 1)
+    group = row // hot_rows
+    place = (group % 2) * 4 + (group // 2) * 2
+    within = place * HOT_PAD + row % hot_rows
+    for odd, out_ref in ((1, send_ref), (0, keep_ref)):
+        chosen = (column == within + odd * HOT_PAD).astype(F32).astype(BF16)
+        picked_hidden = matmul(chosen, hidden).astype(BF16)
+        picked_grad = matmul(chosen, act_grad).astype(BF16)
+        out_ref[:, :width] = matmul(picked_hidden, down).astype(BF16)
+        out_ref[:, width:] = matmul(picked_grad, up).astype(BF16)
+
+
+def hot_partials(here, arrived, blocks, units, lines, hot_rows, after):
     ring = len(blocks)
     flat, spans = [], []
     for block in blocks:
         spans.append(len(block) if isinstance(block, tuple) else 0)
         flat += list(block) if isinstance(block, tuple) else [block]
-
-    def kernel(where_ref, weight_ref, *refs):
+    width = flat[0].shape[1]
+
+    def kernel(where_ref, arrived_ref, after_ref, *refs):
         refs, grouped = list(refs), []
         for span in spans:
             grouped.append(tuple(refs.pop(0) for _ in range(span)) if span else refs.pop(0))
-        hot_kernel(units, hot_rows, order, where_ref, weight_ref, *grouped, *refs)
-
+        hot_kernel(units, lines, hot_rows, where_ref, arrived_ref, *grouped, *refs)
+
+    inside = pl.BlockSpec(memory_space=pltpu.VMEM)
+    packed = jax.ShapeDtypeStruct((ring // 2 * hot_rows, 2 * width), BF16)
     return pl.pallas_call(
         kernel,
-        out_shape=jax.ShapeDtypeStruct((ring, hot_rows, 2 * width), BF16),
-        in_specs=[
-            pl.BlockSpec(memory_space=pltpu.SMEM),
-            pl.BlockSpec(memory_space=pltpu.VMEM),
-        ]
-        + [pl.BlockSpec(memory_space=pl.ANY)] * len(flat),
-        out_specs=pl.BlockSpec(memory_space=pltpu.VMEM),
+        out_shape=(packed, packed),
+        in_specs=[pl.BlockSpec(memory_space=pltpu.SMEM), inside]
+        + [pl.BlockSpec(memory_space=pl.ANY)] * (1 + len(flat)),
+        out_specs=(inside, inside),
         scratch_shapes=[
             pltpu.VMEM((ring * HOT_PAD, width), BF16),
             pltpu.VMEM((ring * HOT_PAD, width), BF16),
+            pltpu.VMEM((2 * units, width), BF16),
             pltpu.SemaphoreType.DMA((ring, 2)),
         ],
         compiler_params=pltpu.CompilerParams(vmem_limit_bytes=VMEM_LIMIT),
         name="hot",
-    )(here, weights, *map(outside, flat))
+    )(here, arrived, after, *map(outside, flat))
 
 
 def thirds(x):
@@ -308,17 +395,17 @@
 
 
 def tick_kernel(token_ref, *refs):
-    refs[-1][...] = token_ref[...]
+    refs[-1][0, 0] = token_ref[0, 0]
 
 
 def tick(token, *after, through=False):
     count = len(after) if through else 0
-    anywhere, inside = pl.BlockSpec(memory_space=pl.ANY), pl.BlockSpec(memory_space=pltpu.VMEM)
+    anywhere, scalar = pl.BlockSpec(memory_space=pl.ANY), pl.BlockSpec(memory_space=pltpu.SMEM)
     out = pl.pallas_call(
         tick_kernel,
         out_shape=tuple(jax.ShapeDtypeStruct(x.shape, x.dtype) for x in after[:count] + (token,)),
-        in_specs=[inside] + [anywhere] * len(after),
-        out_specs=tuple([anywhere] * count + [inside]),
+        in_specs=[scalar] + [anywhere] * len(after),
+        out_specs=tuple([anywhere] * count + [scalar]),
         input_output_aliases={i + 1: i for i in range(count)},
         compiler_params=pltpu.CompilerParams(vmem_limit_bytes=1 << 20),
         cost_estimate=pl.CostEstimate(flops=1 << 35, bytes_accessed=1 << 25, transcendentals=0),
@@ -363,40 +450,26 @@
         left.append(l)
     far_up, far_down = shift(right[-1][:half], 1), shift(left[-1][half:], -1)
 
-    piece = 2 * units * width // (experts * capacity)
-    pieces = jnp.concatenate([up, down], 0).reshape(experts, capacity, piece)
-    dealt = lax.all_to_all(pieces, "expert", 0, 0, tiled=True)
-    mine = lax.dynamic_index_in_dim(dealt, token[0, 0], 0)
-    outgoing = jnp.concatenate(
-        [outgoing.reshape(experts, capacity, 2 * width), jnp.broadcast_to(mine, pieces.shape)], 2
-    )
+    dealt = lax.all_to_all(deal(up, down, experts), "expert", 0, 0, tiled=True)
+    lines = capacity * 2 * width // 128
+    outgoing = assemble(token, outgoing.reshape(experts, lines, 128), dealt)
     arrived = lax.all_to_all(outgoing, "expert", 0, 0, tiled=True)
-    hot_weights = arrived[:, :, 2 * width :].reshape(2 * units, width)
-    arrived = arrived[:, :, : 2 * width].reshape(slots, 2 * width)
-
-    acc = gathered(arrived, [own] + right[1:] + left[1:], units)
-    results = last(arrived, acc, far_up, far_down, units)
-    results, hot_weights = lax.optimization_barrier((results, hot_weights))
-    came_back = lax.all_to_all(
-        results.reshape(experts, capacity, 2 * width), "expert", 0, 0, tiled=True
-    ).reshape(slots, 2 * width)
+
+    acc, rows = gathered(arrived, [own] + right[1:] + left[1:], units, slots)
+    results = last(rows, acc, far_up, far_down, units)
+    results = results.reshape(capacity, experts, 2 * width).transpose(1, 0, 2)
+    came_back = lax.all_to_all(results, "expert", 0, 0, tiled=True).reshape(slots, 2 * width)
 
     blocks = left + [(far_up, far_down)] + right[:0:-1]
     here = lax.axis_index("dp").astype(I32).reshape(1)
-    partials = hot_partials(here, hot_weights, blocks, units, hot_rows, (1, 3, 5, 7, 0, 4, 2, 6))
-
-    def part(first, count):
-        return partials[first : first + count].astype(F32)
-
-    got = swap(partials[0:4], 1).astype(F32)
-    onward = (part(6, 2) + got[1::2]).astype(BF16)
-    stay = part(4, 2) + got[0::2]
-    got = swap(onward, 2).astype(F32)
-    stay = stay + got
-    sent = swap(stay[1].astype(BF16), 4)
+    send, keep = hot_partials(here, arrived, blocks, units, lines, hot_rows, results)
+    both = keep.astype(F32) + swap(send, 1).astype(F32)
+    stay = both[: 2 * hot_rows] + swap(both[2 * hot_rows :].astype(BF16), 2).astype(F32)
+    sent = swap(stay[hot_rows:].astype(BF16), 4)
+    kept = stay[:hot_rows]
     sums, dots = cold_combine(ids, gates, cotangent, came_back, capacity)
     mixture, input_grad, gate_grad = final_combine(
-        ids, gates, cotangent, sums, dots, stay[0], sent, slots, capacity
+        ids, gates, cotangent, sums, dots, kept, sent, slots, capacity
     )
     return mixture, input_grad, gate_grad.T
 

time: 185 us -> 162 us (0.88)
  local copies, waits for them, and re-layouts: 24.6 us -> 9.13 us
  Pallas kernels: 12.4 us -> 19 us
  other arithmetic: 6.52 us -> 0.19 us
  blocking collectives: 41.8 us -> 35.7 us
  between operations: 2.97 us -> 1.04 us
    reshape x6 -> x3, local copies, waits for them, and re-layouts: 12.4 us -> 4.08 us  [the longest x1 2.08 us: shards(): results = results.reshape(capacity, experts, 2 * width).transpose(1, 0, 2)]
    slice x5 -> x1, local copies, waits for them, and re-layouts: 6.29 us -> 0.02 us  [shards(): kept = stay[:hot_rows]]
    concatenate x2 -> x0, other arithmetic: 6.26 us -> none  [the longest x1 4.16 us: shards(): jnp.concatenate([outgoing.reshape(experts, capacity, 2 * width), jnp.broa...]
    all_gather x3, blocking collectives: 41.8 us -> 35.7 us  [swap(): both = lax.all_gather(x, 'dp', axis=0, axis_index_groups=pairs, tiled=False)]
    pallas_call x2 -> x4, Pallas kernels: 7.53 us -> 10.7 us  [the longest x1 5.33 us: gathered(): pl.pallas_call(functools.partial(gathered_kernel, units, lines), out_shap...]
    unnamed x28 -> x24, local copies, waits for them, and re-layouts: 3.79 us -> 3.2 us
  transfers between devices with their start and end apart: 11 -> 11, of which waited for: 5 -> 4; matrix products, arithmetic and copies ran while one was open for 13% -> 2% of each run, Pallas kernels for 4% -> 8%
where the time goes in v4:
time: 162 us; the launch traced here: 161 us
  starting transfers between devices  58.1 us (36%)
  waiting for transfers between devices  37.8 us (23%)
  blocking collectives  35.7 us (22%)
  Pallas kernels  19 us (12%)
  local copies, waits for them, and re-layouts  9.13 us (6%)
    all_gather x3, blocking collectives, swap(): both = lax.all_gather(x, 'dp', axis=0, axis_index_groups=pairs, tiled=False)  35.7 us
    ppermute x8, starting transfers between devices, shift(): return lax.ppermute(x, 'dp', [(i, (i + by) % ring) for i in range(ring)])  28.4 us
    ppermute x8, waiting for transfers between devices, shift(): return lax.ppermute(x, 'dp', [(i, (i + by) % ring) for i in range(ring)])  19.5 us
    all_to_all x1, starting transfers between devices, shards(): dealt = lax.all_to_all(deal(up, down, experts), 'expert', 0, 0, tiled=True)  14 us
    all_to_all x1, waiting for transfers between devices, shards(): dealt = lax.all_to_all(deal(up, down, experts), 'expert', 0, 0, tiled=True)  11.3 us
    all_to_all x1, starting transfers between devices, shards(): lax.all_to_all(results, 'expert', 0, 0, tiled=True)  8.39 us
    all_to_all x1, starting transfers between devices, shards(): arrived = lax.all_to_all(outgoing, 'expert', 0, 0, tiled=True)  7.26 us
    all_to_all x1, waiting for transfers between devices, shards(): arrived = lax.all_to_all(outgoing, 'expert', 0, 0, tiled=True)  7.06 us
  transfers between devices with their start and end apart: 11, of which 4 were waited for; matrix products, arithmetic and copies ran while one was open for 2% of the time, Pallas kernels for 8%

profile of v4, /device:TPU:6, one launch (start us, length us, event | category | flops | bytes accessed | tf_op | source)
XLA Modules:
  0.0 161.0 jit_solution(17976493160472915434)
XLA Ops:
  0.6 0.0 copy-start.6
  0.6 0.7 copy-done.6
  1.3 1.9 %route.1 = (bf16[128,4096]{1,0:T(8,128)(2,1)S(1)}, bf16[224,2048]{1,0:T(8,128)(2,1)S(1)}, s32[1,1]{1,0:T(1,128)}) custom-call(s32[8,16]{1,0:T(8,128)S(1)} %bitcast.29, bf16[16,2048]{1,0:T(8,128)(2,1)} %tok_ref.1, bf16[16,2048]{1,0:T(8,128)(2,1)} %cot_ref.5, bf16[96,2048]{1,0:T(8,128)(2,1)} %bitcast.34, bf16[96,2048]{1,0:T(8,128)(2,1)} %bitcast.36), custom_call_target="tpu_custom_call" | custom-call | tf_op jit(solution)/shard_map/route/pallas_call | solution.py:86
  3.2 0.0 copy-start.4
  3.2 0.0 copy-start.1
  3.2 1.0 copy-done.4
  4.2 3.5 %collective-permute-start = (bf16[224,2048]{1,0:T(8,128)(2,1)S(1)}, bf16[224,2048]{1,0:T(8,128)(2,1)}, u32[]{:S(2)}, u32[]{:S(2)}) collective-permute-start(bf16[224,2048]{1,0:T(8,128)(2,1)S(1)} %get-tuple-element.18.refs_0_), channel_id=1, source_target_pairs={{0,64},{64,128},{128,192},{192,256},{256,320},{320,384},{384,448},... | collective-permute-start | bytes 2752520 | tf_op jit(solution)/shard_map/ppermute | solution.py:419
  7.7 3.8 %collective-permute-start.1 = (bf16[224,2048]{1,0:T(8,128)(2,1)S(1)}, bf16[224,2048]{1,0:T(8,128)(2,1)}, u32[]{:S(2)}, u32[]{:S(2)}) collective-permute-start(bf16[224,2048]{1,0:T(8,128)(2,1)S(1)} %get-tuple-element.18.refs_0_), channel_id=1, source_target_pairs={{0,448},{64,0},{128,64},{192,128},{256,192},{320,256},{384,320},{4... | collective-permute-start | bytes 2752520 | tf_op jit(solution)/shard_map/ppermute | solution.py:419
  11.5 2.1 %deal.1 = bf16[64,48,128]{2,1,0:T(8,128)(2,1)} custom-call(bf16[96,2048]{1,0:T(8,128)(2,1)} %bitcast.35, bf16[96,2048]{1,0:T(8,128)(2,1)} %bitcast.37), custom_call_target="tpu_custom_call" | custom-call | tf_op jit(solution)/shard_map/deal/pallas_call | solution.py:123
  13.6 14.0 %all-to-all-start = ((bf16[64,48,128]{2,1,0:T(8,128)(2,1)}), bf16[64,48,128]{2,1,0:T(8,128)(2,1)S(1)}, u32[]{:S(2)}, u32[]{:S(2)}) async-start(bf16[64,48,128]{2,1,0:T(8,128)(2,1)} %deal.1), calls=%async_computation | async-start | bytes 1572864 | tf_op jit(solution)/shard_map/all_to_all | solution.py:453
  27.6 1.6 reshape.28.rows_ref
  29.2 0.0 copy-done.1
  29.2 0.8 collective-permute-done.refs_0_.refs_1_.refs_8_
  30.0 1.9 %collective-permute-start.2 = (bf16[224,2048]{1,0:T(8,128)(2,1)}, bf16[224,2048]{1,0:T(8,128)(2,1)}, u32[]{:S(2)}, u32[]{:S(2)}) collective-permute-start(bf16[224,2048]{1,0:T(8,128)(2,1)} %collective-permute-done.refs_0_.refs_1_.refs_8_), channel_id=1, source_target_pairs={{0,64},{64,128},{128,192},{192,256},{256,320},{320,384},{384,448},... | collective-permute-start | bytes 2752520 | tf_op jit(solution)/shard_map/ppermute | solution.py:419
  31.9 0.0 collective-permute-done.1.refs_1_.refs_4_
  31.9 5.1 %collective-permute-start.3 = (bf16[224,2048]{1,0:T(8,128)(2,1)}, bf16[224,2048]{1,0:T(8,128)(2,1)S(1)}, u32[]{:S(2)}, u32[]{:S(2)}) collective-permute-start(bf16[224,2048]{1,0:T(8,128)(2,1)} %collective-permute-done.1.refs_1_.refs_4_), channel_id=1, source_target_pairs={{0,448},{64,0},{128,64},{192,128},{256,192},{320,256},{384,320},{4... | collective-permute-start | bytes 2752520 | tf_op jit(solution)/shard_map/ppermute | solution.py:419
  37.1 1.2 tick.2.hottest_ref
  38.2 11.3 %all-to-all-done.dealt_ref = bf16[64,48,128]{2,1,0:T(8,128)(2,1)S(1)} async-done(((bf16[64,48,128]{2,1,0:T(8,128)(2,1)}), bf16[64,48,128]{2,1,0:T(8,128)(2,1)S(1)}, u32[]{:S(2)}, u32[]{:S(2)}) %all-to-all-start) | async-done | bytes 786464 | tf_op jit(solution)/shard_map/all_to_all | solution.py:453
  49.5 0.8 assemble.1
  50.4 0.0 copy-start
  50.4 1.3 copy-done
  51.6 7.3 %all-to-all-start.1 = ((bf16[64,112,128]{2,1,0:T(8,128)(2,1)}), bf16[64,112,128]{2,1,0:T(8,128)(2,1)S(1)}, u32[]{:S(2)}, u32[]{:S(2)}) async-start(bf16[64,112,128]{2,1,0:T(8,128)(2,1)} %copy-done), calls=%async_computation.1 | async-start | bytes 3670016 | tf_op jit(solution)/shard_map/all_to_all | solution.py:456
  58.9 0.0 collective-permute-done.2.refs_0_
  58.9 0.0 collective-permute-done.3.refs_1_
  58.9 1.2 tick.3
  60.1 0.0 copy-start.2
  60.1 2.0 %collective-permute-start.4 = (bf16[224,2048]{1,0:T(8,128)(2,1)}, bf16[224,2048]{1,0:T(8,128)(2,1)S(1)}, u32[]{:S(2)}, u32[]{:S(2)}) collective-permute-start(bf16[224,2048]{1,0:T(8,128)(2,1)} %get-tuple-element.20.refs_2_.refs_7_), channel_id=1, source_target_pairs={{0,64},{64,128},{128,192},{192,256},{256,320},{320,384},{384,448},... | collective-permute-start | bytes 2752520 | tf_op jit(solution)/shard_map/ppermute | solution.py:419
  62.2 5.0 %collective-permute-start.5 = (bf16[224,2048]{1,0:T(8,128)(2,1)S(1)}, bf16[224,2048]{1,0:T(8,128)(2,1)S(1)}, u32[]{:S(2)}, u32[]{:S(2)}) collective-permute-start(bf16[224,2048]{1,0:T(8,128)(2,1)S(1)} %get-tuple-element.21.refs_5_.refs_2_), channel_id=1, source_target_pairs={{0,448},{64,0},{128,64},{192,128},{256,192},{320,256},{384,320},{4... | collective-permute-start | bytes 2752520 | tf_op jit(solution)/shard_map/ppermute | solution.py:419
  67.2 18.6 %collective-permute-done.4.refs_3_.refs_6_ = bf16[224,2048]{1,0:T(8,128)(2,1)S(1)} collective-permute-done((bf16[224,2048]{1,0:T(8,128)(2,1)}, bf16[224,2048]{1,0:T(8,128)(2,1)S(1)}, u32[]{:S(2)}, u32[]{:S(2)}) %collective-permute-start.4) | collective-permute-done | bytes 917536 | tf_op jit(solution)/shard_map/ppermute | solution.py:419
  85.8 0.0 copy-start.9
  85.8 1.0 slice.62
  86.8 1.9 %collective-permute-start.6 = (bf16[112,2048]{1,0:T(8,128)(2,1)}, bf16[112,2048]{1,0:T(8,128)(2,1)S(1)}, u32[]{:S(2)}, u32[]{:S(2)}) collective-permute-start(bf16[112,2048]{1,0:T(8,128)(2,1)} %slice.62), channel_id=1, source_target_pairs={{0,64},{64,128},{128,192},{192,256},{256,320},{320,384},{384,448},... | collective-permute-start | bytes 1376264 | tf_op jit(solution)/shard_map/ppermute | solution.py:419
  88.7 0.0 collective-permute-done.5.refs_6_.refs_3_
  88.7 0.0 copy-done.9
  88.7 0.0 copy-start.10
  88.7 0.9 slice.63
  89.6 0.2 copy-done.10
  89.8 5.1 %collective-permute-start.7 = (bf16[112,2048]{1,0:T(8,128)(2,1)}, bf16[112,2048]{1,0:T(8,128)(2,1)}, u32[]{:S(2)}, u32[]{:S(2)}) collective-permute-start(bf16[112,2048]{1,0:T(8,128)(2,1)} %slice.63), channel_id=1, source_target_pairs={{0,448},{64,0},{128,64},{192,128},{256,192},{320,256},{384,320},{4... | collective-permute-start | bytes 1376264 | tf_op jit(solution)/shard_map/ppermute | solution.py:419
  95.0 7.1 %all-to-all-done.1.arrived_ref = bf16[64,112,128]{2,1,0:T(8,128)(2,1)S(1)} async-done(((bf16[64,112,128]{2,1,0:T(8,128)(2,1)}), bf16[64,112,128]{2,1,0:T(8,128)(2,1)S(1)}, u32[]{:S(2)}, u32[]{:S(2)}) %all-to-all-start.1) | async-done | bytes 1835040 | tf_op jit(solution)/shard_map/all_to_all | solution.py:456
  102.0 0.0 copy-done.2
  102.0 5.3 %gathered.1 = (f32[128,4096]{1,0:T(8,128)S(1)}, bf16[128,4096]{1,0:T(8,128)(2,1)S(1)}) custom-call(bf16[64,112,128]{2,1,0:T(8,128)(2,1)S(1)} %all-to-all-done.1.arrived_ref, bf16[224,2048]{1,0:T(8,128)(2,1)} %copy-done.1, bf16[224,2048]{1,0:T(8,128)(2,1)} %collective-permute-done.refs_0_.refs_1_.refs_8_, ...), custom_call_target="tpu_custom_call" | custom-call | flops 1409286144 | bytes 5505024 | tf_op jit(solution)/shard_map/gathered/pallas_call | solution.py:206
  107.4 0.0 collective-permute-done.6.up_ref.refs_4_
  107.4 0.0 copy-start.3
  107.4 0.0 collective-permute-done.7.down_ref.refs_5_
  107.4 2.0 %last.1 = bf16[128,4096]{1,0:T(8,128)(2,1)S(1)} custom-call(bf16[128,4096]{1,0:T(8,128)(2,1)S(1)} %get-tuple-element.22.rows_ref, f32[128,4096]{1,0:T(8,128)S(1)} %get-tuple-element.23.acc_ref, bf16[112,2048]{1,0:T(8,128)(2,1)S(1)} %collective-permute-done.6.up_ref.refs_4_, bf16[112,2048]{1,0:T(8,128)(2,1)} %collective-permute-done.7.down_ref.refs_5_), custom_call_target="tpu_custom_call" | custom-call | tf_op jit(solution)/shard_map/last/pallas_call | solution.py:240
  109.4 0.0 copy-done.3
  109.4 2.1 %copy.14 = bf16[2,64,4096]{2,0,1:T(2,128)(2,1)} copy(bf16[2,64,4096]{2,1,0:T(8,128)(2,1)S(1)} %bitcast.27) | data formatting | bytes 2097152 | tf_op jit(solution)/shard_map/reshape | solution.py:460
  111.5 8.4 %all-to-all-start.2 = ((bf16[64,2,4096]{2,1,0:T(2,128)(2,1)}), bf16[64,2,4096]{2,1,0:T(2,128)(2,1)S(1)}, u32[]{:S(2)}, u32[]{:S(2)}) async-start(bf16[64,2,4096]{2,1,0:T(2,128)(2,1)} %bitcast.26.after_ref), calls=%async_computation.2 | async-start | bytes 2097152 | tf_op jit(solution)/shard_map/all_to_all | solution.py:461
  119.9 2.5 %hot.1 = (bf16[36,4096]{1,0:T(8,128)(2,1)S(1)}, bf16[36,4096]{1,0:T(8,128)(2,1)S(1)}) custom-call(s32[1]{0:T(128)} %bitcast.6.where_ref, bf16[64,112,128]{2,1,0:T(8,128)(2,1)S(1)} %all-to-all-done.1.arrived_ref, bf16[64,2,4096]{2,1,0:T(2,128)(2,1)} %bitcast.26.after_ref, bf16[224,2048]{1,0:T(8,128)(2,1)} %copy-done.1, ...), custom_call_target="tpu_custom_call" | custom-call | tf_op jit(solution)/shard_map/hot/pallas_call | solution.py:303
  122.3 10.4 %all-gather.3 = bf16[2,36,4096]{2,1,0:T(8,128)(2,1)S(1)} all-gather(bf16[1,36,4096]{2,1,0:T(8,128)(2,1)S(1)} %bitcast.28), channel_id=2, replica_groups={{0,64},{128,192},{256,320},{384,448},{1,65},{129,193},{257,321},{385,44..., dimensions={0}, use_global_device_ids=true | all-gather | bytes 884736 | tf_op jit(solution)/shard_map/all_gather | solution.py:425
  132.8 0.1 convert_add_fusion
  132.9 12.9 %all-gather.4 = bf16[2,18,4096]{2,1,0:T(8,128)(2,1)S(1)} all-gather(bf16[1,18,4096]{2,1,0:T(8,128)(2,1)S(1)} %fusion.1), channel_id=3, replica_groups={{0,128},{64,192},{256,384},{320,448},{1,129},{65,193},{257,385},{321,44..., dimensions={0}, use_global_device_ids=true | all-gather | bytes 442368 | tf_op jit(solution)/shard_map/all_gather | solution.py:425
  145.8 0.1 slice_add_fusion
  145.9 0.0 copy-start.5
  145.9 0.0 copy-start.7
  145.9 0.0 copy-start.8
  146.0 12.4 %all-gather.5 = bf16[2,9,4096]{2,1,0:T(8,128)(2,1)S(1)} all-gather(bf16[1,9,4096]{2,1,0:T(8,128)(2,1)S(1)} %fusion.3), channel_id=4, replica_groups={{0,256},{64,320},{128,384},{192,448},{1,257},{65,321},{129,385},{193,44..., dimensions={0}, use_global_device_ids=true | all-gather | bytes 221184 | tf_op jit(solution)/shard_map/all_gather | solution.py:425
  158.3 0.0 all-to-all-done.2
  158.4 0.4 reshape.30.cold_ref
  158.8 0.0 copy-done.5
  158.8 0.0 copy-done.7
  158.8 0.0 copy-done.8
  158.8 1.0 cold_combine.1
  159.8 1.2 final_combine.1
  (4 shorter events, 0.1 us)
Async XLA Ops:
  0.6 0.7 copy-start.6
  3.2 1.0 copy-start.4
  3.2 26.0 %copy-start.1 = (bf16[224,2048]{1,0:T(8,128)(2,1)}, bf16[224,2048]{1,0:T(8,128)(2,1)S(1)}, u32[]{:S(2)}) copy-start(bf16[224,2048]{1,0:T(8,128)(2,1)S(1)} %get-tuple-element.18.refs_0_) | copy-start | bytes 2752516
  4.2 25.8 %collective-permute-start = (bf16[224,2048]{1,0:T(8,128)(2,1)S(1)}, bf16[224,2048]{1,0:T(8,128)(2,1)}, u32[]{:S(2)}, u32[]{:S(2)}) collective-permute-start(bf16[224,2048]{1,0:T(8,128)(2,1)S(1)} %get-tuple-element.18.refs_0_), channel_id=1, source_target_pairs={{0,64},{64,128},{128,192},{192,256},{256,320},{320,384},{384,448},... | collective-permute-start | bytes 2752520 | tf_op jit(solution)/shard_map/ppermute | solution.py:419
  7.7 24.3 %collective-permute-start.1 = (bf16[224,2048]{1,0:T(8,128)(2,1)S(1)}, bf16[224,2048]{1,0:T(8,128)(2,1)}, u32[]{:S(2)}, u32[]{:S(2)}) collective-permute-start(bf16[224,2048]{1,0:T(8,128)(2,1)S(1)} %get-tuple-element.18.refs_0_), channel_id=1, source_target_pairs={{0,448},{64,0},{128,64},{192,128},{256,192},{320,256},{384,320},{4... | collective-permute-start | bytes 2752520 | tf_op jit(solution)/shard_map/ppermute | solution.py:419
  13.6 35.9 %all-to-all-start = ((bf16[64,48,128]{2,1,0:T(8,128)(2,1)}), bf16[64,48,128]{2,1,0:T(8,128)(2,1)S(1)}, u32[]{:S(2)}, u32[]{:S(2)}) async-start(bf16[64,48,128]{2,1,0:T(8,128)(2,1)} %deal.1), calls=%async_computation | async-start | bytes 1572864 | tf_op jit(solution)/shard_map/all_to_all | solution.py:453
  30.0 28.9 %collective-permute-start.2 = (bf16[224,2048]{1,0:T(8,128)(2,1)}, bf16[224,2048]{1,0:T(8,128)(2,1)}, u32[]{:S(2)}, u32[]{:S(2)}) collective-permute-start(bf16[224,2048]{1,0:T(8,128)(2,1)} %collective-permute-done.refs_0_.refs_1_.refs_8_), channel_id=1, source_target_pairs={{0,64},{64,128},{128,192},{192,256},{256,320},{320,384},{384,448},... | collective-permute-start | bytes 2752520 | tf_op jit(solution)/shard_map/ppermute | solution.py:419
  31.9 27.0 %collective-permute-start.3 = (bf16[224,2048]{1,0:T(8,128)(2,1)}, bf16[224,2048]{1,0:T(8,128)(2,1)S(1)}, u32[]{:S(2)}, u32[]{:S(2)}) collective-permute-start(bf16[224,2048]{1,0:T(8,128)(2,1)} %collective-permute-done.1.refs_1_.refs_4_), channel_id=1, source_target_pairs={{0,448},{64,0},{128,64},{192,128},{256,192},{320,256},{384,320},{4... | collective-permute-start | bytes 2752520 | tf_op jit(solution)/shard_map/ppermute | solution.py:419
  50.4 1.3 copy-start
  51.6 50.4 %all-to-all-start.1 = ((bf16[64,112,128]{2,1,0:T(8,128)(2,1)}), bf16[64,112,128]{2,1,0:T(8,128)(2,1)S(1)}, u32[]{:S(2)}, u32[]{:S(2)}) async-start(bf16[64,112,128]{2,1,0:T(8,128)(2,1)} %copy-done), calls=%async_computation.1 | async-start | bytes 3670016 | tf_op jit(solution)/shard_map/all_to_all | solution.py:456
  60.1 41.9 %copy-start.2 = (bf16[224,2048]{1,0:T(8,128)(2,1)}, bf16[224,2048]{1,0:T(8,128)(2,1)S(1)}, u32[]{:S(2)}) copy-start(bf16[224,2048]{1,0:T(8,128)(2,1)S(1)} %get-tuple-element.21.refs_5_.refs_2_) | copy-start | bytes 2752516
  60.1 25.7 %collective-permute-start.4 = (bf16[224,2048]{1,0:T(8,128)(2,1)}, bf16[224,2048]{1,0:T(8,128)(2,1)S(1)}, u32[]{:S(2)}, u32[]{:S(2)}) collective-permute-start(bf16[224,2048]{1,0:T(8,128)(2,1)} %get-tuple-element.20.refs_2_.refs_7_), channel_id=1, source_target_pairs={{0,64},{64,128},{128,192},{192,256},{256,320},{320,384},{384,448},... | collective-permute-start | bytes 2752520 | tf_op jit(solution)/shard_map/ppermute | solution.py:419
  62.2 26.6 %collective-permute-start.5 = (bf16[224,2048]{1,0:T(8,128)(2,1)S(1)}, bf16[224,2048]{1,0:T(8,128)(2,1)S(1)}, u32[]{:S(2)}, u32[]{:S(2)}) collective-permute-start(bf16[224,2048]{1,0:T(8,128)(2,1)S(1)} %get-tuple-element.21.refs_5_.refs_2_), channel_id=1, source_target_pairs={{0,448},{64,0},{128,64},{192,128},{256,192},{320,256},{384,320},{4... | collective-permute-start | bytes 2752520 | tf_op jit(solution)/shard_map/ppermute | solution.py:419
  85.8 2.9 %copy-start.9 = (bf16[224,2048]{1,0:T(8,128)(2,1)}, bf16[224,2048]{1,0:T(8,128)(2,1)S(1)}, u32[]{:S(2)}) copy-start(bf16[224,2048]{1,0:T(8,128)(2,1)S(1)} %collective-permute-done.4.refs_3_.refs_6_) | copy-start | bytes 2752516
  86.8 20.6 %collective-permute-start.6 = (bf16[112,2048]{1,0:T(8,128)(2,1)}, bf16[112,2048]{1,0:T(8,128)(2,1)S(1)}, u32[]{:S(2)}, u32[]{:S(2)}) collective-permute-start(bf16[112,2048]{1,0:T(8,128)(2,1)} %slice.62), channel_id=1, source_target_pairs={{0,64},{64,128},{128,192},{192,256},{256,320},{320,384},{384,448},... | collective-permute-start | bytes 1376264 | tf_op jit(solution)/shard_map/ppermute | solution.py:419
  88.7 1.1 copy-start.10
  89.8 17.6 %collective-permute-start.7 = (bf16[112,2048]{1,0:T(8,128)(2,1)}, bf16[112,2048]{1,0:T(8,128)(2,1)}, u32[]{:S(2)}, u32[]{:S(2)}) collective-permute-start(bf16[112,2048]{1,0:T(8,128)(2,1)} %slice.63), channel_id=1, source_target_pairs={{0,448},{64,0},{128,64},{192,128},{256,192},{320,256},{384,320},{4... | collective-permute-start | bytes 1376264 | tf_op jit(solution)/shard_map/ppermute | solution.py:419
  107.4 2.0 %copy-start.3 = (bf16[112,2048]{1,0:T(8,128)(2,1)}, bf16[112,2048]{1,0:T(8,128)(2,1)S(1)}, u32[]{:S(2)}) copy-start(bf16[112,2048]{1,0:T(8,128)(2,1)S(1)} %collective-permute-done.6.up_ref.refs_4_) | copy-start | bytes 1376260
  111.5 46.9 %all-to-all-start.2 = ((bf16[64,2,4096]{2,1,0:T(2,128)(2,1)}), bf16[64,2,4096]{2,1,0:T(2,128)(2,1)S(1)}, u32[]{:S(2)}, u32[]{:S(2)}) async-start(bf16[64,2,4096]{2,1,0:T(2,128)(2,1)} %bitcast.26.after_ref), calls=%async_computation.2 | async-start | bytes 2097152 | tf_op jit(solution)/shard_map/all_to_all | solution.py:461
  145.9 12.9 %copy-start.5 = (bf16[16,2048]{1,0:T(8,128)(2,1)S(1)}, bf16[16,2048]{1,0:T(8,128)(2,1)}, u32[]{:S(2)}) copy-start(bf16[16,2048]{1,0:T(8,128)(2,1)} %cot_ref.5) | copy-start | bytes 196612
  145.9 12.9 %copy-start.7 = (s32[16,8]{0,1:T(8,128)S(1)}, s32[16,8]{0,1:T(8,128)}, u32[]{:S(2)}) copy-start(s32[16,8]{0,1:T(8,128)} %param.9) | copy-start | bytes 1540
  145.9 12.9 %copy-start.8 = (f32[16,8]{0,1:T(8,128)S(1)}, f32[16,8]{0,1:T(8,128)}, u32[]{:S(2)}) copy-start(f32[16,8]{0,1:T(8,128)} %param.8) | copy-start | bytes 1540

commit v5 on v4

--- a/solution.py
+++ b/solution.py
@@ -102,28 +102,33 @@
     )(ids, *map(outside, (tokens, cotangent, up, down)))
 
 
-def deal_kernel(tall, up_ref, down_ref, out_ref, up, down, sems):
-    columns = up.shape[1] // 128
+def assemble_kernel(tall, rows_ref, up_ref, down_ref, out_ref, up, down, sems):
     copies = []
     for i, (source, here) in enumerate(((up_ref, up), (down_ref, down))):
         copy = pltpu.make_async_copy(source, here, sems.at[i])
         copy.start()
         copies.append(copy)
+    lines = rows_ref.shape[1]
+    out_ref[:, :lines, :] = rows_ref[...]
+    columns = up.shape[1] // 128
     groups = up.shape[0] // tall
     for i, here in enumerate((up, down)):
         copies[i].wait()
         for g in range(groups):
             for j in range(columns):
-                out_ref[(i * groups + g) * columns + j] = here[g * tall : (g + 1) * tall, j * 128 : (j + 1) * 128]
-
-
-def deal(up, down, experts):
+                out_ref[(i * groups + g) * columns + j, lines:, :] = here[
+                    g * tall : (g + 1) * tall, j * 128 : (j + 1) * 128
+                ]
+
+
+def assemble(rows, up, down):
+    experts, lines, lanes = rows.shape
     units, width = up.shape
-    tall = 2 * units * width // (experts * 128)
-    return pl.pallas_call(
-        functools.partial(deal_kernel, tall),
-        out_shape=jax.ShapeDtypeStruct((experts, tall, 128), BF16),
-        in_specs=[pl.BlockSpec(memory_space=pl.ANY)] * 2,
+    tall = 2 * units * width // (experts * lanes)
+    return pl.pallas_call(
+        functools.partial(assemble_kernel, tall),
+        out_shape=jax.ShapeDtypeStruct((experts, lines + tall, lanes), BF16),
+        in_specs=[pl.BlockSpec(memory_space=pltpu.VMEM)] + [pl.BlockSpec(memory_space=pl.ANY)] * 2,
         out_specs=pl.BlockSpec(memory_space=pltpu.VMEM),
         scratch_shapes=[
             pltpu.VMEM((units, width), BF16),
@@ -131,35 +136,26 @@
             pltpu.SemaphoreType.DMA((2,)),
         ],
         compiler_params=pltpu.CompilerParams(vmem_limit_bytes=VMEM_LIMIT),
-        name="deal",
-    )(outside(up), outside(down))
-
-
-def assemble_kernel(hottest_ref, rows_ref, dealt_ref, out_ref, mine, sem):
-    copy = pltpu.make_async_copy(dealt_ref.at[hottest_ref[0, 0]], mine, sem)
-    copy.start()
-    lines = rows_ref.shape[1]
-    out_ref[:, :lines, :] = rows_ref[...]
-    copy.wait()
-    out_ref[:, lines:, :] = jnp.broadcast_to(mine[...][None], (out_ref.shape[0],) + mine.shape)
-
-
-def assemble(hottest, rows, dealt):
-    experts, lines, lanes = rows.shape
-    tall = dealt.shape[1]
-    return pl.pallas_call(
-        assemble_kernel,
-        out_shape=jax.ShapeDtypeStruct((experts, lines + tall, lanes), BF16),
-        in_specs=[
-            pl.BlockSpec(memory_space=pltpu.SMEM),
-            pl.BlockSpec(memory_space=pltpu.VMEM),
-            pl.BlockSpec(memory_space=pl.ANY),
-        ],
-        out_specs=pl.BlockSpec(memory_space=pltpu.VMEM),
-        scratch_shapes=[pltpu.VMEM((tall, lanes), BF16), pltpu.SemaphoreType.DMA],
-        compiler_params=pltpu.CompilerParams(vmem_limit_bytes=VMEM_LIMIT),
         name="assemble",
-    )(hottest, rows, dealt)
+    )(rows, outside(up), outside(down))
+
+
+def repeat_kernel(lines, hottest_ref, arrived_ref, out_ref):
+    mine = arrived_ref[hottest_ref[0, 0], lines:, :]
+    out_ref[...] = jnp.broadcast_to(mine[None], out_ref.shape)
+
+
+def repeat(hottest, arrived, lines):
+    experts, height, lanes = arrived.shape
+    inside = pl.BlockSpec(memory_space=pltpu.VMEM)
+    return pl.pallas_call(
+        functools.partial(repeat_kernel, lines),
+        out_shape=jax.ShapeDtypeStruct((experts, height - lines, lanes), BF16),
+        in_specs=[pl.BlockSpec(memory_space=pltpu.SMEM), inside],
+        out_specs=inside,
+        compiler_params=pltpu.CompilerParams(vmem_limit_bytes=VMEM_LIMIT),
+        name="repeat",
+    )(hottest, arrived)
 
 
 def activations(pre_act, hidden_grad):
@@ -245,7 +241,7 @@
     )(rows, acc, up_half, down_half)
 
 
-def hot_kernel(units, lines, hot_rows, where_ref, arrived_ref, *refs):
+def hot_kernel(units, hot_rows, where_ref, pieces_ref, *refs):
     blocks, (send_ref, keep_ref, tok, cot, weights, sems) = refs[:-6], refs[-6:]
     ring = len(blocks)
     width = tok.shape[1]
@@ -262,10 +258,10 @@
             copy.start()
             copies.append(copy)
     columns = width // 128
-    tall = arrived_ref.shape[1] - lines
-    for k in range(arrived_ref.shape[0]):
+    tall = pieces_ref.shape[1]
+    for k in range(pieces_ref.shape[0]):
         i, j = k // columns, k % columns
-        weights[i * tall : (i + 1) * tall, j * 128 : (j + 1) * 128] = arrived_ref[k, lines:, :]
+        weights[i * tall : (i + 1) * tall, j * 128 : (j + 1) * 128] = pieces_ref[k]
     for copy in copies:
         copy.wait()
     up, down = weights[:units, :], weights[units:, :]
@@ -284,7 +280,7 @@
         out_ref[:, width:] = matmul(picked_grad, up).astype(BF16)
 
 
-def hot_partials(here, arrived, blocks, units, lines, hot_rows, after):
+def hot_partials(here, pieces, blocks, units, hot_rows, after):
     ring = len(blocks)
     flat, spans = [], []
     for block in blocks:
@@ -292,11 +288,11 @@
         flat += list(block) if isinstance(block, tuple) else [block]
     width = flat[0].shape[1]
 
-    def kernel(where_ref, arrived_ref, after_ref, *refs):
+    def kernel(where_ref, pieces_ref, after_ref, *refs):
         refs, grouped = list(refs), []
         for span in spans:
             grouped.append(tuple(refs.pop(0) for _ in range(span)) if span else refs.pop(0))
-        hot_kernel(units, lines, hot_rows, where_ref, arrived_ref, *grouped, *refs)
+        hot_kernel(units, hot_rows, where_ref, pieces_ref, *grouped, *refs)
 
     inside = pl.BlockSpec(memory_space=pltpu.VMEM)
     packed = jax.ShapeDtypeStruct((ring // 2 * hot_rows, 2 * width), BF16)
@@ -314,7 +310,7 @@
         ],
         compiler_params=pltpu.CompilerParams(vmem_limit_bytes=VMEM_LIMIT),
         name="hot",
-    )(here, arrived, after, *map(outside, flat))
+    )(here, pieces, after, *map(outside, flat))
 
 
 def thirds(x):
@@ -394,24 +390,42 @@
     )(ids, gates, cotangent, sums, dots, kept, sent)
 
 
+TICK = pl.CostEstimate(flops=1 << 35, bytes_accessed=1 << 25, transcendentals=0)
+
+
 def tick_kernel(token_ref, *refs):
     refs[-1][0, 0] = token_ref[0, 0]
 
 
-def tick(token, *after, through=False):
-    count = len(after) if through else 0
-    anywhere, scalar = pl.BlockSpec(memory_space=pl.ANY), pl.BlockSpec(memory_space=pltpu.SMEM)
-    out = pl.pallas_call(
+def tick(token, *after):
+    scalar = pl.BlockSpec(memory_space=pltpu.SMEM)
+    return pl.pallas_call(
         tick_kernel,
-        out_shape=tuple(jax.ShapeDtypeStruct(x.shape, x.dtype) for x in after[:count] + (token,)),
-        in_specs=[scalar] + [anywhere] * len(after),
-        out_specs=tuple([anywhere] * count + [scalar]),
-        input_output_aliases={i + 1: i for i in range(count)},
+        out_shape=jax.ShapeDtypeStruct(token.shape, token.dtype),
+        in_specs=[scalar] + [pl.BlockSpec(memory_space=pl.ANY)] * len(after),
+        out_specs=scalar,
         compiler_params=pltpu.CompilerParams(vmem_limit_bytes=1 << 20),
-        cost_estimate=pl.CostEstimate(flops=1 << 35, bytes_accessed=1 << 25, transcendentals=0),
+        cost_estimate=pl.CostEstimate(flops=22 << 30, bytes_accessed=1 << 10, transcendentals=0),
         name="tick",
     )(token, *after)
-    return out if through else out[0]
+
+
+def gate_kernel(*refs):
+    pass
+
+
+def gate(*arrays):
+    anywhere = pl.BlockSpec(memory_space=pl.ANY)
+    return pl.pallas_call(
+        gate_kernel,
+        out_shape=tuple(jax.ShapeDtypeStruct(x.shape, x.dtype) for x in arrays),
+        in_specs=[anywhere] * len(arrays),
+        out_specs=tuple([anywhere] * len(arrays)),
+        input_output_aliases={i: i for i in range(len(arrays))},
+        compiler_params=pltpu.CompilerParams(vmem_limit_bytes=1 << 20),
+        cost_estimate=TICK,
+        name="gate",
+    )(*arrays)
 
 
 def shift(x, by):
@@ -442,18 +456,18 @@
     right, left = [own], [own]
     for step in range(3):
         r, l = shift(right[-1], 1), shift(left[-1], -1)
-        if step == 0:
+        if step == 1:
             token = tick(hottest, r, l)
-        if step == 1:
-            r, l, _ = tick(hottest, r, l, through=True)
+        if step in (2,):
+            r, l = gate(r, l)
         right.append(r)
         left.append(l)
     far_up, far_down = shift(right[-1][:half], 1), shift(left[-1][half:], -1)
 
-    dealt = lax.all_to_all(deal(up, down, experts), "expert", 0, 0, tiled=True)
     lines = capacity * 2 * width // 128
-    outgoing = assemble(token, outgoing.reshape(experts, lines, 128), dealt)
+    outgoing = assemble(outgoing.reshape(experts, lines, 128), up, down)
     arrived = lax.all_to_all(outgoing, "expert", 0, 0, tiled=True)
+    hot_pieces = lax.all_to_all(repeat(token, arrived, lines), "expert", 0, 0, tiled=True)
 
     acc, rows = gathered(arrived, [own] + right[1:] + left[1:], units, slots)
     results = last(rows, acc, far_up, far_down, units)
@@ -462,11 +476,16 @@
 
     blocks = left + [(far_up, far_down)] + right[:0:-1]
     here = lax.axis_index("dp").astype(I32).reshape(1)
-    send, keep = hot_partials(here, arrived, blocks, units, lines, hot_rows, results)
+    send, keep = hot_partials(here, hot_pieces, blocks, units, hot_rows, results)
     both = keep.astype(F32) + swap(send, 1).astype(F32)
-    stay = both[: 2 * hot_rows] + swap(both[2 * hot_rows :].astype(BF16), 2).astype(F32)
-    sent = swap(stay[hot_rows:].astype(BF16), 4)
-    kept = stay[:hot_rows]
+    kept, onward = both[:hot_rows], both[hot_rows:].astype(BF16)
+    ring = lax.axis_size("dp")
+    parity = [[i for i in range(ring) if i % 2 == odd] for odd in range(2)]
+    quad = lax.all_gather(onward, "dp", axis=0, axis_index_groups=parity, tiled=False)
+    sent = jnp.zeros(kept.shape, F32)
+    for i, place in enumerate((4, 2, 6)):
+        theirs = lax.dynamic_index_in_dim(quad, (here[0] ^ place) // 2, 0, keepdims=False)
+        sent = sent + theirs[i * hot_rows : (i + 1) * hot_rows].astype(F32)
     sums, dots = cold_combine(ids, gates, cotangent, came_back, capacity)
     mixture, input_grad, gate_grad = final_combine(
         ids, gates, cotangent, sums, dots, kept, sent, slots, capacity

time: 162 us -> 159 us (0.981)
  blocking collectives: 35.7 us -> 32 us
  starting transfers between devices: 58.1 us -> 61.1 us
  Pallas kernels: 19 us -> 17.3 us
    all_gather x3 -> x1, blocking collectives: 35.7 us -> 10.4 us  [swap(): both = lax.all_gather(x, 'dp', axis=0, axis_index_groups=pairs, tiled=False)]
    all_gather x0 -> x1, blocking collectives: none -> 21.6 us  [shards(): lax.all_gather(onward, 'dp', axis=0, axis_index_groups=parity, tiled=False)]
    all_to_all x1, waiting for transfers between devices: 11.3 us -> 0.01 us  [shards(): lax.all_to_all(repeat(token, arrived, lines), 'expert', 0, 0, tiled=True)]
    ppermute x8, waiting for transfers between devices: 19.5 us -> 27.6 us  [shift(): return lax.ppermute(x, 'dp', [(i, (i + by) % ring) for i in range(ring)])]
    all_to_all x1, starting transfers between devices: 7.26 us -> 14 us  [shards(): arrived = lax.all_to_all(outgoing, 'expert', 0, 0, tiled=True)]
    all_to_all x1, starting transfers between devices: 14 us -> 8.39 us  [shards(): lax.all_to_all(repeat(token, arrived, lines), 'expert', 0, 0, tiled=True)]
    pallas_call x4, Pallas kernels: 5.25 us -> 3.12 us  [the longest x1 1.2 us: assemble(): pl.pallas_call(functools.partial(assemble_kernel, tall), out_shape=jax.Sh...]
    all_to_all x1, starting transfers between devices: 8.39 us -> 10.5 us  [shards(): lax.all_to_all(results, 'expert', 0, 0, tiled=True)]
  transfers between devices with their start and end apart: 11 -> 11, of which waited for: 4 -> 6; matrix products, arithmetic and copies ran while one was open for 2% -> 4% of each run, Pallas kernels for 8% -> 8%
where the time goes in v5:
time: 159 us; the launch traced here: 158 us
  starting transfers between devices  61.1 us (38%)
  waiting for transfers between devices  36.5 us (23%)
  blocking collectives  32 us (20%)
  Pallas kernels  17.3 us (11%)
  local copies, waits for them, and re-layouts  9.98 us (6%)
    ppermute x8, starting transfers between devices, shift(): return lax.ppermute(x, 'dp', [(i, (i + by) % ring) for i in range(ring)])  28.2 us
    ppermute x8, waiting for transfers between devices, shift(): return lax.ppermute(x, 'dp', [(i, (i + by) % ring) for i in range(ring)])  27.6 us
    all_gather x1, blocking collectives, shards(): lax.all_gather(onward, 'dp', axis=0, axis_index_groups=parity, tiled=False)  21.6 us
    all_to_all x1, starting transfers between devices, shards(): arrived = lax.all_to_all(outgoing, 'expert', 0, 0, tiled=True)  14 us
    all_to_all x1, starting transfers between devices, shards(): lax.all_to_all(results, 'expert', 0, 0, tiled=True)  10.5 us
    all_gather x1, blocking collectives, swap(): both = lax.all_gather(x, 'dp', axis=0, axis_index_groups=pairs, tiled=False)  10.4 us
    all_to_all x1, waiting for transfers between devices, shards(): arrived = lax.all_to_all(outgoing, 'expert', 0, 0, tiled=True)  8.82 us
    all_to_all x1, starting transfers between devices, shards(): lax.all_to_all(repeat(token, arrived, lines), 'expert', 0, 0, tiled=True)  8.39 us
  transfers between devices with their start and end apart: 11, of which 6 were waited for; matrix products, arithmetic and copies ran while one was open for 4% of the time, Pallas kernels for 8%

profile of v5, /device:TPU:6, one launch (start us, length us, event | category | flops | bytes accessed | tf_op | source)
XLA Modules:
  0.0 158.1 jit_solution(17182461504955486021)
XLA Ops:
  0.6 0.0 copy-start.4
  0.6 0.7 copy-done.4
  1.3 2.3 %route.1 = (bf16[128,4096]{1,0:T(8,128)(2,1)S(1)}, bf16[224,2048]{1,0:T(8,128)(2,1)}, s32[1,1]{1,0:T(1,128)}) custom-call(s32[8,16]{1,0:T(8,128)S(1)} %bitcast.22, bf16[16,2048]{1,0:T(8,128)(2,1)} %tok_ref.1, bf16[16,2048]{1,0:T(8,128)(2,1)} %cot_ref.5, bf16[96,2048]{1,0:T(8,128)(2,1)} %bitcast.27, bf16[96,2048]{1,0:T(8,128)(2,1)} %bitcast.29), custom_call_target="tpu_custom_call" | custom-call | tf_op jit(solution)/shard_map/route/pallas_call | solution.py:86
  3.6 5.4 %collective-permute-start.3 = (bf16[224,2048]{1,0:T(8,128)(2,1)}, bf16[224,2048]{1,0:T(8,128)(2,1)}, u32[]{:S(2)}, u32[]{:S(2)}) collective-permute-start(bf16[224,2048]{1,0:T(8,128)(2,1)} %get-tuple-element.18.refs_0_), channel_id=1, source_target_pairs={{0,448},{64,0},{128,64},{192,128},{256,192},{320,256},{384,320},{4... | collective-permute-start | bytes 2752520 | tf_op jit(solution)/shard_map/ppermute | solution.py:433
  9.0 1.9 %collective-permute-start = (bf16[224,2048]{1,0:T(8,128)(2,1)}, bf16[224,2048]{1,0:T(8,128)(2,1)}, u32[]{:S(2)}, u32[]{:S(2)}) collective-permute-start(bf16[224,2048]{1,0:T(8,128)(2,1)} %get-tuple-element.18.refs_0_), channel_id=1, source_target_pairs={{0,64},{64,128},{128,192},{192,256},{256,320},{320,384},{384,448},... | collective-permute-start | bytes 2752520 | tf_op jit(solution)/shard_map/ppermute | solution.py:433
  10.9 0.5 reshape.30.rows_ref
  11.5 1.2 assemble.1
  12.7 0.0 copy-start
  12.7 1.2 copy-done
  14.0 14.0 %all-to-all-start = ((bf16[64,112,128]{2,1,0:T(8,128)(2,1)}), bf16[64,112,128]{2,1,0:T(8,128)(2,1)S(1)}, u32[]{:S(2)}, u32[]{:S(2)}) async-start(bf16[64,112,128]{2,1,0:T(8,128)(2,1)} %copy-done), calls=%async_computation | async-start | bytes 3670016 | tf_op jit(solution)/shard_map/all_to_all | solution.py:469
  28.0 0.9 collective-permute-done.3.refs_4_.refs_1_
  28.9 5.6 %collective-permute-start.4 = (bf16[224,2048]{1,0:T(8,128)(2,1)}, bf16[224,2048]{1,0:T(8,128)(2,1)}, u32[]{:S(2)}, u32[]{:S(2)}) collective-permute-start(bf16[224,2048]{1,0:T(8,128)(2,1)} %collective-permute-done.3.refs_4_.refs_1_), channel_id=1, source_target_pairs={{0,448},{64,0},{128,64},{192,128},{256,192},{320,256},{384,320},{4... | collective-permute-start | bytes 2752520 | tf_op jit(solution)/shard_map/ppermute | solution.py:433
  34.5 0.0 collective-permute-done.refs_1_.refs_8_
  34.5 1.9 %collective-permute-start.1 = (bf16[224,2048]{1,0:T(8,128)(2,1)}, bf16[224,2048]{1,0:T(8,128)(2,1)}, u32[]{:S(2)}, u32[]{:S(2)}) collective-permute-start(bf16[224,2048]{1,0:T(8,128)(2,1)} %collective-permute-done.refs_1_.refs_8_), channel_id=1, source_target_pairs={{0,64},{64,128},{128,192},{192,256},{256,320},{320,384},{384,448},... | collective-permute-start | bytes 2752520 | tf_op jit(solution)/shard_map/ppermute | solution.py:433
  36.5 17.1 %collective-permute-done.4.refs_5_.refs_1_.refs_2_ = bf16[224,2048]{1,0:T(8,128)(2,1)} collective-permute-done((bf16[224,2048]{1,0:T(8,128)(2,1)}, bf16[224,2048]{1,0:T(8,128)(2,1)}, u32[]{:S(2)}, u32[]{:S(2)}) %collective-permute-start.4) | collective-permute-done | bytes 917536 | tf_op jit(solution)/shard_map/ppermute | solution.py:433
  53.5 5.6 %collective-permute-start.5 = (bf16[224,2048]{1,0:T(8,128)(2,1)}, bf16[224,2048]{1,0:T(8,128)(2,1)S(1)}, u32[]{:S(2)}, u32[]{:S(2)}) collective-permute-start(bf16[224,2048]{1,0:T(8,128)(2,1)} %collective-permute-done.4.refs_5_.refs_1_.refs_2_), channel_id=1, source_target_pairs={{0,448},{64,0},{128,64},{192,128},{256,192},{320,256},{384,320},{4... | collective-permute-start | bytes 2752520 | tf_op jit(solution)/shard_map/ppermute | solution.py:433
  59.1 0.0 collective-permute-done.1.refs_2_.refs_0_.refs_7_
  59.1 1.9 %collective-permute-start.2 = (bf16[224,2048]{1,0:T(8,128)(2,1)}, bf16[224,2048]{1,0:T(8,128)(2,1)}, u32[]{:S(2)}, u32[]{:S(2)}) collective-permute-start(bf16[224,2048]{1,0:T(8,128)(2,1)} %collective-permute-done.1.refs_2_.refs_0_.refs_7_), channel_id=1, source_target_pairs={{0,64},{64,128},{128,192},{192,256},{256,320},{320,384},{384,448},... | collective-permute-start | bytes 2752520 | tf_op jit(solution)/shard_map/ppermute | solution.py:433
  61.1 1.2 tick.1.hottest_ref
  62.2 8.8 %all-to-all-done.arrived_ref = bf16[64,112,128]{2,1,0:T(8,128)(2,1)S(1)} async-done(((bf16[64,112,128]{2,1,0:T(8,128)(2,1)}), bf16[64,112,128]{2,1,0:T(8,128)(2,1)S(1)}, u32[]{:S(2)}, u32[]{:S(2)}) %all-to-all-start) | async-done | bytes 1835040 | tf_op jit(solution)/shard_map/all_to_all | solution.py:469
  71.1 0.7 repeat.1
  71.8 0.0 copy-start.2
  71.8 0.9 copy-done.2
  72.7 8.4 %all-to-all-start.2 = ((bf16[64,48,128]{2,1,0:T(8,128)(2,1)}), bf16[64,48,128]{2,1,0:T(8,128)(2,1)S(1)}, u32[]{:S(2)}, u32[]{:S(2)}) async-start(bf16[64,48,128]{2,1,0:T(8,128)(2,1)} %copy-done.2), calls=%async_computation.2 | async-start | bytes 1572864 | tf_op jit(solution)/shard_map/all_to_all | solution.py:470
  81.1 0.0 collective-permute-done.5.refs_1_
  81.1 1.4 collective-permute-done.2.refs_0_
  82.6 0.0 copy-start.1
  82.6 2.1 %slice.31 = bf16[112,2048]{1,0:T(8,128)(2,1)} slice(bf16[224,2048]{1,0:T(8,128)(2,1)} %get-tuple-element.19.refs_3_.refs_6_), slice={[0:112], [0:2048]} | slice | bytes 917504 | tf_op jit(solution)/shard_map/slice | solution.py:465
  84.7 0.8 slice.32
  85.5 3.7 %collective-permute-start.7 = (bf16[112,2048]{1,0:T(8,128)(2,1)}, bf16[112,2048]{1,0:T(8,128)(2,1)}, u32[]{:S(2)}, u32[]{:S(2)}) collective-permute-start(bf16[112,2048]{1,0:T(8,128)(2,1)} %slice.32), channel_id=1, source_target_pairs={{0,448},{64,0},{128,64},{192,128},{256,192},{320,256},{384,320},{4... | collective-permute-start | bytes 1376264 | tf_op jit(solution)/shard_map/ppermute | solution.py:433
  89.3 2.1 %collective-permute-start.6 = (bf16[112,2048]{1,0:T(8,128)(2,1)}, bf16[112,2048]{1,0:T(8,128)(2,1)}, u32[]{:S(2)}, u32[]{:S(2)}) collective-permute-start(bf16[112,2048]{1,0:T(8,128)(2,1)} %slice.31), channel_id=1, source_target_pairs={{0,64},{64,128},{128,192},{192,256},{256,320},{320,384},{384,448},... | collective-permute-start | bytes 1376264 | tf_op jit(solution)/shard_map/ppermute | solution.py:433
  91.5 0.0 copy-done.1
  91.5 5.3 %gathered.1 = (f32[128,4096]{1,0:T(8,128)S(1)}, bf16[128,4096]{1,0:T(8,128)(2,1)S(1)}) custom-call(bf16[64,112,128]{2,1,0:T(8,128)(2,1)S(1)} %all-to-all-done.arrived_ref, bf16[224,2048]{1,0:T(8,128)(2,1)} %get-tuple-element.18.refs_0_, bf16[224,2048]{1,0:T(8,128)(2,1)} %collective-permute-done.refs_1_.refs_8_, ...), custom_call_target="tpu_custom_call" | custom-call | flops 1409286144 | bytes 5505024 | tf_op jit(solution)/shard_map/gathered/pallas_call | solution.py:202
  96.8 2.8 %collective-permute-done.7.down_ref.refs_5_ = bf16[112,2048]{1,0:T(8,128)(2,1)} collective-permute-done((bf16[112,2048]{1,0:T(8,128)(2,1)}, bf16[112,2048]{1,0:T(8,128)(2,1)}, u32[]{:S(2)}, u32[]{:S(2)}) %collective-permute-start.7) | collective-permute-done | bytes 458784 | tf_op jit(solution)/shard_map/ppermute | solution.py:433
  99.7 5.3 %collective-permute-done.6.up_ref.refs_4_ = bf16[112,2048]{1,0:T(8,128)(2,1)} collective-permute-done((bf16[112,2048]{1,0:T(8,128)(2,1)}, bf16[112,2048]{1,0:T(8,128)(2,1)}, u32[]{:S(2)}, u32[]{:S(2)}) %collective-permute-start.6) | collective-permute-done | bytes 458784 | tf_op jit(solution)/shard_map/ppermute | solution.py:433
  105.0 2.0 %last.1 = bf16[128,4096]{1,0:T(8,128)(2,1)S(1)} custom-call(bf16[128,4096]{1,0:T(8,128)(2,1)S(1)} %get-tuple-element.21.rows_ref, f32[128,4096]{1,0:T(8,128)S(1)} %get-tuple-element.22.acc_ref, bf16[112,2048]{1,0:T(8,128)(2,1)} %collective-permute-done.6.up_ref.refs_4_, bf16[112,2048]{1,0:T(8,128)(2,1)} %collective-permute-done.7.down_ref.refs_5_), custom_call_target="tpu_custom_call" | custom-call | tf_op jit(solution)/shard_map/last/pallas_call | solution.py:236
  107.0 2.1 %copy.14 = bf16[2,64,4096]{2,0,1:T(2,128)(2,1)} copy(bf16[2,64,4096]{2,1,0:T(8,128)(2,1)S(1)} %bitcast.20) | data formatting | bytes 2097152 | tf_op jit(solution)/shard_map/reshape | solution.py:474
  109.1 0.0 all-to-all-done.2.pieces_ref
  109.1 10.5 %all-to-all-start.1 = ((bf16[64,2,4096]{2,1,0:T(2,128)(2,1)}), bf16[64,2,4096]{2,1,0:T(2,128)(2,1)}, u32[]{:S(2)}, u32[]{:S(2)}) async-start(bf16[64,2,4096]{2,1,0:T(2,128)(2,1)} %bitcast.19.after_ref), calls=%async_computation.1 | async-start | bytes 2097152 | tf_op jit(solution)/shard_map/all_to_all | solution.py:475
  119.6 2.5 %hot.1 = (bf16[36,4096]{1,0:T(8,128)(2,1)S(1)}, bf16[36,4096]{1,0:T(8,128)(2,1)S(1)}) custom-call(s32[1]{0:T(128)} %bitcast.6.where_ref, bf16[64,48,128]{2,1,0:T(8,128)(2,1)S(1)} %all-to-all-done.2.pieces_ref, bf16[64,2,4096]{2,1,0:T(2,128)(2,1)} %bitcast.19.after_ref, bf16[224,2048]{1,0:T(8,128)(2,1)} %get-tuple-element.18.refs_0_, ...), custom_call_target="tpu_custom_call" | custom-call | tf_op jit(solution)/shard_map/hot/pallas_call | solution.py:299
  122.1 10.4 %all-gather.2 = bf16[2,36,4096]{2,1,0:T(8,128)(2,1)S(1)} all-gather(bf16[1,36,4096]{2,1,0:T(8,128)(2,1)S(1)} %bitcast.21), channel_id=2, replica_groups={{0,64},{128,192},{256,320},{384,448},{1,65},{129,193},{257,321},{385,44..., dimensions={0}, use_global_device_ids=true | all-gather | bytes 884736 | tf_op jit(solution)/shard_map/all_gather | solution.py:439
  132.5 0.1 convert_add_fusion
  132.7 0.0 copy-start.3
  132.7 0.0 copy-start.5
  132.7 0.0 copy-start.6
  132.7 21.6 %all-gather.3 = bf16[4,27,4096]{2,1,0:T(8,128)(2,1)S(1)} all-gather(bf16[1,27,4096]{2,1,0:T(8,128)(2,1)S(1)} %fusion.1), channel_id=3, replica_groups={{0,128,256,384},{64,192,320,448},{1,129,257,385},{65,193,321,449},{2,13..., dimensions={0}, use_global_device_ids=true | all-gather | bytes 1105920 | tf_op jit(solution)/shard_map/all_gather | solution.py:484
  154.3 0.1 add_bitcast_fusion.sent_ref
  154.4 0.0 all-to-all-done.1
  154.4 1.5 reshape.32.cold_ref
  155.9 0.0 copy-done.3
  155.9 0.0 copy-done.5
  155.9 0.0 copy-done.6
  155.9 1.0 cold_combine.1
  156.9 1.2 final_combine.1
  (3 shorter events, 0.1 us)
Async XLA Ops:
  0.6 0.7 copy-start.4
  3.6 25.3 %collective-permute-start.3 = (bf16[224,2048]{1,0:T(8,128)(2,1)}, bf16[224,2048]{1,0:T(8,128)(2,1)}, u32[]{:S(2)}, u32[]{:S(2)}) collective-permute-start(bf16[224,2048]{1,0:T(8,128)(2,1)} %get-tuple-element.18.refs_0_), channel_id=1, source_target_pairs={{0,448},{64,0},{128,64},{192,128},{256,192},{320,256},{384,320},{4... | collective-permute-start | bytes 2752520 | tf_op jit(solution)/shard_map/ppermute | solution.py:433
  9.0 25.5 %collective-permute-start = (bf16[224,2048]{1,0:T(8,128)(2,1)}, bf16[224,2048]{1,0:T(8,128)(2,1)}, u32[]{:S(2)}, u32[]{:S(2)}) collective-permute-start(bf16[224,2048]{1,0:T(8,128)(2,1)} %get-tuple-element.18.refs_0_), channel_id=1, source_target_pairs={{0,64},{64,128},{128,192},{192,256},{256,320},{320,384},{384,448},... | collective-permute-start | bytes 2752520 | tf_op jit(solution)/shard_map/ppermute | solution.py:433
  12.7 1.3 copy-start
  14.0 57.1 %all-to-all-start = ((bf16[64,112,128]{2,1,0:T(8,128)(2,1)}), bf16[64,112,128]{2,1,0:T(8,128)(2,1)S(1)}, u32[]{:S(2)}, u32[]{:S(2)}) async-start(bf16[64,112,128]{2,1,0:T(8,128)(2,1)} %copy-done), calls=%async_computation | async-start | bytes 3670016 | tf_op jit(solution)/shard_map/all_to_all | solution.py:469
  28.9 24.6 %collective-permute-start.4 = (bf16[224,2048]{1,0:T(8,128)(2,1)}, bf16[224,2048]{1,0:T(8,128)(2,1)}, u32[]{:S(2)}, u32[]{:S(2)}) collective-permute-start(bf16[224,2048]{1,0:T(8,128)(2,1)} %collective-permute-done.3.refs_4_.refs_1_), channel_id=1, source_target_pairs={{0,448},{64,0},{128,64},{192,128},{256,192},{320,256},{384,320},{4... | collective-permute-start | bytes 2752520 | tf_op jit(solution)/shard_map/ppermute | solution.py:433
  34.5 24.6 %collective-permute-start.1 = (bf16[224,2048]{1,0:T(8,128)(2,1)}, bf16[224,2048]{1,0:T(8,128)(2,1)}, u32[]{:S(2)}, u32[]{:S(2)}) collective-permute-start(bf16[224,2048]{1,0:T(8,128)(2,1)} %collective-permute-done.refs_1_.refs_8_), channel_id=1, source_target_pairs={{0,64},{64,128},{128,192},{192,256},{256,320},{320,384},{384,448},... | collective-permute-start | bytes 2752520 | tf_op jit(solution)/shard_map/ppermute | solution.py:433
  53.5 27.6 %collective-permute-start.5 = (bf16[224,2048]{1,0:T(8,128)(2,1)}, bf16[224,2048]{1,0:T(8,128)(2,1)S(1)}, u32[]{:S(2)}, u32[]{:S(2)}) collective-permute-start(bf16[224,2048]{1,0:T(8,128)(2,1)} %collective-permute-done.4.refs_5_.refs_1_.refs_2_), channel_id=1, source_target_pairs={{0,448},{64,0},{128,64},{192,128},{256,192},{320,256},{384,320},{4... | collective-permute-start | bytes 2752520 | tf_op jit(solution)/shard_map/ppermute | solution.py:433
  59.1 23.4 %collective-permute-start.2 = (bf16[224,2048]{1,0:T(8,128)(2,1)}, bf16[224,2048]{1,0:T(8,128)(2,1)}, u32[]{:S(2)}, u32[]{:S(2)}) collective-permute-start(bf16[224,2048]{1,0:T(8,128)(2,1)} %collective-permute-done.1.refs_2_.refs_0_.refs_7_), channel_id=1, source_target_pairs={{0,64},{64,128},{128,192},{192,256},{256,320},{320,384},{384,448},... | collective-permute-start | bytes 2752520 | tf_op jit(solution)/shard_map/ppermute | solution.py:433
  71.8 0.9 copy-start.2
  72.7 36.4 %all-to-all-start.2 = ((bf16[64,48,128]{2,1,0:T(8,128)(2,1)}), bf16[64,48,128]{2,1,0:T(8,128)(2,1)S(1)}, u32[]{:S(2)}, u32[]{:S(2)}) async-start(bf16[64,48,128]{2,1,0:T(8,128)(2,1)} %copy-done.2), calls=%async_computation.2 | async-start | bytes 1572864 | tf_op jit(solution)/shard_map/all_to_all | solution.py:470
  82.6 8.9 %copy-start.1 = (bf16[224,2048]{1,0:T(8,128)(2,1)}, bf16[224,2048]{1,0:T(8,128)(2,1)S(1)}, u32[]{:S(2)}) copy-start(bf16[224,2048]{1,0:T(8,128)(2,1)S(1)} %get-tuple-element.20.refs_6_.refs_3_) | copy-start | bytes 2752516
  85.5 14.1 %collective-permute-start.7 = (bf16[112,2048]{1,0:T(8,128)(2,1)}, bf16[112,2048]{1,0:T(8,128)(2,1)}, u32[]{:S(2)}, u32[]{:S(2)}) collective-permute-start(bf16[112,2048]{1,0:T(8,128)(2,1)} %slice.32), channel_id=1, source_target_pairs={{0,448},{64,0},{128,64},{192,128},{256,192},{320,256},{384,320},{4... | collective-permute-start | bytes 1376264 | tf_op jit(solution)/shard_map/ppermute | solution.py:433
  89.3 15.7 %collective-permute-start.6 = (bf16[112,2048]{1,0:T(8,128)(2,1)}, bf16[112,2048]{1,0:T(8,128)(2,1)}, u32[]{:S(2)}, u32[]{:S(2)}) collective-permute-start(bf16[112,2048]{1,0:T(8,128)(2,1)} %slice.31), channel_id=1, source_target_pairs={{0,64},{64,128},{128,192},{192,256},{256,320},{320,384},{384,448},... | collective-permute-start | bytes 1376264 | tf_op jit(solution)/shard_map/ppermute | solution.py:433
  109.1 45.4 %all-to-all-start.1 = ((bf16[64,2,4096]{2,1,0:T(2,128)(2,1)}), bf16[64,2,4096]{2,1,0:T(2,128)(2,1)}, u32[]{:S(2)}, u32[]{:S(2)}) async-start(bf16[64,2,4096]{2,1,0:T(2,128)(2,1)} %bitcast.19.after_ref), calls=%async_computation.1 | async-start | bytes 2097152 | tf_op jit(solution)/shard_map/all_to_all | solution.py:475
  132.7 23.2 %copy-start.3 = (bf16[16,2048]{1,0:T(8,128)(2,1)S(1)}, bf16[16,2048]{1,0:T(8,128)(2,1)}, u32[]{:S(2)}) copy-start(bf16[16,2048]{1,0:T(8,128)(2,1)} %cot_ref.5) | copy-start | bytes 196612
  132.7 23.2 %copy-start.5 = (s32[16,8]{0,1:T(8,128)S(1)}, s32[16,8]{0,1:T(8,128)}, u32[]{:S(2)}) copy-start(s32[16,8]{0,1:T(8,128)} %param.9) | copy-start | bytes 1540
  132.7 23.2 %copy-start.6 = (f32[16,8]{0,1:T(8,128)S(1)}, f32[16,8]{0,1:T(8,128)}, u32[]{:S(2)}) copy-start(f32[16,8]{0,1:T(8,128)} %param.8) | copy-start | bytes 1540

commit v6 on v5

--- a/solution.py
+++ b/solution.py
@@ -28,10 +28,11 @@
     return lax.dot_general(a, b, (((0,), (0,)), ((), ())), preferred_element_type=F32)
 
 
-def slot_maps(ids, slots, capacity):
+def slot_maps(ids, slots, capacity, slot_major=False):
     top_count, tok_rows = ids.shape
     slot = lax.broadcasted_iota(I32, (slots, tok_rows), 0)
-    expert = slot // capacity
+    experts = slots // capacity
+    expert, within = (slot % experts, slot // experts) if slot_major else (slot // capacity, slot % capacity)
     named = jnp.zeros((slots, tok_rows), F32)
     for k in range(top_count):
         named = named + (ids[k : k + 1, :] == expert).astype(F32)
@@ -42,8 +43,8 @@
         < lax.broadcasted_iota(I32, (tok_rows, tok_rows), 1)
     ).astype(BF16)
     rank = matmul(named.astype(BF16), earlier)
-    cold = named * (1.0 - is_hot) * (rank == (slot % capacity).astype(F32)).astype(F32)
-    first = is_hot * (slot[:, :1] % capacity == 0).astype(F32)
+    cold = named * (1.0 - is_hot) * (rank == within.astype(F32)).astype(F32)
+    first = is_hot * (within[:, :1] == 0).astype(F32)
     hot_token = jnp.sum(named * first, 0, keepdims=True)
     hot_rank = jnp.sum(rank * first, 0, keepdims=True)
     hot_row = lax.broadcasted_iota(I32, (HOT_PAD, tok_rows), 0).astype(F32)
@@ -223,19 +224,32 @@
     )(arrived, *map(outside, pieces))
 
 
-def last_kernel(units, rows_ref, acc_ref, up_ref, down_ref, out_ref):
+def last_kernel(units, rows_ref, acc_ref, up_ref, down_ref, out_ref, wide):
     width = up_ref.shape[1]
+    experts, lines, _ = out_ref.shape
+    capacity = rows_ref.shape[0] // experts
+    blocks = lines // capacity
     up, down = up_ref[:units, :], down_ref[:units, :]
     tok, cot = rows_ref[:, :width], rows_ref[:, width:]
     hidden, act_grad = activations(matmul_nt(tok, up), matmul_nt(cot, down))
-    out_ref[:, :width] = (acc_ref[:, :width] + matmul(hidden, down)).astype(BF16)
-    out_ref[:, width:] = (acc_ref[:, width:] + matmul(act_grad, up)).astype(BF16)
-
-
-def last(rows, acc, up_half, down_half, units):
+    for part, (acts, weights) in enumerate(((hidden, down), (act_grad, up))):
+        sums = acc_ref[:, part * width : (part + 1) * width] + matmul(acts, weights)
+        for b in range(width // 128):
+            line = part * (width // 128) + b
+            for r in range(capacity):
+                wide[pl.ds(r * blocks + line, experts, stride=lines), :] = sums[
+                    r * experts : (r + 1) * experts, b * 128 : (b + 1) * 128
+                ]
+    for e in range(experts):
+        out_ref[e] = wide[e * lines : (e + 1) * lines, :].astype(BF16)
+
+
+def last(rows, acc, up_half, down_half, units, experts):
+    lines = rows.shape[0] * rows.shape[1] // (experts * 128)
     return pl.pallas_call(
         functools.partial(last_kernel, units),
-        out_shape=jax.ShapeDtypeStruct(rows.shape, BF16),
+        out_shape=jax.ShapeDtypeStruct((experts, lines, 128), BF16),
+        scratch_shapes=[pltpu.VMEM((experts * lines, 128), F32)],
         compiler_params=pltpu.CompilerParams(vmem_limit_bytes=VMEM_LIMIT),
         name="last",
     )(rows, acc, up_half, down_half)
@@ -321,32 +335,44 @@
     return first, second, third
 
 
-def cold_kernel(capacity, ids_ref, gate_ref, cot_ref, cold_ref, sum_ref, dots_ref):
+def cold_kernel(capacity, ids_ref, gate_ref, cot_ref, cold_ref, sum_ref, dots_ref, wide, rows):
     ids, gates, cot = ids_ref[...], gate_ref[...], cot_ref[...]
     top_count = ids.shape[0]
-    slots = cold_ref.shape[0]
+    experts, lines, _ = cold_ref.shape
+    blocks = lines // capacity
     width = cot.shape[1]
-    cold, _, expert, _, _ = slot_maps(ids, slots, capacity)
+    for e in range(experts):
+        wide[e * lines : (e + 1) * lines, :] = cold_ref[e].astype(F32)
+    for r in range(capacity):
+        for b in range(blocks):
+            line = wide[pl.ds(r * blocks + b, experts, stride=lines), :]
+            rows[r * experts : (r + 1) * experts, b * 128 : (b + 1) * 128] = line.astype(BF16)
+    cold, _, expert, _, _ = slot_maps(ids, experts * capacity, capacity, slot_major=True)
     per_slot = jnp.zeros(cold.shape, F32)
     for k in range(top_count):
         per_slot = per_slot + jnp.where(ids[k : k + 1, :] == expert, gates[k : k + 1, :], 0.0)
     scale = thirds(jnp.where(cold > 0, per_slot, 0.0))
     for lo in (0, width):
-        rows = cold_ref[:, lo : lo + width]
-        sum_ref[:, lo : lo + width] = matmul_tn(scale[0], rows) + matmul_tn(scale[1], rows) + matmul_tn(scale[2], rows)
-    dots = jnp.where(cold > 0, matmul_nt(cold_ref[:, :width], cot), 0.0)
+        part = rows[:, lo : lo + width]
+        sum_ref[:, lo : lo + width] = matmul_tn(scale[0], part) + matmul_tn(scale[1], part) + matmul_tn(scale[2], part)
+    dots = jnp.where(cold > 0, matmul_nt(rows[:, :width], cot), 0.0)
     for k in range(top_count):
         dots_ref[k : k + 1, :] = jnp.sum(jnp.where(ids[k : k + 1, :] == expert, dots, 0.0), 0, keepdims=True)
 
 
 def cold_combine(ids, gates, cotangent, results, capacity):
     tok_rows, width = cotangent.shape
+    experts, lines, _ = results.shape
     return pl.pallas_call(
         functools.partial(cold_kernel, capacity),
         out_shape=(
             jax.ShapeDtypeStruct((tok_rows, 2 * width), F32),
             jax.ShapeDtypeStruct(gates.shape, F32),
         ),
+        scratch_shapes=[
+            pltpu.VMEM((experts * lines, 128), F32),
+            pltpu.VMEM((experts * capacity, 2 * width), BF16),
+        ],
         compiler_params=pltpu.CompilerParams(vmem_limit_bytes=VMEM_LIMIT),
         cost_estimate=pl.CostEstimate(flops=1 << 36, bytes_accessed=1 << 26, transcendentals=0),
         name="cold_combine",
@@ -354,8 +380,9 @@
 
 
 def final_kernel(
-    capacity, slots, ids_ref, gate_ref, cot_ref, sum_ref, dots_ref, kept_ref, sent_ref, mix_ref, grad_ref, gate_grad_ref
+    capacity, slots, ids_ref, gate_ref, cot_ref, sum_ref, dots_ref, kept_ref, *refs
 ):
+    sent, (mix_ref, grad_ref, gate_grad_ref) = refs[:-3], refs[-3:]
     ids, gates, cot = ids_ref[...], gate_ref[...], cot_ref[...]
     top_count, tok_rows = ids.shape
     width = cot.shape[1]
@@ -367,7 +394,10 @@
         gate = gate + jnp.where(ids[k : k + 1, :] == hottest, gates[k : k + 1, :], 0.0)
     hot = hot[:hot_rows]
     scale = thirds(jnp.where(hot > 0, gate, 0.0))
-    result = (kept_ref[...] + sent_ref[...].astype(F32)).astype(BF16)
+    result = kept_ref[...]
+    for ref in sent:
+        result = result + ref[...].astype(F32)
+    result = result.astype(BF16)
     for lo, out_ref in ((0, mix_ref), (width, grad_ref)):
         rows = result[:, lo : lo + width]
         total = matmul_tn(scale[0], rows) + matmul_tn(scale[1], rows) + matmul_tn(scale[2], rows)
@@ -387,7 +417,7 @@
         ),
         compiler_params=pltpu.CompilerParams(vmem_limit_bytes=VMEM_LIMIT),
         name="final_combine",
-    )(ids, gates, cotangent, sums, dots, kept, sent)
+    )(ids, gates, cotangent, sums, dots, kept, *sent)
 
 
 TICK = pl.CostEstimate(flops=1 << 35, bytes_accessed=1 << 25, transcendentals=0)
@@ -410,22 +440,33 @@
     )(token, *after)
 
 
-def gate_kernel(*refs):
-    pass
-
-
-def gate(*arrays):
-    anywhere = pl.BlockSpec(memory_space=pl.ANY)
-    return pl.pallas_call(
-        gate_kernel,
-        out_shape=tuple(jax.ShapeDtypeStruct(x.shape, x.dtype) for x in arrays),
-        in_specs=[anywhere] * len(arrays),
-        out_specs=tuple([anywhere] * len(arrays)),
-        input_output_aliases={i: i for i in range(len(arrays))},
-        compiler_params=pltpu.CompilerParams(vmem_limit_bytes=1 << 20),
+def split_kernel(right_ref, left_ref, right_out, left_out, top_ref, bottom_ref, sems):
+    half = top_ref.shape[0]
+    copies = [
+        pltpu.make_async_copy(right_ref.at[pl.ds(0, half)], top_ref, sems.at[0]),
+        pltpu.make_async_copy(left_ref.at[pl.ds(half, half)], bottom_ref, sems.at[1]),
+    ]
+    for copy in copies:
+        copy.start()
+    for copy in copies:
+        copy.wait()
+
+
+def split(right, left):
+    anywhere, inside = pl.BlockSpec(memory_space=pl.ANY), pl.BlockSpec(memory_space=pltpu.VMEM)
+    whole = jax.ShapeDtypeStruct(right.shape, right.dtype)
+    part = jax.ShapeDtypeStruct((right.shape[0] // 2, right.shape[1]), right.dtype)
+    return pl.pallas_call(
+        split_kernel,
+        out_shape=(whole, whole, part, part),
+        in_specs=[anywhere] * 2,
+        out_specs=(anywhere, anywhere, inside, inside),
+        input_output_aliases={0: 0, 1: 1},
+        scratch_shapes=[pltpu.SemaphoreType.DMA((2,))],
+        compiler_params=pltpu.CompilerParams(vmem_limit_bytes=1 << 22),
         cost_estimate=TICK,
-        name="gate",
-    )(*arrays)
+        name="split",
+    )(right, left)
 
 
 def shift(x, by):
@@ -438,6 +479,11 @@
     pairs = [[i, i ^ bit] for i in range(ring) if not i & bit]
     both = lax.all_gather(x, "dp", axis=0, axis_index_groups=pairs, tiled=False)
     return jnp.where(lax.axis_index("dp") & bit == 0, both[1], both[0])
+
+
+def send_on(x, bits):
+    ring = lax.axis_size("dp")
+    return lax.ppermute(x, "dp", [(i, i ^ bits) for i in range(ring)])
 
 
 def shards(tokens, cotangent, gate_probs, expert_ids, up_weight, down_weight):
@@ -458,11 +504,11 @@
         r, l = shift(right[-1], 1), shift(left[-1], -1)
         if step == 1:
             token = tick(hottest, r, l)
-        if step in (2,):
-            r, l = gate(r, l)
+        if step == 2:
+            r, l, top, bottom = split(r, l)
         right.append(r)
         left.append(l)
-    far_up, far_down = shift(right[-1][:half], 1), shift(left[-1][half:], -1)
+    far_up, far_down = shift(top, 1), shift(bottom, -1)
 
     lines = capacity * 2 * width // 128
     outgoing = assemble(outgoing.reshape(experts, lines, 128), up, down)
@@ -470,22 +516,17 @@
     hot_pieces = lax.all_to_all(repeat(token, arrived, lines), "expert", 0, 0, tiled=True)
 
     acc, rows = gathered(arrived, [own] + right[1:] + left[1:], units, slots)
-    results = last(rows, acc, far_up, far_down, units)
-    results = results.reshape(capacity, experts, 2 * width).transpose(1, 0, 2)
-    came_back = lax.all_to_all(results, "expert", 0, 0, tiled=True).reshape(slots, 2 * width)
+    results = last(rows, acc, far_up, far_down, units, experts)
+    came_back = lax.all_to_all(results, "expert", 0, 0, tiled=True)
 
     blocks = left + [(far_up, far_down)] + right[:0:-1]
     here = lax.axis_index("dp").astype(I32).reshape(1)
     send, keep = hot_partials(here, hot_pieces, blocks, units, hot_rows, results)
     both = keep.astype(F32) + swap(send, 1).astype(F32)
-    kept, onward = both[:hot_rows], both[hot_rows:].astype(BF16)
-    ring = lax.axis_size("dp")
-    parity = [[i for i in range(ring) if i % 2 == odd] for odd in range(2)]
-    quad = lax.all_gather(onward, "dp", axis=0, axis_index_groups=parity, tiled=False)
-    sent = jnp.zeros(kept.shape, F32)
-    for i, place in enumerate((4, 2, 6)):
-        theirs = lax.dynamic_index_in_dim(quad, (here[0] ^ place) // 2, 0, keepdims=False)
-        sent = sent + theirs[i * hot_rows : (i + 1) * hot_rows].astype(F32)
+    kept = both[:hot_rows]
+    sent = [
+        send_on(both[i * hot_rows : (i + 1) * hot_rows].astype(BF16), place) for i, place in ((1, 4), (2, 2), (3, 6))
+    ]
     sums, dots = cold_combine(ids, gates, cotangent, came_back, capacity)
     mixture, input_grad, gate_grad = final_combine(
         ids, gates, cotangent, sums, dots, kept, sent, slots, capacity

time: 159 us -> 150 us (0.943)
  blocking collectives: 32 us -> 10.4 us
  starting transfers between devices: 61.1 us -> 75.2 us
  local copies, waits for them, and re-layouts: 9.98 us -> 3.48 us
  Pallas kernels: 17.3 us -> 20.6 us
  waiting for transfers between devices: 36.5 us -> 38.4 us
    all_gather x1 -> x0, blocking collectives: 21.6 us -> none  [shards(): lax.all_gather(onward, 'dp', axis=0, axis_index_groups=parity, tiled=False)]
    ppermute x0 -> x3, starting transfers between devices: none -> 12.4 us  [send_on(): return lax.ppermute(x, 'dp', [(i, i ^ bits) for i in range(ring)])]
    ppermute x0 -> x3, waiting for transfers between devices: none -> 5.38 us  [send_on(): return lax.ppermute(x, 'dp', [(i, i ^ bits) for i in range(ring)])]
    ppermute x8, waiting for transfers between devices: 27.6 us -> 22.5 us  [shift(): return lax.ppermute(x, 'dp', [(i, (i + by) % ring) for i in range(ring)])]
    reshape x2 -> x0, local copies, waits for them, and re-layouts: 3.58 us -> none  [the longest x1 2.11 us: shards(): results = results.reshape(capacity, experts, 2 * width).transpose(1, 0, 2)]
    slice x3 -> x2, local copies, waits for them, and re-layouts: 2.98 us -> 0.1 us  [the longest x1 0.08 us: shards(): both[i * hot_rows:(i + 1) * hot_rows].astype(BF16)]
  transfers between devices with their start and end apart: 11 -> 14, of which waited for: 6 -> 9; matrix products, arithmetic and copies ran while one was open for 4% -> 1% of each run, Pallas kernels for 8% -> 12%
where the time goes in v6:
time: 150 us; the launch traced here: 149 us
  starting transfers between devices  75.2 us (50%)
  waiting for transfers between devices  38.4 us (26%)
  Pallas kernels  20.6 us (14%)
  blocking collectives  10.4 us (7%)
  local copies, waits for them, and re-layouts  3.48 us (2%)
    ppermute x8, starting transfers between devices, shift(): return lax.ppermute(x, 'dp', [(i, (i + by) % ring) for i in range(ring)])  29.5 us
    ppermute x8, waiting for transfers between devices, shift(): return lax.ppermute(x, 'dp', [(i, (i + by) % ring) for i in range(ring)])  22.5 us
    all_to_all x1, starting transfers between devices, shards(): arrived = lax.all_to_all(outgoing, 'expert', 0, 0, tiled=True)  14 us
    ppermute x3, starting transfers between devices, send_on(): return lax.ppermute(x, 'dp', [(i, i ^ bits) for i in range(ring)])  12.4 us
    all_to_all x1, starting transfers between devices, shards(): came_back = lax.all_to_all(results, 'expert', 0, 0, tiled=True)  11 us
    all_gather x1, blocking collectives, swap(): both = lax.all_gather(x, 'dp', axis=0, axis_index_groups=pairs, tiled=False)  10.4 us
    all_to_all x1, waiting for transfers between devices, shards(): arrived = lax.all_to_all(outgoing, 'expert', 0, 0, tiled=True)  9 us
    all_to_all x1, starting transfers between devices, shards(): lax.all_to_all(repeat(token, arrived, lines), 'expert', 0, 0, tiled=True)  8.39 us
  transfers between devices with their start and end apart: 14, of which 9 were waited for; matrix products, arithmetic and copies ran while one was open for 1% of the time, Pallas kernels for 12%

profile of v6, /device:TPU:6, one launch (start us, length us, event | category | flops | bytes accessed | tf_op | source)
XLA Modules:
  0.0 149.2 jit_solution(8566407063883128337)
XLA Ops:
  0.6 0.0 copy-start.7
  0.6 0.7 copy-done.7
  1.3 1.9 %route.1 = (bf16[128,4096]{1,0:T(8,128)(2,1)S(1)}, bf16[224,2048]{1,0:T(8,128)(2,1)S(1)}, s32[1,1]{1,0:T(1,128)}) custom-call(s32[8,16]{1,0:T(8,128)S(1)} %bitcast.14, bf16[16,2048]{1,0:T(8,128)(2,1)} %tok_ref.1, bf16[16,2048]{1,0:T(8,128)(2,1)} %cot_ref.5, bf16[96,2048]{1,0:T(8,128)(2,1)} %bitcast.19, bf16[96,2048]{1,0:T(8,128)(2,1)} %bitcast.21), custom_call_target="tpu_custom_call" | custom-call | tf_op jit(solution)/shard_map/route/pallas_call | solution.py:87
  3.2 0.0 copy-start.1
  3.2 5.4 %collective-permute-start.3 = (bf16[224,2048]{1,0:T(8,128)(2,1)S(1)}, bf16[224,2048]{1,0:T(8,128)(2,1)}, u32[]{:S(2)}, u32[]{:S(2)}) collective-permute-start(bf16[224,2048]{1,0:T(8,128)(2,1)S(1)} %get-tuple-element.20.refs_0_), channel_id=1, source_target_pairs={{0,448},{64,0},{128,64},{192,128},{256,192},{320,256},{384,320},{4... | collective-permute-start | bytes 2752520 | tf_op jit(solution)/shard_map/ppermute | solution.py:474
  8.6 1.9 %collective-permute-start = (bf16[224,2048]{1,0:T(8,128)(2,1)S(1)}, bf16[224,2048]{1,0:T(8,128)(2,1)}, u32[]{:S(2)}, u32[]{:S(2)}) collective-permute-start(bf16[224,2048]{1,0:T(8,128)(2,1)S(1)} %get-tuple-element.20.refs_0_), channel_id=1, source_target_pairs={{0,64},{64,128},{128,192},{192,256},{256,320},{320,384},{384,448},... | collective-permute-start | bytes 2752520 | tf_op jit(solution)/shard_map/ppermute | solution.py:474
  10.5 0.5 reshape.16.rows_ref
  11.1 1.2 assemble.1
  12.3 0.0 copy-done.1
  12.3 0.0 copy-start
  12.3 1.3 copy-done
  13.5 14.0 %all-to-all-start = ((bf16[64,112,128]{2,1,0:T(8,128)(2,1)}), bf16[64,112,128]{2,1,0:T(8,128)(2,1)S(1)}, u32[]{:S(2)}, u32[]{:S(2)}) async-start(bf16[64,112,128]{2,1,0:T(8,128)(2,1)} %copy-done), calls=%async_computation | async-start | bytes 3670016 | tf_op jit(solution)/shard_map/all_to_all | solution.py:515
  27.6 0.6 collective-permute-done.3.refs_4_.refs_1_
  28.2 5.7 %collective-permute-start.4 = (bf16[224,2048]{1,0:T(8,128)(2,1)}, bf16[224,2048]{1,0:T(8,128)(2,1)}, u32[]{:S(2)}, u32[]{:S(2)}) collective-permute-start(bf16[224,2048]{1,0:T(8,128)(2,1)} %collective-permute-done.3.refs_4_.refs_1_), channel_id=1, source_target_pairs={{0,448},{64,0},{128,64},{192,128},{256,192},{320,256},{384,320},{4... | collective-permute-start | bytes 2752520 | tf_op jit(solution)/shard_map/ppermute | solution.py:474
  33.9 0.0 collective-permute-done.refs_1_.refs_8_
  33.9 1.9 %collective-permute-start.1 = (bf16[224,2048]{1,0:T(8,128)(2,1)}, bf16[224,2048]{1,0:T(8,128)(2,1)S(1)}, u32[]{:S(2)}, u32[]{:S(2)}) collective-permute-start(bf16[224,2048]{1,0:T(8,128)(2,1)} %collective-permute-done.refs_1_.refs_8_), channel_id=1, source_target_pairs={{0,64},{64,128},{128,192},{192,256},{256,320},{320,384},{384,448},... | collective-permute-start | bytes 2752520 | tf_op jit(solution)/shard_map/ppermute | solution.py:474
  35.8 17.1 %collective-permute-done.4.refs_5_.refs_1_.refs_2_ = bf16[224,2048]{1,0:T(8,128)(2,1)} collective-permute-done((bf16[224,2048]{1,0:T(8,128)(2,1)}, bf16[224,2048]{1,0:T(8,128)(2,1)}, u32[]{:S(2)}, u32[]{:S(2)}) %collective-permute-start.4) | collective-permute-done | bytes 917536 | tf_op jit(solution)/shard_map/ppermute | solution.py:474
  52.9 5.6 %collective-permute-start.5 = (bf16[224,2048]{1,0:T(8,128)(2,1)}, bf16[224,2048]{1,0:T(8,128)(2,1)}, u32[]{:S(2)}, u32[]{:S(2)}) collective-permute-start(bf16[224,2048]{1,0:T(8,128)(2,1)} %collective-permute-done.4.refs_5_.refs_1_.refs_2_), channel_id=1, source_target_pairs={{0,448},{64,0},{128,64},{192,128},{256,192},{320,256},{384,320},{4... | collective-permute-start | bytes 2752520 | tf_op jit(solution)/shard_map/ppermute | solution.py:474
  58.5 0.0 collective-permute-done.1.refs_2_.refs_0_.refs_7_
  58.6 0.0 copy-start.2
  58.6 1.9 %collective-permute-start.2 = (bf16[224,2048]{1,0:T(8,128)(2,1)S(1)}, bf16[224,2048]{1,0:T(8,128)(2,1)}, u32[]{:S(2)}, u32[]{:S(2)}) collective-permute-start(bf16[224,2048]{1,0:T(8,128)(2,1)S(1)} %collective-permute-done.1.refs_2_.refs_0_.refs_7_), channel_id=1, source_target_pairs={{0,64},{64,128},{128,192},{192,256},{256,320},{320,384},{384,448},... | collective-permute-start | bytes 2752520 | tf_op jit(solution)/shard_map/ppermute | solution.py:474
  60.5 1.2 tick.1.hottest_ref
  61.7 0.0 copy-done.2
  61.7 9.0 %all-to-all-done.arrived_ref = bf16[64,112,128]{2,1,0:T(8,128)(2,1)S(1)} async-done(((bf16[64,112,128]{2,1,0:T(8,128)(2,1)}), bf16[64,112,128]{2,1,0:T(8,128)(2,1)S(1)}, u32[]{:S(2)}, u32[]{:S(2)}) %all-to-all-start) | async-done | bytes 1835040 | tf_op jit(solution)/shard_map/all_to_all | solution.py:515
  70.7 0.7 repeat.1
  71.4 0.0 copy-start.3
  71.4 0.9 copy-done.3
  72.3 8.4 %all-to-all-start.2 = ((bf16[64,48,128]{2,1,0:T(8,128)(2,1)}), bf16[64,48,128]{2,1,0:T(8,128)(2,1)S(1)}, u32[]{:S(2)}, u32[]{:S(2)}) async-start(bf16[64,48,128]{2,1,0:T(8,128)(2,1)} %copy-done.3), calls=%async_computation.2 | async-start | bytes 1572864 | tf_op jit(solution)/shard_map/all_to_all | solution.py:516
  80.7 0.0 collective-permute-done.5.left_ref
  80.7 1.1 collective-permute-done.2.right_ref
  81.8 1.2 split.1
  83.0 1.9 %collective-permute-start.6 = (bf16[112,2048]{1,0:T(8,128)(2,1)S(1)}, bf16[112,2048]{1,0:T(8,128)(2,1)S(1)}, u32[]{:S(2)}, u32[]{:S(2)}) collective-permute-start(bf16[112,2048]{1,0:T(8,128)(2,1)S(1)} %get-tuple-element.25), channel_id=1, source_target_pairs={{0,64},{64,128},{128,192},{192,256},{256,320},{320,384},{384,448},... | collective-permute-start | bytes 1376264 | tf_op jit(solution)/shard_map/ppermute | solution.py:474
  84.9 5.1 %collective-permute-start.7 = (bf16[112,2048]{1,0:T(8,128)(2,1)S(1)}, bf16[112,2048]{1,0:T(8,128)(2,1)S(1)}, u32[]{:S(2)}, u32[]{:S(2)}) collective-permute-start(bf16[112,2048]{1,0:T(8,128)(2,1)S(1)} %get-tuple-element.26), channel_id=1, source_target_pairs={{0,448},{64,0},{128,64},{192,128},{256,192},{320,256},{384,320},{4... | collective-permute-start | bytes 1376264 | tf_op jit(solution)/shard_map/ppermute | solution.py:474
  90.1 5.3 %gathered.1 = (f32[128,4096]{1,0:T(8,128)S(1)}, bf16[128,4096]{1,0:T(8,128)(2,1)S(1)}) custom-call(bf16[64,112,128]{2,1,0:T(8,128)(2,1)S(1)} %all-to-all-done.arrived_ref, bf16[224,2048]{1,0:T(8,128)(2,1)} %copy-done.1, bf16[224,2048]{1,0:T(8,128)(2,1)} %collective-permute-done.refs_1_.refs_8_, bf16[224,2048]{1,0:T(8,128)(2,1)} %copy-done.2, ...), custom_call_target="tpu_custom_call" | custom-call | flops 1409286144 | bytes 5505024 | tf_op jit(solution)/shard_map/gathered/pallas_call | solution.py:203
  95.4 2.5 %collective-permute-done.6.up_ref.refs_4_ = bf16[112,2048]{1,0:T(8,128)(2,1)S(1)} collective-permute-done((bf16[112,2048]{1,0:T(8,128)(2,1)S(1)}, bf16[112,2048]{1,0:T(8,128)(2,1)S(1)}, u32[]{:S(2)}, u32[]{:S(2)}) %collective-permute-start.6) | collective-permute-done | bytes 458784 | tf_op jit(solution)/shard_map/ppermute | solution.py:474
  97.9 0.0 copy-start.4
  97.9 1.2 collective-permute-done.7.down_ref.refs_5_
  99.1 0.0 copy-start.5
  99.1 3.0 %last.1.after_ref = bf16[64,64,128]{2,1,0:T(8,128)(2,1)} custom-call(bf16[128,4096]{1,0:T(8,128)(2,1)S(1)} %get-tuple-element.23.rows_ref, f32[128,4096]{1,0:T(8,128)S(1)} %get-tuple-element.24.acc_ref, bf16[112,2048]{1,0:T(8,128)(2,1)S(1)} %collective-permute-done.6.up_ref.refs_4_, bf16[112,2048]{1,0:T(8,128)(2,1)S(1)} %collective-permute-done.7.down_ref.refs_5_), custom_call_target="tpu_custom_call" | custom-call | tf_op jit(solution)/shard_map/last/pallas_call | solution.py:249
  102.1 0.0 copy-done.4
  102.1 0.0 copy-done.5
  102.1 0.5 all-to-all-done.2.pieces_ref
  102.6 11.0 %all-to-all-start.1 = ((bf16[64,64,128]{2,1,0:T(8,128)(2,1)}), bf16[64,64,128]{2,1,0:T(8,128)(2,1)S(1)}, u32[]{:S(2)}, u32[]{:S(2)}) async-start(bf16[64,64,128]{2,1,0:T(8,128)(2,1)} %last.1.after_ref), calls=%async_computation.1 | async-start | bytes 2097152 | tf_op jit(solution)/shard_map/all_to_all | solution.py:520
  113.6 2.5 %hot.1 = (bf16[36,4096]{1,0:T(8,128)(2,1)S(1)}, bf16[36,4096]{1,0:T(8,128)(2,1)S(1)}) custom-call(s32[1]{0:T(128)} %bitcast.4.where_ref, bf16[64,48,128]{2,1,0:T(8,128)(2,1)S(1)} %all-to-all-done.2.pieces_ref, bf16[64,64,128]{2,1,0:T(8,128)(2,1)} %last.1.after_ref, bf16[224,2048]{1,0:T(8,128)(2,1)} %copy-done.1, ...), custom_call_target="tpu_custom_call" | custom-call | tf_op jit(solution)/shard_map/hot/pallas_call | solution.py:313
  116.1 10.4 %all-gather.1 = bf16[2,36,4096]{2,1,0:T(8,128)(2,1)S(1)} all-gather(bf16[1,36,4096]{2,1,0:T(8,128)(2,1)S(1)} %bitcast.13), channel_id=2, replica_groups={{0,64},{128,192},{256,320},{384,448},{1,65},{129,193},{257,321},{385,44..., dimensions={0}, use_global_device_ids=true | all-gather | bytes 884736 | tf_op jit(solution)/shard_map/all_gather | solution.py:480
  126.5 0.0 copy-start.6
  126.5 0.0 copy-start.8
  126.5 0.0 copy-start.9
  126.5 0.1 fusion.1
  126.6 0.1 fusion.2
  126.7 5.3 %collective-permute-start.10 = (bf16[9,4096]{1,0:T(8,128)(2,1)S(1)}, bf16[9,4096]{1,0:T(8,128)(2,1)S(1)}, u32[]{:S(2)}, u32[]{:S(2)}) collective-permute-start(bf16[9,4096]{1,0:T(8,128)(2,1)S(1)} %get-tuple-element.37), channel_id=1, source_target_pairs={{0,384},{64,448},{128,256},{192,320},{256,128},{320,192},{384,0},{... | collective-permute-start | bytes 221192 | tf_op jit(solution)/shard_map/ppermute | solution.py:486
  132.0 2.0 %collective-permute-start.9 = (bf16[9,4096]{1,0:T(8,128)(2,1)S(1)}, bf16[9,4096]{1,0:T(8,128)(2,1)S(1)}, u32[]{:S(2)}, u32[]{:S(2)}) collective-permute-start(bf16[9,4096]{1,0:T(8,128)(2,1)S(1)} %get-tuple-element.38), channel_id=1, source_target_pairs={{0,128},{64,192},{128,0},{192,64},{256,384},{320,448},{384,256},{4... | collective-permute-start | bytes 221192 | tf_op jit(solution)/shard_map/ppermute | solution.py:486
  134.1 5.1 %collective-permute-start.8 = (bf16[9,4096]{1,0:T(8,128)(2,1)S(1)}, bf16[9,4096]{1,0:T(8,128)(2,1)S(1)}, u32[]{:S(2)}, u32[]{:S(2)}) collective-permute-start(bf16[9,4096]{1,0:T(8,128)(2,1)S(1)} %get-tuple-element.39), channel_id=1, source_target_pairs={{0,256},{64,320},{128,384},{192,448},{256,0},{320,64},{384,128},{4... | collective-permute-start | bytes 221192 | tf_op jit(solution)/shard_map/ppermute | solution.py:486
  139.2 1.1 all-to-all-done.1.cold_ref
  140.2 0.0 copy-done.6
  140.2 0.0 copy-done.8
  140.2 0.0 copy-done.9
  140.3 2.4 %cold_combine.1 = (f32[16,4096]{1,0:T(8,128)S(1)}, f32[8,16]{1,0:T(8,128)S(1)}) custom-call(s32[8,16]{1,0:T(8,128)S(1)} %bitcast.15, f32[8,16]{1,0:T(8,128)S(1)} %bitcast.17, bf16[16,2048]{1,0:T(8,128)(2,1)S(1)} %copy-done.6, bf16[64,64,128]{2,1,0:T(8,128)(2,1)S(1)} %all-to-all-done.1.cold_ref), custom_call_target="tpu_custom_call" | custom-call | flops 68719476736 | bytes 67108864 | tf_op jit(solution)/shard_map/cold_combine/pallas_call | solution.py:366
  142.6 0.0 collective-permute-done.10.refs_2_
  142.6 5.4 %collective-permute-done.9.refs_1_ = bf16[9,4096]{1,0:T(8,128)(2,1)S(1)} collective-permute-done((bf16[9,4096]{1,0:T(8,128)(2,1)S(1)}, bf16[9,4096]{1,0:T(8,128)(2,1)S(1)}, u32[]{:S(2)}, u32[]{:S(2)}) %collective-permute-start.9) | collective-permute-done | bytes 73760 | tf_op jit(solution)/shard_map/ppermute | solution.py:486
  148.0 0.0 collective-permute-done.8.refs_0_
  148.0 1.2 final_combine.1
  (1 shorter events, 0.0 us)
Async XLA Ops:
  0.6 0.7 copy-start.7
  3.2 9.1 %copy-start.1 = (bf16[224,2048]{1,0:T(8,128)(2,1)}, bf16[224,2048]{1,0:T(8,128)(2,1)S(1)}, u32[]{:S(2)}) copy-start(bf16[224,2048]{1,0:T(8,128)(2,1)S(1)} %get-tuple-element.20.refs_0_) | copy-start | bytes 2752516
  3.2 25.0 %collective-permute-start.3 = (bf16[224,2048]{1,0:T(8,128)(2,1)S(1)}, bf16[224,2048]{1,0:T(8,128)(2,1)}, u32[]{:S(2)}, u32[]{:S(2)}) collective-permute-start(bf16[224,2048]{1,0:T(8,128)(2,1)S(1)} %get-tuple-element.20.refs_0_), channel_id=1, source_target_pairs={{0,448},{64,0},{128,64},{192,128},{256,192},{320,256},{384,320},{4... | collective-permute-start | bytes 2752520 | tf_op jit(solution)/shard_map/ppermute | solution.py:474
  8.6 25.3 %collective-permute-start = (bf16[224,2048]{1,0:T(8,128)(2,1)S(1)}, bf16[224,2048]{1,0:T(8,128)(2,1)}, u32[]{:S(2)}, u32[]{:S(2)}) collective-permute-start(bf16[224,2048]{1,0:T(8,128)(2,1)S(1)} %get-tuple-element.20.refs_0_), channel_id=1, source_target_pairs={{0,64},{64,128},{128,192},{192,256},{256,320},{320,384},{384,448},... | collective-permute-start | bytes 2752520 | tf_op jit(solution)/shard_map/ppermute | solution.py:474
  12.3 1.3 copy-start
  13.5 57.1 %all-to-all-start = ((bf16[64,112,128]{2,1,0:T(8,128)(2,1)}), bf16[64,112,128]{2,1,0:T(8,128)(2,1)S(1)}, u32[]{:S(2)}, u32[]{:S(2)}) async-start(bf16[64,112,128]{2,1,0:T(8,128)(2,1)} %copy-done), calls=%async_computation | async-start | bytes 3670016 | tf_op jit(solution)/shard_map/all_to_all | solution.py:515
  28.2 24.8 %collective-permute-start.4 = (bf16[224,2048]{1,0:T(8,128)(2,1)}, bf16[224,2048]{1,0:T(8,128)(2,1)}, u32[]{:S(2)}, u32[]{:S(2)}) collective-permute-start(bf16[224,2048]{1,0:T(8,128)(2,1)} %collective-permute-done.3.refs_4_.refs_1_), channel_id=1, source_target_pairs={{0,448},{64,0},{128,64},{192,128},{256,192},{320,256},{384,320},{4... | collective-permute-start | bytes 2752520 | tf_op jit(solution)/shard_map/ppermute | solution.py:474
  33.9 24.6 %collective-permute-start.1 = (bf16[224,2048]{1,0:T(8,128)(2,1)}, bf16[224,2048]{1,0:T(8,128)(2,1)S(1)}, u32[]{:S(2)}, u32[]{:S(2)}) collective-permute-start(bf16[224,2048]{1,0:T(8,128)(2,1)} %collective-permute-done.refs_1_.refs_8_), channel_id=1, source_target_pairs={{0,64},{64,128},{128,192},{192,256},{256,320},{320,384},{384,448},... | collective-permute-start | bytes 2752520 | tf_op jit(solution)/shard_map/ppermute | solution.py:474
  52.9 27.8 %collective-permute-start.5 = (bf16[224,2048]{1,0:T(8,128)(2,1)}, bf16[224,2048]{1,0:T(8,128)(2,1)}, u32[]{:S(2)}, u32[]{:S(2)}) collective-permute-start(bf16[224,2048]{1,0:T(8,128)(2,1)} %collective-permute-done.4.refs_5_.refs_1_.refs_2_), channel_id=1, source_target_pairs={{0,448},{64,0},{128,64},{192,128},{256,192},{320,256},{384,320},{4... | collective-permute-start | bytes 2752520 | tf_op jit(solution)/shard_map/ppermute | solution.py:474
  58.6 3.1 %copy-start.2 = (bf16[224,2048]{1,0:T(8,128)(2,1)}, bf16[224,2048]{1,0:T(8,128)(2,1)S(1)}, u32[]{:S(2)}) copy-start(bf16[224,2048]{1,0:T(8,128)(2,1)S(1)} %collective-permute-done.1.refs_2_.refs_0_.refs_7_) | copy-start | bytes 2752516
  58.6 23.2 %collective-permute-start.2 = (bf16[224,2048]{1,0:T(8,128)(2,1)S(1)}, bf16[224,2048]{1,0:T(8,128)(2,1)}, u32[]{:S(2)}, u32[]{:S(2)}) collective-permute-start(bf16[224,2048]{1,0:T(8,128)(2,1)S(1)} %collective-permute-done.1.refs_2_.refs_0_.refs_7_), channel_id=1, source_target_pairs={{0,64},{64,128},{128,192},{192,256},{256,320},{320,384},{384,448},... | collective-permute-start | bytes 2752520 | tf_op jit(solution)/shard_map/ppermute | solution.py:474
  71.4 0.9 copy-start.3
  72.3 30.3 %all-to-all-start.2 = ((bf16[64,48,128]{2,1,0:T(8,128)(2,1)}), bf16[64,48,128]{2,1,0:T(8,128)(2,1)S(1)}, u32[]{:S(2)}, u32[]{:S(2)}) async-start(bf16[64,48,128]{2,1,0:T(8,128)(2,1)} %copy-done.3), calls=%async_computation.2 | async-start | bytes 1572864 | tf_op jit(solution)/shard_map/all_to_all | solution.py:516
  83.0 14.9 %collective-permute-start.6 = (bf16[112,2048]{1,0:T(8,128)(2,1)S(1)}, bf16[112,2048]{1,0:T(8,128)(2,1)S(1)}, u32[]{:S(2)}, u32[]{:S(2)}) collective-permute-start(bf16[112,2048]{1,0:T(8,128)(2,1)S(1)} %get-tuple-element.25), channel_id=1, source_target_pairs={{0,64},{64,128},{128,192},{192,256},{256,320},{320,384},{384,448},... | collective-permute-start | bytes 1376264 | tf_op jit(solution)/shard_map/ppermute | solution.py:474
  84.9 14.1 %collective-permute-start.7 = (bf16[112,2048]{1,0:T(8,128)(2,1)S(1)}, bf16[112,2048]{1,0:T(8,128)(2,1)S(1)}, u32[]{:S(2)}, u32[]{:S(2)}) collective-permute-start(bf16[112,2048]{1,0:T(8,128)(2,1)S(1)} %get-tuple-element.26), channel_id=1, source_target_pairs={{0,448},{64,0},{128,64},{192,128},{256,192},{320,256},{384,320},{4... | collective-permute-start | bytes 1376264 | tf_op jit(solution)/shard_map/ppermute | solution.py:474
  97.9 4.2 %copy-start.4 = (bf16[112,2048]{1,0:T(8,128)(2,1)}, bf16[112,2048]{1,0:T(8,128)(2,1)S(1)}, u32[]{:S(2)}) copy-start(bf16[112,2048]{1,0:T(8,128)(2,1)S(1)} %collective-permute-done.6.up_ref.refs_4_) | copy-start | bytes 1376260
  99.1 3.1 %copy-start.5 = (bf16[112,2048]{1,0:T(8,128)(2,1)}, bf16[112,2048]{1,0:T(8,128)(2,1)S(1)}, u32[]{:S(2)}) copy-start(bf16[112,2048]{1,0:T(8,128)(2,1)S(1)} %collective-permute-done.7.down_ref.refs_5_) | copy-start | bytes 1376260
  102.6 37.6 %all-to-all-start.1 = ((bf16[64,64,128]{2,1,0:T(8,128)(2,1)}), bf16[64,64,128]{2,1,0:T(8,128)(2,1)S(1)}, u32[]{:S(2)}, u32[]{:S(2)}) async-start(bf16[64,64,128]{2,1,0:T(8,128)(2,1)} %last.1.after_ref), calls=%async_computation.1 | async-start | bytes 2097152 | tf_op jit(solution)/shard_map/all_to_all | solution.py:520
  126.5 13.7 %copy-start.6 = (bf16[16,2048]{1,0:T(8,128)(2,1)S(1)}, bf16[16,2048]{1,0:T(8,128)(2,1)}, u32[]{:S(2)}) copy-start(bf16[16,2048]{1,0:T(8,128)(2,1)} %cot_ref.5) | copy-start | bytes 196612
  126.5 13.7 %copy-start.8 = (s32[16,8]{0,1:T(8,128)S(1)}, s32[16,8]{0,1:T(8,128)}, u32[]{:S(2)}) copy-start(s32[16,8]{0,1:T(8,128)} %param.9) | copy-start | bytes 1540
  126.5 13.7 %copy-start.9 = (f32[16,8]{0,1:T(8,128)S(1)}, f32[16,8]{0,1:T(8,128)}, u32[]{:S(2)}) copy-start(f32[16,8]{0,1:T(8,128)} %param.8) | copy-start | bytes 1540
  126.7 15.9 %collective-permute-start.10 = (bf16[9,4096]{1,0:T(8,128)(2,1)S(1)}, bf16[9,4096]{1,0:T(8,128)(2,1)S(1)}, u32[]{:S(2)}, u32[]{:S(2)}) collective-permute-start(bf16[9,4096]{1,0:T(8,128)(2,1)S(1)} %get-tuple-element.37), channel_id=1, source_target_pairs={{0,384},{64,448},{128,256},{192,320},{256,128},{320,192},{384,0},{... | collective-permute-start | bytes 221192 | tf_op jit(solution)/shard_map/ppermute | solution.py:486
  132.0 16.0 %collective-permute-start.9 = (bf16[9,4096]{1,0:T(8,128)(2,1)S(1)}, bf16[9,4096]{1,0:T(8,128)(2,1)S(1)}, u32[]{:S(2)}, u32[]{:S(2)}) collective-permute-start(bf16[9,4096]{1,0:T(8,128)(2,1)S(1)} %get-tuple-element.38), channel_id=1, source_target_pairs={{0,128},{64,192},{128,0},{192,64},{256,384},{320,448},{384,256},{4... | collective-permute-start | bytes 221192 | tf_op jit(solution)/shard_map/ppermute | solution.py:486
  134.1 13.9 %collective-permute-start.8 = (bf16[9,4096]{1,0:T(8,128)(2,1)S(1)}, bf16[9,4096]{1,0:T(8,128)(2,1)S(1)}, u32[]{:S(2)}, u32[]{:S(2)}) collective-permute-start(bf16[9,4096]{1,0:T(8,128)(2,1)S(1)} %get-tuple-element.39), channel_id=1, source_target_pairs={{0,256},{64,320},{128,384},{192,448},{256,0},{320,64},{384,128},{4... | collective-permute-start | bytes 221192 | tf_op jit(solution)/shard_map/ppermute | solution.py:486

commit v7 on v6

--- a/solution.py
+++ b/solution.py
@@ -54,7 +54,7 @@
 
 
 def route_kernel(
-    capacity, ids_ref, tok_ref, cot_ref, up_ref, down_ref, out_ref, own_ref, hottest_ref, tok, cot, sems
+    capacity, ids_hbm, tok_ref, cot_ref, up_ref, down_ref, out_ref, own_ref, hottest_ref, ids_ref, tok, cot, sems
 ):
     slots, width = out_ref.shape[0], tok.shape[1]
     units = up_ref.shape[0]
@@ -64,8 +64,10 @@
         pltpu.make_async_copy(up_ref, own_ref.at[pl.ds(0, units)], sems.at[2]),
         pltpu.make_async_copy(down_ref, own_ref.at[pl.ds(half, units)], sems.at[3]),
     ]
-    for copy in loads + copies:
+    first = pltpu.make_async_copy(ids_hbm, ids_ref, sems.at[4])
+    for copy in [first] + loads + copies:
         copy.start()
+    first.wait()
     cold, hot, _, _, hottest = slot_maps(ids_ref[...], slots, capacity)
     cold, hot = cold.astype(BF16), hot.astype(BF16)
     hottest_ref[0, 0] = jnp.max(hottest).astype(I32)
@@ -91,16 +93,17 @@
             jax.ShapeDtypeStruct((2 * (units + HOT_PAD), width), BF16),
             jax.ShapeDtypeStruct((1, 1), I32),
         ),
-        in_specs=[inside] + [anywhere] * 4,
+        in_specs=[anywhere] * 5,
         out_specs=(inside, inside, pl.BlockSpec(memory_space=pltpu.SMEM)),
         scratch_shapes=[
+            pltpu.VMEM(ids.shape, I32),
             pltpu.VMEM((tok_rows, width), BF16),
             pltpu.VMEM((tok_rows, width), BF16),
-            pltpu.SemaphoreType.DMA((4,)),
+            pltpu.SemaphoreType.DMA((5,)),
         ],
         compiler_params=pltpu.CompilerParams(vmem_limit_bytes=VMEM_LIMIT),
         name="route",
-    )(ids, *map(outside, (tokens, cotangent, up, down)))
+    )(*map(outside, (ids, tokens, cotangent, up, down)))
 
 
 def assemble_kernel(tall, rows_ref, up_ref, down_ref, out_ref, up, down, sems):
@@ -256,7 +259,7 @@
 
 
 def hot_kernel(units, hot_rows, where_ref, pieces_ref, *refs):
-    blocks, (send_ref, keep_ref, tok, cot, weights, sems) = refs[:-6], refs[-6:]
+    blocks, out_refs, (tok, cot, weights, sems) = refs[:-8], refs[-8:-4], refs[-4:]
     ring = len(blocks)
     width = tok.shape[1]
     here = where_ref[0]
@@ -280,18 +283,18 @@
         copy.wait()
     up, down = weights[:units, :], weights[units:, :]
     hidden, act_grad = activations(matmul_nt(tok[...], up), matmul_nt(cot[...], down))
-    packed = send_ref.shape[0]
-    row = lax.broadcasted_iota(I32, (packed, ring * HOT_PAD), 0)
-    column = lax.broadcasted_iota(I32, (packed, ring * HOT_PAD), 1)
-    group = row // hot_rows
-    place = (group % 2) * 4 + (group // 2) * 2
-    within = place * HOT_PAD + row % hot_rows
-    for odd, out_ref in ((1, send_ref), (0, keep_ref)):
-        chosen = (column == within + odd * HOT_PAD).astype(F32).astype(BF16)
-        picked_hidden = matmul(chosen, hidden).astype(BF16)
-        picked_grad = matmul(chosen, act_grad).astype(BF16)
-        out_ref[:, :width] = matmul(picked_hidden, down).astype(BF16)
-        out_ref[:, width:] = matmul(picked_grad, up).astype(BF16)
+    groups, stride = len(out_refs), 24
+    row = lax.broadcasted_iota(I32, (groups * stride, ring * HOT_PAD), 0)
+    column = lax.broadcasted_iota(I32, (groups * stride, ring * HOT_PAD), 1)
+    group, within = row // stride, row % stride
+    place = (group % 2) * 4 + (group // 2) * 2 + within // hot_rows
+    chosen = (column == place * HOT_PAD + within % hot_rows) & (within < 2 * hot_rows)
+    chosen = chosen.astype(F32).astype(BF16)
+    picked_hidden = matmul(chosen, hidden).astype(BF16)
+    picked_grad = matmul(chosen, act_grad).astype(BF16)
+    for lo, sums in ((0, matmul(picked_hidden, down)), (width, matmul(picked_grad, up))):
+        for g, out_ref in enumerate(out_refs):
+            out_ref[:, lo : lo + width] = sums[g * stride : g * stride + 2 * hot_rows].astype(BF16)
 
 
 def hot_partials(here, pieces, blocks, units, hot_rows, after):
@@ -309,13 +312,13 @@
         hot_kernel(units, hot_rows, where_ref, pieces_ref, *grouped, *refs)
 
     inside = pl.BlockSpec(memory_space=pltpu.VMEM)
-    packed = jax.ShapeDtypeStruct((ring // 2 * hot_rows, 2 * width), BF16)
+    packed = jax.ShapeDtypeStruct((2 * hot_rows, 2 * width), BF16)
     return pl.pallas_call(
         kernel,
-        out_shape=(packed, packed),
+        out_shape=(packed,) * 4,
         in_specs=[pl.BlockSpec(memory_space=pltpu.SMEM), inside]
         + [pl.BlockSpec(memory_space=pl.ANY)] * (1 + len(flat)),
-        out_specs=(inside, inside),
+        out_specs=(inside,) * 4,
         scratch_shapes=[
             pltpu.VMEM((ring * HOT_PAD, width), BF16),
             pltpu.VMEM((ring * HOT_PAD, width), BF16),
@@ -474,13 +477,6 @@
     return lax.ppermute(x, "dp", [(i, (i + by) % ring) for i in range(ring)])
 
 
-def swap(x, bit):
-    ring = lax.axis_size("dp")
-    pairs = [[i, i ^ bit] for i in range(ring) if not i & bit]
-    both = lax.all_gather(x, "dp", axis=0, axis_index_groups=pairs, tiled=False)
-    return jnp.where(lax.axis_index("dp") & bit == 0, both[1], both[0])
-
-
 def send_on(x, bits):
     ring = lax.axis_size("dp")
     return lax.ppermute(x, "dp", [(i, i ^ bits) for i in range(ring)])
@@ -521,12 +517,12 @@
 
     blocks = left + [(far_up, far_down)] + right[:0:-1]
     here = lax.axis_index("dp").astype(I32).reshape(1)
-    send, keep = hot_partials(here, hot_pieces, blocks, units, hot_rows, results)
-    both = keep.astype(F32) + swap(send, 1).astype(F32)
+    keep, *sends = hot_partials(here, hot_pieces, blocks, units, hot_rows, results)
+    both = keep.astype(F32)
+    for send, place in zip(sends, (4, 2, 6)):
+        both = both + send_on(send, place).astype(F32)
     kept = both[:hot_rows]
-    sent = [
-        send_on(both[i * hot_rows : (i + 1) * hot_rows].astype(BF16), place) for i, place in ((1, 4), (2, 2), (3, 6))
-    ]
+    sent = [send_on(both[hot_rows:].astype(BF16), 1)]
     sums, dots = cold_combine(ids, gates, cotangent, came_back, capacity)
     mixture, input_grad, gate_grad = final_combine(
         ids, gates, cotangent, sums, dots, kept, sent, slots, capacity

time: 150 us -> 153 us (1.020)
  waiting for transfers between devices: 38.4 us -> 49.1 us
  blocking collectives: 10.4 us -> 0 us
    ppermute x3 -> x4, waiting for transfers between devices: 5.38 us -> 16.6 us  [send_on(): return lax.ppermute(x, 'dp', [(i, i ^ bits) for i in range(ring)])]
    all_gather x1 -> x0, blocking collectives: 10.4 us -> none  [swap(): both = lax.all_gather(x, 'dp', axis=0, axis_index_groups=pairs, tiled=False)]
    ppermute x3 -> x4, starting transfers between devices: 12.4 us -> 14.9 us  [send_on(): return lax.ppermute(x, 'dp', [(i, i ^ bits) for i in range(ring)])]
  transfers between devices with their start and end apart: 14 -> 15, of which waited for: 9 -> 9; matrix products, arithmetic and copies ran while one was open for 1% -> 1% of each run, Pallas kernels for 12% -> 11%
where the time goes in v7:
time: 153 us; the launch traced here: 152 us
  starting transfers between devices  76.2 us (50%)
  waiting for transfers between devices  49.1 us (32%)
  Pallas kernels  20.5 us (13%)
  local copies, waits for them, and re-layouts  4.75 us (3%)
    ppermute x8, starting transfers between devices, shift(): return lax.ppermute(x, 'dp', [(i, (i + by) % ring) for i in range(ring)])  29 us
    ppermute x8, waiting for transfers between devices, shift(): return lax.ppermute(x, 'dp', [(i, (i + by) % ring) for i in range(ring)])  22.9 us
    ppermute x4, waiting for transfers between devices, send_on(): return lax.ppermute(x, 'dp', [(i, i ^ bits) for i in range(ring)])  16.6 us
    ppermute x4, starting transfers between devices, send_on(): return lax.ppermute(x, 'dp', [(i, i ^ bits) for i in range(ring)])  14.9 us
    all_to_all x1, starting transfers between devices, shards(): arrived = lax.all_to_all(outgoing, 'expert', 0, 0, tiled=True)  14 us
    all_to_all x1, starting transfers between devices, shards(): came_back = lax.all_to_all(results, 'expert', 0, 0, tiled=True)  9.9 us
    all_to_all x1, waiting for transfers between devices, shards(): arrived = lax.all_to_all(outgoing, 'expert', 0, 0, tiled=True)  9 us
    all_to_all x1, starting transfers between devices, shards(): lax.all_to_all(repeat(token, arrived, lines), 'expert', 0, 0, tiled=True)  8.39 us
  transfers between devices with their start and end apart: 15, of which 9 were waited for; matrix products, arithmetic and copies ran while one was open for 1% of the time, Pallas kernels for 11%

profile of v7, /device:TPU:6, one launch (start us, length us, event | category | flops | bytes accessed | tf_op | source)
XLA Modules:
  0.0 151.6 jit_solution(10284276738808448355)
XLA Ops:
  0.6 2.0 %route.1 = (bf16[128,4096]{1,0:T(8,128)(2,1)S(1)}, bf16[224,2048]{1,0:T(8,128)(2,1)S(1)}, s32[1,1]{1,0:T(1,128)}) custom-call(s32[8,16]{1,0:T(8,128)} %bitcast.6, bf16[16,2048]{1,0:T(8,128)(2,1)} %tok_ref.1, bf16[16,2048]{1,0:T(8,128)(2,1)} %cot_ref.5, bf16[96,2048]{1,0:T(8,128)(2,1)} %bitcast.11, bf16[96,2048]{1,0:T(8,128)(2,1)} %bitcast.13), custom_call_target="tpu_custom_call" | custom-call | tf_op jit(solution)/shard_map/route/pallas_call | solution.py:89
  2.6 0.0 copy-start.6
  2.6 1.0 copy-done.6
  3.6 0.0 copy-start.1
  3.6 5.4 %collective-permute-start.3 = (bf16[224,2048]{1,0:T(8,128)(2,1)S(1)}, bf16[224,2048]{1,0:T(8,128)(2,1)}, u32[]{:S(2)}, u32[]{:S(2)}) collective-permute-start(bf16[224,2048]{1,0:T(8,128)(2,1)S(1)} %get-tuple-element.22.refs_0_), channel_id=1, source_target_pairs={{0,448},{64,0},{128,64},{192,128},{256,192},{320,256},{384,320},{4... | collective-permute-start | bytes 2752520 | tf_op jit(solution)/shard_map/ppermute | solution.py:477
  9.0 1.9 %collective-permute-start = (bf16[224,2048]{1,0:T(8,128)(2,1)S(1)}, bf16[224,2048]{1,0:T(8,128)(2,1)}, u32[]{:S(2)}, u32[]{:S(2)}) collective-permute-start(bf16[224,2048]{1,0:T(8,128)(2,1)S(1)} %get-tuple-element.22.refs_0_), channel_id=1, source_target_pairs={{0,64},{64,128},{128,192},{192,256},{256,320},{320,384},{384,448},... | collective-permute-start | bytes 2752520 | tf_op jit(solution)/shard_map/ppermute | solution.py:477
  10.9 1.6 %reshape.12.rows_ref = bf16[64,64,128]{2,1,0:T(8,128)(2,1)S(1)} reshape(bf16[128,4096]{1,0:T(8,128)(2,1)} %copy-done.6) | data formatting | bytes 2097152 | tf_op jit(solution)/shard_map/reshape | solution.py:510
  12.5 1.2 assemble.1
  13.7 0.0 copy-done.1
  13.7 0.0 copy-start
  13.7 1.3 copy-done
  14.9 14.0 %all-to-all-start = ((bf16[64,112,128]{2,1,0:T(8,128)(2,1)}), bf16[64,112,128]{2,1,0:T(8,128)(2,1)S(1)}, u32[]{:S(2)}, u32[]{:S(2)}) async-start(bf16[64,112,128]{2,1,0:T(8,128)(2,1)} %copy-done), calls=%async_computation | async-start | bytes 3670016 | tf_op jit(solution)/shard_map/all_to_all | solution.py:511
  29.0 0.0 collective-permute-done.3.refs_4_.refs_1_
  29.0 5.3 %collective-permute-start.4 = (bf16[224,2048]{1,0:T(8,128)(2,1)}, bf16[224,2048]{1,0:T(8,128)(2,1)}, u32[]{:S(2)}, u32[]{:S(2)}) collective-permute-start(bf16[224,2048]{1,0:T(8,128)(2,1)} %collective-permute-done.3.refs_4_.refs_1_), channel_id=1, source_target_pairs={{0,448},{64,0},{128,64},{192,128},{256,192},{320,256},{384,320},{4... | collective-permute-start | bytes 2752520 | tf_op jit(solution)/shard_map/ppermute | solution.py:477
  34.2 0.0 collective-permute-done.refs_1_.refs_8_
  34.3 1.9 %collective-permute-start.1 = (bf16[224,2048]{1,0:T(8,128)(2,1)}, bf16[224,2048]{1,0:T(8,128)(2,1)S(1)}, u32[]{:S(2)}, u32[]{:S(2)}) collective-permute-start(bf16[224,2048]{1,0:T(8,128)(2,1)} %collective-permute-done.refs_1_.refs_8_), channel_id=1, source_target_pairs={{0,64},{64,128},{128,192},{192,256},{256,320},{320,384},{384,448},... | collective-permute-start | bytes 2752520 | tf_op jit(solution)/shard_map/ppermute | solution.py:477
  36.2 18.1 %collective-permute-done.4.refs_5_.refs_1_.refs_2_ = bf16[224,2048]{1,0:T(8,128)(2,1)} collective-permute-done((bf16[224,2048]{1,0:T(8,128)(2,1)}, bf16[224,2048]{1,0:T(8,128)(2,1)}, u32[]{:S(2)}, u32[]{:S(2)}) %collective-permute-start.4) | collective-permute-done | bytes 917536 | tf_op jit(solution)/shard_map/ppermute | solution.py:477
  54.3 5.6 %collective-permute-start.5 = (bf16[224,2048]{1,0:T(8,128)(2,1)}, bf16[224,2048]{1,0:T(8,128)(2,1)}, u32[]{:S(2)}, u32[]{:S(2)}) collective-permute-start(bf16[224,2048]{1,0:T(8,128)(2,1)} %collective-permute-done.4.refs_5_.refs_1_.refs_2_), channel_id=1, source_target_pairs={{0,448},{64,0},{128,64},{192,128},{256,192},{320,256},{384,320},{4... | collective-permute-start | bytes 2752520 | tf_op jit(solution)/shard_map/ppermute | solution.py:477
  59.9 0.0 collective-permute-done.1.refs_2_.refs_0_.refs_7_
  59.9 0.0 copy-start.2
  60.0 1.9 %collective-permute-start.2 = (bf16[224,2048]{1,0:T(8,128)(2,1)S(1)}, bf16[224,2048]{1,0:T(8,128)(2,1)}, u32[]{:S(2)}, u32[]{:S(2)}) collective-permute-start(bf16[224,2048]{1,0:T(8,128)(2,1)S(1)} %collective-permute-done.1.refs_2_.refs_0_.refs_7_), channel_id=1, source_target_pairs={{0,64},{64,128},{128,192},{192,256},{256,320},{320,384},{384,448},... | collective-permute-start | bytes 2752520 | tf_op jit(solution)/shard_map/ppermute | solution.py:477
  61.9 1.2 tick.1.hottest_ref
  63.1 0.0 copy-done.2
  63.1 9.0 %all-to-all-done.arrived_ref = bf16[64,112,128]{2,1,0:T(8,128)(2,1)S(1)} async-done(((bf16[64,112,128]{2,1,0:T(8,128)(2,1)}), bf16[64,112,128]{2,1,0:T(8,128)(2,1)S(1)}, u32[]{:S(2)}, u32[]{:S(2)}) %all-to-all-start) | async-done | bytes 1835040 | tf_op jit(solution)/shard_map/all_to_all | solution.py:511
  72.1 0.7 repeat.1
  72.8 0.0 copy-start.3
  72.8 0.9 copy-done.3
  73.7 8.4 %all-to-all-start.2 = ((bf16[64,48,128]{2,1,0:T(8,128)(2,1)}), bf16[64,48,128]{2,1,0:T(8,128)(2,1)S(1)}, u32[]{:S(2)}, u32[]{:S(2)}) async-start(bf16[64,48,128]{2,1,0:T(8,128)(2,1)} %copy-done.3), calls=%async_computation.2 | async-start | bytes 1572864 | tf_op jit(solution)/shard_map/all_to_all | solution.py:512
  82.1 0.0 collective-permute-done.5.left_ref
  82.1 2.2 %collective-permute-done.2.right_ref = bf16[224,2048]{1,0:T(8,128)(2,1)} collective-permute-done((bf16[224,2048]{1,0:T(8,128)(2,1)S(1)}, bf16[224,2048]{1,0:T(8,128)(2,1)}, u32[]{:S(2)}, u32[]{:S(2)}) %collective-permute-start.2) | collective-permute-done | bytes 917536 | tf_op jit(solution)/shard_map/ppermute | solution.py:477
  84.3 1.2 split.1
  85.5 1.9 %collective-permute-start.6 = (bf16[112,2048]{1,0:T(8,128)(2,1)S(1)}, bf16[112,2048]{1,0:T(8,128)(2,1)S(1)}, u32[]{:S(2)}, u32[]{:S(2)}) collective-permute-start(bf16[112,2048]{1,0:T(8,128)(2,1)S(1)} %get-tuple-element.27), channel_id=1, source_target_pairs={{0,64},{64,128},{128,192},{192,256},{256,320},{320,384},{384,448},... | collective-permute-start | bytes 1376264 | tf_op jit(solution)/shard_map/ppermute | solution.py:477
  87.4 5.1 %collective-permute-start.7 = (bf16[112,2048]{1,0:T(8,128)(2,1)S(1)}, bf16[112,2048]{1,0:T(8,128)(2,1)S(1)}, u32[]{:S(2)}, u32[]{:S(2)}) collective-permute-start(bf16[112,2048]{1,0:T(8,128)(2,1)S(1)} %get-tuple-element.28), channel_id=1, source_target_pairs={{0,448},{64,0},{128,64},{192,128},{256,192},{320,256},{384,320},{4... | collective-permute-start | bytes 1376264 | tf_op jit(solution)/shard_map/ppermute | solution.py:477
  92.6 5.3 %gathered.1 = (f32[128,4096]{1,0:T(8,128)S(1)}, bf16[128,4096]{1,0:T(8,128)(2,1)S(1)}) custom-call(bf16[64,112,128]{2,1,0:T(8,128)(2,1)S(1)} %all-to-all-done.arrived_ref, bf16[224,2048]{1,0:T(8,128)(2,1)} %copy-done.1, bf16[224,2048]{1,0:T(8,128)(2,1)} %collective-permute-done.refs_1_.refs_8_, bf16[224,2048]{1,0:T(8,128)(2,1)} %copy-done.2, ...), custom_call_target="tpu_custom_call" | custom-call | flops 1409286144 | bytes 5505024 | tf_op jit(solution)/shard_map/gathered/pallas_call | solution.py:206
  97.9 1.4 collective-permute-done.6.up_ref.refs_4_
  99.3 0.0 copy-start.4
  99.3 1.2 collective-permute-done.7.down_ref.refs_5_
  100.5 0.0 copy-start.5
  100.5 3.0 %last.1.after_ref = bf16[64,64,128]{2,1,0:T(8,128)(2,1)} custom-call(bf16[128,4096]{1,0:T(8,128)(2,1)S(1)} %get-tuple-element.25.rows_ref, f32[128,4096]{1,0:T(8,128)S(1)} %get-tuple-element.26.acc_ref, bf16[112,2048]{1,0:T(8,128)(2,1)S(1)} %collective-permute-done.6.up_ref.refs_4_, bf16[112,2048]{1,0:T(8,128)(2,1)S(1)} %collective-permute-done.7.down_ref.refs_5_), custom_call_target="tpu_custom_call" | custom-call | tf_op jit(solution)/shard_map/last/pallas_call | solution.py:252
  103.5 0.0 copy-done.4
  103.5 0.0 copy-done.5
  103.5 0.5 all-to-all-done.2.pieces_ref
  104.0 9.9 %all-to-all-start.1 = ((bf16[64,64,128]{2,1,0:T(8,128)(2,1)}), bf16[64,64,128]{2,1,0:T(8,128)(2,1)S(1)}, u32[]{:S(2)}, u32[]{:S(2)}) async-start(bf16[64,64,128]{2,1,0:T(8,128)(2,1)} %last.1.after_ref), calls=%async_computation.1 | async-start | bytes 2097152 | tf_op jit(solution)/shard_map/all_to_all | solution.py:516
  113.9 2.3 %hot.1 = (bf16[18,4096]{1,0:T(8,128)(2,1)S(1)}, bf16[18,4096]{1,0:T(8,128)(2,1)S(1)}, bf16[18,4096]{1,0:T(8,128)(2,1)S(1)}, bf16[18,4096]{1,0:T(8,128)(2,1)S(1)}) custom-call(s32[1]{0:T(128)} %bitcast.4.where_ref, bf16[64,48,128]{2,1,0:T(8,128)(2,1)S(1)} %all-to-all-done.2.pieces_ref, bf16[64,64,128]{2,1,0:T(8,128)(2,1)} %last.1.after_ref, ...), custom_call_target="tpu_custom_call" | custom-call | tf_op jit(solution)/shard_map/hot/pallas_call | solution.py:316
  116.3 0.0 copy-start.7
  116.3 0.0 copy-start.8
  116.3 0.0 copy-start.9
  116.3 6.0 %collective-permute-start.8 = (bf16[18,4096]{1,0:T(8,128)(2,1)S(1)}, bf16[18,4096]{1,0:T(8,128)(2,1)S(1)}, u32[]{:S(2)}, u32[]{:S(2)}) collective-permute-start(bf16[18,4096]{1,0:T(8,128)(2,1)S(1)} %get-tuple-element.33), channel_id=1, source_target_pairs={{0,256},{64,320},{128,384},{192,448},{256,0},{320,64},{384,128},{4... | collective-permute-start | bytes 442376 | tf_op jit(solution)/shard_map/ppermute | solution.py:482
  122.4 3.8 %collective-permute-start.9 = (bf16[18,4096]{1,0:T(8,128)(2,1)S(1)}, bf16[18,4096]{1,0:T(8,128)(2,1)S(1)}, u32[]{:S(2)}, u32[]{:S(2)}) collective-permute-start(bf16[18,4096]{1,0:T(8,128)(2,1)S(1)} %get-tuple-element.34), channel_id=1, source_target_pairs={{0,128},{64,192},{128,0},{192,64},{256,384},{320,448},{384,256},{4... | collective-permute-start | bytes 442376 | tf_op jit(solution)/shard_map/ppermute | solution.py:482
  126.2 2.5 %collective-permute-start.10 = (bf16[18,4096]{1,0:T(8,128)(2,1)S(1)}, bf16[18,4096]{1,0:T(8,128)(2,1)S(1)}, u32[]{:S(2)}, u32[]{:S(2)}) collective-permute-start(bf16[18,4096]{1,0:T(8,128)(2,1)S(1)} %get-tuple-element.35), channel_id=1, source_target_pairs={{0,384},{64,448},{128,256},{192,320},{256,128},{320,192},{384,0},{... | collective-permute-start | bytes 442376 | tf_op jit(solution)/shard_map/ppermute | solution.py:482
  128.7 1.3 collective-permute-done.8
  130.0 12.9 %collective-permute-done.9 = bf16[18,4096]{1,0:T(8,128)(2,1)S(1)} collective-permute-done((bf16[18,4096]{1,0:T(8,128)(2,1)S(1)}, bf16[18,4096]{1,0:T(8,128)(2,1)S(1)}, u32[]{:S(2)}, u32[]{:S(2)}) %collective-permute-start.9) | collective-permute-done | bytes 147488 | tf_op jit(solution)/shard_map/ppermute | solution.py:482
  143.0 0.0 collective-permute-done.10
  143.0 0.1 convert_add_fusion
  143.1 2.5 %collective-permute-start.11 = (bf16[9,4096]{1,0:T(8,128)(2,1)S(1)}, bf16[9,4096]{1,0:T(8,128)(2,1)S(1)}, u32[]{:S(2)}, u32[]{:S(2)}) collective-permute-start(bf16[9,4096]{1,0:T(8,128)(2,1)S(1)} %slice.12), channel_id=1, source_target_pairs={{0,64},{64,0},{128,192},{192,128},{256,320},{320,256},{384,448},{4... | collective-permute-start | bytes 221192 | tf_op jit(solution)/shard_map/ppermute | solution.py:482
  145.7 0.0 all-to-all-done.1.cold_ref
  145.7 0.0 copy-done.7
  145.7 0.0 copy-done.8
  145.7 0.0 copy-done.9
  145.7 2.4 %cold_combine.1 = (f32[16,4096]{1,0:T(8,128)S(1)}, f32[8,16]{1,0:T(8,128)S(1)}) custom-call(s32[8,16]{1,0:T(8,128)S(1)} %bitcast.7, f32[8,16]{1,0:T(8,128)S(1)} %bitcast.9, bf16[16,2048]{1,0:T(8,128)(2,1)S(1)} %copy-done.7, bf16[64,64,128]{2,1,0:T(8,128)(2,1)S(1)} %all-to-all-done.1.cold_ref), custom_call_target="tpu_custom_call" | custom-call | flops 68719476736 | bytes 67108864 | tf_op jit(solution)/shard_map/cold_combine/pallas_call | solution.py:369
  148.1 2.4 %collective-permute-done.11.refs_0_ = bf16[9,4096]{1,0:T(8,128)(2,1)S(1)} collective-permute-done((bf16[9,4096]{1,0:T(8,128)(2,1)S(1)}, bf16[9,4096]{1,0:T(8,128)(2,1)S(1)}, u32[]{:S(2)}, u32[]{:S(2)}) %collective-permute-start.11) | collective-permute-done | bytes 73760 | tf_op jit(solution)/shard_map/ppermute | solution.py:482
  150.4 1.2 final_combine.1
  (2 shorter events, 0.0 us)
Async XLA Ops:
  2.6 1.0 copy-start.6
  3.6 10.1 %copy-start.1 = (bf16[224,2048]{1,0:T(8,128)(2,1)}, bf16[224,2048]{1,0:T(8,128)(2,1)S(1)}, u32[]{:S(2)}) copy-start(bf16[224,2048]{1,0:T(8,128)(2,1)S(1)} %get-tuple-element.22.refs_0_) | copy-start | bytes 2752516
  3.6 25.4 %collective-permute-start.3 = (bf16[224,2048]{1,0:T(8,128)(2,1)S(1)}, bf16[224,2048]{1,0:T(8,128)(2,1)}, u32[]{:S(2)}, u32[]{:S(2)}) collective-permute-start(bf16[224,2048]{1,0:T(8,128)(2,1)S(1)} %get-tuple-element.22.refs_0_), channel_id=1, source_target_pairs={{0,448},{64,0},{128,64},{192,128},{256,192},{320,256},{384,320},{4... | collective-permute-start | bytes 2752520 | tf_op jit(solution)/shard_map/ppermute | solution.py:477
  9.0 25.3 %collective-permute-start = (bf16[224,2048]{1,0:T(8,128)(2,1)S(1)}, bf16[224,2048]{1,0:T(8,128)(2,1)}, u32[]{:S(2)}, u32[]{:S(2)}) collective-permute-start(bf16[224,2048]{1,0:T(8,128)(2,1)S(1)} %get-tuple-element.22.refs_0_), channel_id=1, source_target_pairs={{0,64},{64,128},{128,192},{192,256},{256,320},{320,384},{384,448},... | collective-permute-start | bytes 2752520 | tf_op jit(solution)/shard_map/ppermute | solution.py:477
  13.7 1.3 copy-start
  14.9 57.1 %all-to-all-start = ((bf16[64,112,128]{2,1,0:T(8,128)(2,1)}), bf16[64,112,128]{2,1,0:T(8,128)(2,1)S(1)}, u32[]{:S(2)}, u32[]{:S(2)}) async-start(bf16[64,112,128]{2,1,0:T(8,128)(2,1)} %copy-done), calls=%async_computation | async-start | bytes 3670016 | tf_op jit(solution)/shard_map/all_to_all | solution.py:511
  29.0 25.4 %collective-permute-start.4 = (bf16[224,2048]{1,0:T(8,128)(2,1)}, bf16[224,2048]{1,0:T(8,128)(2,1)}, u32[]{:S(2)}, u32[]{:S(2)}) collective-permute-start(bf16[224,2048]{1,0:T(8,128)(2,1)} %collective-permute-done.3.refs_4_.refs_1_), channel_id=1, source_target_pairs={{0,448},{64,0},{128,64},{192,128},{256,192},{320,256},{384,320},{4... | collective-permute-start | bytes 2752520 | tf_op jit(solution)/shard_map/ppermute | solution.py:477
  34.3 25.7 %collective-permute-start.1 = (bf16[224,2048]{1,0:T(8,128)(2,1)}, bf16[224,2048]{1,0:T(8,128)(2,1)S(1)}, u32[]{:S(2)}, u32[]{:S(2)}) collective-permute-start(bf16[224,2048]{1,0:T(8,128)(2,1)} %collective-permute-done.refs_1_.refs_8_), channel_id=1, source_target_pairs={{0,64},{64,128},{128,192},{192,256},{256,320},{320,384},{384,448},... | collective-permute-start | bytes 2752520 | tf_op jit(solution)/shard_map/ppermute | solution.py:477
  54.3 27.8 %collective-permute-start.5 = (bf16[224,2048]{1,0:T(8,128)(2,1)}, bf16[224,2048]{1,0:T(8,128)(2,1)}, u32[]{:S(2)}, u32[]{:S(2)}) collective-permute-start(bf16[224,2048]{1,0:T(8,128)(2,1)} %collective-permute-done.4.refs_5_.refs_1_.refs_2_), channel_id=1, source_target_pairs={{0,448},{64,0},{128,64},{192,128},{256,192},{320,256},{384,320},{4... | collective-permute-start | bytes 2752520 | tf_op jit(solution)/shard_map/ppermute | solution.py:477
  59.9 3.1 %copy-start.2 = (bf16[224,2048]{1,0:T(8,128)(2,1)}, bf16[224,2048]{1,0:T(8,128)(2,1)S(1)}, u32[]{:S(2)}) copy-start(bf16[224,2048]{1,0:T(8,128)(2,1)S(1)} %collective-permute-done.1.refs_2_.refs_0_.refs_7_) | copy-start | bytes 2752516
  60.0 24.4 %collective-permute-start.2 = (bf16[224,2048]{1,0:T(8,128)(2,1)S(1)}, bf16[224,2048]{1,0:T(8,128)(2,1)}, u32[]{:S(2)}, u32[]{:S(2)}) collective-permute-start(bf16[224,2048]{1,0:T(8,128)(2,1)S(1)} %collective-permute-done.1.refs_2_.refs_0_.refs_7_), channel_id=1, source_target_pairs={{0,64},{64,128},{128,192},{192,256},{256,320},{320,384},{384,448},... | collective-permute-start | bytes 2752520 | tf_op jit(solution)/shard_map/ppermute | solution.py:477
  72.8 0.9 copy-start.3
  73.7 30.3 %all-to-all-start.2 = ((bf16[64,48,128]{2,1,0:T(8,128)(2,1)}), bf16[64,48,128]{2,1,0:T(8,128)(2,1)S(1)}, u32[]{:S(2)}, u32[]{:S(2)}) async-start(bf16[64,48,128]{2,1,0:T(8,128)(2,1)} %copy-done.3), calls=%async_computation.2 | async-start | bytes 1572864 | tf_op jit(solution)/shard_map/all_to_all | solution.py:512
  85.5 13.8 %collective-permute-start.6 = (bf16[112,2048]{1,0:T(8,128)(2,1)S(1)}, bf16[112,2048]{1,0:T(8,128)(2,1)S(1)}, u32[]{:S(2)}, u32[]{:S(2)}) collective-permute-start(bf16[112,2048]{1,0:T(8,128)(2,1)S(1)} %get-tuple-element.27), channel_id=1, source_target_pairs={{0,64},{64,128},{128,192},{192,256},{256,320},{320,384},{384,448},... | collective-permute-start | bytes 1376264 | tf_op jit(solution)/shard_map/ppermute | solution.py:477
  87.4 13.0 %collective-permute-start.7 = (bf16[112,2048]{1,0:T(8,128)(2,1)S(1)}, bf16[112,2048]{1,0:T(8,128)(2,1)S(1)}, u32[]{:S(2)}, u32[]{:S(2)}) collective-permute-start(bf16[112,2048]{1,0:T(8,128)(2,1)S(1)} %get-tuple-element.28), channel_id=1, source_target_pairs={{0,448},{64,0},{128,64},{192,128},{256,192},{320,256},{384,320},{4... | collective-permute-start | bytes 1376264 | tf_op jit(solution)/shard_map/ppermute | solution.py:477
  99.3 4.2 %copy-start.4 = (bf16[112,2048]{1,0:T(8,128)(2,1)}, bf16[112,2048]{1,0:T(8,128)(2,1)S(1)}, u32[]{:S(2)}) copy-start(bf16[112,2048]{1,0:T(8,128)(2,1)S(1)} %collective-permute-done.6.up_ref.refs_4_) | copy-start | bytes 1376260
  100.5 3.0 %copy-start.5 = (bf16[112,2048]{1,0:T(8,128)(2,1)}, bf16[112,2048]{1,0:T(8,128)(2,1)S(1)}, u32[]{:S(2)}) copy-start(bf16[112,2048]{1,0:T(8,128)(2,1)S(1)} %collective-permute-done.7.down_ref.refs_5_) | copy-start | bytes 1376260
  104.0 41.6 %all-to-all-start.1 = ((bf16[64,64,128]{2,1,0:T(8,128)(2,1)}), bf16[64,64,128]{2,1,0:T(8,128)(2,1)S(1)}, u32[]{:S(2)}, u32[]{:S(2)}) async-start(bf16[64,64,128]{2,1,0:T(8,128)(2,1)} %last.1.after_ref), calls=%async_computation.1 | async-start | bytes 2097152 | tf_op jit(solution)/shard_map/all_to_all | solution.py:516
  116.3 29.4 %copy-start.7 = (bf16[16,2048]{1,0:T(8,128)(2,1)S(1)}, bf16[16,2048]{1,0:T(8,128)(2,1)}, u32[]{:S(2)}) copy-start(bf16[16,2048]{1,0:T(8,128)(2,1)} %cot_ref.5) | copy-start | bytes 196612
  116.3 29.4 %copy-start.8 = (s32[16,8]{0,1:T(8,128)S(1)}, s32[16,8]{0,1:T(8,128)}, u32[]{:S(2)}) copy-start(s32[16,8]{0,1:T(8,128)} %param.9) | copy-start | bytes 1540
  116.3 29.4 %copy-start.9 = (f32[16,8]{0,1:T(8,128)S(1)}, f32[16,8]{0,1:T(8,128)}, u32[]{:S(2)}) copy-start(f32[16,8]{0,1:T(8,128)} %param.8) | copy-start | bytes 1540
  116.3 13.7 %collective-permute-start.8 = (bf16[18,4096]{1,0:T(8,128)(2,1)S(1)}, bf16[18,4096]{1,0:T(8,128)(2,1)S(1)}, u32[]{:S(2)}, u32[]{:S(2)}) collective-permute-start(bf16[18,4096]{1,0:T(8,128)(2,1)S(1)} %get-tuple-element.33), channel_id=1, source_target_pairs={{0,256},{64,320},{128,384},{192,448},{256,0},{320,64},{384,128},{4... | collective-permute-start | bytes 442376 | tf_op jit(solution)/shard_map/ppermute | solution.py:482
  122.4 20.6 %collective-permute-start.9 = (bf16[18,4096]{1,0:T(8,128)(2,1)S(1)}, bf16[18,4096]{1,0:T(8,128)(2,1)S(1)}, u32[]{:S(2)}, u32[]{:S(2)}) collective-permute-start(bf16[18,4096]{1,0:T(8,128)(2,1)S(1)} %get-tuple-element.34), channel_id=1, source_target_pairs={{0,128},{64,192},{128,0},{192,64},{256,384},{320,448},{384,256},{4... | collective-permute-start | bytes 442376 | tf_op jit(solution)/shard_map/ppermute | solution.py:482
  126.2 16.8 %collective-permute-start.10 = (bf16[18,4096]{1,0:T(8,128)(2,1)S(1)}, bf16[18,4096]{1,0:T(8,128)(2,1)S(1)}, u32[]{:S(2)}, u32[]{:S(2)}) collective-permute-start(bf16[18,4096]{1,0:T(8,128)(2,1)S(1)} %get-tuple-element.35), channel_id=1, source_target_pairs={{0,384},{64,448},{128,256},{192,320},{256,128},{320,192},{384,0},{... | collective-permute-start | bytes 442376 | tf_op jit(solution)/shard_map/ppermute | solution.py:482
  143.1 7.3 %collective-permute-start.11 = (bf16[9,4096]{1,0:T(8,128)(2,1)S(1)}, bf16[9,4096]{1,0:T(8,128)(2,1)S(1)}, u32[]{:S(2)}, u32[]{:S(2)}) collective-permute-start(bf16[9,4096]{1,0:T(8,128)(2,1)S(1)} %slice.12), channel_id=1, source_target_pairs={{0,64},{64,0},{128,192},{192,128},{256,320},{320,256},{384,448},{4... | collective-permute-start | bytes 221192 | tf_op jit(solution)/shard_map/ppermute | solution.py:482

commit v8 on v6

--- a/solution.py
+++ b/solution.py
@@ -54,15 +54,14 @@
 
 
 def route_kernel(
-    capacity, ids_ref, tok_ref, cot_ref, up_ref, down_ref, out_ref, own_ref, hottest_ref, tok, cot, sems
+    capacity, ids_ref, tok_ref, cot_ref, up_ref, down_ref, out_ref, own_up_ref, own_down_ref, hottest_ref, tok, cot, sems
 ):
     slots, width = out_ref.shape[0], tok.shape[1]
     units = up_ref.shape[0]
-    half = own_ref.shape[0] // 2
     loads = [pltpu.make_async_copy(tok_ref, tok, sems.at[0]), pltpu.make_async_copy(cot_ref, cot, sems.at[1])]
     copies = [
-        pltpu.make_async_copy(up_ref, own_ref.at[pl.ds(0, units)], sems.at[2]),
-        pltpu.make_async_copy(down_ref, own_ref.at[pl.ds(half, units)], sems.at[3]),
+        pltpu.make_async_copy(up_ref, own_up_ref.at[pl.ds(0, units)], sems.at[2]),
+        pltpu.make_async_copy(down_ref, own_down_ref.at[pl.ds(0, units)], sems.at[3]),
     ]
     for copy in loads + copies:
         copy.start()
@@ -71,8 +70,8 @@
     hottest_ref[0, 0] = jnp.max(hottest).astype(I32)
     for copy in loads:
         copy.wait()
-    own_ref[units:half, :] = matmul(hot, tok[...]).astype(BF16)
-    own_ref[half + units :, :] = matmul(hot, cot[...]).astype(BF16)
+    own_up_ref[units:, :] = matmul(hot, tok[...]).astype(BF16)
+    own_down_ref[units:, :] = matmul(hot, cot[...]).astype(BF16)
     out_ref[:, :width] = matmul(cold, tok[...]).astype(BF16)
     out_ref[:, width:] = matmul(cold, cot[...]).astype(BF16)
     for copy in copies:
@@ -88,11 +87,12 @@
         functools.partial(route_kernel, capacity),
         out_shape=(
             jax.ShapeDtypeStruct((slots, 2 * width), BF16),
-            jax.ShapeDtypeStruct((2 * (units + HOT_PAD), width), BF16),
+            jax.ShapeDtypeStruct((units + HOT_PAD, width), BF16),
+            jax.ShapeDtypeStruct((units + HOT_PAD, width), BF16),
             jax.ShapeDtypeStruct((1, 1), I32),
         ),
         in_specs=[inside] + [anywhere] * 4,
-        out_specs=(inside, inside, pl.BlockSpec(memory_space=pltpu.SMEM)),
+        out_specs=(inside, inside, inside, pl.BlockSpec(memory_space=pltpu.SMEM)),
         scratch_shapes=[
             pltpu.VMEM((tok_rows, width), BF16),
             pltpu.VMEM((tok_rows, width), BF16),
@@ -169,14 +169,13 @@
 def gathered_kernel(units, lines, arrived_ref, *refs):
     pieces, (acc_ref, rows_ref, up, down, wide, sems) = refs[:-6], refs[-6:]
     width = up.shape[1]
-    half = pieces[0].shape[0] // 2
     experts = arrived_ref.shape[0]
     capacity = rows_ref.shape[0] // experts
     copies = []
-    for i, piece in enumerate(pieces):
+    for i in range(len(pieces) // 2):
         for j, whole in enumerate((up, down)):
             copy = pltpu.make_async_copy(
-                piece.at[pl.ds(j * half, units)], whole.at[pl.ds(i * units, units)], sems.at[i, j]
+                pieces[2 * i + j].at[pl.ds(0, units)], whole.at[pl.ds(i * units, units)], sems.at[i, j]
             )
             copy.start()
             copies.append(copy)
@@ -199,14 +198,14 @@
     experts = arrived.shape[0]
     width = pieces[0].shape[1]
     lines = slots * 2 * width // (experts * 128)
-    count = len(pieces)
+    count = len(pieces) // 2
     return pl.pallas_call(
         functools.partial(gathered_kernel, units, lines),
         out_shape=(
             jax.ShapeDtypeStruct((slots, 2 * width), F32),
             jax.ShapeDtypeStruct((slots, 2 * width), BF16),
         ),
-        in_specs=[pl.BlockSpec(memory_space=pltpu.VMEM)] + [pl.BlockSpec(memory_space=pl.ANY)] * count,
+        in_specs=[pl.BlockSpec(memory_space=pltpu.VMEM)] + [pl.BlockSpec(memory_space=pl.ANY)] * len(pieces),
         out_specs=(pl.BlockSpec(memory_space=pltpu.VMEM), pl.BlockSpec(memory_space=pltpu.VMEM)),
         scratch_shapes=[
             pltpu.VMEM((count * units, width), BF16),
@@ -440,33 +439,22 @@
     )(token, *after)
 
 
-def split_kernel(right_ref, left_ref, right_out, left_out, top_ref, bottom_ref, sems):
-    half = top_ref.shape[0]
-    copies = [
-        pltpu.make_async_copy(right_ref.at[pl.ds(0, half)], top_ref, sems.at[0]),
-        pltpu.make_async_copy(left_ref.at[pl.ds(half, half)], bottom_ref, sems.at[1]),
-    ]
-    for copy in copies:
-        copy.start()
-    for copy in copies:
-        copy.wait()
-
-
-def split(right, left):
-    anywhere, inside = pl.BlockSpec(memory_space=pl.ANY), pl.BlockSpec(memory_space=pltpu.VMEM)
-    whole = jax.ShapeDtypeStruct(right.shape, right.dtype)
-    part = jax.ShapeDtypeStruct((right.shape[0] // 2, right.shape[1]), right.dtype)
-    return pl.pallas_call(
-        split_kernel,
-        out_shape=(whole, whole, part, part),
-        in_specs=[anywhere] * 2,
-        out_specs=(anywhere, anywhere, inside, inside),
-        input_output_aliases={0: 0, 1: 1},
-        scratch_shapes=[pltpu.SemaphoreType.DMA((2,))],
-        compiler_params=pltpu.CompilerParams(vmem_limit_bytes=1 << 22),
+def gate_kernel(*refs):
+    pass
+
+
+def gate(*arrays):
+    anywhere = pl.BlockSpec(memory_space=pl.ANY)
+    return pl.pallas_call(
+        gate_kernel,
+        out_shape=tuple(jax.ShapeDtypeStruct(x.shape, x.dtype) for x in arrays),
+        in_specs=[anywhere] * len(arrays),
+        out_specs=tuple([anywhere] * len(arrays)),
+        input_output_aliases={i: i for i in range(len(arrays))},
+        compiler_params=pltpu.CompilerParams(vmem_limit_bytes=1 << 20),
         cost_estimate=TICK,
-        name="split",
-    )(right, left)
+        name="gate",
+    )(*arrays)
 
 
 def shift(x, by):
@@ -497,25 +485,25 @@
     units = up.shape[0]
     ids, gates = expert_ids.T, gate_probs.T
 
-    outgoing, own, hottest = route(ids, tokens, cotangent, up, down, slots, capacity)
-    half = own.shape[0] // 2
-    right, left = [own], [own]
+    outgoing, own_up, own_down, hottest = route(ids, tokens, cotangent, up, down, slots, capacity)
+    right, left = [(own_up, own_down)], [(own_up, own_down)]
     for step in range(3):
-        r, l = shift(right[-1], 1), shift(left[-1], -1)
+        r = [shift(x, 1) for x in right[-1]]
+        l = [shift(x, -1) for x in left[-1]]
         if step == 1:
-            token = tick(hottest, r, l)
+            token = tick(hottest, *r, *l)
         if step == 2:
-            r, l, top, bottom = split(r, l)
-        right.append(r)
-        left.append(l)
-    far_up, far_down = shift(top, 1), shift(bottom, -1)
+            r[0], l[1] = gate(r[0], l[1])
+        right.append(tuple(r))
+        left.append(tuple(l))
+    far_up, far_down = shift(right[-1][0], 1), shift(left[-1][1], -1)
 
     lines = capacity * 2 * width // 128
     outgoing = assemble(outgoing.reshape(experts, lines, 128), up, down)
     arrived = lax.all_to_all(outgoing, "expert", 0, 0, tiled=True)
     hot_pieces = lax.all_to_all(repeat(token, arrived, lines), "expert", 0, 0, tiled=True)
 
-    acc, rows = gathered(arrived, [own] + right[1:] + left[1:], units, slots)
+    acc, rows = gathered(arrived, [x for pair in right + left[1:] for x in pair], units, slots)
     results = last(rows, acc, far_up, far_down, units, experts)
     came_back = lax.all_to_all(results, "expert", 0, 0, tiled=True)
 

time: 150 us -> 157 us (1.047)
  starting transfers between devices: 75.2 us -> 97.2 us
  waiting for transfers between devices: 38.4 us -> 21.6 us
    ppermute x8 -> x14, starting transfers between devices: 29.5 us -> 51.6 us  [shift(): return lax.ppermute(x, 'dp', [(i, (i + by) % ring) for i in range(ring)])]
    all_to_all x1, waiting for transfers between devices: 9 us -> 0.01 us  [shards(): arrived = lax.all_to_all(outgoing, 'expert', 0, 0, tiled=True)]
    ppermute x8 -> x14, waiting for transfers between devices: 22.5 us -> 13.7 us  [shift(): return lax.ppermute(x, 'dp', [(i, (i + by) % ring) for i in range(ring)])]
    all_to_all x1, starting transfers between devices: 11 us -> 8.97 us  [shards(): came_back = lax.all_to_all(results, 'expert', 0, 0, tiled=True)]
    all_to_all x1, starting transfers between devices: 8.39 us -> 10.3 us  [shards(): lax.all_to_all(repeat(token, arrived, lines), 'expert', 0, 0, tiled=True)]
  transfers between devices with their start and end apart: 14 -> 20, of which waited for: 9 -> 12; matrix products, arithmetic and copies ran while one was open for 1% -> 0% of each run, Pallas kernels for 12% -> 10%
where the time goes in v8:
time: 157 us; the launch traced here: 156 us
  starting transfers between devices  97.2 us (62%)
  waiting for transfers between devices  21.6 us (14%)
  Pallas kernels  20.3 us (13%)
  blocking collectives  10.6 us (7%)
  local copies, waits for them, and re-layouts  4.96 us (3%)
    ppermute x14, starting transfers between devices, shift(): return lax.ppermute(x, 'dp', [(i, (i + by) % ring) for i in range(ring)])  51.6 us
    all_to_all x1, starting transfers between devices, shards(): arrived = lax.all_to_all(outgoing, 'expert', 0, 0, tiled=True)  14 us
    ppermute x14, waiting for transfers between devices, shift(): return lax.ppermute(x, 'dp', [(i, (i + by) % ring) for i in range(ring)])  13.7 us
    ppermute x3, starting transfers between devices, send_on(): return lax.ppermute(x, 'dp', [(i, i ^ bits) for i in range(ring)])  12.2 us
    all_gather x1, blocking collectives, swap(): both = lax.all_gather(x, 'dp', axis=0, axis_index_groups=pairs, tiled=False)  10.6 us
    all_to_all x1, starting transfers between devices, shards(): lax.all_to_all(repeat(token, arrived, lines), 'expert', 0, 0, tiled=True)  10.3 us
    all_to_all x1, starting transfers between devices, shards(): came_back = lax.all_to_all(results, 'expert', 0, 0, tiled=True)  8.97 us
    ppermute x3, waiting for transfers between devices, send_on(): return lax.ppermute(x, 'dp', [(i, i ^ bits) for i in range(ring)])  5.39 us
  transfers between devices with their start and end apart: 20, of which 12 were waited for; matrix products, arithmetic and copies ran while one was open for 0% of the time, Pallas kernels for 10%

profile of v8, /device:TPU:6, one launch (start us, length us, event | category | flops | bytes accessed | tf_op | source)
XLA Modules:
  0.0 155.7 jit_solution(12399934287904729431)
XLA Ops:
  0.6 0.0 copy-start.8
  0.6 0.7 copy-done.8
  1.3 1.9 %route.1 = (bf16[128,4096]{1,0:T(8,128)(2,1)S(1)}, bf16[112,2048]{1,0:T(8,128)(2,1)S(1)}, bf16[112,2048]{1,0:T(8,128)(2,1)S(1)}, s32[1,1]{1,0:T(1,128)}) custom-call(s32[8,16]{1,0:T(8,128)S(1)} %bitcast.14, bf16[16,2048]{1,0:T(8,128)(2,1)} %tok_ref.1, bf16[16,2048]{1,0:T(8,128)(2,1)} %cot_ref.5, bf16[96,2048]{1,0:T(8,128)(2,1)} %bitcast.19, ...), custom_call_target="tpu_custom_call" | custom-call | tf_op jit(solution)/shard_map/route/pallas_call | solution.py:86
  3.2 0.0 copy-start.6
  3.2 1.0 copy-done.6
  4.2 1.9 %reshape.16.rows_ref = bf16[64,64,128]{2,1,0:T(8,128)(2,1)S(1)} reshape(bf16[128,4096]{1,0:T(8,128)(2,1)} %copy-done.6) | data formatting | bytes 2097152 | tf_op jit(solution)/shard_map/reshape | solution.py:502
  6.1 1.2 assemble.1
  7.3 0.0 copy-start
  7.3 1.3 copy-done
  8.6 14.0 %all-to-all-start = ((bf16[64,112,128]{2,1,0:T(8,128)(2,1)}), bf16[64,112,128]{2,1,0:T(8,128)(2,1)S(1)}, u32[]{:S(2)}, u32[]{:S(2)}) async-start(bf16[64,112,128]{2,1,0:T(8,128)(2,1)} %copy-done), calls=%async_computation | async-start | bytes 3670016 | tf_op jit(solution)/shard_map/all_to_all | solution.py:503
  22.6 5.4 %collective-permute-start.9 = (bf16[112,2048]{1,0:T(8,128)(2,1)S(1)}, bf16[112,2048]{1,0:T(8,128)(2,1)S(1)}, u32[]{:S(2)}, u32[]{:S(2)}) collective-permute-start(bf16[112,2048]{1,0:T(8,128)(2,1)S(1)} %get-tuple-element.19.refs_0_), channel_id=1, source_target_pairs={{0,448},{64,0},{128,64},{192,128},{256,192},{320,256},{384,320},{4... | collective-permute-start | bytes 1376264 | tf_op jit(solution)/shard_map/ppermute | solution.py:462
  28.0 0.0 copy-done.3
  28.0 1.9 %collective-permute-start = (bf16[112,2048]{1,0:T(8,128)(2,1)S(1)}, bf16[112,2048]{1,0:T(8,128)(2,1)S(1)}, u32[]{:S(2)}, u32[]{:S(2)}) collective-permute-start(bf16[112,2048]{1,0:T(8,128)(2,1)S(1)} %get-tuple-element.19.refs_0_), channel_id=1, source_target_pairs={{0,64},{64,128},{128,192},{192,256},{256,320},{320,384},{384,448},... | collective-permute-start | bytes 1376264 | tf_op jit(solution)/shard_map/ppermute | solution.py:462
  29.9 5.1 %collective-permute-start.5 = (bf16[112,2048]{1,0:T(8,128)(2,1)S(1)}, bf16[112,2048]{1,0:T(8,128)(2,1)S(1)}, u32[]{:S(2)}, u32[]{:S(2)}) collective-permute-start(bf16[112,2048]{1,0:T(8,128)(2,1)S(1)} %get-tuple-element.20.refs_1_), channel_id=1, source_target_pairs={{0,448},{64,0},{128,64},{192,128},{256,192},{320,256},{384,320},{4... | collective-permute-start | bytes 1376264 | tf_op jit(solution)/shard_map/ppermute | solution.py:462
  35.1 0.0 copy-done.4
  35.1 1.9 %collective-permute-start.1 = (bf16[112,2048]{1,0:T(8,128)(2,1)S(1)}, bf16[112,2048]{1,0:T(8,128)(2,1)S(1)}, u32[]{:S(2)}, u32[]{:S(2)}) collective-permute-start(bf16[112,2048]{1,0:T(8,128)(2,1)S(1)} %get-tuple-element.20.refs_1_), channel_id=1, source_target_pairs={{0,64},{64,128},{128,192},{192,256},{256,320},{320,384},{384,448},... | collective-permute-start | bytes 1376264 | tf_op jit(solution)/shard_map/ppermute | solution.py:462
  37.0 1.8 %collective-permute-done.9.refs_8_.refs_2_ = bf16[112,2048]{1,0:T(8,128)(2,1)S(1)} collective-permute-done((bf16[112,2048]{1,0:T(8,128)(2,1)S(1)}, bf16[112,2048]{1,0:T(8,128)(2,1)S(1)}, u32[]{:S(2)}, u32[]{:S(2)}) %collective-permute-start.9) | collective-permute-done | bytes 458784 | tf_op jit(solution)/shard_map/ppermute | solution.py:462
  38.8 5.6 %collective-permute-start.10 = (bf16[112,2048]{1,0:T(8,128)(2,1)S(1)}, bf16[112,2048]{1,0:T(8,128)(2,1)}, u32[]{:S(2)}, u32[]{:S(2)}) collective-permute-start(bf16[112,2048]{1,0:T(8,128)(2,1)S(1)} %collective-permute-done.9.refs_8_.refs_2_), channel_id=1, source_target_pairs={{0,448},{64,0},{128,64},{192,128},{256,192},{320,256},{384,320},{4... | collective-permute-start | bytes 1376264 | tf_op jit(solution)/shard_map/ppermute | solution.py:462
  44.4 0.1 collective-permute-done.refs_2_.refs_14_
  44.5 1.9 %collective-permute-start.2 = (bf16[112,2048]{1,0:T(8,128)(2,1)S(1)}, bf16[112,2048]{1,0:T(8,128)(2,1)S(1)}, u32[]{:S(2)}, u32[]{:S(2)}) collective-permute-start(bf16[112,2048]{1,0:T(8,128)(2,1)S(1)} %collective-permute-done.refs_2_.refs_14_), channel_id=1, source_target_pairs={{0,64},{64,128},{128,192},{192,256},{256,320},{320,384},{384,448},... | collective-permute-start | bytes 1376264 | tf_op jit(solution)/shard_map/ppermute | solution.py:462
  46.4 2.3 %collective-permute-done.5.refs_9_.refs_3_ = bf16[112,2048]{1,0:T(8,128)(2,1)S(1)} collective-permute-done((bf16[112,2048]{1,0:T(8,128)(2,1)S(1)}, bf16[112,2048]{1,0:T(8,128)(2,1)S(1)}, u32[]{:S(2)}, u32[]{:S(2)}) %collective-permute-start.5) | collective-permute-done | bytes 458784 | tf_op jit(solution)/shard_map/ppermute | solution.py:462
  48.7 5.6 %collective-permute-start.6 = (bf16[112,2048]{1,0:T(8,128)(2,1)S(1)}, bf16[112,2048]{1,0:T(8,128)(2,1)}, u32[]{:S(2)}, u32[]{:S(2)}) collective-permute-start(bf16[112,2048]{1,0:T(8,128)(2,1)S(1)} %collective-permute-done.5.refs_9_.refs_3_), channel_id=1, source_target_pairs={{0,448},{64,0},{128,64},{192,128},{256,192},{320,256},{384,320},{4... | collective-permute-start | bytes 1376264 | tf_op jit(solution)/shard_map/ppermute | solution.py:462
  54.3 0.1 collective-permute-done.1.refs_3_.refs_15_
  54.3 1.9 %collective-permute-start.3 = (bf16[112,2048]{1,0:T(8,128)(2,1)S(1)}, bf16[112,2048]{1,0:T(8,128)(2,1)}, u32[]{:S(2)}, u32[]{:S(2)}) collective-permute-start(bf16[112,2048]{1,0:T(8,128)(2,1)S(1)} %collective-permute-done.1.refs_3_.refs_15_), channel_id=1, source_target_pairs={{0,64},{64,128},{128,192},{192,256},{256,320},{320,384},{384,448},... | collective-permute-start | bytes 1376264 | tf_op jit(solution)/shard_map/ppermute | solution.py:462
  56.2 2.3 %collective-permute-done.10.refs_10_.refs_2_.refs_4_ = bf16[112,2048]{1,0:T(8,128)(2,1)} collective-permute-done((bf16[112,2048]{1,0:T(8,128)(2,1)S(1)}, bf16[112,2048]{1,0:T(8,128)(2,1)}, u32[]{:S(2)}, u32[]{:S(2)}) %collective-permute-start.10) | collective-permute-done | bytes 458784 | tf_op jit(solution)/shard_map/ppermute | solution.py:462
  58.5 5.7 %collective-permute-start.11 = (bf16[112,2048]{1,0:T(8,128)(2,1)}, bf16[112,2048]{1,0:T(8,128)(2,1)}, u32[]{:S(2)}, u32[]{:S(2)}) collective-permute-start(bf16[112,2048]{1,0:T(8,128)(2,1)} %collective-permute-done.10.refs_10_.refs_2_.refs_4_), channel_id=1, source_target_pairs={{0,448},{64,0},{128,64},{192,128},{256,192},{320,256},{384,320},{4... | collective-permute-start | bytes 1376264 | tf_op jit(solution)/shard_map/ppermute | solution.py:462
  64.2 0.0 collective-permute-done.2.refs_4_.refs_0_.refs_12_
  64.2 0.0 copy-start.5
  64.2 1.9 %collective-permute-start.4 = (bf16[112,2048]{1,0:T(8,128)(2,1)S(1)}, bf16[112,2048]{1,0:T(8,128)(2,1)}, u32[]{:S(2)}, u32[]{:S(2)}) collective-permute-start(bf16[112,2048]{1,0:T(8,128)(2,1)S(1)} %collective-permute-done.2.refs_4_.refs_0_.refs_12_), channel_id=1, source_target_pairs={{0,64},{64,128},{128,192},{192,256},{256,320},{320,384},{384,448},... | collective-permute-start | bytes 1376264 | tf_op jit(solution)/shard_map/ppermute | solution.py:462
  66.2 2.2 %collective-permute-done.6.refs_11_.refs_3_.refs_5_ = bf16[112,2048]{1,0:T(8,128)(2,1)} collective-permute-done((bf16[112,2048]{1,0:T(8,128)(2,1)S(1)}, bf16[112,2048]{1,0:T(8,128)(2,1)}, u32[]{:S(2)}, u32[]{:S(2)}) %collective-permute-start.6) | collective-permute-done | bytes 458784 | tf_op jit(solution)/shard_map/ppermute | solution.py:462
  68.3 5.7 %collective-permute-start.7 = (bf16[112,2048]{1,0:T(8,128)(2,1)}, bf16[112,2048]{1,0:T(8,128)(2,1)}, u32[]{:S(2)}, u32[]{:S(2)}) collective-permute-start(bf16[112,2048]{1,0:T(8,128)(2,1)} %collective-permute-done.6.refs_11_.refs_3_.refs_5_), channel_id=1, source_target_pairs={{0,448},{64,0},{128,64},{192,128},{256,192},{320,256},{384,320},{4... | collective-permute-start | bytes 1376264 | tf_op jit(solution)/shard_map/ppermute | solution.py:462
  74.0 0.1 collective-permute-done.3.refs_5_.refs_1_.refs_13_
  74.1 1.9 %collective-permute-start.8 = (bf16[112,2048]{1,0:T(8,128)(2,1)}, bf16[112,2048]{1,0:T(8,128)(2,1)}, u32[]{:S(2)}, u32[]{:S(2)}) collective-permute-start(bf16[112,2048]{1,0:T(8,128)(2,1)} %collective-permute-done.3.refs_5_.refs_1_.refs_13_), channel_id=1, source_target_pairs={{0,64},{64,128},{128,192},{192,256},{256,320},{320,384},{384,448},... | collective-permute-start | bytes 1376264 | tf_op jit(solution)/shard_map/ppermute | solution.py:462
  76.0 0.0 copy-done.11
  76.1 1.2 tick.1.hottest_ref
  77.2 0.0 all-to-all-done.arrived_ref
  77.2 1.6 %repeat.1 = bf16[64,48,128]{2,1,0:T(8,128)(2,1)} custom-call(s32[1,1]{1,0:T(1,128)} %tick.1.hottest_ref, bf16[64,112,128]{2,1,0:T(8,128)(2,1)S(1)} %all-to-all-done.arrived_ref), custom_call_target="tpu_custom_call" | custom-call | tf_op jit(solution)/shard_map/repeat/pallas_call | solution.py:152
  78.9 10.3 %all-to-all-start.2 = ((bf16[64,48,128]{2,1,0:T(8,128)(2,1)}), bf16[64,48,128]{2,1,0:T(8,128)(2,1)S(1)}, u32[]{:S(2)}, u32[]{:S(2)}) async-start(bf16[64,48,128]{2,1,0:T(8,128)(2,1)} %repeat.1), calls=%async_computation.2 | async-start | bytes 1572864 | tf_op jit(solution)/shard_map/all_to_all | solution.py:504
  89.2 0.0 collective-permute-done.4.refs_0_
  89.2 0.0 collective-permute-done.7.refs_1_
  89.2 1.9 %collective-permute-start.12 = (bf16[112,2048]{1,0:T(8,128)(2,1)}, bf16[112,2048]{1,0:T(8,128)(2,1)S(1)}, u32[]{:S(2)}, u32[]{:S(2)}) collective-permute-start(bf16[112,2048]{1,0:T(8,128)(2,1)} %get-tuple-element.21.refs_6_.refs_10_), channel_id=1, source_target_pairs={{0,64},{64,128},{128,192},{192,256},{256,320},{320,384},{384,448},... | collective-permute-start | bytes 1376264 | tf_op jit(solution)/shard_map/ppermute | solution.py:462
  91.2 5.1 %collective-permute-start.13 = (bf16[112,2048]{1,0:T(8,128)(2,1)}, bf16[112,2048]{1,0:T(8,128)(2,1)S(1)}, u32[]{:S(2)}, u32[]{:S(2)}) collective-permute-start(bf16[112,2048]{1,0:T(8,128)(2,1)} %get-tuple-element.22.refs_13_.refs_7_), channel_id=1, source_target_pairs={{0,448},{64,0},{128,64},{192,128},{256,192},{320,256},{384,320},{4... | collective-permute-start | bytes 1376264 | tf_op jit(solution)/shard_map/ppermute | solution.py:462
  96.3 0.0 collective-permute-done.11.refs_12_.refs_6_
  96.3 0.0 collective-permute-done.8.refs_7_.refs_11_
  96.3 5.3 %gathered.1 = (f32[128,4096]{1,0:T(8,128)S(1)}, bf16[128,4096]{1,0:T(8,128)(2,1)S(1)}) custom-call(bf16[64,112,128]{2,1,0:T(8,128)(2,1)S(1)} %all-to-all-done.arrived_ref, bf16[112,2048]{1,0:T(8,128)(2,1)} %copy-done.3, bf16[112,2048]{1,0:T(8,128)(2,1)} %copy-done.4, bf16[112,2048]{1,0:T(8,128)(2,1)} %copy-done.12, bf16[112,2048]{1,0:T(8,128)(2,1)} %copy-done.14, ...), custom_call_target="tpu_custom_call" | custom-call | flops 1409286144 | bytes 5505024 | tf_op jit(solution)/shard_map/gathered/pallas_call | solution.py:202
  101.7 3.7 %collective-permute-done.12.up_ref.refs_8_ = bf16[112,2048]{1,0:T(8,128)(2,1)S(1)} collective-permute-done((bf16[112,2048]{1,0:T(8,128)(2,1)}, bf16[112,2048]{1,0:T(8,128)(2,1)S(1)}, u32[]{:S(2)}, u32[]{:S(2)}) %collective-permute-start.12) | collective-permute-done | bytes 458784 | tf_op jit(solution)/shard_map/ppermute | solution.py:462
  105.4 1.3 collective-permute-done.13.down_ref.refs_9_
  106.7 3.1 %last.1.after_ref = bf16[64,64,128]{2,1,0:T(8,128)(2,1)} custom-call(bf16[128,4096]{1,0:T(8,128)(2,1)S(1)} %get-tuple-element.23.rows_ref, f32[128,4096]{1,0:T(8,128)S(1)} %get-tuple-element.24.acc_ref, bf16[112,2048]{1,0:T(8,128)(2,1)S(1)} %collective-permute-done.12.up_ref.refs_8_, bf16[112,2048]{1,0:T(8,128)(2,1)S(1)} %collective-permute-done.13.down_ref.refs_9_), custom_call_target="tpu_custom_call" | custom-call | tf_op jit(solution)/shard_map/last/pallas_call | solution.py:248
  109.7 1.4 all-to-all-done.2.pieces_ref
  111.1 9.0 %all-to-all-start.1 = ((bf16[64,64,128]{2,1,0:T(8,128)(2,1)}), bf16[64,64,128]{2,1,0:T(8,128)(2,1)S(1)}, u32[]{:S(2)}, u32[]{:S(2)}) async-start(bf16[64,64,128]{2,1,0:T(8,128)(2,1)} %last.1.after_ref), calls=%async_computation.1 | async-start | bytes 2097152 | tf_op jit(solution)/shard_map/all_to_all | solution.py:508
  120.1 2.5 %hot.1 = (bf16[36,4096]{1,0:T(8,128)(2,1)S(1)}, bf16[36,4096]{1,0:T(8,128)(2,1)S(1)}) custom-call(s32[1]{0:T(128)} %bitcast.4.where_ref, bf16[64,48,128]{2,1,0:T(8,128)(2,1)S(1)} %all-to-all-done.2.pieces_ref, bf16[64,64,128]{2,1,0:T(8,128)(2,1)} %last.1.after_ref, bf16[112,2048]{1,0:T(8,128)(2,1)} %copy-done.3, bf16[112,2048]{1,0:T(8,128)(2,1)} %copy-done.4, ...), custom_call_target="tpu_custom_call" | custom-call | tf_op jit(solution)/shard_map/hot/pallas_call | solution.py:312
  122.6 10.6 %all-gather.1 = bf16[2,36,4096]{2,1,0:T(8,128)(2,1)S(1)} all-gather(bf16[1,36,4096]{2,1,0:T(8,128)(2,1)S(1)} %bitcast.13), channel_id=2, replica_groups={{0,64},{128,192},{256,320},{384,448},{1,65},{129,193},{257,321},{385,44..., dimensions={0}, use_global_device_ids=true | all-gather | bytes 884736 | tf_op jit(solution)/shard_map/all_gather | solution.py:468
  133.2 0.1 fusion.1
  133.3 0.1 fusion.2
  133.4 5.5 %collective-permute-start.16 = (bf16[9,4096]{1,0:T(8,128)(2,1)S(1)}, bf16[9,4096]{1,0:T(8,128)(2,1)S(1)}, u32[]{:S(2)}, u32[]{:S(2)}) collective-permute-start(bf16[9,4096]{1,0:T(8,128)(2,1)S(1)} %get-tuple-element.35), channel_id=1, source_target_pairs={{0,384},{64,448},{128,256},{192,320},{256,128},{320,192},{384,0},{... | collective-permute-start | bytes 221192 | tf_op jit(solution)/shard_map/ppermute | solution.py:474
  138.9 1.9 %collective-permute-start.15 = (bf16[9,4096]{1,0:T(8,128)(2,1)S(1)}, bf16[9,4096]{1,0:T(8,128)(2,1)S(1)}, u32[]{:S(2)}, u32[]{:S(2)}) collective-permute-start(bf16[9,4096]{1,0:T(8,128)(2,1)S(1)} %get-tuple-element.36), channel_id=1, source_target_pairs={{0,128},{64,192},{128,0},{192,64},{256,384},{320,448},{384,256},{4... | collective-permute-start | bytes 221192 | tf_op jit(solution)/shard_map/ppermute | solution.py:474
  140.8 4.8 %collective-permute-start.14 = (bf16[9,4096]{1,0:T(8,128)(2,1)S(1)}, bf16[9,4096]{1,0:T(8,128)(2,1)S(1)}, u32[]{:S(2)}, u32[]{:S(2)}) collective-permute-start(bf16[9,4096]{1,0:T(8,128)(2,1)S(1)} %get-tuple-element.37), channel_id=1, source_target_pairs={{0,256},{64,320},{128,384},{192,448},{256,0},{320,64},{384,128},{4... | collective-permute-start | bytes 221192 | tf_op jit(solution)/shard_map/ppermute | solution.py:474
  145.7 1.1 all-to-all-done.1.cold_ref
  146.8 0.0 copy-done.10
  146.8 2.4 %cold_combine.1 = (f32[16,4096]{1,0:T(8,128)S(1)}, f32[8,16]{1,0:T(8,128)S(1)}) custom-call(s32[8,16]{1,0:T(8,128)S(1)} %bitcast.15, f32[8,16]{1,0:T(8,128)S(1)} %bitcast.17, bf16[16,2048]{1,0:T(8,128)(2,1)S(1)} %copy-done.7, bf16[64,64,128]{2,1,0:T(8,128)(2,1)S(1)} %all-to-all-done.1.cold_ref), custom_call_target="tpu_custom_call" | custom-call | flops 68719476736 | bytes 67108864 | tf_op jit(solution)/shard_map/cold_combine/pallas_call | solution.py:365
  149.1 0.0 collective-permute-done.16.refs_2_
  149.2 5.4 %collective-permute-done.15.refs_1_ = bf16[9,4096]{1,0:T(8,128)(2,1)S(1)} collective-permute-done((bf16[9,4096]{1,0:T(8,128)(2,1)S(1)}, bf16[9,4096]{1,0:T(8,128)(2,1)S(1)}, u32[]{:S(2)}, u32[]{:S(2)}) %collective-permute-start.15) | collective-permute-done | bytes 73760 | tf_op jit(solution)/shard_map/ppermute | solution.py:474
  154.5 0.0 collective-permute-done.14.refs_0_
  154.5 1.2 final_combine.1
  (21 shorter events, 0.1 us)
Async XLA Ops:
  0.6 0.7 copy-start.8
  3.2 1.0 copy-start.6
  4.2 23.8 %copy-start.3 = (bf16[112,2048]{1,0:T(8,128)(2,1)}, bf16[112,2048]{1,0:T(8,128)(2,1)S(1)}, u32[]{:S(2)}) copy-start(bf16[112,2048]{1,0:T(8,128)(2,1)S(1)} %get-tuple-element.19.refs_0_) | copy-start | bytes 1376260
  4.2 30.9 %copy-start.4 = (bf16[112,2048]{1,0:T(8,128)(2,1)}, bf16[112,2048]{1,0:T(8,128)(2,1)S(1)}, u32[]{:S(2)}) copy-start(bf16[112,2048]{1,0:T(8,128)(2,1)S(1)} %get-tuple-element.20.refs_1_) | copy-start | bytes 1376260
  7.3 1.3 copy-start
  8.6 68.7 %all-to-all-start = ((bf16[64,112,128]{2,1,0:T(8,128)(2,1)}), bf16[64,112,128]{2,1,0:T(8,128)(2,1)S(1)}, u32[]{:S(2)}, u32[]{:S(2)}) async-start(bf16[64,112,128]{2,1,0:T(8,128)(2,1)} %copy-done), calls=%async_computation | async-start | bytes 3670016 | tf_op jit(solution)/shard_map/all_to_all | solution.py:503
  22.6 16.2 %collective-permute-start.9 = (bf16[112,2048]{1,0:T(8,128)(2,1)S(1)}, bf16[112,2048]{1,0:T(8,128)(2,1)S(1)}, u32[]{:S(2)}, u32[]{:S(2)}) collective-permute-start(bf16[112,2048]{1,0:T(8,128)(2,1)S(1)} %get-tuple-element.19.refs_0_), channel_id=1, source_target_pairs={{0,448},{64,0},{128,64},{192,128},{256,192},{320,256},{384,320},{4... | collective-permute-start | bytes 1376264 | tf_op jit(solution)/shard_map/ppermute | solution.py:462
  28.0 16.5 %collective-permute-start = (bf16[112,2048]{1,0:T(8,128)(2,1)S(1)}, bf16[112,2048]{1,0:T(8,128)(2,1)S(1)}, u32[]{:S(2)}, u32[]{:S(2)}) collective-permute-start(bf16[112,2048]{1,0:T(8,128)(2,1)S(1)} %get-tuple-element.19.refs_0_), channel_id=1, source_target_pairs={{0,64},{64,128},{128,192},{192,256},{256,320},{320,384},{384,448},... | collective-permute-start | bytes 1376264 | tf_op jit(solution)/shard_map/ppermute | solution.py:462
  29.9 18.8 %collective-permute-start.5 = (bf16[112,2048]{1,0:T(8,128)(2,1)S(1)}, bf16[112,2048]{1,0:T(8,128)(2,1)S(1)}, u32[]{:S(2)}, u32[]{:S(2)}) collective-permute-start(bf16[112,2048]{1,0:T(8,128)(2,1)S(1)} %get-tuple-element.20.refs_1_), channel_id=1, source_target_pairs={{0,448},{64,0},{128,64},{192,128},{256,192},{320,256},{384,320},{4... | collective-permute-start | bytes 1376264 | tf_op jit(solution)/shard_map/ppermute | solution.py:462
  35.1 19.3 %collective-permute-start.1 = (bf16[112,2048]{1,0:T(8,128)(2,1)S(1)}, bf16[112,2048]{1,0:T(8,128)(2,1)S(1)}, u32[]{:S(2)}, u32[]{:S(2)}) collective-permute-start(bf16[112,2048]{1,0:T(8,128)(2,1)S(1)} %get-tuple-element.20.refs_1_), channel_id=1, source_target_pairs={{0,64},{64,128},{128,192},{192,256},{256,320},{320,384},{384,448},... | collective-permute-start | bytes 1376264 | tf_op jit(solution)/shard_map/ppermute | solution.py:462
  38.8 37.2 %copy-start.11 = (bf16[112,2048]{1,0:T(8,128)(2,1)}, bf16[112,2048]{1,0:T(8,128)(2,1)S(1)}, u32[]{:S(2)}) copy-start(bf16[112,2048]{1,0:T(8,128)(2,1)S(1)} %collective-permute-done.9.refs_8_.refs_2_) | copy-start | bytes 1376260
  38.8 19.7 %collective-permute-start.10 = (bf16[112,2048]{1,0:T(8,128)(2,1)S(1)}, bf16[112,2048]{1,0:T(8,128)(2,1)}, u32[]{:S(2)}, u32[]{:S(2)}) collective-permute-start(bf16[112,2048]{1,0:T(8,128)(2,1)S(1)} %collective-permute-done.9.refs_8_.refs_2_), channel_id=1, source_target_pairs={{0,448},{64,0},{128,64},{192,128},{256,192},{320,256},{384,320},{4... | collective-permute-start | bytes 1376264 | tf_op jit(solution)/shard_map/ppermute | solution.py:462
  44.5 31.5 %copy-start.12 = (bf16[112,2048]{1,0:T(8,128)(2,1)}, bf16[112,2048]{1,0:T(8,128)(2,1)S(1)}, u32[]{:S(2)}) copy-start(bf16[112,2048]{1,0:T(8,128)(2,1)S(1)} %collective-permute-done.refs_2_.refs_14_) | copy-start | bytes 1376260
  44.5 19.7 %collective-permute-start.2 = (bf16[112,2048]{1,0:T(8,128)(2,1)S(1)}, bf16[112,2048]{1,0:T(8,128)(2,1)S(1)}, u32[]{:S(2)}, u32[]{:S(2)}) collective-permute-start(bf16[112,2048]{1,0:T(8,128)(2,1)S(1)} %collective-permute-done.refs_2_.refs_14_), channel_id=1, source_target_pairs={{0,64},{64,128},{128,192},{192,256},{256,320},{320,384},{384,448},... | collective-permute-start | bytes 1376264 | tf_op jit(solution)/shard_map/ppermute | solution.py:462
  48.7 27.4 %copy-start.13 = (bf16[112,2048]{1,0:T(8,128)(2,1)}, bf16[112,2048]{1,0:T(8,128)(2,1)S(1)}, u32[]{:S(2)}) copy-start(bf16[112,2048]{1,0:T(8,128)(2,1)S(1)} %collective-permute-done.5.refs_9_.refs_3_) | copy-start | bytes 1376260
  48.7 19.7 %collective-permute-start.6 = (bf16[112,2048]{1,0:T(8,128)(2,1)S(1)}, bf16[112,2048]{1,0:T(8,128)(2,1)}, u32[]{:S(2)}, u32[]{:S(2)}) collective-permute-start(bf16[112,2048]{1,0:T(8,128)(2,1)S(1)} %collective-permute-done.5.refs_9_.refs_3_), channel_id=1, source_target_pairs={{0,448},{64,0},{128,64},{192,128},{256,192},{320,256},{384,320},{4... | collective-permute-start | bytes 1376264 | tf_op jit(solution)/shard_map/ppermute | solution.py:462
  54.3 21.7 %copy-start.14 = (bf16[112,2048]{1,0:T(8,128)(2,1)}, bf16[112,2048]{1,0:T(8,128)(2,1)S(1)}, u32[]{:S(2)}) copy-start(bf16[112,2048]{1,0:T(8,128)(2,1)S(1)} %collective-permute-done.1.refs_3_.refs_15_) | copy-start | bytes 1376260
  54.3 19.8 %collective-permute-start.3 = (bf16[112,2048]{1,0:T(8,128)(2,1)S(1)}, bf16[112,2048]{1,0:T(8,128)(2,1)}, u32[]{:S(2)}, u32[]{:S(2)}) collective-permute-start(bf16[112,2048]{1,0:T(8,128)(2,1)S(1)} %collective-permute-done.1.refs_3_.refs_15_), channel_id=1, source_target_pairs={{0,64},{64,128},{128,192},{192,256},{256,320},{320,384},{384,448},... | collective-permute-start | bytes 1376264 | tf_op jit(solution)/shard_map/ppermute | solution.py:462
  58.5 37.8 %collective-permute-start.11 = (bf16[112,2048]{1,0:T(8,128)(2,1)}, bf16[112,2048]{1,0:T(8,128)(2,1)}, u32[]{:S(2)}, u32[]{:S(2)}) collective-permute-start(bf16[112,2048]{1,0:T(8,128)(2,1)} %collective-permute-done.10.refs_10_.refs_2_.refs_4_), channel_id=1, source_target_pairs={{0,448},{64,0},{128,64},{192,128},{256,192},{320,256},{384,320},{4... | collective-permute-start | bytes 1376264 | tf_op jit(solution)/shard_map/ppermute | solution.py:462
  64.2 13.0 %copy-start.5 = (bf16[112,2048]{1,0:T(8,128)(2,1)}, bf16[112,2048]{1,0:T(8,128)(2,1)S(1)}, u32[]{:S(2)}) copy-start(bf16[112,2048]{1,0:T(8,128)(2,1)S(1)} %collective-permute-done.2.refs_4_.refs_0_.refs_12_) | copy-start | bytes 1376260
  64.2 25.0 %collective-permute-start.4 = (bf16[112,2048]{1,0:T(8,128)(2,1)S(1)}, bf16[112,2048]{1,0:T(8,128)(2,1)}, u32[]{:S(2)}, u32[]{:S(2)}) collective-permute-start(bf16[112,2048]{1,0:T(8,128)(2,1)S(1)} %collective-permute-done.2.refs_4_.refs_0_.refs_12_), channel_id=1, source_target_pairs={{0,64},{64,128},{128,192},{192,256},{256,320},{320,384},{384,448},... | collective-permute-start | bytes 1376264 | tf_op jit(solution)/shard_map/ppermute | solution.py:462
  68.3 20.9 %collective-permute-start.7 = (bf16[112,2048]{1,0:T(8,128)(2,1)}, bf16[112,2048]{1,0:T(8,128)(2,1)}, u32[]{:S(2)}, u32[]{:S(2)}) collective-permute-start(bf16[112,2048]{1,0:T(8,128)(2,1)} %collective-permute-done.6.refs_11_.refs_3_.refs_5_), channel_id=1, source_target_pairs={{0,448},{64,0},{128,64},{192,128},{256,192},{320,256},{384,320},{4... | collective-permute-start | bytes 1376264 | tf_op jit(solution)/shard_map/ppermute | solution.py:462
  74.1 22.2 %collective-permute-start.8 = (bf16[112,2048]{1,0:T(8,128)(2,1)}, bf16[112,2048]{1,0:T(8,128)(2,1)}, u32[]{:S(2)}, u32[]{:S(2)}) collective-permute-start(bf16[112,2048]{1,0:T(8,128)(2,1)} %collective-permute-done.3.refs_5_.refs_1_.refs_13_), channel_id=1, source_target_pairs={{0,64},{64,128},{128,192},{192,256},{256,320},{320,384},{384,448},... | collective-permute-start | bytes 1376264 | tf_op jit(solution)/shard_map/ppermute | solution.py:462
  78.9 32.2 %all-to-all-start.2 = ((bf16[64,48,128]{2,1,0:T(8,128)(2,1)}), bf16[64,48,128]{2,1,0:T(8,128)(2,1)S(1)}, u32[]{:S(2)}, u32[]{:S(2)}) async-start(bf16[64,48,128]{2,1,0:T(8,128)(2,1)} %repeat.1), calls=%async_computation.2 | async-start | bytes 1572864 | tf_op jit(solution)/shard_map/all_to_all | solution.py:504
  89.2 16.2 %collective-permute-start.12 = (bf16[112,2048]{1,0:T(8,128)(2,1)}, bf16[112,2048]{1,0:T(8,128)(2,1)S(1)}, u32[]{:S(2)}, u32[]{:S(2)}) collective-permute-start(bf16[112,2048]{1,0:T(8,128)(2,1)} %get-tuple-element.21.refs_6_.refs_10_), channel_id=1, source_target_pairs={{0,64},{64,128},{128,192},{192,256},{256,320},{320,384},{384,448},... | collective-permute-start | bytes 1376264 | tf_op jit(solution)/shard_map/ppermute | solution.py:462
  91.2 15.5 %collective-permute-start.13 = (bf16[112,2048]{1,0:T(8,128)(2,1)}, bf16[112,2048]{1,0:T(8,128)(2,1)S(1)}, u32[]{:S(2)}, u32[]{:S(2)}) collective-permute-start(bf16[112,2048]{1,0:T(8,128)(2,1)} %get-tuple-element.22.refs_13_.refs_7_), channel_id=1, source_target_pairs={{0,448},{64,0},{128,64},{192,128},{256,192},{320,256},{384,320},{4... | collective-permute-start | bytes 1376264 | tf_op jit(solution)/shard_map/ppermute | solution.py:462
  105.4 4.3 %copy-start.1 = (bf16[112,2048]{1,0:T(8,128)(2,1)}, bf16[112,2048]{1,0:T(8,128)(2,1)S(1)}, u32[]{:S(2)}) copy-start(bf16[112,2048]{1,0:T(8,128)(2,1)S(1)} %collective-permute-done.12.up_ref.refs_8_) | copy-start | bytes 1376260
  106.7 3.1 %copy-start.2 = (bf16[112,2048]{1,0:T(8,128)(2,1)}, bf16[112,2048]{1,0:T(8,128)(2,1)S(1)}, u32[]{:S(2)}) copy-start(bf16[112,2048]{1,0:T(8,128)(2,1)S(1)} %collective-permute-done.13.down_ref.refs_9_) | copy-start | bytes 1376260
  111.1 35.6 %all-to-all-start.1 = ((bf16[64,64,128]{2,1,0:T(8,128)(2,1)}), bf16[64,64,128]{2,1,0:T(8,128)(2,1)S(1)}, u32[]{:S(2)}, u32[]{:S(2)}) async-start(bf16[64,64,128]{2,1,0:T(8,128)(2,1)} %last.1.after_ref), calls=%async_computation.1 | async-start | bytes 2097152 | tf_op jit(solution)/shard_map/all_to_all | solution.py:508
  133.2 13.6 %copy-start.7 = (bf16[16,2048]{1,0:T(8,128)(2,1)S(1)}, bf16[16,2048]{1,0:T(8,128)(2,1)}, u32[]{:S(2)}) copy-start(bf16[16,2048]{1,0:T(8,128)(2,1)} %cot_ref.5) | copy-start | bytes 196612
  133.2 13.6 %copy-start.9 = (s32[16,8]{0,1:T(8,128)S(1)}, s32[16,8]{0,1:T(8,128)}, u32[]{:S(2)}) copy-start(s32[16,8]{0,1:T(8,128)} %param.9) | copy-start | bytes 1540
  133.2 13.6 %copy-start.10 = (f32[16,8]{0,1:T(8,128)S(1)}, f32[16,8]{0,1:T(8,128)}, u32[]{:S(2)}) copy-start(f32[16,8]{0,1:T(8,128)} %param.8) | copy-start | bytes 1540
  133.4 15.7 %collective-permute-start.16 = (bf16[9,4096]{1,0:T(8,128)(2,1)S(1)}, bf16[9,4096]{1,0:T(8,128)(2,1)S(1)}, u32[]{:S(2)}, u32[]{:S(2)}) collective-permute-start(bf16[9,4096]{1,0:T(8,128)(2,1)S(1)} %get-tuple-element.35), channel_id=1, source_target_pairs={{0,384},{64,448},{128,256},{192,320},{256,128},{320,192},{384,0},{... | collective-permute-start | bytes 221192 | tf_op jit(solution)/shard_map/ppermute | solution.py:474
  138.9 15.7 %collective-permute-start.15 = (bf16[9,4096]{1,0:T(8,128)(2,1)S(1)}, bf16[9,4096]{1,0:T(8,128)(2,1)S(1)}, u32[]{:S(2)}, u32[]{:S(2)}) collective-permute-start(bf16[9,4096]{1,0:T(8,128)(2,1)S(1)} %get-tuple-element.36), channel_id=1, source_target_pairs={{0,128},{64,192},{128,0},{192,64},{256,384},{320,448},{384,256},{4... | collective-permute-start | bytes 221192 | tf_op jit(solution)/shard_map/ppermute | solution.py:474
  140.8 13.7 %collective-permute-start.14 = (bf16[9,4096]{1,0:T(8,128)(2,1)S(1)}, bf16[9,4096]{1,0:T(8,128)(2,1)S(1)}, u32[]{:S(2)}, u32[]{:S(2)}) collective-permute-start(bf16[9,4096]{1,0:T(8,128)(2,1)S(1)} %get-tuple-element.37), channel_id=1, source_target_pairs={{0,256},{64,320},{128,384},{192,448},{256,0},{320,64},{384,128},{4... | collective-permute-start | bytes 221192 | tf_op jit(solution)/shard_map/ppermute | solution.py:474

commit v9 on v6

--- a/solution.py
+++ b/solution.py
@@ -9,6 +9,7 @@
 
 BF16, F32, I32 = jnp.bfloat16, jnp.float32, jnp.int32
 HOT_PAD = 16
+LANES = 1024
 VMEM_LIMIT = 16 * 1024 * 1024
 
 
@@ -280,18 +281,21 @@
         copy.wait()
     up, down = weights[:units, :], weights[units:, :]
     hidden, act_grad = activations(matmul_nt(tok[...], up), matmul_nt(cot[...], down))
-    packed = send_ref.shape[0]
+    packed, lanes = send_ref.shape
+    blocks_of = 2 * width // lanes
     row = lax.broadcasted_iota(I32, (packed, ring * HOT_PAD), 0)
     column = lax.broadcasted_iota(I32, (packed, ring * HOT_PAD), 1)
-    group = row // hot_rows
-    place = (group % 2) * 4 + (group // 2) * 2
-    within = place * HOT_PAD + row % hot_rows
+    group = row // (blocks_of * hot_rows)
+    block_of = row // hot_rows % blocks_of
+    within = ((group % 2) * 4 + (group // 2) * 2) * HOT_PAD + row % hot_rows
     for odd, out_ref in ((1, send_ref), (0, keep_ref)):
-        chosen = (column == within + odd * HOT_PAD).astype(F32).astype(BF16)
-        picked_hidden = matmul(chosen, hidden).astype(BF16)
-        picked_grad = matmul(chosen, act_grad).astype(BF16)
-        out_ref[:, :width] = matmul(picked_hidden, down).astype(BF16)
-        out_ref[:, width:] = matmul(picked_grad, up).astype(BF16)
+        total = jnp.zeros((packed, lanes), F32)
+        for b in range(blocks_of):
+            chosen = ((column == within + odd * HOT_PAD) & (block_of == b)).astype(F32).astype(BF16)
+            acts, matrix = (hidden, down) if b * lanes < width else (act_grad, up)
+            lo = b * lanes % width
+            total = total + matmul(matmul(chosen, acts).astype(BF16), matrix[:, lo : lo + lanes])
+        out_ref[...] = total.astype(BF16)
 
 
 def hot_partials(here, pieces, blocks, units, hot_rows, after):
@@ -309,7 +313,7 @@
         hot_kernel(units, hot_rows, where_ref, pieces_ref, *grouped, *refs)
 
     inside = pl.BlockSpec(memory_space=pltpu.VMEM)
-    packed = jax.ShapeDtypeStruct((ring // 2 * hot_rows, 2 * width), BF16)
+    packed = jax.ShapeDtypeStruct((ring // 2 * hot_rows * (2 * width // LANES), LANES), BF16)
     return pl.pallas_call(
         kernel,
         out_shape=(packed, packed),
@@ -386,7 +390,8 @@
     ids, gates, cot = ids_ref[...], gate_ref[...], cot_ref[...]
     top_count, tok_rows = ids.shape
     width = cot.shape[1]
-    hot_rows = kept_ref.shape[0]
+    lanes = kept_ref.shape[1]
+    hot_rows = kept_ref.shape[0] * lanes // (2 * width)
     _, hot, _, _, hottest = slot_maps(ids, slots, capacity)
     hottest = hottest.astype(I32)
     gate = jnp.zeros((1, tok_rows), F32)
@@ -397,13 +402,16 @@
     result = kept_ref[...]
     for ref in sent:
         result = result + ref[...].astype(F32)
-    result = result.astype(BF16)
-    for lo, out_ref in ((0, mix_ref), (width, grad_ref)):
-        rows = result[:, lo : lo + width]
+    dots = jnp.zeros(hot.shape, F32)
+    for b in range(2 * width // lanes):
+        rows = result[b * hot_rows : (b + 1) * hot_rows].astype(BF16)
+        lo, at = b * lanes, b * lanes % width
         total = matmul_tn(scale[0], rows) + matmul_tn(scale[1], rows) + matmul_tn(scale[2], rows)
-        out_ref[...] = (sum_ref[:, lo : lo + width] + total).astype(BF16)
-    dots = jnp.where(hot > 0, matmul_nt(result[:, :width], cot), 0.0)
-    dot = jnp.sum(dots, 0, keepdims=True)
+        out_ref = mix_ref if lo < width else grad_ref
+        out_ref[:, at : at + lanes] = (sum_ref[:, lo : lo + lanes] + total).astype(BF16)
+        if lo < width:
+            dots = dots + matmul_nt(rows, cot[:, at : at + lanes])
+    dot = jnp.sum(jnp.where(hot > 0, dots, 0.0), 0, keepdims=True)
     gate_grad_ref[...] = dots_ref[...] + jnp.where(ids == hottest, dot, 0.0)
 
 
@@ -523,10 +531,9 @@
     here = lax.axis_index("dp").astype(I32).reshape(1)
     send, keep = hot_partials(here, hot_pieces, blocks, units, hot_rows, results)
     both = keep.astype(F32) + swap(send, 1).astype(F32)
-    kept = both[:hot_rows]
-    sent = [
-        send_on(both[i * hot_rows : (i + 1) * hot_rows].astype(BF16), place) for i, place in ((1, 4), (2, 2), (3, 6))
-    ]
+    dense = both.shape[0] // 4
+    kept = both[:dense]
+    sent = [send_on(both[i * dense : (i + 1) * dense].astype(BF16), place) for i, place in ((1, 4), (2, 2), (3, 6))]
     sums, dots = cold_combine(ids, gates, cotangent, came_back, capacity)
     mixture, input_grad, gate_grad = final_combine(
         ids, gates, cotangent, sums, dots, kept, sent, slots, capacity

time: 150 us -> 148 us (0.987)
  waiting for transfers between devices: 38.4 us -> 35 us
    ppermute x3, waiting for transfers between devices: 5.38 us -> 2.34 us  [send_on(): return lax.ppermute(x, 'dp', [(i, i ^ bits) for i in range(ring)])]
  transfers between devices with their start and end apart: 14 -> 14, of which waited for: 9 -> 9; matrix products, arithmetic and copies ran while one was open for 1% -> 1% of each run, Pallas kernels for 12% -> 13%
where the time goes in v9:
time: 148 us; the launch traced here: 146 us
  starting transfers between devices  75.2 us (51%)
  waiting for transfers between devices  35 us (24%)
  Pallas kernels  21.5 us (15%)
  blocking collectives  9.87 us (7%)
  local copies, waits for them, and re-layouts  3.44 us (2%)
    ppermute x8, starting transfers between devices, shift(): return lax.ppermute(x, 'dp', [(i, (i + by) % ring) for i in range(ring)])  29.5 us
    ppermute x8, waiting for transfers between devices, shift(): return lax.ppermute(x, 'dp', [(i, (i + by) % ring) for i in range(ring)])  22.5 us
    all_to_all x1, starting transfers between devices, shards(): arrived = lax.all_to_all(outgoing, 'expert', 0, 0, tiled=True)  14 us
    ppermute x3, starting transfers between devices, send_on(): return lax.ppermute(x, 'dp', [(i, i ^ bits) for i in range(ring)])  12.4 us
    all_to_all x1, starting transfers between devices, shards(): came_back = lax.all_to_all(results, 'expert', 0, 0, tiled=True)  11 us
    all_gather x1, blocking collectives, swap(): both = lax.all_gather(x, 'dp', axis=0, axis_index_groups=pairs, tiled=False)  9.87 us
    all_to_all x1, waiting for transfers between devices, shards(): arrived = lax.all_to_all(outgoing, 'expert', 0, 0, tiled=True)  9 us
    all_to_all x1, starting transfers between devices, shards(): lax.all_to_all(repeat(token, arrived, lines), 'expert', 0, 0, tiled=True)  8.39 us
  transfers between devices with their start and end apart: 14, of which 9 were waited for; matrix products, arithmetic and copies ran while one was open for 1% of the time, Pallas kernels for 13%

profile of v9, /device:TPU:6, one launch (start us, length us, event | category | flops | bytes accessed | tf_op | source)
XLA Modules:
  0.0 146.2 jit_solution(6564841836545368429)
XLA Ops:
  0.6 0.0 copy-start.7
  0.6 0.7 copy-done.7
  1.3 1.9 %route.1 = (bf16[128,4096]{1,0:T(8,128)(2,1)S(1)}, bf16[224,2048]{1,0:T(8,128)(2,1)S(1)}, s32[1,1]{1,0:T(1,128)}) custom-call(s32[8,16]{1,0:T(8,128)S(1)} %bitcast.6, bf16[16,2048]{1,0:T(8,128)(2,1)} %tok_ref.1, bf16[16,2048]{1,0:T(8,128)(2,1)} %cot_ref.5, bf16[96,2048]{1,0:T(8,128)(2,1)} %bitcast.11, bf16[96,2048]{1,0:T(8,128)(2,1)} %bitcast.13), custom_call_target="tpu_custom_call" | custom-call | tf_op jit(solution)/shard_map/route/pallas_call | solution.py:88
  3.2 0.0 copy-start.1
  3.2 5.4 %collective-permute-start.3 = (bf16[224,2048]{1,0:T(8,128)(2,1)S(1)}, bf16[224,2048]{1,0:T(8,128)(2,1)}, u32[]{:S(2)}, u32[]{:S(2)}) collective-permute-start(bf16[224,2048]{1,0:T(8,128)(2,1)S(1)} %get-tuple-element.20.refs_0_), channel_id=1, source_target_pairs={{0,448},{64,0},{128,64},{192,128},{256,192},{320,256},{384,320},{4... | collective-permute-start | bytes 2752520 | tf_op jit(solution)/shard_map/ppermute | solution.py:482
  8.6 1.9 %collective-permute-start = (bf16[224,2048]{1,0:T(8,128)(2,1)S(1)}, bf16[224,2048]{1,0:T(8,128)(2,1)}, u32[]{:S(2)}, u32[]{:S(2)}) collective-permute-start(bf16[224,2048]{1,0:T(8,128)(2,1)S(1)} %get-tuple-element.20.refs_0_), channel_id=1, source_target_pairs={{0,64},{64,128},{128,192},{192,256},{256,320},{320,384},{384,448},... | collective-permute-start | bytes 2752520 | tf_op jit(solution)/shard_map/ppermute | solution.py:482
  10.5 0.5 reshape.16.rows_ref
  11.1 1.2 assemble.1
  12.3 0.0 copy-done.1
  12.3 0.0 copy-start
  12.3 1.3 copy-done
  13.5 14.0 %all-to-all-start = ((bf16[64,112,128]{2,1,0:T(8,128)(2,1)}), bf16[64,112,128]{2,1,0:T(8,128)(2,1)S(1)}, u32[]{:S(2)}, u32[]{:S(2)}) async-start(bf16[64,112,128]{2,1,0:T(8,128)(2,1)} %copy-done), calls=%async_computation | async-start | bytes 3670016 | tf_op jit(solution)/shard_map/all_to_all | solution.py:523
  27.6 0.6 collective-permute-done.3.refs_4_.refs_1_
  28.2 5.7 %collective-permute-start.4 = (bf16[224,2048]{1,0:T(8,128)(2,1)}, bf16[224,2048]{1,0:T(8,128)(2,1)}, u32[]{:S(2)}, u32[]{:S(2)}) collective-permute-start(bf16[224,2048]{1,0:T(8,128)(2,1)} %collective-permute-done.3.refs_4_.refs_1_), channel_id=1, source_target_pairs={{0,448},{64,0},{128,64},{192,128},{256,192},{320,256},{384,320},{4... | collective-permute-start | bytes 2752520 | tf_op jit(solution)/shard_map/ppermute | solution.py:482
  33.9 0.0 collective-permute-done.refs_1_.refs_8_
  33.9 1.9 %collective-permute-start.1 = (bf16[224,2048]{1,0:T(8,128)(2,1)}, bf16[224,2048]{1,0:T(8,128)(2,1)S(1)}, u32[]{:S(2)}, u32[]{:S(2)}) collective-permute-start(bf16[224,2048]{1,0:T(8,128)(2,1)} %collective-permute-done.refs_1_.refs_8_), channel_id=1, source_target_pairs={{0,64},{64,128},{128,192},{192,256},{256,320},{320,384},{384,448},... | collective-permute-start | bytes 2752520 | tf_op jit(solution)/shard_map/ppermute | solution.py:482
  35.8 17.1 %collective-permute-done.4.refs_5_.refs_1_.refs_2_ = bf16[224,2048]{1,0:T(8,128)(2,1)} collective-permute-done((bf16[224,2048]{1,0:T(8,128)(2,1)}, bf16[224,2048]{1,0:T(8,128)(2,1)}, u32[]{:S(2)}, u32[]{:S(2)}) %collective-permute-start.4) | collective-permute-done | bytes 917536 | tf_op jit(solution)/shard_map/ppermute | solution.py:482
  52.9 5.6 %collective-permute-start.5 = (bf16[224,2048]{1,0:T(8,128)(2,1)}, bf16[224,2048]{1,0:T(8,128)(2,1)}, u32[]{:S(2)}, u32[]{:S(2)}) collective-permute-start(bf16[224,2048]{1,0:T(8,128)(2,1)} %collective-permute-done.4.refs_5_.refs_1_.refs_2_), channel_id=1, source_target_pairs={{0,448},{64,0},{128,64},{192,128},{256,192},{320,256},{384,320},{4... | collective-permute-start | bytes 2752520 | tf_op jit(solution)/shard_map/ppermute | solution.py:482
  58.5 0.0 collective-permute-done.1.refs_2_.refs_0_.refs_7_
  58.6 0.0 copy-start.2
  58.6 1.9 %collective-permute-start.2 = (bf16[224,2048]{1,0:T(8,128)(2,1)S(1)}, bf16[224,2048]{1,0:T(8,128)(2,1)}, u32[]{:S(2)}, u32[]{:S(2)}) collective-permute-start(bf16[224,2048]{1,0:T(8,128)(2,1)S(1)} %collective-permute-done.1.refs_2_.refs_0_.refs_7_), channel_id=1, source_target_pairs={{0,64},{64,128},{128,192},{192,256},{256,320},{320,384},{384,448},... | collective-permute-start | bytes 2752520 | tf_op jit(solution)/shard_map/ppermute | solution.py:482
  60.5 1.2 tick.1.hottest_ref
  61.7 0.0 copy-done.2
  61.7 9.0 %all-to-all-done.arrived_ref = bf16[64,112,128]{2,1,0:T(8,128)(2,1)S(1)} async-done(((bf16[64,112,128]{2,1,0:T(8,128)(2,1)}), bf16[64,112,128]{2,1,0:T(8,128)(2,1)S(1)}, u32[]{:S(2)}, u32[]{:S(2)}) %all-to-all-start) | async-done | bytes 1835040 | tf_op jit(solution)/shard_map/all_to_all | solution.py:523
  70.7 0.7 repeat.1
  71.4 0.0 copy-start.3
  71.4 0.9 copy-done.3
  72.3 8.4 %all-to-all-start.2 = ((bf16[64,48,128]{2,1,0:T(8,128)(2,1)}), bf16[64,48,128]{2,1,0:T(8,128)(2,1)S(1)}, u32[]{:S(2)}, u32[]{:S(2)}) async-start(bf16[64,48,128]{2,1,0:T(8,128)(2,1)} %copy-done.3), calls=%async_computation.2 | async-start | bytes 1572864 | tf_op jit(solution)/shard_map/all_to_all | solution.py:524
  80.7 0.0 collective-permute-done.5.left_ref
  80.7 1.1 collective-permute-done.2.right_ref
  81.8 1.2 split.1
  83.0 1.9 %collective-permute-start.6 = (bf16[112,2048]{1,0:T(8,128)(2,1)S(1)}, bf16[112,2048]{1,0:T(8,128)(2,1)S(1)}, u32[]{:S(2)}, u32[]{:S(2)}) collective-permute-start(bf16[112,2048]{1,0:T(8,128)(2,1)S(1)} %get-tuple-element.25), channel_id=1, source_target_pairs={{0,64},{64,128},{128,192},{192,256},{256,320},{320,384},{384,448},... | collective-permute-start | bytes 1376264 | tf_op jit(solution)/shard_map/ppermute | solution.py:482
  84.9 5.1 %collective-permute-start.7 = (bf16[112,2048]{1,0:T(8,128)(2,1)S(1)}, bf16[112,2048]{1,0:T(8,128)(2,1)S(1)}, u32[]{:S(2)}, u32[]{:S(2)}) collective-permute-start(bf16[112,2048]{1,0:T(8,128)(2,1)S(1)} %get-tuple-element.26), channel_id=1, source_target_pairs={{0,448},{64,0},{128,64},{192,128},{256,192},{320,256},{384,320},{4... | collective-permute-start | bytes 1376264 | tf_op jit(solution)/shard_map/ppermute | solution.py:482
  90.1 5.3 %gathered.1 = (f32[128,4096]{1,0:T(8,128)S(1)}, bf16[128,4096]{1,0:T(8,128)(2,1)S(1)}) custom-call(bf16[64,112,128]{2,1,0:T(8,128)(2,1)S(1)} %all-to-all-done.arrived_ref, bf16[224,2048]{1,0:T(8,128)(2,1)} %copy-done.1, bf16[224,2048]{1,0:T(8,128)(2,1)} %collective-permute-done.refs_1_.refs_8_, bf16[224,2048]{1,0:T(8,128)(2,1)} %copy-done.2, ...), custom_call_target="tpu_custom_call" | custom-call | flops 1409286144 | bytes 5505024 | tf_op jit(solution)/shard_map/gathered/pallas_call | solution.py:204
  95.4 2.5 %collective-permute-done.6.up_ref.refs_4_ = bf16[112,2048]{1,0:T(8,128)(2,1)S(1)} collective-permute-done((bf16[112,2048]{1,0:T(8,128)(2,1)S(1)}, bf16[112,2048]{1,0:T(8,128)(2,1)S(1)}, u32[]{:S(2)}, u32[]{:S(2)}) %collective-permute-start.6) | collective-permute-done | bytes 458784 | tf_op jit(solution)/shard_map/ppermute | solution.py:482
  97.9 0.0 copy-start.4
  97.9 1.2 collective-permute-done.7.down_ref.refs_5_
  99.1 0.0 copy-start.5
  99.1 3.0 %last.1.after_ref = bf16[64,64,128]{2,1,0:T(8,128)(2,1)} custom-call(bf16[128,4096]{1,0:T(8,128)(2,1)S(1)} %get-tuple-element.23.rows_ref, f32[128,4096]{1,0:T(8,128)S(1)} %get-tuple-element.24.acc_ref, bf16[112,2048]{1,0:T(8,128)(2,1)S(1)} %collective-permute-done.6.up_ref.refs_4_, bf16[112,2048]{1,0:T(8,128)(2,1)S(1)} %collective-permute-done.7.down_ref.refs_5_), custom_call_target="tpu_custom_call" | custom-call | tf_op jit(solution)/shard_map/last/pallas_call | solution.py:250
  102.1 0.0 copy-done.4
  102.1 0.0 copy-done.5
  102.1 0.5 all-to-all-done.2.pieces_ref
  102.6 11.0 %all-to-all-start.1 = ((bf16[64,64,128]{2,1,0:T(8,128)(2,1)}), bf16[64,64,128]{2,1,0:T(8,128)(2,1)S(1)}, u32[]{:S(2)}, u32[]{:S(2)}) async-start(bf16[64,64,128]{2,1,0:T(8,128)(2,1)} %last.1.after_ref), calls=%async_computation.1 | async-start | bytes 2097152 | tf_op jit(solution)/shard_map/all_to_all | solution.py:528
  113.6 3.4 %hot.1 = (bf16[144,1024]{1,0:T(8,128)(2,1)S(1)}, bf16[144,1024]{1,0:T(8,128)(2,1)S(1)}) custom-call(s32[1]{0:T(128)} %bitcast.4.where_ref, bf16[64,48,128]{2,1,0:T(8,128)(2,1)S(1)} %all-to-all-done.2.pieces_ref, bf16[64,64,128]{2,1,0:T(8,128)(2,1)} %last.1.after_ref, bf16[224,2048]{1,0:T(8,128)(2,1)} %copy-done.1, ...), custom_call_target="tpu_custom_call" | custom-call | tf_op jit(solution)/shard_map/hot/pallas_call | solution.py:317
  117.0 0.0 copy-start.6
  117.0 0.0 copy-start.8
  117.0 0.0 copy-start.9
  117.1 9.9 %all-gather = bf16[288,1024]{1,0:T(8,128)(2,1)S(1)} all-gather(bf16[144,1024]{1,0:T(8,128)(2,1)S(1)} %get-tuple-element.31), channel_id=2, replica_groups={{0,64},{128,192},{256,320},{384,448},{1,65},{129,193},{257,321},{385,44..., dimensions={0}, use_global_device_ids=true | all-gather | bytes 884736 | tf_op jit(solution)/shard_map/all_gather | solution.py:488
  126.9 0.1 fusion
  127.1 5.3 %collective-permute-start.10 = (bf16[36,1024]{1,0:T(8,128)(2,1)S(1)}, bf16[36,1024]{1,0:T(8,128)(2,1)S(1)}, u32[]{:S(2)}, u32[]{:S(2)}) collective-permute-start(bf16[36,1024]{1,0:T(8,128)(2,1)S(1)} %get-tuple-element.37), channel_id=1, source_target_pairs={{0,384},{64,448},{128,256},{192,320},{256,128},{320,192},{384,0},{... | collective-permute-start | bytes 221192 | tf_op jit(solution)/shard_map/ppermute | solution.py:494
  132.5 2.2 %collective-permute-start.9 = (bf16[36,1024]{1,0:T(8,128)(2,1)S(1)}, bf16[36,1024]{1,0:T(8,128)(2,1)S(1)}, u32[]{:S(2)}, u32[]{:S(2)}) collective-permute-start(bf16[36,1024]{1,0:T(8,128)(2,1)S(1)} %get-tuple-element.38), channel_id=1, source_target_pairs={{0,128},{64,192},{128,0},{192,64},{256,384},{320,448},{384,256},{4... | collective-permute-start | bytes 221192 | tf_op jit(solution)/shard_map/ppermute | solution.py:494
  134.7 4.9 %collective-permute-start.8 = (bf16[36,1024]{1,0:T(8,128)(2,1)S(1)}, bf16[36,1024]{1,0:T(8,128)(2,1)S(1)}, u32[]{:S(2)}, u32[]{:S(2)}) collective-permute-start(bf16[36,1024]{1,0:T(8,128)(2,1)S(1)} %get-tuple-element.39), channel_id=1, source_target_pairs={{0,256},{64,320},{128,384},{192,448},{256,0},{320,64},{384,128},{4... | collective-permute-start | bytes 221192 | tf_op jit(solution)/shard_map/ppermute | solution.py:494
  139.6 0.7 all-to-all-done.1.cold_ref
  140.2 0.0 copy-done.6
  140.2 0.0 copy-done.8
  140.2 0.0 copy-done.9
  140.3 2.4 %cold_combine.1 = (f32[16,4096]{1,0:T(8,128)S(1)}, f32[8,16]{1,0:T(8,128)S(1)}) custom-call(s32[8,16]{1,0:T(8,128)S(1)} %bitcast.7, f32[8,16]{1,0:T(8,128)S(1)} %bitcast.9, bf16[16,2048]{1,0:T(8,128)(2,1)S(1)} %copy-done.6, bf16[64,64,128]{2,1,0:T(8,128)(2,1)S(1)} %all-to-all-done.1.cold_ref), custom_call_target="tpu_custom_call" | custom-call | flops 68719476736 | bytes 67108864 | tf_op jit(solution)/shard_map/cold_combine/pallas_call | solution.py:370
  142.6 0.0 collective-permute-done.10.refs_2_
  142.6 0.0 collective-permute-done.9.refs_1_
  142.7 2.3 %collective-permute-done.8.refs_0_ = bf16[36,1024]{1,0:T(8,128)(2,1)S(1)} collective-permute-done((bf16[36,1024]{1,0:T(8,128)(2,1)S(1)}, bf16[36,1024]{1,0:T(8,128)(2,1)S(1)}, u32[]{:S(2)}, u32[]{:S(2)}) %collective-permute-start.8) | collective-permute-done | bytes 73760 | tf_op jit(solution)/shard_map/ppermute | solution.py:494
  145.0 1.2 final_combine.1
  (2 shorter events, 0.1 us)
Async XLA Ops:
  0.6 0.7 copy-start.7
  3.2 9.1 %copy-start.1 = (bf16[224,2048]{1,0:T(8,128)(2,1)}, bf16[224,2048]{1,0:T(8,128)(2,1)S(1)}, u32[]{:S(2)}) copy-start(bf16[224,2048]{1,0:T(8,128)(2,1)S(1)} %get-tuple-element.20.refs_0_) | copy-start | bytes 2752516
  3.2 25.0 %collective-permute-start.3 = (bf16[224,2048]{1,0:T(8,128)(2,1)S(1)}, bf16[224,2048]{1,0:T(8,128)(2,1)}, u32[]{:S(2)}, u32[]{:S(2)}) collective-permute-start(bf16[224,2048]{1,0:T(8,128)(2,1)S(1)} %get-tuple-element.20.refs_0_), channel_id=1, source_target_pairs={{0,448},{64,0},{128,64},{192,128},{256,192},{320,256},{384,320},{4... | collective-permute-start | bytes 2752520 | tf_op jit(solution)/shard_map/ppermute | solution.py:482
  8.6 25.3 %collective-permute-start = (bf16[224,2048]{1,0:T(8,128)(2,1)S(1)}, bf16[224,2048]{1,0:T(8,128)(2,1)}, u32[]{:S(2)}, u32[]{:S(2)}) collective-permute-start(bf16[224,2048]{1,0:T(8,128)(2,1)S(1)} %get-tuple-element.20.refs_0_), channel_id=1, source_target_pairs={{0,64},{64,128},{128,192},{192,256},{256,320},{320,384},{384,448},... | collective-permute-start | bytes 2752520 | tf_op jit(solution)/shard_map/ppermute | solution.py:482
  12.3 1.3 copy-start
  13.5 57.1 %all-to-all-start = ((bf16[64,112,128]{2,1,0:T(8,128)(2,1)}), bf16[64,112,128]{2,1,0:T(8,128)(2,1)S(1)}, u32[]{:S(2)}, u32[]{:S(2)}) async-start(bf16[64,112,128]{2,1,0:T(8,128)(2,1)} %copy-done), calls=%async_computation | async-start | bytes 3670016 | tf_op jit(solution)/shard_map/all_to_all | solution.py:523
  28.2 24.8 %collective-permute-start.4 = (bf16[224,2048]{1,0:T(8,128)(2,1)}, bf16[224,2048]{1,0:T(8,128)(2,1)}, u32[]{:S(2)}, u32[]{:S(2)}) collective-permute-start(bf16[224,2048]{1,0:T(8,128)(2,1)} %collective-permute-done.3.refs_4_.refs_1_), channel_id=1, source_target_pairs={{0,448},{64,0},{128,64},{192,128},{256,192},{320,256},{384,320},{4... | collective-permute-start | bytes 2752520 | tf_op jit(solution)/shard_map/ppermute | solution.py:482
  33.9 24.6 %collective-permute-start.1 = (bf16[224,2048]{1,0:T(8,128)(2,1)}, bf16[224,2048]{1,0:T(8,128)(2,1)S(1)}, u32[]{:S(2)}, u32[]{:S(2)}) collective-permute-start(bf16[224,2048]{1,0:T(8,128)(2,1)} %collective-permute-done.refs_1_.refs_8_), channel_id=1, source_target_pairs={{0,64},{64,128},{128,192},{192,256},{256,320},{320,384},{384,448},... | collective-permute-start | bytes 2752520 | tf_op jit(solution)/shard_map/ppermute | solution.py:482
  52.9 27.8 %collective-permute-start.5 = (bf16[224,2048]{1,0:T(8,128)(2,1)}, bf16[224,2048]{1,0:T(8,128)(2,1)}, u32[]{:S(2)}, u32[]{:S(2)}) collective-permute-start(bf16[224,2048]{1,0:T(8,128)(2,1)} %collective-permute-done.4.refs_5_.refs_1_.refs_2_), channel_id=1, source_target_pairs={{0,448},{64,0},{128,64},{192,128},{256,192},{320,256},{384,320},{4... | collective-permute-start | bytes 2752520 | tf_op jit(solution)/shard_map/ppermute | solution.py:482
  58.6 3.1 %copy-start.2 = (bf16[224,2048]{1,0:T(8,128)(2,1)}, bf16[224,2048]{1,0:T(8,128)(2,1)S(1)}, u32[]{:S(2)}) copy-start(bf16[224,2048]{1,0:T(8,128)(2,1)S(1)} %collective-permute-done.1.refs_2_.refs_0_.refs_7_) | copy-start | bytes 2752516
  58.6 23.2 %collective-permute-start.2 = (bf16[224,2048]{1,0:T(8,128)(2,1)S(1)}, bf16[224,2048]{1,0:T(8,128)(2,1)}, u32[]{:S(2)}, u32[]{:S(2)}) collective-permute-start(bf16[224,2048]{1,0:T(8,128)(2,1)S(1)} %collective-permute-done.1.refs_2_.refs_0_.refs_7_), channel_id=1, source_target_pairs={{0,64},{64,128},{128,192},{192,256},{256,320},{320,384},{384,448},... | collective-permute-start | bytes 2752520 | tf_op jit(solution)/shard_map/ppermute | solution.py:482
  71.4 0.9 copy-start.3
  72.3 30.3 %all-to-all-start.2 = ((bf16[64,48,128]{2,1,0:T(8,128)(2,1)}), bf16[64,48,128]{2,1,0:T(8,128)(2,1)S(1)}, u32[]{:S(2)}, u32[]{:S(2)}) async-start(bf16[64,48,128]{2,1,0:T(8,128)(2,1)} %copy-done.3), calls=%async_computation.2 | async-start | bytes 1572864 | tf_op jit(solution)/shard_map/all_to_all | solution.py:524
  83.0 14.9 %collective-permute-start.6 = (bf16[112,2048]{1,0:T(8,128)(2,1)S(1)}, bf16[112,2048]{1,0:T(8,128)(2,1)S(1)}, u32[]{:S(2)}, u32[]{:S(2)}) collective-permute-start(bf16[112,2048]{1,0:T(8,128)(2,1)S(1)} %get-tuple-element.25), channel_id=1, source_target_pairs={{0,64},{64,128},{128,192},{192,256},{256,320},{320,384},{384,448},... | collective-permute-start | bytes 1376264 | tf_op jit(solution)/shard_map/ppermute | solution.py:482
  84.9 14.1 %collective-permute-start.7 = (bf16[112,2048]{1,0:T(8,128)(2,1)S(1)}, bf16[112,2048]{1,0:T(8,128)(2,1)S(1)}, u32[]{:S(2)}, u32[]{:S(2)}) collective-permute-start(bf16[112,2048]{1,0:T(8,128)(2,1)S(1)} %get-tuple-element.26), channel_id=1, source_target_pairs={{0,448},{64,0},{128,64},{192,128},{256,192},{320,256},{384,320},{4... | collective-permute-start | bytes 1376264 | tf_op jit(solution)/shard_map/ppermute | solution.py:482
  97.9 4.2 %copy-start.4 = (bf16[112,2048]{1,0:T(8,128)(2,1)}, bf16[112,2048]{1,0:T(8,128)(2,1)S(1)}, u32[]{:S(2)}) copy-start(bf16[112,2048]{1,0:T(8,128)(2,1)S(1)} %collective-permute-done.6.up_ref.refs_4_) | copy-start | bytes 1376260
  99.1 3.1 %copy-start.5 = (bf16[112,2048]{1,0:T(8,128)(2,1)}, bf16[112,2048]{1,0:T(8,128)(2,1)S(1)}, u32[]{:S(2)}) copy-start(bf16[112,2048]{1,0:T(8,128)(2,1)S(1)} %collective-permute-done.7.down_ref.refs_5_) | copy-start | bytes 1376260
  102.6 37.6 %all-to-all-start.1 = ((bf16[64,64,128]{2,1,0:T(8,128)(2,1)}), bf16[64,64,128]{2,1,0:T(8,128)(2,1)S(1)}, u32[]{:S(2)}, u32[]{:S(2)}) async-start(bf16[64,64,128]{2,1,0:T(8,128)(2,1)} %last.1.after_ref), calls=%async_computation.1 | async-start | bytes 2097152 | tf_op jit(solution)/shard_map/all_to_all | solution.py:528
  117.0 23.2 %copy-start.6 = (bf16[16,2048]{1,0:T(8,128)(2,1)S(1)}, bf16[16,2048]{1,0:T(8,128)(2,1)}, u32[]{:S(2)}) copy-start(bf16[16,2048]{1,0:T(8,128)(2,1)} %cot_ref.5) | copy-start | bytes 196612
  117.0 23.2 %copy-start.8 = (s32[16,8]{0,1:T(8,128)S(1)}, s32[16,8]{0,1:T(8,128)}, u32[]{:S(2)}) copy-start(s32[16,8]{0,1:T(8,128)} %param.9) | copy-start | bytes 1540
  117.0 23.2 %copy-start.9 = (f32[16,8]{0,1:T(8,128)S(1)}, f32[16,8]{0,1:T(8,128)}, u32[]{:S(2)}) copy-start(f32[16,8]{0,1:T(8,128)} %param.8) | copy-start | bytes 1540
  127.1 15.5 %collective-permute-start.10 = (bf16[36,1024]{1,0:T(8,128)(2,1)S(1)}, bf16[36,1024]{1,0:T(8,128)(2,1)S(1)}, u32[]{:S(2)}, u32[]{:S(2)}) collective-permute-start(bf16[36,1024]{1,0:T(8,128)(2,1)S(1)} %get-tuple-element.37), channel_id=1, source_target_pairs={{0,384},{64,448},{128,256},{192,320},{256,128},{320,192},{384,0},{... | collective-permute-start | bytes 221192 | tf_op jit(solution)/shard_map/ppermute | solution.py:494
  132.5 10.2 %collective-permute-start.9 = (bf16[36,1024]{1,0:T(8,128)(2,1)S(1)}, bf16[36,1024]{1,0:T(8,128)(2,1)S(1)}, u32[]{:S(2)}, u32[]{:S(2)}) collective-permute-start(bf16[36,1024]{1,0:T(8,128)(2,1)S(1)} %get-tuple-element.38), channel_id=1, source_target_pairs={{0,128},{64,192},{128,0},{192,64},{256,384},{320,448},{384,256},{4... | collective-permute-start | bytes 221192 | tf_op jit(solution)/shard_map/ppermute | solution.py:494
  134.7 10.3 %collective-permute-start.8 = (bf16[36,1024]{1,0:T(8,128)(2,1)S(1)}, bf16[36,1024]{1,0:T(8,128)(2,1)S(1)}, u32[]{:S(2)}, u32[]{:S(2)}) collective-permute-start(bf16[36,1024]{1,0:T(8,128)(2,1)S(1)} %get-tuple-element.39), channel_id=1, source_target_pairs={{0,256},{64,320},{128,384},{192,448},{256,0},{320,64},{384,128},{4... | collective-permute-start | bytes 221192 | tf_op jit(solution)/shard_map/ppermute | solution.py:494

commit v10 on v9

--- a/solution.py
+++ b/solution.py
@@ -9,6 +9,7 @@
 
 BF16, F32, I32 = jnp.bfloat16, jnp.float32, jnp.int32
 HOT_PAD = 16
+MOST_VMEM = 58 << 20
 LANES = 1024
 VMEM_LIMIT = 16 * 1024 * 1024
 
@@ -131,33 +132,33 @@
         functools.partial(assemble_kernel, tall),
         out_shape=jax.ShapeDtypeStruct((experts, lines + tall, lanes), BF16),
         in_specs=[pl.BlockSpec(memory_space=pltpu.VMEM)] + [pl.BlockSpec(memory_space=pl.ANY)] * 2,
-        out_specs=pl.BlockSpec(memory_space=pltpu.VMEM),
         scratch_shapes=[
             pltpu.VMEM((units, width), BF16),
             pltpu.VMEM((units, width), BF16),
             pltpu.SemaphoreType.DMA((2,)),
         ],
-        compiler_params=pltpu.CompilerParams(vmem_limit_bytes=VMEM_LIMIT),
+        compiler_params=pltpu.CompilerParams(vmem_limit_bytes=MOST_VMEM),
         name="assemble",
     )(rows, outside(up), outside(down))
 
 
-def repeat_kernel(lines, hottest_ref, arrived_ref, out_ref):
-    mine = arrived_ref[hottest_ref[0, 0], lines:, :]
-    out_ref[...] = jnp.broadcast_to(mine[None], out_ref.shape)
+def repeat_kernel(lines, hottest_ref, arrived_ref, out_ref, mine, sem):
+    copy = pltpu.make_async_copy(arrived_ref.at[hottest_ref[0, 0], pl.ds(lines, mine.shape[0])], mine, sem)
+    copy.start()
+    copy.wait()
+    out_ref[...] = jnp.broadcast_to(mine[...][None], out_ref.shape)
 
 
 def repeat(hottest, arrived, lines):
     experts, height, lanes = arrived.shape
-    inside = pl.BlockSpec(memory_space=pltpu.VMEM)
     return pl.pallas_call(
         functools.partial(repeat_kernel, lines),
         out_shape=jax.ShapeDtypeStruct((experts, height - lines, lanes), BF16),
-        in_specs=[pl.BlockSpec(memory_space=pltpu.SMEM), inside],
-        out_specs=inside,
-        compiler_params=pltpu.CompilerParams(vmem_limit_bytes=VMEM_LIMIT),
+        in_specs=[pl.BlockSpec(memory_space=pltpu.SMEM), pl.BlockSpec(memory_space=pl.ANY)],
+        scratch_shapes=[pltpu.VMEM((height - lines, lanes), BF16), pltpu.SemaphoreType.DMA],
+        compiler_params=pltpu.CompilerParams(vmem_limit_bytes=MOST_VMEM),
         name="repeat",
-    )(hottest, arrived)
+    )(hottest, outside(arrived))
 
 
 def activations(pre_act, hidden_grad):
@@ -168,7 +169,9 @@
 
 
 def gathered_kernel(units, lines, arrived_ref, *refs):
-    pieces, (acc_ref, rows_ref, up, down, wide, sems) = refs[:-6], refs[-6:]
+    pieces, (acc_ref, rows_ref, up, down, held, wide, sem, sems) = refs[:-8], refs[-8:]
+    rows_copy = pltpu.make_async_copy(arrived_ref.at[:, pl.ds(0, lines)], held, sem)
+    rows_copy.start()
     width = up.shape[1]
     half = pieces[0].shape[0] // 2
     experts = arrived_ref.shape[0]
@@ -181,8 +184,9 @@
             )
             copy.start()
             copies.append(copy)
+    rows_copy.wait()
     for e in range(experts):
-        wide[e * lines : (e + 1) * lines, :] = arrived_ref[e, :lines, :].astype(F32)
+        wide[e * lines : (e + 1) * lines, :] = held[e].astype(F32)
     blocks = lines // capacity
     for r in range(capacity):
         for b in range(blocks):
@@ -207,12 +211,14 @@
             jax.ShapeDtypeStruct((slots, 2 * width), F32),
             jax.ShapeDtypeStruct((slots, 2 * width), BF16),
         ),
-        in_specs=[pl.BlockSpec(memory_space=pltpu.VMEM)] + [pl.BlockSpec(memory_space=pl.ANY)] * count,
+        in_specs=[pl.BlockSpec(memory_space=pl.ANY)] * (1 + count),
         out_specs=(pl.BlockSpec(memory_space=pltpu.VMEM), pl.BlockSpec(memory_space=pltpu.VMEM)),
         scratch_shapes=[
             pltpu.VMEM((count * units, width), BF16),
             pltpu.VMEM((count * units, width), BF16),
+            pltpu.VMEM((experts, lines, 128), BF16),
             pltpu.VMEM((experts * lines, 128), F32),
+            pltpu.SemaphoreType.DMA,
             pltpu.SemaphoreType.DMA((count, 2)),
         ],
         compiler_params=pltpu.CompilerParams(vmem_limit_bytes=VMEM_LIMIT + (4 << 20)),
@@ -222,7 +228,7 @@
             transcendentals=0,
         ),
         name="gathered",
-    )(arrived, *map(outside, pieces))
+    )(outside(arrived), *map(outside, pieces))
 
 
 def last_kernel(units, rows_ref, acc_ref, up_ref, down_ref, out_ref, wide):

time: 148 us -> 152 us (1.027)
  Pallas kernels: 21.5 us -> 27.1 us
  waiting for transfers between devices: 35 us -> 33.4 us
    pallas_call x1, Pallas kernels: 1.2 us -> 3.65 us  [assemble(): pl.pallas_call(functools.partial(assemble_kernel, tall), out_shape=jax.Sh...]
    pallas_call x1, Pallas kernels: 5.33 us -> 6.97 us  [gathered(): pl.pallas_call(functools.partial(gathered_kernel, units, lines), out_shap...]
    pallas_call x1, Pallas kernels: 0.75 us -> 2.36 us  [repeat(): pl.pallas_call(functools.partial(repeat_kernel, lines), out_shape=jax.Sha...]
  transfers between devices with their start and end apart: 14 -> 14, of which waited for: 9 -> 6; matrix products, arithmetic and copies ran while one was open for 1% -> 1% of each run, Pallas kernels for 13% -> 16%
where the time goes in v10:
time: 152 us; the launch traced here: 150 us
  starting transfers between devices  75.1 us (49%)
  waiting for transfers between devices  33.4 us (22%)
  Pallas kernels  27.1 us (18%)
  blocking collectives  10.1 us (7%)
  local copies, waits for them, and re-layouts  3.03 us (2%)
    ppermute x8, starting transfers between devices, shift(): return lax.ppermute(x, 'dp', [(i, (i + by) % ring) for i in range(ring)])  28.9 us
    ppermute x8, waiting for transfers between devices, shift(): return lax.ppermute(x, 'dp', [(i, (i + by) % ring) for i in range(ring)])  21.1 us
    all_to_all x1, starting transfers between devices, shards(): arrived = lax.all_to_all(outgoing, 'expert', 0, 0, tiled=True)  14.2 us
    ppermute x3, starting transfers between devices, send_on(): return lax.ppermute(x, 'dp', [(i, i ^ bits) for i in range(ring)])  13.2 us
    all_to_all x1, starting transfers between devices, shards(): came_back = lax.all_to_all(results, 'expert', 0, 0, tiled=True)  10.3 us
    all_gather x1, blocking collectives, swap(): both = lax.all_gather(x, 'dp', axis=0, axis_index_groups=pairs, tiled=False)  10.1 us
    all_to_all x1, waiting for transfers between devices, shards(): arrived = lax.all_to_all(outgoing, 'expert', 0, 0, tiled=True)  9.23 us
    all_to_all x1, starting transfers between devices, shards(): lax.all_to_all(repeat(token, arrived, lines), 'expert', 0, 0, tiled=True)  8.4 us
  transfers between devices with their start and end apart: 14, of which 6 were waited for; matrix products, arithmetic and copies ran while one was open for 1% of the time, Pallas kernels for 16%

profile of v10, /device:TPU:6, one launch (start us, length us, event | category | flops | bytes accessed | tf_op | source)
XLA Modules:
  0.0 149.8 jit_solution(8463372358295788751)
XLA Ops:
  0.6 0.0 copy-start.7
  0.6 0.7 copy-done.7
  1.3 1.9 %route.1 = (bf16[128,4096]{1,0:T(8,128)(2,1)S(1)}, bf16[224,2048]{1,0:T(8,128)(2,1)S(1)}, s32[1,1]{1,0:T(1,128)}) custom-call(s32[8,16]{1,0:T(8,128)S(1)} %bitcast.6, bf16[16,2048]{1,0:T(8,128)(2,1)} %tok_ref.1, bf16[16,2048]{1,0:T(8,128)(2,1)} %cot_ref.5, bf16[96,2048]{1,0:T(8,128)(2,1)} %bitcast.11, bf16[96,2048]{1,0:T(8,128)(2,1)} %bitcast.13), custom_call_target="tpu_custom_call" | custom-call | tf_op jit(solution)/shard_map/route/pallas_call | solution.py:89
  3.2 0.0 copy-start
  3.2 5.4 %collective-permute-start.3 = (bf16[224,2048]{1,0:T(8,128)(2,1)S(1)}, bf16[224,2048]{1,0:T(8,128)(2,1)S(1)}, u32[]{:S(2)}, u32[]{:S(2)}) collective-permute-start(bf16[224,2048]{1,0:T(8,128)(2,1)S(1)} %get-tuple-element.20.refs_0_), channel_id=1, source_target_pairs={{0,448},{64,0},{128,64},{192,128},{256,192},{320,256},{384,320},{4... | collective-permute-start | bytes 2752520 | tf_op jit(solution)/shard_map/ppermute | solution.py:488
  8.6 1.9 %collective-permute-start = (bf16[224,2048]{1,0:T(8,128)(2,1)S(1)}, bf16[224,2048]{1,0:T(8,128)(2,1)}, u32[]{:S(2)}, u32[]{:S(2)}) collective-permute-start(bf16[224,2048]{1,0:T(8,128)(2,1)S(1)} %get-tuple-element.20.refs_0_), channel_id=1, source_target_pairs={{0,64},{64,128},{128,192},{192,256},{256,320},{320,384},{384,448},... | collective-permute-start | bytes 2752520 | tf_op jit(solution)/shard_map/ppermute | solution.py:488
  10.5 1.3 reshape.16.rows_ref
  11.9 3.6 %assemble.1 = bf16[64,112,128]{2,1,0:T(8,128)(2,1)} custom-call(bf16[64,64,128]{2,1,0:T(8,128)(2,1)} %reshape.16.rows_ref, bf16[96,2048]{1,0:T(8,128)(2,1)} %bitcast.12, bf16[96,2048]{1,0:T(8,128)(2,1)} %bitcast.14), custom_call_target="tpu_custom_call" | custom-call | tf_op jit(solution)/shard_map/assemble/pallas_call | solution.py:131
  15.5 0.0 copy-done
  15.5 14.2 %all-to-all-start = ((bf16[64,112,128]{2,1,0:T(8,128)(2,1)}), bf16[64,112,128]{2,1,0:T(8,128)(2,1)}, u32[]{:S(2)}, u32[]{:S(2)}) async-start(bf16[64,112,128]{2,1,0:T(8,128)(2,1)} %assemble.1), calls=%async_computation | async-start | bytes 3670016 | tf_op jit(solution)/shard_map/all_to_all | solution.py:529
  29.7 0.0 collective-permute-done.3.refs_4_.refs_1_
  29.7 0.0 copy-start.10
  29.7 5.1 %collective-permute-start.4 = (bf16[224,2048]{1,0:T(8,128)(2,1)S(1)}, bf16[224,2048]{1,0:T(8,128)(2,1)S(1)}, u32[]{:S(2)}, u32[]{:S(2)}) collective-permute-start(bf16[224,2048]{1,0:T(8,128)(2,1)S(1)} %collective-permute-done.3.refs_4_.refs_1_), channel_id=1, source_target_pairs={{0,448},{64,0},{128,64},{192,128},{256,192},{320,256},{384,320},{4... | collective-permute-start | bytes 2752520 | tf_op jit(solution)/shard_map/ppermute | solution.py:488
  34.9 0.0 collective-permute-done.refs_1_.refs_8_
  34.9 1.9 %collective-permute-start.1 = (bf16[224,2048]{1,0:T(8,128)(2,1)}, bf16[224,2048]{1,0:T(8,128)(2,1)S(1)}, u32[]{:S(2)}, u32[]{:S(2)}) collective-permute-start(bf16[224,2048]{1,0:T(8,128)(2,1)} %collective-permute-done.refs_1_.refs_8_), channel_id=1, source_target_pairs={{0,64},{64,128},{128,192},{192,256},{256,320},{320,384},{384,448},... | collective-permute-start | bytes 2752520 | tf_op jit(solution)/shard_map/ppermute | solution.py:488
  36.8 0.0 copy-done.10
  36.8 18.0 %collective-permute-done.4.refs_5_.refs_1_.refs_2_ = bf16[224,2048]{1,0:T(8,128)(2,1)S(1)} collective-permute-done((bf16[224,2048]{1,0:T(8,128)(2,1)S(1)}, bf16[224,2048]{1,0:T(8,128)(2,1)S(1)}, u32[]{:S(2)}, u32[]{:S(2)}) %collective-permute-start.4) | collective-permute-done | bytes 917536 | tf_op jit(solution)/shard_map/ppermute | solution.py:488
  54.8 0.0 copy-start.1
  54.8 5.6 %collective-permute-start.5 = (bf16[224,2048]{1,0:T(8,128)(2,1)S(1)}, bf16[224,2048]{1,0:T(8,128)(2,1)S(1)}, u32[]{:S(2)}, u32[]{:S(2)}) collective-permute-start(bf16[224,2048]{1,0:T(8,128)(2,1)S(1)} %collective-permute-done.4.refs_5_.refs_1_.refs_2_), channel_id=1, source_target_pairs={{0,448},{64,0},{128,64},{192,128},{256,192},{320,256},{384,320},{4... | collective-permute-start | bytes 2752520 | tf_op jit(solution)/shard_map/ppermute | solution.py:488
  60.4 0.0 collective-permute-done.1.refs_2_.refs_0_.refs_7_
  60.4 0.0 copy-start.2
  60.4 1.9 %collective-permute-start.2 = (bf16[224,2048]{1,0:T(8,128)(2,1)S(1)}, bf16[224,2048]{1,0:T(8,128)(2,1)}, u32[]{:S(2)}, u32[]{:S(2)}) collective-permute-start(bf16[224,2048]{1,0:T(8,128)(2,1)S(1)} %collective-permute-done.1.refs_2_.refs_0_.refs_7_), channel_id=1, source_target_pairs={{0,64},{64,128},{128,192},{192,256},{256,320},{320,384},{384,448},... | collective-permute-start | bytes 2752520 | tf_op jit(solution)/shard_map/ppermute | solution.py:488
  62.3 1.2 tick.1.hottest_ref
  63.5 0.0 copy-done.1
  63.5 0.0 copy-done.2
  63.5 9.2 %all-to-all-done.arrived_ref = bf16[64,112,128]{2,1,0:T(8,128)(2,1)} async-done(((bf16[64,112,128]{2,1,0:T(8,128)(2,1)}), bf16[64,112,128]{2,1,0:T(8,128)(2,1)}, u32[]{:S(2)}, u32[]{:S(2)}) %all-to-all-start) | async-done | bytes 1835040 | tf_op jit(solution)/shard_map/all_to_all | solution.py:529
  72.8 2.4 %repeat.1 = bf16[64,48,128]{2,1,0:T(8,128)(2,1)} custom-call(s32[1,1]{1,0:T(1,128)} %tick.1.hottest_ref, bf16[64,112,128]{2,1,0:T(8,128)(2,1)} %all-to-all-done.arrived_ref), custom_call_target="tpu_custom_call" | custom-call | tf_op jit(solution)/shard_map/repeat/pallas_call | solution.py:154
  75.1 8.4 %all-to-all-start.2 = ((bf16[64,48,128]{2,1,0:T(8,128)(2,1)}), bf16[64,48,128]{2,1,0:T(8,128)(2,1)S(1)}, u32[]{:S(2)}, u32[]{:S(2)}) async-start(bf16[64,48,128]{2,1,0:T(8,128)(2,1)} %repeat.1), calls=%async_computation.2 | async-start | bytes 1572864 | tf_op jit(solution)/shard_map/all_to_all | solution.py:530
  83.5 0.0 collective-permute-done.5.left_ref
  83.5 1.5 collective-permute-done.2.right_ref
  85.0 1.0 split.1
  86.1 0.0 copy-start.3
  86.1 0.9 copy-done.3
  87.0 1.9 %collective-permute-start.6 = (bf16[112,2048]{1,0:T(8,128)(2,1)S(1)}, bf16[112,2048]{1,0:T(8,128)(2,1)S(1)}, u32[]{:S(2)}, u32[]{:S(2)}) collective-permute-start(bf16[112,2048]{1,0:T(8,128)(2,1)S(1)} %get-tuple-element.25), channel_id=1, source_target_pairs={{0,64},{64,128},{128,192},{192,256},{256,320},{320,384},{384,448},... | collective-permute-start | bytes 1376264 | tf_op jit(solution)/shard_map/ppermute | solution.py:488
  88.9 5.1 %collective-permute-start.7 = (bf16[112,2048]{1,0:T(8,128)(2,1)S(1)}, bf16[112,2048]{1,0:T(8,128)(2,1)S(1)}, u32[]{:S(2)}, u32[]{:S(2)}) collective-permute-start(bf16[112,2048]{1,0:T(8,128)(2,1)S(1)} %get-tuple-element.26), channel_id=1, source_target_pairs={{0,448},{64,0},{128,64},{192,128},{256,192},{320,256},{384,320},{4... | collective-permute-start | bytes 1376264 | tf_op jit(solution)/shard_map/ppermute | solution.py:488
  94.0 7.0 %gathered.1 = (f32[128,4096]{1,0:T(8,128)S(1)}, bf16[128,4096]{1,0:T(8,128)(2,1)S(1)}) custom-call(bf16[64,112,128]{2,1,0:T(8,128)(2,1)} %all-to-all-done.arrived_ref, bf16[224,2048]{1,0:T(8,128)(2,1)} %copy-done, bf16[224,2048]{1,0:T(8,128)(2,1)} %collective-permute-done.refs_1_.refs_8_, bf16[224,2048]{1,0:T(8,128)(2,1)} %copy-done.2, ...), custom_call_target="tpu_custom_call" | custom-call | flops 1409286144 | bytes 5505024 | tf_op jit(solution)/shard_map/gathered/pallas_call | solution.py:208
  101.0 0.4 collective-permute-done.6.up_ref.refs_4_
  101.5 0.0 copy-start.4
  101.5 1.2 collective-permute-done.7.down_ref.refs_5_
  102.7 0.0 copy-start.5
  102.7 3.0 %last.1.after_ref = bf16[64,64,128]{2,1,0:T(8,128)(2,1)} custom-call(bf16[128,4096]{1,0:T(8,128)(2,1)S(1)} %get-tuple-element.23.rows_ref, f32[128,4096]{1,0:T(8,128)S(1)} %get-tuple-element.24.acc_ref, bf16[112,2048]{1,0:T(8,128)(2,1)S(1)} %collective-permute-done.6.up_ref.refs_4_, bf16[112,2048]{1,0:T(8,128)(2,1)S(1)} %collective-permute-done.7.down_ref.refs_5_), custom_call_target="tpu_custom_call" | custom-call | tf_op jit(solution)/shard_map/last/pallas_call | solution.py:256
  105.7 0.0 copy-done.4
  105.7 0.0 copy-done.5
  105.7 0.0 all-to-all-done.2.pieces_ref
  105.7 10.3 %all-to-all-start.1 = ((bf16[64,64,128]{2,1,0:T(8,128)(2,1)}), bf16[64,64,128]{2,1,0:T(8,128)(2,1)S(1)}, u32[]{:S(2)}, u32[]{:S(2)}) async-start(bf16[64,64,128]{2,1,0:T(8,128)(2,1)} %last.1.after_ref), calls=%async_computation.1 | async-start | bytes 2097152 | tf_op jit(solution)/shard_map/all_to_all | solution.py:534
  116.1 3.4 %hot.1 = (bf16[144,1024]{1,0:T(8,128)(2,1)S(1)}, bf16[144,1024]{1,0:T(8,128)(2,1)S(1)}) custom-call(s32[1]{0:T(128)} %bitcast.4.where_ref, bf16[64,48,128]{2,1,0:T(8,128)(2,1)S(1)} %all-to-all-done.2.pieces_ref, bf16[64,64,128]{2,1,0:T(8,128)(2,1)} %last.1.after_ref, bf16[224,2048]{1,0:T(8,128)(2,1)} %copy-done, bf16[224,2048]{1,0:T(8,128)(2,1)} %copy-done.10, ...), custom_call_target="tpu_custom_call" | custom-call | tf_op jit(solution)/shard_map/hot/pallas_call | solution.py:323
  119.5 0.0 copy-start.6
  119.5 0.0 copy-start.8
  119.5 0.0 copy-start.9
  119.5 10.1 %all-gather = bf16[288,1024]{1,0:T(8,128)(2,1)S(1)} all-gather(bf16[144,1024]{1,0:T(8,128)(2,1)S(1)} %get-tuple-element.31), channel_id=2, replica_groups={{0,64},{128,192},{256,320},{384,448},{1,65},{129,193},{257,321},{385,44..., dimensions={0}, use_global_device_ids=true | all-gather | bytes 884736 | tf_op jit(solution)/shard_map/all_gather | solution.py:494
  129.6 0.1 fusion
  129.8 5.6 %collective-permute-start.10 = (bf16[36,1024]{1,0:T(8,128)(2,1)S(1)}, bf16[36,1024]{1,0:T(8,128)(2,1)S(1)}, u32[]{:S(2)}, u32[]{:S(2)}) collective-permute-start(bf16[36,1024]{1,0:T(8,128)(2,1)S(1)} %get-tuple-element.37), channel_id=1, source_target_pairs={{0,384},{64,448},{128,256},{192,320},{256,128},{320,192},{384,0},{... | collective-permute-start | bytes 221192 | tf_op jit(solution)/shard_map/ppermute | solution.py:500
  135.3 2.9 %collective-permute-start.9 = (bf16[36,1024]{1,0:T(8,128)(2,1)S(1)}, bf16[36,1024]{1,0:T(8,128)(2,1)S(1)}, u32[]{:S(2)}, u32[]{:S(2)}) collective-permute-start(bf16[36,1024]{1,0:T(8,128)(2,1)S(1)} %get-tuple-element.38), channel_id=1, source_target_pairs={{0,128},{64,192},{128,0},{192,64},{256,384},{320,448},{384,256},{4... | collective-permute-start | bytes 221192 | tf_op jit(solution)/shard_map/ppermute | solution.py:500
  138.2 4.8 %collective-permute-start.8 = (bf16[36,1024]{1,0:T(8,128)(2,1)S(1)}, bf16[36,1024]{1,0:T(8,128)(2,1)S(1)}, u32[]{:S(2)}, u32[]{:S(2)}) collective-permute-start(bf16[36,1024]{1,0:T(8,128)(2,1)S(1)} %get-tuple-element.39), channel_id=1, source_target_pairs={{0,256},{64,320},{128,384},{192,448},{256,0},{320,64},{384,128},{4... | collective-permute-start | bytes 221192 | tf_op jit(solution)/shard_map/ppermute | solution.py:500
  143.0 0.0 all-to-all-done.1.cold_ref
  143.0 0.0 copy-done.6
  143.1 0.0 copy-done.8
  143.1 0.0 copy-done.9
  143.1 2.4 %cold_combine.1 = (f32[16,4096]{1,0:T(8,128)S(1)}, f32[8,16]{1,0:T(8,128)S(1)}) custom-call(s32[8,16]{1,0:T(8,128)S(1)} %bitcast.7, f32[8,16]{1,0:T(8,128)S(1)} %bitcast.9, bf16[16,2048]{1,0:T(8,128)(2,1)S(1)} %copy-done.6, bf16[64,64,128]{2,1,0:T(8,128)(2,1)S(1)} %all-to-all-done.1.cold_ref), custom_call_target="tpu_custom_call" | custom-call | flops 68719476736 | bytes 67108864 | tf_op jit(solution)/shard_map/cold_combine/pallas_call | solution.py:376
  145.5 0.0 collective-permute-done.10.refs_2_
  145.5 0.0 collective-permute-done.9.refs_1_
  145.5 3.1 %collective-permute-done.8.refs_0_ = bf16[36,1024]{1,0:T(8,128)(2,1)S(1)} collective-permute-done((bf16[36,1024]{1,0:T(8,128)(2,1)S(1)}, bf16[36,1024]{1,0:T(8,128)(2,1)S(1)}, u32[]{:S(2)}, u32[]{:S(2)}) %collective-permute-start.8) | collective-permute-done | bytes 73760 | tf_op jit(solution)/shard_map/ppermute | solution.py:500
  148.6 1.2 final_combine.1
  (2 shorter events, 0.1 us)
Async XLA Ops:
  0.6 0.7 copy-start.7
  3.2 12.3 %copy-start = (bf16[224,2048]{1,0:T(8,128)(2,1)}, bf16[224,2048]{1,0:T(8,128)(2,1)S(1)}, u32[]{:S(2)}) copy-start(bf16[224,2048]{1,0:T(8,128)(2,1)S(1)} %get-tuple-element.20.refs_0_) | copy-start | bytes 2752516
  3.2 26.5 %collective-permute-start.3 = (bf16[224,2048]{1,0:T(8,128)(2,1)S(1)}, bf16[224,2048]{1,0:T(8,128)(2,1)S(1)}, u32[]{:S(2)}, u32[]{:S(2)}) collective-permute-start(bf16[224,2048]{1,0:T(8,128)(2,1)S(1)} %get-tuple-element.20.refs_0_), channel_id=1, source_target_pairs={{0,448},{64,0},{128,64},{192,128},{256,192},{320,256},{384,320},{4... | collective-permute-start | bytes 2752520 | tf_op jit(solution)/shard_map/ppermute | solution.py:488
  8.6 26.3 %collective-permute-start = (bf16[224,2048]{1,0:T(8,128)(2,1)S(1)}, bf16[224,2048]{1,0:T(8,128)(2,1)}, u32[]{:S(2)}, u32[]{:S(2)}) collective-permute-start(bf16[224,2048]{1,0:T(8,128)(2,1)S(1)} %get-tuple-element.20.refs_0_), channel_id=1, source_target_pairs={{0,64},{64,128},{128,192},{192,256},{256,320},{320,384},{384,448},... | collective-permute-start | bytes 2752520 | tf_op jit(solution)/shard_map/ppermute | solution.py:488
  15.5 57.2 %all-to-all-start = ((bf16[64,112,128]{2,1,0:T(8,128)(2,1)}), bf16[64,112,128]{2,1,0:T(8,128)(2,1)}, u32[]{:S(2)}, u32[]{:S(2)}) async-start(bf16[64,112,128]{2,1,0:T(8,128)(2,1)} %assemble.1), calls=%async_computation | async-start | bytes 3670016 | tf_op jit(solution)/shard_map/all_to_all | solution.py:529
  29.7 7.1 %copy-start.10 = (bf16[224,2048]{1,0:T(8,128)(2,1)}, bf16[224,2048]{1,0:T(8,128)(2,1)S(1)}, u32[]{:S(2)}) copy-start(bf16[224,2048]{1,0:T(8,128)(2,1)S(1)} %collective-permute-done.3.refs_4_.refs_1_) | copy-start | bytes 2752516
  29.7 25.0 %collective-permute-start.4 = (bf16[224,2048]{1,0:T(8,128)(2,1)S(1)}, bf16[224,2048]{1,0:T(8,128)(2,1)S(1)}, u32[]{:S(2)}, u32[]{:S(2)}) collective-permute-start(bf16[224,2048]{1,0:T(8,128)(2,1)S(1)} %collective-permute-done.3.refs_4_.refs_1_), channel_id=1, source_target_pairs={{0,448},{64,0},{128,64},{192,128},{256,192},{320,256},{384,320},{4... | collective-permute-start | bytes 2752520 | tf_op jit(solution)/shard_map/ppermute | solution.py:488
  34.9 25.5 %collective-permute-start.1 = (bf16[224,2048]{1,0:T(8,128)(2,1)}, bf16[224,2048]{1,0:T(8,128)(2,1)S(1)}, u32[]{:S(2)}, u32[]{:S(2)}) collective-permute-start(bf16[224,2048]{1,0:T(8,128)(2,1)} %collective-permute-done.refs_1_.refs_8_), channel_id=1, source_target_pairs={{0,64},{64,128},{128,192},{192,256},{256,320},{320,384},{384,448},... | collective-permute-start | bytes 2752520 | tf_op jit(solution)/shard_map/ppermute | solution.py:488
  54.8 8.7 %copy-start.1 = (bf16[224,2048]{1,0:T(8,128)(2,1)}, bf16[224,2048]{1,0:T(8,128)(2,1)S(1)}, u32[]{:S(2)}) copy-start(bf16[224,2048]{1,0:T(8,128)(2,1)S(1)} %collective-permute-done.4.refs_5_.refs_1_.refs_2_) | copy-start | bytes 2752516
  54.8 28.7 %collective-permute-start.5 = (bf16[224,2048]{1,0:T(8,128)(2,1)S(1)}, bf16[224,2048]{1,0:T(8,128)(2,1)S(1)}, u32[]{:S(2)}, u32[]{:S(2)}) collective-permute-start(bf16[224,2048]{1,0:T(8,128)(2,1)S(1)} %collective-permute-done.4.refs_5_.refs_1_.refs_2_), channel_id=1, source_target_pairs={{0,448},{64,0},{128,64},{192,128},{256,192},{320,256},{384,320},{4... | collective-permute-start | bytes 2752520 | tf_op jit(solution)/shard_map/ppermute | solution.py:488
  60.4 3.1 %copy-start.2 = (bf16[224,2048]{1,0:T(8,128)(2,1)}, bf16[224,2048]{1,0:T(8,128)(2,1)S(1)}, u32[]{:S(2)}) copy-start(bf16[224,2048]{1,0:T(8,128)(2,1)S(1)} %collective-permute-done.1.refs_2_.refs_0_.refs_7_) | copy-start | bytes 2752516
  60.4 24.6 %collective-permute-start.2 = (bf16[224,2048]{1,0:T(8,128)(2,1)S(1)}, bf16[224,2048]{1,0:T(8,128)(2,1)}, u32[]{:S(2)}, u32[]{:S(2)}) collective-permute-start(bf16[224,2048]{1,0:T(8,128)(2,1)S(1)} %collective-permute-done.1.refs_2_.refs_0_.refs_7_), channel_id=1, source_target_pairs={{0,64},{64,128},{128,192},{192,256},{256,320},{320,384},{384,448},... | collective-permute-start | bytes 2752520 | tf_op jit(solution)/shard_map/ppermute | solution.py:488
  75.1 30.6 %all-to-all-start.2 = ((bf16[64,48,128]{2,1,0:T(8,128)(2,1)}), bf16[64,48,128]{2,1,0:T(8,128)(2,1)S(1)}, u32[]{:S(2)}, u32[]{:S(2)}) async-start(bf16[64,48,128]{2,1,0:T(8,128)(2,1)} %repeat.1), calls=%async_computation.2 | async-start | bytes 1572864 | tf_op jit(solution)/shard_map/all_to_all | solution.py:530
  86.1 0.9 copy-start.3
  87.0 14.5 %collective-permute-start.6 = (bf16[112,2048]{1,0:T(8,128)(2,1)S(1)}, bf16[112,2048]{1,0:T(8,128)(2,1)S(1)}, u32[]{:S(2)}, u32[]{:S(2)}) collective-permute-start(bf16[112,2048]{1,0:T(8,128)(2,1)S(1)} %get-tuple-element.25), channel_id=1, source_target_pairs={{0,64},{64,128},{128,192},{192,256},{256,320},{320,384},{384,448},... | collective-permute-start | bytes 1376264 | tf_op jit(solution)/shard_map/ppermute | solution.py:488
  88.9 13.7 %collective-permute-start.7 = (bf16[112,2048]{1,0:T(8,128)(2,1)S(1)}, bf16[112,2048]{1,0:T(8,128)(2,1)S(1)}, u32[]{:S(2)}, u32[]{:S(2)}) collective-permute-start(bf16[112,2048]{1,0:T(8,128)(2,1)S(1)} %get-tuple-element.26), channel_id=1, source_target_pairs={{0,448},{64,0},{128,64},{192,128},{256,192},{320,256},{384,320},{4... | collective-permute-start | bytes 1376264 | tf_op jit(solution)/shard_map/ppermute | solution.py:488
  101.5 4.2 %copy-start.4 = (bf16[112,2048]{1,0:T(8,128)(2,1)}, bf16[112,2048]{1,0:T(8,128)(2,1)S(1)}, u32[]{:S(2)}) copy-start(bf16[112,2048]{1,0:T(8,128)(2,1)S(1)} %collective-permute-done.6.up_ref.refs_4_) | copy-start | bytes 1376260
  102.7 3.0 %copy-start.5 = (bf16[112,2048]{1,0:T(8,128)(2,1)}, bf16[112,2048]{1,0:T(8,128)(2,1)S(1)}, u32[]{:S(2)}) copy-start(bf16[112,2048]{1,0:T(8,128)(2,1)S(1)} %collective-permute-done.7.down_ref.refs_5_) | copy-start | bytes 1376260
  105.7 37.3 %all-to-all-start.1 = ((bf16[64,64,128]{2,1,0:T(8,128)(2,1)}), bf16[64,64,128]{2,1,0:T(8,128)(2,1)S(1)}, u32[]{:S(2)}, u32[]{:S(2)}) async-start(bf16[64,64,128]{2,1,0:T(8,128)(2,1)} %last.1.after_ref), calls=%async_computation.1 | async-start | bytes 2097152 | tf_op jit(solution)/shard_map/all_to_all | solution.py:534
  119.5 23.6 %copy-start.6 = (bf16[16,2048]{1,0:T(8,128)(2,1)S(1)}, bf16[16,2048]{1,0:T(8,128)(2,1)}, u32[]{:S(2)}) copy-start(bf16[16,2048]{1,0:T(8,128)(2,1)} %cot_ref.5) | copy-start | bytes 196612
  119.5 23.6 %copy-start.8 = (s32[16,8]{0,1:T(8,128)S(1)}, s32[16,8]{0,1:T(8,128)}, u32[]{:S(2)}) copy-start(s32[16,8]{0,1:T(8,128)} %param.9) | copy-start | bytes 1540
  119.5 23.6 %copy-start.9 = (f32[16,8]{0,1:T(8,128)S(1)}, f32[16,8]{0,1:T(8,128)}, u32[]{:S(2)}) copy-start(f32[16,8]{0,1:T(8,128)} %param.8) | copy-start | bytes 1540
  129.8 15.7 %collective-permute-start.10 = (bf16[36,1024]{1,0:T(8,128)(2,1)S(1)}, bf16[36,1024]{1,0:T(8,128)(2,1)S(1)}, u32[]{:S(2)}, u32[]{:S(2)}) collective-permute-start(bf16[36,1024]{1,0:T(8,128)(2,1)S(1)} %get-tuple-element.37), channel_id=1, source_target_pairs={{0,384},{64,448},{128,256},{192,320},{256,128},{320,192},{384,0},{... | collective-permute-start | bytes 221192 | tf_op jit(solution)/shard_map/ppermute | solution.py:500
  135.3 10.1 %collective-permute-start.9 = (bf16[36,1024]{1,0:T(8,128)(2,1)S(1)}, bf16[36,1024]{1,0:T(8,128)(2,1)S(1)}, u32[]{:S(2)}, u32[]{:S(2)}) collective-permute-start(bf16[36,1024]{1,0:T(8,128)(2,1)S(1)} %get-tuple-element.38), channel_id=1, source_target_pairs={{0,128},{64,192},{128,0},{192,64},{256,384},{320,448},{384,256},{4... | collective-permute-start | bytes 221192 | tf_op jit(solution)/shard_map/ppermute | solution.py:500
  138.2 10.3 %collective-permute-start.8 = (bf16[36,1024]{1,0:T(8,128)(2,1)S(1)}, bf16[36,1024]{1,0:T(8,128)(2,1)S(1)}, u32[]{:S(2)}, u32[]{:S(2)}) collective-permute-start(bf16[36,1024]{1,0:T(8,128)(2,1)S(1)} %get-tuple-element.39), channel_id=1, source_target_pairs={{0,256},{64,320},{128,384},{192,448},{256,0},{320,64},{384,128},{4... | collective-permute-start | bytes 221192 | tf_op jit(solution)/shard_map/ppermute | solution.py:500

commit v11 on v9

--- a/solution.py
+++ b/solution.py
@@ -225,7 +225,7 @@
     )(arrived, *map(outside, pieces))
 
 
-def last_kernel(units, rows_ref, acc_ref, up_ref, down_ref, out_ref, wide):
+def last_kernel(units, rows_ref, acc_ref, up_ref, down_ref, out_hbm, out_ref, wide, sems):
     width = up_ref.shape[1]
     experts, lines, _ = out_ref.shape
     capacity = rows_ref.shape[0] // experts
@@ -241,8 +241,17 @@
                 wide[pl.ds(r * blocks + line, experts, stride=lines), :] = sums[
                     r * experts : (r + 1) * experts, b * 128 : (b + 1) * 128
                 ]
-    for e in range(experts):
-        out_ref[e] = wide[e * lines : (e + 1) * lines, :].astype(BF16)
+    parts = sems.shape[0]
+    share = experts // parts
+    stores = []
+    for part in range(parts):
+        for e in range(part * share, (part + 1) * share):
+            out_ref[e] = wide[e * lines : (e + 1) * lines, :].astype(BF16)
+        span = pl.ds(part * share, share)
+        stores.append(pltpu.make_async_copy(out_ref.at[span], out_hbm.at[span], sems.at[part]))
+        stores[-1].start()
+    for store in stores:
+        store.wait()
 
 
 def last(rows, acc, up_half, down_half, units, experts):
@@ -250,7 +259,13 @@
     return pl.pallas_call(
         functools.partial(last_kernel, units),
         out_shape=jax.ShapeDtypeStruct((experts, lines, 128), BF16),
-        scratch_shapes=[pltpu.VMEM((experts * lines, 128), F32)],
+        in_specs=[pl.BlockSpec(memory_space=pltpu.VMEM)] * 4,
+        out_specs=pl.BlockSpec(memory_space=pl.ANY),
+        scratch_shapes=[
+            pltpu.VMEM((experts, lines, 128), BF16),
+            pltpu.VMEM((experts * lines, 128), F32),
+            pltpu.SemaphoreType.DMA((4,)),
+        ],
         compiler_params=pltpu.CompilerParams(vmem_limit_bytes=VMEM_LIMIT),
         name="last",
     )(rows, acc, up_half, down_half)

time: 148 us -> 148 us (level)
  no operation moved by 1% of the time
where the time goes in v11:
time: 148 us; the launch traced here: 146 us
  starting transfers between devices  75.3 us (51%)
  waiting for transfers between devices  35 us (24%)
  Pallas kernels  21.5 us (15%)
  blocking collectives  9.87 us (7%)
  local copies, waits for them, and re-layouts  3.44 us (2%)
    ppermute x8, starting transfers between devices, shift(): return lax.ppermute(x, 'dp', [(i, (i + by) % ring) for i in range(ring)])  29.5 us
    ppermute x8, waiting for transfers between devices, shift(): return lax.ppermute(x, 'dp', [(i, (i + by) % ring) for i in range(ring)])  22.5 us
    all_to_all x1, starting transfers between devices, shards(): arrived = lax.all_to_all(outgoing, 'expert', 0, 0, tiled=True)  14 us
    ppermute x3, starting transfers between devices, send_on(): return lax.ppermute(x, 'dp', [(i, i ^ bits) for i in range(ring)])  12.4 us
    all_to_all x1, starting transfers between devices, shards(): came_back = lax.all_to_all(results, 'expert', 0, 0, tiled=True)  11 us
    all_gather x1, blocking collectives, swap(): both = lax.all_gather(x, 'dp', axis=0, axis_index_groups=pairs, tiled=False)  9.87 us
    all_to_all x1, waiting for transfers between devices, shards(): arrived = lax.all_to_all(outgoing, 'expert', 0, 0, tiled=True)  9 us
    all_to_all x1, starting transfers between devices, shards(): lax.all_to_all(repeat(token, arrived, lines), 'expert', 0, 0, tiled=True)  8.39 us
  transfers between devices with their start and end apart: 14, of which 9 were waited for; matrix products, arithmetic and copies ran while one was open for 1% of the time, Pallas kernels for 13%

profile of v11, /device:TPU:6, one launch (start us, length us, event | category | flops | bytes accessed | tf_op | source)
XLA Modules:
  0.0 146.2 jit_solution(13873085448380687509)
XLA Ops:
  0.6 0.0 copy-start.7
  0.6 0.7 copy-done.7
  1.3 1.9 %route.1 = (bf16[128,4096]{1,0:T(8,128)(2,1)S(1)}, bf16[224,2048]{1,0:T(8,128)(2,1)S(1)}, s32[1,1]{1,0:T(1,128)}) custom-call(s32[8,16]{1,0:T(8,128)S(1)} %bitcast.6, bf16[16,2048]{1,0:T(8,128)(2,1)} %tok_ref.1, bf16[16,2048]{1,0:T(8,128)(2,1)} %cot_ref.5, bf16[96,2048]{1,0:T(8,128)(2,1)} %bitcast.11, bf16[96,2048]{1,0:T(8,128)(2,1)} %bitcast.13), custom_call_target="tpu_custom_call" | custom-call | tf_op jit(solution)/shard_map/route/pallas_call | solution.py:88
  3.2 0.0 copy-start.1
  3.2 5.4 %collective-permute-start.3 = (bf16[224,2048]{1,0:T(8,128)(2,1)S(1)}, bf16[224,2048]{1,0:T(8,128)(2,1)}, u32[]{:S(2)}, u32[]{:S(2)}) collective-permute-start(bf16[224,2048]{1,0:T(8,128)(2,1)S(1)} %get-tuple-element.20.refs_0_), channel_id=1, source_target_pairs={{0,448},{64,0},{128,64},{192,128},{256,192},{320,256},{384,320},{4... | collective-permute-start | bytes 2752520 | tf_op jit(solution)/shard_map/ppermute | solution.py:497
  8.6 1.9 %collective-permute-start = (bf16[224,2048]{1,0:T(8,128)(2,1)S(1)}, bf16[224,2048]{1,0:T(8,128)(2,1)}, u32[]{:S(2)}, u32[]{:S(2)}) collective-permute-start(bf16[224,2048]{1,0:T(8,128)(2,1)S(1)} %get-tuple-element.20.refs_0_), channel_id=1, source_target_pairs={{0,64},{64,128},{128,192},{192,256},{256,320},{320,384},{384,448},... | collective-permute-start | bytes 2752520 | tf_op jit(solution)/shard_map/ppermute | solution.py:497
  10.5 0.5 reshape.16.rows_ref
  11.1 1.2 assemble.1
  12.3 0.0 copy-done.1
  12.3 0.0 copy-start
  12.3 1.3 copy-done
  13.5 14.0 %all-to-all-start = ((bf16[64,112,128]{2,1,0:T(8,128)(2,1)}), bf16[64,112,128]{2,1,0:T(8,128)(2,1)S(1)}, u32[]{:S(2)}, u32[]{:S(2)}) async-start(bf16[64,112,128]{2,1,0:T(8,128)(2,1)} %copy-done), calls=%async_computation | async-start | bytes 3670016 | tf_op jit(solution)/shard_map/all_to_all | solution.py:538
  27.6 0.6 collective-permute-done.3.refs_4_.refs_1_
  28.2 5.7 %collective-permute-start.4 = (bf16[224,2048]{1,0:T(8,128)(2,1)}, bf16[224,2048]{1,0:T(8,128)(2,1)}, u32[]{:S(2)}, u32[]{:S(2)}) collective-permute-start(bf16[224,2048]{1,0:T(8,128)(2,1)} %collective-permute-done.3.refs_4_.refs_1_), channel_id=1, source_target_pairs={{0,448},{64,0},{128,64},{192,128},{256,192},{320,256},{384,320},{4... | collective-permute-start | bytes 2752520 | tf_op jit(solution)/shard_map/ppermute | solution.py:497
  33.9 0.0 collective-permute-done.refs_1_.refs_8_
  33.9 1.9 %collective-permute-start.1 = (bf16[224,2048]{1,0:T(8,128)(2,1)}, bf16[224,2048]{1,0:T(8,128)(2,1)S(1)}, u32[]{:S(2)}, u32[]{:S(2)}) collective-permute-start(bf16[224,2048]{1,0:T(8,128)(2,1)} %collective-permute-done.refs_1_.refs_8_), channel_id=1, source_target_pairs={{0,64},{64,128},{128,192},{192,256},{256,320},{320,384},{384,448},... | collective-permute-start | bytes 2752520 | tf_op jit(solution)/shard_map/ppermute | solution.py:497
  35.8 17.1 %collective-permute-done.4.refs_5_.refs_1_.refs_2_ = bf16[224,2048]{1,0:T(8,128)(2,1)} collective-permute-done((bf16[224,2048]{1,0:T(8,128)(2,1)}, bf16[224,2048]{1,0:T(8,128)(2,1)}, u32[]{:S(2)}, u32[]{:S(2)}) %collective-permute-start.4) | collective-permute-done | bytes 917536 | tf_op jit(solution)/shard_map/ppermute | solution.py:497
  52.9 5.6 %collective-permute-start.5 = (bf16[224,2048]{1,0:T(8,128)(2,1)}, bf16[224,2048]{1,0:T(8,128)(2,1)}, u32[]{:S(2)}, u32[]{:S(2)}) collective-permute-start(bf16[224,2048]{1,0:T(8,128)(2,1)} %collective-permute-done.4.refs_5_.refs_1_.refs_2_), channel_id=1, source_target_pairs={{0,448},{64,0},{128,64},{192,128},{256,192},{320,256},{384,320},{4... | collective-permute-start | bytes 2752520 | tf_op jit(solution)/shard_map/ppermute | solution.py:497
  58.5 0.0 collective-permute-done.1.refs_2_.refs_0_.refs_7_
  58.6 0.0 copy-start.2
  58.6 1.9 %collective-permute-start.2 = (bf16[224,2048]{1,0:T(8,128)(2,1)S(1)}, bf16[224,2048]{1,0:T(8,128)(2,1)}, u32[]{:S(2)}, u32[]{:S(2)}) collective-permute-start(bf16[224,2048]{1,0:T(8,128)(2,1)S(1)} %collective-permute-done.1.refs_2_.refs_0_.refs_7_), channel_id=1, source_target_pairs={{0,64},{64,128},{128,192},{192,256},{256,320},{320,384},{384,448},... | collective-permute-start | bytes 2752520 | tf_op jit(solution)/shard_map/ppermute | solution.py:497
  60.5 1.2 tick.1.hottest_ref
  61.7 0.0 copy-done.2
  61.7 9.0 %all-to-all-done.arrived_ref = bf16[64,112,128]{2,1,0:T(8,128)(2,1)S(1)} async-done(((bf16[64,112,128]{2,1,0:T(8,128)(2,1)}), bf16[64,112,128]{2,1,0:T(8,128)(2,1)S(1)}, u32[]{:S(2)}, u32[]{:S(2)}) %all-to-all-start) | async-done | bytes 1835040 | tf_op jit(solution)/shard_map/all_to_all | solution.py:538
  70.7 0.7 repeat.1
  71.4 0.0 copy-start.3
  71.4 0.9 copy-done.3
  72.3 8.4 %all-to-all-start.2 = ((bf16[64,48,128]{2,1,0:T(8,128)(2,1)}), bf16[64,48,128]{2,1,0:T(8,128)(2,1)S(1)}, u32[]{:S(2)}, u32[]{:S(2)}) async-start(bf16[64,48,128]{2,1,0:T(8,128)(2,1)} %copy-done.3), calls=%async_computation.2 | async-start | bytes 1572864 | tf_op jit(solution)/shard_map/all_to_all | solution.py:539
  80.7 0.0 collective-permute-done.5.left_ref
  80.7 1.1 collective-permute-done.2.right_ref
  81.8 1.2 split.1
  83.0 1.9 %collective-permute-start.6 = (bf16[112,2048]{1,0:T(8,128)(2,1)S(1)}, bf16[112,2048]{1,0:T(8,128)(2,1)S(1)}, u32[]{:S(2)}, u32[]{:S(2)}) collective-permute-start(bf16[112,2048]{1,0:T(8,128)(2,1)S(1)} %get-tuple-element.25), channel_id=1, source_target_pairs={{0,64},{64,128},{128,192},{192,256},{256,320},{320,384},{384,448},... | collective-permute-start | bytes 1376264 | tf_op jit(solution)/shard_map/ppermute | solution.py:497
  84.9 5.1 %collective-permute-start.7 = (bf16[112,2048]{1,0:T(8,128)(2,1)S(1)}, bf16[112,2048]{1,0:T(8,128)(2,1)S(1)}, u32[]{:S(2)}, u32[]{:S(2)}) collective-permute-start(bf16[112,2048]{1,0:T(8,128)(2,1)S(1)} %get-tuple-element.26), channel_id=1, source_target_pairs={{0,448},{64,0},{128,64},{192,128},{256,192},{320,256},{384,320},{4... | collective-permute-start | bytes 1376264 | tf_op jit(solution)/shard_map/ppermute | solution.py:497
  90.1 5.3 %gathered.1 = (f32[128,4096]{1,0:T(8,128)S(1)}, bf16[128,4096]{1,0:T(8,128)(2,1)S(1)}) custom-call(bf16[64,112,128]{2,1,0:T(8,128)(2,1)S(1)} %all-to-all-done.arrived_ref, bf16[224,2048]{1,0:T(8,128)(2,1)} %copy-done.1, bf16[224,2048]{1,0:T(8,128)(2,1)} %collective-permute-done.refs_1_.refs_8_, bf16[224,2048]{1,0:T(8,128)(2,1)} %copy-done.2, ...), custom_call_target="tpu_custom_call" | custom-call | flops 1409286144 | bytes 5505024 | tf_op jit(solution)/shard_map/gathered/pallas_call | solution.py:204
  95.4 2.5 %collective-permute-done.6.up_ref.refs_4_ = bf16[112,2048]{1,0:T(8,128)(2,1)S(1)} collective-permute-done((bf16[112,2048]{1,0:T(8,128)(2,1)S(1)}, bf16[112,2048]{1,0:T(8,128)(2,1)S(1)}, u32[]{:S(2)}, u32[]{:S(2)}) %collective-permute-start.6) | collective-permute-done | bytes 458784 | tf_op jit(solution)/shard_map/ppermute | solution.py:497
  97.9 0.0 copy-start.4
  97.9 1.2 collective-permute-done.7.down_ref.refs_5_
  99.1 0.0 copy-start.5
  99.1 3.0 %last.1.after_ref = bf16[64,64,128]{2,1,0:T(8,128)(2,1)} custom-call(bf16[128,4096]{1,0:T(8,128)(2,1)S(1)} %get-tuple-element.23.rows_ref, f32[128,4096]{1,0:T(8,128)S(1)} %get-tuple-element.24.acc_ref, bf16[112,2048]{1,0:T(8,128)(2,1)S(1)} %collective-permute-done.6.up_ref.refs_4_, bf16[112,2048]{1,0:T(8,128)(2,1)S(1)} %collective-permute-done.7.down_ref.refs_5_), custom_call_target="tpu_custom_call" | custom-call | tf_op jit(solution)/shard_map/last/pallas_call | solution.py:259
  102.1 0.0 copy-done.4
  102.1 0.0 copy-done.5
  102.1 0.5 all-to-all-done.2.pieces_ref
  102.6 11.0 %all-to-all-start.1 = ((bf16[64,64,128]{2,1,0:T(8,128)(2,1)}), bf16[64,64,128]{2,1,0:T(8,128)(2,1)S(1)}, u32[]{:S(2)}, u32[]{:S(2)}) async-start(bf16[64,64,128]{2,1,0:T(8,128)(2,1)} %last.1.after_ref), calls=%async_computation.1 | async-start | bytes 2097152 | tf_op jit(solution)/shard_map/all_to_all | solution.py:543
  113.6 3.4 %hot.1 = (bf16[144,1024]{1,0:T(8,128)(2,1)S(1)}, bf16[144,1024]{1,0:T(8,128)(2,1)S(1)}) custom-call(s32[1]{0:T(128)} %bitcast.4.where_ref, bf16[64,48,128]{2,1,0:T(8,128)(2,1)S(1)} %all-to-all-done.2.pieces_ref, bf16[64,64,128]{2,1,0:T(8,128)(2,1)} %last.1.after_ref, bf16[224,2048]{1,0:T(8,128)(2,1)} %copy-done.1, ...), custom_call_target="tpu_custom_call" | custom-call | tf_op jit(solution)/shard_map/hot/pallas_call | solution.py:332
  117.0 0.0 copy-start.6
  117.0 0.0 copy-start.8
  117.1 0.0 copy-start.9
  117.1 9.9 %all-gather = bf16[288,1024]{1,0:T(8,128)(2,1)S(1)} all-gather(bf16[144,1024]{1,0:T(8,128)(2,1)S(1)} %get-tuple-element.31), channel_id=2, replica_groups={{0,64},{128,192},{256,320},{384,448},{1,65},{129,193},{257,321},{385,44..., dimensions={0}, use_global_device_ids=true | all-gather | bytes 884736 | tf_op jit(solution)/shard_map/all_gather | solution.py:503
  126.9 0.1 fusion
  127.2 5.5 %collective-permute-start.10 = (bf16[36,1024]{1,0:T(8,128)(2,1)S(1)}, bf16[36,1024]{1,0:T(8,128)(2,1)S(1)}, u32[]{:S(2)}, u32[]{:S(2)}) collective-permute-start(bf16[36,1024]{1,0:T(8,128)(2,1)S(1)} %get-tuple-element.37), channel_id=1, source_target_pairs={{0,384},{64,448},{128,256},{192,320},{256,128},{320,192},{384,0},{... | collective-permute-start | bytes 221192 | tf_op jit(solution)/shard_map/ppermute | solution.py:509
  132.7 2.0 %collective-permute-start.9 = (bf16[36,1024]{1,0:T(8,128)(2,1)S(1)}, bf16[36,1024]{1,0:T(8,128)(2,1)S(1)}, u32[]{:S(2)}, u32[]{:S(2)}) collective-permute-start(bf16[36,1024]{1,0:T(8,128)(2,1)S(1)} %get-tuple-element.38), channel_id=1, source_target_pairs={{0,128},{64,192},{128,0},{192,64},{256,384},{320,448},{384,256},{4... | collective-permute-start | bytes 221192 | tf_op jit(solution)/shard_map/ppermute | solution.py:509
  134.7 4.9 %collective-permute-start.8 = (bf16[36,1024]{1,0:T(8,128)(2,1)S(1)}, bf16[36,1024]{1,0:T(8,128)(2,1)S(1)}, u32[]{:S(2)}, u32[]{:S(2)}) collective-permute-start(bf16[36,1024]{1,0:T(8,128)(2,1)S(1)} %get-tuple-element.39), channel_id=1, source_target_pairs={{0,256},{64,320},{128,384},{192,448},{256,0},{320,64},{384,128},{4... | collective-permute-start | bytes 221192 | tf_op jit(solution)/shard_map/ppermute | solution.py:509
  139.6 0.7 all-to-all-done.1.cold_ref
  140.3 0.0 copy-done.6
  140.3 0.0 copy-done.8
  140.3 0.0 copy-done.9
  140.3 2.4 %cold_combine.1 = (f32[16,4096]{1,0:T(8,128)S(1)}, f32[8,16]{1,0:T(8,128)S(1)}) custom-call(s32[8,16]{1,0:T(8,128)S(1)} %bitcast.7, f32[8,16]{1,0:T(8,128)S(1)} %bitcast.9, bf16[16,2048]{1,0:T(8,128)(2,1)S(1)} %copy-done.6, bf16[64,64,128]{2,1,0:T(8,128)(2,1)S(1)} %all-to-all-done.1.cold_ref), custom_call_target="tpu_custom_call" | custom-call | flops 68719476736 | bytes 67108864 | tf_op jit(solution)/shard_map/cold_combine/pallas_call | solution.py:385
  142.7 0.0 collective-permute-done.10.refs_2_
  142.7 0.0 collective-permute-done.9.refs_1_
  142.7 2.3 %collective-permute-done.8.refs_0_ = bf16[36,1024]{1,0:T(8,128)(2,1)S(1)} collective-permute-done((bf16[36,1024]{1,0:T(8,128)(2,1)S(1)}, bf16[36,1024]{1,0:T(8,128)(2,1)S(1)}, u32[]{:S(2)}, u32[]{:S(2)}) %collective-permute-start.8) | collective-permute-done | bytes 73760 | tf_op jit(solution)/shard_map/ppermute | solution.py:509
  145.0 1.2 final_combine.1
  (2 shorter events, 0.1 us)
Async XLA Ops:
  0.6 0.7 copy-start.7
  3.2 9.1 %copy-start.1 = (bf16[224,2048]{1,0:T(8,128)(2,1)}, bf16[224,2048]{1,0:T(8,128)(2,1)S(1)}, u32[]{:S(2)}) copy-start(bf16[224,2048]{1,0:T(8,128)(2,1)S(1)} %get-tuple-element.20.refs_0_) | copy-start | bytes 2752516
  3.2 25.0 %collective-permute-start.3 = (bf16[224,2048]{1,0:T(8,128)(2,1)S(1)}, bf16[224,2048]{1,0:T(8,128)(2,1)}, u32[]{:S(2)}, u32[]{:S(2)}) collective-permute-start(bf16[224,2048]{1,0:T(8,128)(2,1)S(1)} %get-tuple-element.20.refs_0_), channel_id=1, source_target_pairs={{0,448},{64,0},{128,64},{192,128},{256,192},{320,256},{384,320},{4... | collective-permute-start | bytes 2752520 | tf_op jit(solution)/shard_map/ppermute | solution.py:497
  8.6 25.3 %collective-permute-start = (bf16[224,2048]{1,0:T(8,128)(2,1)S(1)}, bf16[224,2048]{1,0:T(8,128)(2,1)}, u32[]{:S(2)}, u32[]{:S(2)}) collective-permute-start(bf16[224,2048]{1,0:T(8,128)(2,1)S(1)} %get-tuple-element.20.refs_0_), channel_id=1, source_target_pairs={{0,64},{64,128},{128,192},{192,256},{256,320},{320,384},{384,448},... | collective-permute-start | bytes 2752520 | tf_op jit(solution)/shard_map/ppermute | solution.py:497
  12.3 1.3 copy-start
  13.5 57.1 %all-to-all-start = ((bf16[64,112,128]{2,1,0:T(8,128)(2,1)}), bf16[64,112,128]{2,1,0:T(8,128)(2,1)S(1)}, u32[]{:S(2)}, u32[]{:S(2)}) async-start(bf16[64,112,128]{2,1,0:T(8,128)(2,1)} %copy-done), calls=%async_computation | async-start | bytes 3670016 | tf_op jit(solution)/shard_map/all_to_all | solution.py:538
  28.2 24.8 %collective-permute-start.4 = (bf16[224,2048]{1,0:T(8,128)(2,1)}, bf16[224,2048]{1,0:T(8,128)(2,1)}, u32[]{:S(2)}, u32[]{:S(2)}) collective-permute-start(bf16[224,2048]{1,0:T(8,128)(2,1)} %collective-permute-done.3.refs_4_.refs_1_), channel_id=1, source_target_pairs={{0,448},{64,0},{128,64},{192,128},{256,192},{320,256},{384,320},{4... | collective-permute-start | bytes 2752520 | tf_op jit(solution)/shard_map/ppermute | solution.py:497
  33.9 24.6 %collective-permute-start.1 = (bf16[224,2048]{1,0:T(8,128)(2,1)}, bf16[224,2048]{1,0:T(8,128)(2,1)S(1)}, u32[]{:S(2)}, u32[]{:S(2)}) collective-permute-start(bf16[224,2048]{1,0:T(8,128)(2,1)} %collective-permute-done.refs_1_.refs_8_), channel_id=1, source_target_pairs={{0,64},{64,128},{128,192},{192,256},{256,320},{320,384},{384,448},... | collective-permute-start | bytes 2752520 | tf_op jit(solution)/shard_map/ppermute | solution.py:497
  52.9 27.8 %collective-permute-start.5 = (bf16[224,2048]{1,0:T(8,128)(2,1)}, bf16[224,2048]{1,0:T(8,128)(2,1)}, u32[]{:S(2)}, u32[]{:S(2)}) collective-permute-start(bf16[224,2048]{1,0:T(8,128)(2,1)} %collective-permute-done.4.refs_5_.refs_1_.refs_2_), channel_id=1, source_target_pairs={{0,448},{64,0},{128,64},{192,128},{256,192},{320,256},{384,320},{4... | collective-permute-start | bytes 2752520 | tf_op jit(solution)/shard_map/ppermute | solution.py:497
  58.6 3.1 %copy-start.2 = (bf16[224,2048]{1,0:T(8,128)(2,1)}, bf16[224,2048]{1,0:T(8,128)(2,1)S(1)}, u32[]{:S(2)}) copy-start(bf16[224,2048]{1,0:T(8,128)(2,1)S(1)} %collective-permute-done.1.refs_2_.refs_0_.refs_7_) | copy-start | bytes 2752516
  58.6 23.2 %collective-permute-start.2 = (bf16[224,2048]{1,0:T(8,128)(2,1)S(1)}, bf16[224,2048]{1,0:T(8,128)(2,1)}, u32[]{:S(2)}, u32[]{:S(2)}) collective-permute-start(bf16[224,2048]{1,0:T(8,128)(2,1)S(1)} %collective-permute-done.1.refs_2_.refs_0_.refs_7_), channel_id=1, source_target_pairs={{0,64},{64,128},{128,192},{192,256},{256,320},{320,384},{384,448},... | collective-permute-start | bytes 2752520 | tf_op jit(solution)/shard_map/ppermute | solution.py:497
  71.4 0.9 copy-start.3
  72.3 30.3 %all-to-all-start.2 = ((bf16[64,48,128]{2,1,0:T(8,128)(2,1)}), bf16[64,48,128]{2,1,0:T(8,128)(2,1)S(1)}, u32[]{:S(2)}, u32[]{:S(2)}) async-start(bf16[64,48,128]{2,1,0:T(8,128)(2,1)} %copy-done.3), calls=%async_computation.2 | async-start | bytes 1572864 | tf_op jit(solution)/shard_map/all_to_all | solution.py:539
  83.0 14.9 %collective-permute-start.6 = (bf16[112,2048]{1,0:T(8,128)(2,1)S(1)}, bf16[112,2048]{1,0:T(8,128)(2,1)S(1)}, u32[]{:S(2)}, u32[]{:S(2)}) collective-permute-start(bf16[112,2048]{1,0:T(8,128)(2,1)S(1)} %get-tuple-element.25), channel_id=1, source_target_pairs={{0,64},{64,128},{128,192},{192,256},{256,320},{320,384},{384,448},... | collective-permute-start | bytes 1376264 | tf_op jit(solution)/shard_map/ppermute | solution.py:497
  84.9 14.1 %collective-permute-start.7 = (bf16[112,2048]{1,0:T(8,128)(2,1)S(1)}, bf16[112,2048]{1,0:T(8,128)(2,1)S(1)}, u32[]{:S(2)}, u32[]{:S(2)}) collective-permute-start(bf16[112,2048]{1,0:T(8,128)(2,1)S(1)} %get-tuple-element.26), channel_id=1, source_target_pairs={{0,448},{64,0},{128,64},{192,128},{256,192},{320,256},{384,320},{4... | collective-permute-start | bytes 1376264 | tf_op jit(solution)/shard_map/ppermute | solution.py:497
  97.9 4.2 %copy-start.4 = (bf16[112,2048]{1,0:T(8,128)(2,1)}, bf16[112,2048]{1,0:T(8,128)(2,1)S(1)}, u32[]{:S(2)}) copy-start(bf16[112,2048]{1,0:T(8,128)(2,1)S(1)} %collective-permute-done.6.up_ref.refs_4_) | copy-start | bytes 1376260
  99.1 3.1 %copy-start.5 = (bf16[112,2048]{1,0:T(8,128)(2,1)}, bf16[112,2048]{1,0:T(8,128)(2,1)S(1)}, u32[]{:S(2)}) copy-start(bf16[112,2048]{1,0:T(8,128)(2,1)S(1)} %collective-permute-done.7.down_ref.refs_5_) | copy-start | bytes 1376260
  102.6 37.6 %all-to-all-start.1 = ((bf16[64,64,128]{2,1,0:T(8,128)(2,1)}), bf16[64,64,128]{2,1,0:T(8,128)(2,1)S(1)}, u32[]{:S(2)}, u32[]{:S(2)}) async-start(bf16[64,64,128]{2,1,0:T(8,128)(2,1)} %last.1.after_ref), calls=%async_computation.1 | async-start | bytes 2097152 | tf_op jit(solution)/shard_map/all_to_all | solution.py:543
  117.0 23.2 %copy-start.6 = (bf16[16,2048]{1,0:T(8,128)(2,1)S(1)}, bf16[16,2048]{1,0:T(8,128)(2,1)}, u32[]{:S(2)}) copy-start(bf16[16,2048]{1,0:T(8,128)(2,1)} %cot_ref.5) | copy-start | bytes 196612
  117.0 23.2 %copy-start.8 = (s32[16,8]{0,1:T(8,128)S(1)}, s32[16,8]{0,1:T(8,128)}, u32[]{:S(2)}) copy-start(s32[16,8]{0,1:T(8,128)} %param.9) | copy-start | bytes 1540
  117.1 23.2 %copy-start.9 = (f32[16,8]{0,1:T(8,128)S(1)}, f32[16,8]{0,1:T(8,128)}, u32[]{:S(2)}) copy-start(f32[16,8]{0,1:T(8,128)} %param.8) | copy-start | bytes 1540
  127.2 15.5 %collective-permute-start.10 = (bf16[36,1024]{1,0:T(8,128)(2,1)S(1)}, bf16[36,1024]{1,0:T(8,128)(2,1)S(1)}, u32[]{:S(2)}, u32[]{:S(2)}) collective-permute-start(bf16[36,1024]{1,0:T(8,128)(2,1)S(1)} %get-tuple-element.37), channel_id=1, source_target_pairs={{0,384},{64,448},{128,256},{192,320},{256,128},{320,192},{384,0},{... | collective-permute-start | bytes 221192 | tf_op jit(solution)/shard_map/ppermute | solution.py:509
  132.7 10.0 %collective-permute-start.9 = (bf16[36,1024]{1,0:T(8,128)(2,1)S(1)}, bf16[36,1024]{1,0:T(8,128)(2,1)S(1)}, u32[]{:S(2)}, u32[]{:S(2)}) collective-permute-start(bf16[36,1024]{1,0:T(8,128)(2,1)S(1)} %get-tuple-element.38), channel_id=1, source_target_pairs={{0,128},{64,192},{128,0},{192,64},{256,384},{320,448},{384,256},{4... | collective-permute-start | bytes 221192 | tf_op jit(solution)/shard_map/ppermute | solution.py:509
  134.7 10.3 %collective-permute-start.8 = (bf16[36,1024]{1,0:T(8,128)(2,1)S(1)}, bf16[36,1024]{1,0:T(8,128)(2,1)S(1)}, u32[]{:S(2)}, u32[]{:S(2)}) collective-permute-start(bf16[36,1024]{1,0:T(8,128)(2,1)S(1)} %get-tuple-element.39), channel_id=1, source_target_pairs={{0,256},{64,320},{128,384},{192,448},{256,0},{320,64},{384,128},{4... | collective-permute-start | bytes 221192 | tf_op jit(solution)/shard_map/ppermute | solution.py:509

commit v12 on v9

--- a/solution.py
+++ b/solution.py
@@ -55,7 +55,7 @@
 
 
 def route_kernel(
-    capacity, ids_ref, tok_ref, cot_ref, up_ref, down_ref, out_ref, own_ref, hottest_ref, tok, cot, sems
+    capacity, ids_hbm, tok_ref, cot_ref, up_ref, down_ref, out_ref, own_ref, hottest_ref, ids_ref, tok, cot, sems
 ):
     slots, width = out_ref.shape[0], tok.shape[1]
     units = up_ref.shape[0]
@@ -65,8 +65,10 @@
         pltpu.make_async_copy(up_ref, own_ref.at[pl.ds(0, units)], sems.at[2]),
         pltpu.make_async_copy(down_ref, own_ref.at[pl.ds(half, units)], sems.at[3]),
     ]
-    for copy in loads + copies:
+    first = pltpu.make_async_copy(ids_hbm, ids_ref, sems.at[4])
+    for copy in [first] + loads + copies:
         copy.start()
+    first.wait()
     cold, hot, _, _, hottest = slot_maps(ids_ref[...], slots, capacity)
     cold, hot = cold.astype(BF16), hot.astype(BF16)
     hottest_ref[0, 0] = jnp.max(hottest).astype(I32)
@@ -92,16 +94,17 @@
             jax.ShapeDtypeStruct((2 * (units + HOT_PAD), width), BF16),
             jax.ShapeDtypeStruct((1, 1), I32),
         ),
-        in_specs=[inside] + [anywhere] * 4,
+        in_specs=[anywhere] * 5,
         out_specs=(inside, inside, pl.BlockSpec(memory_space=pltpu.SMEM)),
         scratch_shapes=[
+            pltpu.VMEM(ids.shape, I32),
             pltpu.VMEM((tok_rows, width), BF16),
             pltpu.VMEM((tok_rows, width), BF16),
-            pltpu.SemaphoreType.DMA((4,)),
+            pltpu.SemaphoreType.DMA((5,)),
         ],
         compiler_params=pltpu.CompilerParams(vmem_limit_bytes=VMEM_LIMIT),
         name="route",
-    )(ids, *map(outside, (tokens, cotangent, up, down)))
+    )(*map(outside, (ids, tokens, cotangent, up, down)))
 
 
 def assemble_kernel(tall, rows_ref, up_ref, down_ref, out_ref, up, down, sems):

time: 148 us -> 148 us (level)
  no operation moved by 1% of the time
where the time goes in v12:
time: 148 us; the launch traced here: 146 us
  starting transfers between devices  75.2 us (51%)
  waiting for transfers between devices  35 us (24%)
  Pallas kernels  21.6 us (15%)
  blocking collectives  9.87 us (7%)
  local copies, waits for them, and re-layouts  2.77 us (2%)
    ppermute x8, starting transfers between devices, shift(): return lax.ppermute(x, 'dp', [(i, (i + by) % ring) for i in range(ring)])  29.5 us
    ppermute x8, waiting for transfers between devices, shift(): return lax.ppermute(x, 'dp', [(i, (i + by) % ring) for i in range(ring)])  22.5 us
    all_to_all x1, starting transfers between devices, shards(): arrived = lax.all_to_all(outgoing, 'expert', 0, 0, tiled=True)  14 us
    ppermute x3, starting transfers between devices, send_on(): return lax.ppermute(x, 'dp', [(i, i ^ bits) for i in range(ring)])  12.4 us
    all_to_all x1, starting transfers between devices, shards(): came_back = lax.all_to_all(results, 'expert', 0, 0, tiled=True)  10.9 us
    all_gather x1, blocking collectives, swap(): both = lax.all_gather(x, 'dp', axis=0, axis_index_groups=pairs, tiled=False)  9.87 us
    all_to_all x1, waiting for transfers between devices, shards(): arrived = lax.all_to_all(outgoing, 'expert', 0, 0, tiled=True)  9 us
    all_to_all x1, starting transfers between devices, shards(): lax.all_to_all(repeat(token, arrived, lines), 'expert', 0, 0, tiled=True)  8.39 us
  transfers between devices with their start and end apart: 14, of which 9 were waited for; matrix products, arithmetic and copies ran while one was open for 1% of the time, Pallas kernels for 13%

profile of v12, /device:TPU:6, one launch (start us, length us, event | category | flops | bytes accessed | tf_op | source)
XLA Modules:
  0.0 145.6 jit_solution(17078749840437535106)
XLA Ops:
  0.6 2.0 %route.1 = (bf16[128,4096]{1,0:T(8,128)(2,1)S(1)}, bf16[224,2048]{1,0:T(8,128)(2,1)S(1)}, s32[1,1]{1,0:T(1,128)}) custom-call(s32[8,16]{1,0:T(8,128)} %bitcast.6, bf16[16,2048]{1,0:T(8,128)(2,1)} %tok_ref.1, bf16[16,2048]{1,0:T(8,128)(2,1)} %cot_ref.5, bf16[96,2048]{1,0:T(8,128)(2,1)} %bitcast.11, bf16[96,2048]{1,0:T(8,128)(2,1)} %bitcast.13), custom_call_target="tpu_custom_call" | custom-call | tf_op jit(solution)/shard_map/route/pallas_call | solution.py:90
  2.6 0.0 copy-start.1
  2.6 5.4 %collective-permute-start.3 = (bf16[224,2048]{1,0:T(8,128)(2,1)S(1)}, bf16[224,2048]{1,0:T(8,128)(2,1)}, u32[]{:S(2)}, u32[]{:S(2)}) collective-permute-start(bf16[224,2048]{1,0:T(8,128)(2,1)S(1)} %get-tuple-element.20.refs_0_), channel_id=1, source_target_pairs={{0,448},{64,0},{128,64},{192,128},{256,192},{320,256},{384,320},{4... | collective-permute-start | bytes 2752520 | tf_op jit(solution)/shard_map/ppermute | solution.py:485
  8.0 1.9 %collective-permute-start = (bf16[224,2048]{1,0:T(8,128)(2,1)S(1)}, bf16[224,2048]{1,0:T(8,128)(2,1)}, u32[]{:S(2)}, u32[]{:S(2)}) collective-permute-start(bf16[224,2048]{1,0:T(8,128)(2,1)S(1)} %get-tuple-element.20.refs_0_), channel_id=1, source_target_pairs={{0,64},{64,128},{128,192},{192,256},{256,320},{320,384},{384,448},... | collective-permute-start | bytes 2752520 | tf_op jit(solution)/shard_map/ppermute | solution.py:485
  9.9 0.5 reshape.16.rows_ref
  10.5 1.2 assemble.1
  11.7 0.0 copy-done.1
  11.7 0.0 copy-start
  11.7 1.3 copy-done
  13.0 14.0 %all-to-all-start = ((bf16[64,112,128]{2,1,0:T(8,128)(2,1)}), bf16[64,112,128]{2,1,0:T(8,128)(2,1)S(1)}, u32[]{:S(2)}, u32[]{:S(2)}) async-start(bf16[64,112,128]{2,1,0:T(8,128)(2,1)} %copy-done), calls=%async_computation | async-start | bytes 3670016 | tf_op jit(solution)/shard_map/all_to_all | solution.py:526
  27.0 0.6 collective-permute-done.3.refs_4_.refs_1_
  27.6 5.7 %collective-permute-start.4 = (bf16[224,2048]{1,0:T(8,128)(2,1)}, bf16[224,2048]{1,0:T(8,128)(2,1)}, u32[]{:S(2)}, u32[]{:S(2)}) collective-permute-start(bf16[224,2048]{1,0:T(8,128)(2,1)} %collective-permute-done.3.refs_4_.refs_1_), channel_id=1, source_target_pairs={{0,448},{64,0},{128,64},{192,128},{256,192},{320,256},{384,320},{4... | collective-permute-start | bytes 2752520 | tf_op jit(solution)/shard_map/ppermute | solution.py:485
  33.3 0.0 collective-permute-done.refs_1_.refs_8_
  33.3 1.9 %collective-permute-start.1 = (bf16[224,2048]{1,0:T(8,128)(2,1)}, bf16[224,2048]{1,0:T(8,128)(2,1)S(1)}, u32[]{:S(2)}, u32[]{:S(2)}) collective-permute-start(bf16[224,2048]{1,0:T(8,128)(2,1)} %collective-permute-done.refs_1_.refs_8_), channel_id=1, source_target_pairs={{0,64},{64,128},{128,192},{192,256},{256,320},{320,384},{384,448},... | collective-permute-start | bytes 2752520 | tf_op jit(solution)/shard_map/ppermute | solution.py:485
  35.2 17.1 %collective-permute-done.4.refs_5_.refs_1_.refs_2_ = bf16[224,2048]{1,0:T(8,128)(2,1)} collective-permute-done((bf16[224,2048]{1,0:T(8,128)(2,1)}, bf16[224,2048]{1,0:T(8,128)(2,1)}, u32[]{:S(2)}, u32[]{:S(2)}) %collective-permute-start.4) | collective-permute-done | bytes 917536 | tf_op jit(solution)/shard_map/ppermute | solution.py:485
  52.4 5.6 %collective-permute-start.5 = (bf16[224,2048]{1,0:T(8,128)(2,1)}, bf16[224,2048]{1,0:T(8,128)(2,1)}, u32[]{:S(2)}, u32[]{:S(2)}) collective-permute-start(bf16[224,2048]{1,0:T(8,128)(2,1)} %collective-permute-done.4.refs_5_.refs_1_.refs_2_), channel_id=1, source_target_pairs={{0,448},{64,0},{128,64},{192,128},{256,192},{320,256},{384,320},{4... | collective-permute-start | bytes 2752520 | tf_op jit(solution)/shard_map/ppermute | solution.py:485
  57.9 0.0 collective-permute-done.1.refs_2_.refs_0_.refs_7_
  58.0 0.0 copy-start.2
  58.0 1.9 %collective-permute-start.2 = (bf16[224,2048]{1,0:T(8,128)(2,1)S(1)}, bf16[224,2048]{1,0:T(8,128)(2,1)}, u32[]{:S(2)}, u32[]{:S(2)}) collective-permute-start(bf16[224,2048]{1,0:T(8,128)(2,1)S(1)} %collective-permute-done.1.refs_2_.refs_0_.refs_7_), channel_id=1, source_target_pairs={{0,64},{64,128},{128,192},{192,256},{256,320},{320,384},{384,448},... | collective-permute-start | bytes 2752520 | tf_op jit(solution)/shard_map/ppermute | solution.py:485
  59.9 1.2 tick.1.hottest_ref
  61.1 0.0 copy-done.2
  61.1 9.0 %all-to-all-done.arrived_ref = bf16[64,112,128]{2,1,0:T(8,128)(2,1)S(1)} async-done(((bf16[64,112,128]{2,1,0:T(8,128)(2,1)}), bf16[64,112,128]{2,1,0:T(8,128)(2,1)S(1)}, u32[]{:S(2)}, u32[]{:S(2)}) %all-to-all-start) | async-done | bytes 1835040 | tf_op jit(solution)/shard_map/all_to_all | solution.py:526
  70.1 0.7 repeat.1
  70.8 0.0 copy-start.3
  70.8 0.9 copy-done.3
  71.7 8.4 %all-to-all-start.2 = ((bf16[64,48,128]{2,1,0:T(8,128)(2,1)}), bf16[64,48,128]{2,1,0:T(8,128)(2,1)S(1)}, u32[]{:S(2)}, u32[]{:S(2)}) async-start(bf16[64,48,128]{2,1,0:T(8,128)(2,1)} %copy-done.3), calls=%async_computation.2 | async-start | bytes 1572864 | tf_op jit(solution)/shard_map/all_to_all | solution.py:527
  80.1 0.0 collective-permute-done.5.left_ref
  80.1 1.1 collective-permute-done.2.right_ref
  81.2 1.2 split.1
  82.4 1.9 %collective-permute-start.6 = (bf16[112,2048]{1,0:T(8,128)(2,1)S(1)}, bf16[112,2048]{1,0:T(8,128)(2,1)S(1)}, u32[]{:S(2)}, u32[]{:S(2)}) collective-permute-start(bf16[112,2048]{1,0:T(8,128)(2,1)S(1)} %get-tuple-element.25), channel_id=1, source_target_pairs={{0,64},{64,128},{128,192},{192,256},{256,320},{320,384},{384,448},... | collective-permute-start | bytes 1376264 | tf_op jit(solution)/shard_map/ppermute | solution.py:485
  84.3 5.1 %collective-permute-start.7 = (bf16[112,2048]{1,0:T(8,128)(2,1)S(1)}, bf16[112,2048]{1,0:T(8,128)(2,1)S(1)}, u32[]{:S(2)}, u32[]{:S(2)}) collective-permute-start(bf16[112,2048]{1,0:T(8,128)(2,1)S(1)} %get-tuple-element.26), channel_id=1, source_target_pairs={{0,448},{64,0},{128,64},{192,128},{256,192},{320,256},{384,320},{4... | collective-permute-start | bytes 1376264 | tf_op jit(solution)/shard_map/ppermute | solution.py:485
  89.5 5.3 %gathered.1 = (f32[128,4096]{1,0:T(8,128)S(1)}, bf16[128,4096]{1,0:T(8,128)(2,1)S(1)}) custom-call(bf16[64,112,128]{2,1,0:T(8,128)(2,1)S(1)} %all-to-all-done.arrived_ref, bf16[224,2048]{1,0:T(8,128)(2,1)} %copy-done.1, bf16[224,2048]{1,0:T(8,128)(2,1)} %collective-permute-done.refs_1_.refs_8_, bf16[224,2048]{1,0:T(8,128)(2,1)} %copy-done.2, ...), custom_call_target="tpu_custom_call" | custom-call | flops 1409286144 | bytes 5505024 | tf_op jit(solution)/shard_map/gathered/pallas_call | solution.py:207
  94.8 2.5 %collective-permute-done.6.up_ref.refs_4_ = bf16[112,2048]{1,0:T(8,128)(2,1)S(1)} collective-permute-done((bf16[112,2048]{1,0:T(8,128)(2,1)S(1)}, bf16[112,2048]{1,0:T(8,128)(2,1)S(1)}, u32[]{:S(2)}, u32[]{:S(2)}) %collective-permute-start.6) | collective-permute-done | bytes 458784 | tf_op jit(solution)/shard_map/ppermute | solution.py:485
  97.3 0.0 copy-start.4
  97.3 1.2 collective-permute-done.7.down_ref.refs_5_
  98.5 0.0 copy-start.5
  98.5 3.0 %last.1.after_ref = bf16[64,64,128]{2,1,0:T(8,128)(2,1)} custom-call(bf16[128,4096]{1,0:T(8,128)(2,1)S(1)} %get-tuple-element.23.rows_ref, f32[128,4096]{1,0:T(8,128)S(1)} %get-tuple-element.24.acc_ref, bf16[112,2048]{1,0:T(8,128)(2,1)S(1)} %collective-permute-done.6.up_ref.refs_4_, bf16[112,2048]{1,0:T(8,128)(2,1)S(1)} %collective-permute-done.7.down_ref.refs_5_), custom_call_target="tpu_custom_call" | custom-call | tf_op jit(solution)/shard_map/last/pallas_call | solution.py:253
  101.5 0.0 copy-done.4
  101.5 0.0 copy-done.5
  101.5 0.5 all-to-all-done.2.pieces_ref
  102.0 10.9 %all-to-all-start.1 = ((bf16[64,64,128]{2,1,0:T(8,128)(2,1)}), bf16[64,64,128]{2,1,0:T(8,128)(2,1)S(1)}, u32[]{:S(2)}, u32[]{:S(2)}) async-start(bf16[64,64,128]{2,1,0:T(8,128)(2,1)} %last.1.after_ref), calls=%async_computation.1 | async-start | bytes 2097152 | tf_op jit(solution)/shard_map/all_to_all | solution.py:531
  113.0 3.4 %hot.1 = (bf16[144,1024]{1,0:T(8,128)(2,1)S(1)}, bf16[144,1024]{1,0:T(8,128)(2,1)S(1)}) custom-call(s32[1]{0:T(128)} %bitcast.4.where_ref, bf16[64,48,128]{2,1,0:T(8,128)(2,1)S(1)} %all-to-all-done.2.pieces_ref, bf16[64,64,128]{2,1,0:T(8,128)(2,1)} %last.1.after_ref, bf16[224,2048]{1,0:T(8,128)(2,1)} %copy-done.1, ...), custom_call_target="tpu_custom_call" | custom-call | tf_op jit(solution)/shard_map/hot/pallas_call | solution.py:320
  116.4 0.0 copy-start.6
  116.4 0.0 copy-start.7
  116.4 0.0 copy-start.8
  116.4 9.9 %all-gather = bf16[288,1024]{1,0:T(8,128)(2,1)S(1)} all-gather(bf16[144,1024]{1,0:T(8,128)(2,1)S(1)} %get-tuple-element.31), channel_id=2, replica_groups={{0,64},{128,192},{256,320},{384,448},{1,65},{129,193},{257,321},{385,44..., dimensions={0}, use_global_device_ids=true | all-gather | bytes 884736 | tf_op jit(solution)/shard_map/all_gather | solution.py:491
  126.3 0.1 fusion
  126.5 5.3 %collective-permute-start.10 = (bf16[36,1024]{1,0:T(8,128)(2,1)S(1)}, bf16[36,1024]{1,0:T(8,128)(2,1)S(1)}, u32[]{:S(2)}, u32[]{:S(2)}) collective-permute-start(bf16[36,1024]{1,0:T(8,128)(2,1)S(1)} %get-tuple-element.37), channel_id=1, source_target_pairs={{0,384},{64,448},{128,256},{192,320},{256,128},{320,192},{384,0},{... | collective-permute-start | bytes 221192 | tf_op jit(solution)/shard_map/ppermute | solution.py:497
  131.8 2.2 %collective-permute-start.9 = (bf16[36,1024]{1,0:T(8,128)(2,1)S(1)}, bf16[36,1024]{1,0:T(8,128)(2,1)S(1)}, u32[]{:S(2)}, u32[]{:S(2)}) collective-permute-start(bf16[36,1024]{1,0:T(8,128)(2,1)S(1)} %get-tuple-element.38), channel_id=1, source_target_pairs={{0,128},{64,192},{128,0},{192,64},{256,384},{320,448},{384,256},{4... | collective-permute-start | bytes 221192 | tf_op jit(solution)/shard_map/ppermute | solution.py:497
  134.1 4.9 %collective-permute-start.8 = (bf16[36,1024]{1,0:T(8,128)(2,1)S(1)}, bf16[36,1024]{1,0:T(8,128)(2,1)S(1)}, u32[]{:S(2)}, u32[]{:S(2)}) collective-permute-start(bf16[36,1024]{1,0:T(8,128)(2,1)S(1)} %get-tuple-element.39), channel_id=1, source_target_pairs={{0,256},{64,320},{128,384},{192,448},{256,0},{320,64},{384,128},{4... | collective-permute-start | bytes 221192 | tf_op jit(solution)/shard_map/ppermute | solution.py:497
  139.0 0.7 all-to-all-done.1.cold_ref
  139.6 0.0 copy-done.6
  139.6 0.0 copy-done.7
  139.6 0.0 copy-done.8
  139.6 2.4 %cold_combine.1 = (f32[16,4096]{1,0:T(8,128)S(1)}, f32[8,16]{1,0:T(8,128)S(1)}) custom-call(s32[8,16]{1,0:T(8,128)S(1)} %bitcast.7, f32[8,16]{1,0:T(8,128)S(1)} %bitcast.9, bf16[16,2048]{1,0:T(8,128)(2,1)S(1)} %copy-done.6, bf16[64,64,128]{2,1,0:T(8,128)(2,1)S(1)} %all-to-all-done.1.cold_ref), custom_call_target="tpu_custom_call" | custom-call | flops 68719476736 | bytes 67108864 | tf_op jit(solution)/shard_map/cold_combine/pallas_call | solution.py:373
  142.0 0.0 collective-permute-done.10.refs_2_
  142.0 0.0 collective-permute-done.9.refs_1_
  142.1 2.3 %collective-permute-done.8.refs_0_ = bf16[36,1024]{1,0:T(8,128)(2,1)S(1)} collective-permute-done((bf16[36,1024]{1,0:T(8,128)(2,1)S(1)}, bf16[36,1024]{1,0:T(8,128)(2,1)S(1)}, u32[]{:S(2)}, u32[]{:S(2)}) %collective-permute-start.8) | collective-permute-done | bytes 73760 | tf_op jit(solution)/shard_map/ppermute | solution.py:497
  144.4 1.2 final_combine.1
  (2 shorter events, 0.1 us)
Async XLA Ops:
  2.6 9.1 %copy-start.1 = (bf16[224,2048]{1,0:T(8,128)(2,1)}, bf16[224,2048]{1,0:T(8,128)(2,1)S(1)}, u32[]{:S(2)}) copy-start(bf16[224,2048]{1,0:T(8,128)(2,1)S(1)} %get-tuple-element.20.refs_0_) | copy-start | bytes 2752516
  2.6 25.0 %collective-permute-start.3 = (bf16[224,2048]{1,0:T(8,128)(2,1)S(1)}, bf16[224,2048]{1,0:T(8,128)(2,1)}, u32[]{:S(2)}, u32[]{:S(2)}) collective-permute-start(bf16[224,2048]{1,0:T(8,128)(2,1)S(1)} %get-tuple-element.20.refs_0_), channel_id=1, source_target_pairs={{0,448},{64,0},{128,64},{192,128},{256,192},{320,256},{384,320},{4... | collective-permute-start | bytes 2752520 | tf_op jit(solution)/shard_map/ppermute | solution.py:485
  8.0 25.3 %collective-permute-start = (bf16[224,2048]{1,0:T(8,128)(2,1)S(1)}, bf16[224,2048]{1,0:T(8,128)(2,1)}, u32[]{:S(2)}, u32[]{:S(2)}) collective-permute-start(bf16[224,2048]{1,0:T(8,128)(2,1)S(1)} %get-tuple-element.20.refs_0_), channel_id=1, source_target_pairs={{0,64},{64,128},{128,192},{192,256},{256,320},{320,384},{384,448},... | collective-permute-start | bytes 2752520 | tf_op jit(solution)/shard_map/ppermute | solution.py:485
  11.7 1.3 copy-start
  13.0 57.1 %all-to-all-start = ((bf16[64,112,128]{2,1,0:T(8,128)(2,1)}), bf16[64,112,128]{2,1,0:T(8,128)(2,1)S(1)}, u32[]{:S(2)}, u32[]{:S(2)}) async-start(bf16[64,112,128]{2,1,0:T(8,128)(2,1)} %copy-done), calls=%async_computation | async-start | bytes 3670016 | tf_op jit(solution)/shard_map/all_to_all | solution.py:526
  27.6 24.8 %collective-permute-start.4 = (bf16[224,2048]{1,0:T(8,128)(2,1)}, bf16[224,2048]{1,0:T(8,128)(2,1)}, u32[]{:S(2)}, u32[]{:S(2)}) collective-permute-start(bf16[224,2048]{1,0:T(8,128)(2,1)} %collective-permute-done.3.refs_4_.refs_1_), channel_id=1, source_target_pairs={{0,448},{64,0},{128,64},{192,128},{256,192},{320,256},{384,320},{4... | collective-permute-start | bytes 2752520 | tf_op jit(solution)/shard_map/ppermute | solution.py:485
  33.3 24.6 %collective-permute-start.1 = (bf16[224,2048]{1,0:T(8,128)(2,1)}, bf16[224,2048]{1,0:T(8,128)(2,1)S(1)}, u32[]{:S(2)}, u32[]{:S(2)}) collective-permute-start(bf16[224,2048]{1,0:T(8,128)(2,1)} %collective-permute-done.refs_1_.refs_8_), channel_id=1, source_target_pairs={{0,64},{64,128},{128,192},{192,256},{256,320},{320,384},{384,448},... | collective-permute-start | bytes 2752520 | tf_op jit(solution)/shard_map/ppermute | solution.py:485
  52.4 27.8 %collective-permute-start.5 = (bf16[224,2048]{1,0:T(8,128)(2,1)}, bf16[224,2048]{1,0:T(8,128)(2,1)}, u32[]{:S(2)}, u32[]{:S(2)}) collective-permute-start(bf16[224,2048]{1,0:T(8,128)(2,1)} %collective-permute-done.4.refs_5_.refs_1_.refs_2_), channel_id=1, source_target_pairs={{0,448},{64,0},{128,64},{192,128},{256,192},{320,256},{384,320},{4... | collective-permute-start | bytes 2752520 | tf_op jit(solution)/shard_map/ppermute | solution.py:485
  58.0 3.1 %copy-start.2 = (bf16[224,2048]{1,0:T(8,128)(2,1)}, bf16[224,2048]{1,0:T(8,128)(2,1)S(1)}, u32[]{:S(2)}) copy-start(bf16[224,2048]{1,0:T(8,128)(2,1)S(1)} %collective-permute-done.1.refs_2_.refs_0_.refs_7_) | copy-start | bytes 2752516
  58.0 23.2 %collective-permute-start.2 = (bf16[224,2048]{1,0:T(8,128)(2,1)S(1)}, bf16[224,2048]{1,0:T(8,128)(2,1)}, u32[]{:S(2)}, u32[]{:S(2)}) collective-permute-start(bf16[224,2048]{1,0:T(8,128)(2,1)S(1)} %collective-permute-done.1.refs_2_.refs_0_.refs_7_), channel_id=1, source_target_pairs={{0,64},{64,128},{128,192},{192,256},{256,320},{320,384},{384,448},... | collective-permute-start | bytes 2752520 | tf_op jit(solution)/shard_map/ppermute | solution.py:485
  70.8 0.9 copy-start.3
  71.7 30.3 %all-to-all-start.2 = ((bf16[64,48,128]{2,1,0:T(8,128)(2,1)}), bf16[64,48,128]{2,1,0:T(8,128)(2,1)S(1)}, u32[]{:S(2)}, u32[]{:S(2)}) async-start(bf16[64,48,128]{2,1,0:T(8,128)(2,1)} %copy-done.3), calls=%async_computation.2 | async-start | bytes 1572864 | tf_op jit(solution)/shard_map/all_to_all | solution.py:527
  82.4 14.9 %collective-permute-start.6 = (bf16[112,2048]{1,0:T(8,128)(2,1)S(1)}, bf16[112,2048]{1,0:T(8,128)(2,1)S(1)}, u32[]{:S(2)}, u32[]{:S(2)}) collective-permute-start(bf16[112,2048]{1,0:T(8,128)(2,1)S(1)} %get-tuple-element.25), channel_id=1, source_target_pairs={{0,64},{64,128},{128,192},{192,256},{256,320},{320,384},{384,448},... | collective-permute-start | bytes 1376264 | tf_op jit(solution)/shard_map/ppermute | solution.py:485
  84.3 14.1 %collective-permute-start.7 = (bf16[112,2048]{1,0:T(8,128)(2,1)S(1)}, bf16[112,2048]{1,0:T(8,128)(2,1)S(1)}, u32[]{:S(2)}, u32[]{:S(2)}) collective-permute-start(bf16[112,2048]{1,0:T(8,128)(2,1)S(1)} %get-tuple-element.26), channel_id=1, source_target_pairs={{0,448},{64,0},{128,64},{192,128},{256,192},{320,256},{384,320},{4... | collective-permute-start | bytes 1376264 | tf_op jit(solution)/shard_map/ppermute | solution.py:485
  97.3 4.2 %copy-start.4 = (bf16[112,2048]{1,0:T(8,128)(2,1)}, bf16[112,2048]{1,0:T(8,128)(2,1)S(1)}, u32[]{:S(2)}) copy-start(bf16[112,2048]{1,0:T(8,128)(2,1)S(1)} %collective-permute-done.6.up_ref.refs_4_) | copy-start | bytes 1376260
  98.5 3.0 %copy-start.5 = (bf16[112,2048]{1,0:T(8,128)(2,1)}, bf16[112,2048]{1,0:T(8,128)(2,1)S(1)}, u32[]{:S(2)}) copy-start(bf16[112,2048]{1,0:T(8,128)(2,1)S(1)} %collective-permute-done.7.down_ref.refs_5_) | copy-start | bytes 1376260
  102.0 37.6 %all-to-all-start.1 = ((bf16[64,64,128]{2,1,0:T(8,128)(2,1)}), bf16[64,64,128]{2,1,0:T(8,128)(2,1)S(1)}, u32[]{:S(2)}, u32[]{:S(2)}) async-start(bf16[64,64,128]{2,1,0:T(8,128)(2,1)} %last.1.after_ref), calls=%async_computation.1 | async-start | bytes 2097152 | tf_op jit(solution)/shard_map/all_to_all | solution.py:531
  116.4 23.2 %copy-start.6 = (bf16[16,2048]{1,0:T(8,128)(2,1)S(1)}, bf16[16,2048]{1,0:T(8,128)(2,1)}, u32[]{:S(2)}) copy-start(bf16[16,2048]{1,0:T(8,128)(2,1)} %cot_ref.5) | copy-start | bytes 196612
  116.4 23.2 %copy-start.7 = (s32[16,8]{0,1:T(8,128)S(1)}, s32[16,8]{0,1:T(8,128)}, u32[]{:S(2)}) copy-start(s32[16,8]{0,1:T(8,128)} %param.9) | copy-start | bytes 1540
  116.4 23.2 %copy-start.8 = (f32[16,8]{0,1:T(8,128)S(1)}, f32[16,8]{0,1:T(8,128)}, u32[]{:S(2)}) copy-start(f32[16,8]{0,1:T(8,128)} %param.8) | copy-start | bytes 1540
  126.5 15.5 %collective-permute-start.10 = (bf16[36,1024]{1,0:T(8,128)(2,1)S(1)}, bf16[36,1024]{1,0:T(8,128)(2,1)S(1)}, u32[]{:S(2)}, u32[]{:S(2)}) collective-permute-start(bf16[36,1024]{1,0:T(8,128)(2,1)S(1)} %get-tuple-element.37), channel_id=1, source_target_pairs={{0,384},{64,448},{128,256},{192,320},{256,128},{320,192},{384,0},{... | collective-permute-start | bytes 221192 | tf_op jit(solution)/shard_map/ppermute | solution.py:497
  131.8 10.2 %collective-permute-start.9 = (bf16[36,1024]{1,0:T(8,128)(2,1)S(1)}, bf16[36,1024]{1,0:T(8,128)(2,1)S(1)}, u32[]{:S(2)}, u32[]{:S(2)}) collective-permute-start(bf16[36,1024]{1,0:T(8,128)(2,1)S(1)} %get-tuple-element.38), channel_id=1, source_target_pairs={{0,128},{64,192},{128,0},{192,64},{256,384},{320,448},{384,256},{4... | collective-permute-start | bytes 221192 | tf_op jit(solution)/shard_map/ppermute | solution.py:497
  134.1 10.3 %collective-permute-start.8 = (bf16[36,1024]{1,0:T(8,128)(2,1)S(1)}, bf16[36,1024]{1,0:T(8,128)(2,1)S(1)}, u32[]{:S(2)}, u32[]{:S(2)}) collective-permute-start(bf16[36,1024]{1,0:T(8,128)(2,1)S(1)} %get-tuple-element.39), channel_id=1, source_target_pairs={{0,256},{64,320},{128,384},{192,448},{256,0},{320,64},{384,128},{4... | collective-permute-start | bytes 221192 | tf_op jit(solution)/shard_map/ppermute | solution.py:497
